TPU v7x, 32 devices: a whole 2x2x4 slice. The times are simulated.
32 devices in a mesh: groups: 2 (over y), dp: 4 (over x, core), tensor: 4 (over z).
Axes of the slice: x: 2, y: 2, z: 4, core: 2. Of those that a mesh axis runs over, the one named last changes fastest.
Arguments:
- inputs: bfloat16 [4096, 3072], P(('groups', 'dp', 'tensor')), parts along dimension 0, may hold values from -40 to 40
- grad_out: bfloat16 [4096, 3072], P(('groups', 'dp', 'tensor')), parts along dimension 0, may hold values from -6 to 6
- norm_gain: float32 [3072], replicated, may hold values from 0.5 to 1.5
- level_order: int32 [4096], P(('groups', 'dp')), parts along dimension 0, may hold values from 0 to 511, as said below
- level_counts: int32 [8, 4], P(('groups', 'dp')), parts along dimension 0, may hold values from 0 to 256, as said below
- weight_in: bfloat16 [3072, 12288], P(None, 'tensor'), may hold values from -0.109375 to 0.109375
- weight_out: bfloat16 [12288, 3072], P('tensor'), may hold values from -0.0546875 to 0.0546875
Outputs:
- grad_input: bfloat16 [4096, 3072], P(('groups', 'dp', 'tensor')), parts along dimension 0
- grad_weight_in: bfloat16 [6144, 12288], P(('groups', 'dp'), 'tensor'), parts along dimension 0
- grad_weight_out: bfloat16 [24576, 3072], P(('groups', 'tensor'), 'dp'), parts along dimension 0
There are 2 independent parts, one for each index of `groups`. A program takes and returns all parts, laid end to end along the dimension named above; an argument that names none is the same for every part. Nothing has to cross between parts.
Inputs may be any that keep to these rules, and one draw needn't show every extreme that they name: `level_order`: within each aligned block of 512 entries a permutation of 0 to 511; within one level the indices rise. `level_counts`: row b holds the numbers of tokens of levels 0, 1, 2, 3 in block b and sums to 512; counts[b, 3] <= 128, counts[b, 3] + counts[b, 2] <= 256, counts[b, 3] + counts[b, 2] + counts[b, 1] <= 384, each bound met with equality in some block.
All inputs are finite; a program needn't handle non-finite values.
Results may differ from a plain program's by a relative error of at most 0.009.
Values may be sent and summed in bfloat16 or wider, within the bound.
No kernel may reach another device: no remote copies, remote signals or barrier semaphores. Data moves between devices by JAX's collectives and lax.ppermute only.
A program may use at most 256 MiB of HBM per device.

v0:
```python
import jax
import jax.numpy as jnp
from jax import lax
from jax.sharding import PartitionSpec as P

GELU_SCALE = 0.7978845608028654
GELU_CUBE = 0.044715
NORM_EPS = 1e-06


def gelu_parts(pre_act):
    tanh_val = jnp.tanh(GELU_SCALE * (pre_act + GELU_CUBE * pre_act * pre_act * pre_act))
    gelu_value = 0.5 * pre_act * (1.0 + tanh_val)
    gelu_slope = 0.5 * (1.0 + tanh_val) + 0.5 * pre_act * (
        1.0 - tanh_val * tanh_val
    ) * GELU_SCALE * (1.0 + 3.0 * GELU_CUBE * pre_act * pre_act)
    return (gelu_value, gelu_slope)


def token_levels(block_order, count_row):
    above_three = count_row[3]
    above_two = above_three + count_row[2]
    above_one = above_two + count_row[1]
    places = jnp.arange(block_order.shape[0], dtype=jnp.int32)
    ranked = (
        (places < above_three).astype(jnp.int32)
        + (places < above_two).astype(jnp.int32)
        + (places < above_one).astype(jnp.int32)
    )
    return jnp.zeros(block_order.shape[0], jnp.int32).at[block_order].set(ranked)


def column_bands(first_column, column_count, unit_total):
    columns = first_column + jnp.arange(column_count, dtype=jnp.int32)
    return (
        (columns >= unit_total // 8).astype(jnp.int32)
        + (columns >= unit_total // 4).astype(jnp.int32)
        + (columns >= unit_total // 2).astype(jnp.int32)
    )


def norm_backward(grad_normed, standard, row_scale, norm_gain):
    scaled = grad_normed * norm_gain[None, :]
    centre = jnp.mean(scaled, axis=1, keepdims=True)
    along = jnp.mean(scaled * standard, axis=1, keepdims=True)
    return row_scale * (scaled - centre - standard * along)


def shards(inputs, grad_out, norm_gain, level_order, level_counts, weight_in, weight_out):
    own_rows = inputs.shape[0]
    position = lax.axis_index("tensor")
    unit_local = weight_in.shape[1]
    unit_total = unit_local * lax.axis_size("tensor")
    gathered, grad_rows = (
        lax.all_gather(inputs, "tensor", axis=0, tiled=True),
        lax.all_gather(grad_out, "tensor", axis=0, tiled=True),
    )
    as_float = gathered.astype(jnp.float32)
    row_mean = jnp.mean(as_float, axis=1, keepdims=True)
    centred = as_float - row_mean
    row_scale = lax.rsqrt(jnp.mean(centred * centred, axis=1, keepdims=True) + NORM_EPS)
    standard = centred * row_scale
    normed = (standard * norm_gain[None, :]).astype(jnp.bfloat16)
    token_level = token_levels(level_order, level_counts[0])
    unit_band = column_bands(position * unit_local, unit_local, unit_total)
    unit_mask = unit_band[None, :] <= token_level[:, None]
    pre_act = jnp.dot(normed, weight_in, preferred_element_type=jnp.float32)
    gelu_value, gelu_slope = gelu_parts(pre_act)
    hidden = jnp.where(unit_mask, gelu_value, 0.0).astype(jnp.bfloat16)
    out_term = lax.dot_general(
        hidden, grad_rows, (((0,), (0,)), ((), ())), preferred_element_type=jnp.float32
    )
    grad_hidden = lax.dot_general(
        grad_rows, weight_out, (((1,), (1,)), ((), ())), preferred_element_type=jnp.float32
    )
    grad_pre = jnp.where(unit_mask, grad_hidden * gelu_slope, 0.0).astype(jnp.bfloat16)
    grad_normed = lax.dot_general(
        grad_pre, weight_in, (((1,), (1,)), ((), ())), preferred_element_type=jnp.float32
    )
    in_term = lax.dot_general(
        normed, grad_pre, (((0,), (0,)), ((), ())), preferred_element_type=jnp.float32
    )
    grad_normed_part, in_term, out_term = (grad_normed, in_term, out_term)
    blocks = lax.axis_size("dp")
    grad_weight_out = (
        lax.psum_scatter(
            out_term.astype(jnp.bfloat16), "dp", scatter_dimension=1, tiled=True
        ).astype(jnp.float32)
        / blocks
    ).astype(jnp.bfloat16)
    grad_weight_in = (
        lax.psum_scatter(
            in_term.astype(jnp.bfloat16), "dp", scatter_dimension=0, tiled=True
        ).astype(jnp.float32)
        / blocks
    ).astype(jnp.bfloat16)
    row_start = position * own_rows
    own_grad = lax.psum_scatter(
        grad_normed_part.astype(jnp.bfloat16), "tensor", scatter_dimension=0, tiled=True
    ).astype(jnp.float32)
    branch_grad = norm_backward(
        own_grad,
        lax.dynamic_slice_in_dim(standard, row_start, own_rows, 0),
        lax.dynamic_slice_in_dim(row_scale, row_start, own_rows, 0),
        norm_gain,
    )
    grad_input = (grad_out.astype(jnp.float32) + branch_grad).astype(jnp.bfloat16)
    return (grad_input, grad_weight_in, grad_weight_out)


def solution(mesh):
    in_specs = (
        P(("groups", "dp", "tensor"), None),
        P(("groups", "dp", "tensor"), None),
        P(),
        P(("groups", "dp")),
        P(("groups", "dp"), None),
        P(None, "tensor"),
        P("tensor", None),
    )
    out_specs = (
        P(("groups", "dp", "tensor"), None),
        P(("groups", "dp"), "tensor"),
        P(("groups", "tensor"), "dp"),
    )
    return jax.shard_map(shards, mesh=mesh, in_specs=in_specs, out_specs=out_specs, check_vma=False)
```

profile of v0, /device:TPU:0, one launch (start us, length us, event | category | flops | bytes accessed | tf_op | source)
XLA Modules:
  0.0 530.9 jit_solution(16112963595314632483)
XLA Ops:
  7.2 0.7 all-gather.3.cloned.1.call-update
  8.0 0.7 all-gather.5.cloned.1.call-update
  8.7 1.4 fusion.33
  12.0 1.3 compare_select_fusion.2
  13.3 2.4 scatter_custom_fusion
  15.8 60.0 %all-gather.3.cloned.1.call-done = bf16[512,3072]{1,0:T(8,128)(2,1)} async-done(((bf16[128,3072]{1,0:T(8,128)(2,1)}), bf16[512,3072]{1,0:T(8,128)(2,1)}) %all-gather.3.cloned.1.call-update) | async-done | bytes 3145744 | tf_op jit(solution)/shard_map/all_gather | solution.py:55
  75.8 2.5 convert_reduce_fusion
  78.3 2.8 fusion.2
  81.2 16.2 %fusion.20 = f32[512,3072]{1,0:T(8,128)} fusion(bf16[3072,3072]{1,0:T(8,128)(2,1)} %param.12, f32[3072]{0:T(1024)S(1)} %copy-done.1, bf16[512,3072]{1,0:T(8,128)(2,1)S(1)} %copy-done, f32[512]{0:T(512)S(1)} %add_rsqrt_fusion, f32[512]{0:T(512)S(1)} %broadcast_multiply_fusion), kind=kOutput, calls=%fused_computation.35 | convolution fusion | flops 9671540736 | bytes 28327936 | tf_op jit(solution)/shard_map/dot_general | solution.py:67
  97.4 42.2 %all-gather.5.cloned.1.call-done = bf16[512,3072]{1,0:T(8,128)(2,1)} async-done(((bf16[128,3072]{1,0:T(8,128)(2,1)}), bf16[512,3072]{1,0:T(8,128)(2,1)}) %all-gather.5.cloned.1.call-update) | async-done | bytes 3145744 | tf_op jit(solution)/shard_map/all_gather | solution.py:56
  139.6 20.1 %fusion.3 = bf16[512,3072]{1,0:T(8,128)(2,1)} fusion(f32[512,3072]{1,0:T(8,128)} %fusion.20, bf16[512,3072]{1,0:T(8,128)(2,1)} %all-gather.5.cloned.1.call-done, bf16[3072,3072]{1,0:T(8,128)(2,1)} %param.13, s32[3072]{0:T(1024)S(1)} %convert_add_fusion, s32[512]{0:T(512)S(1)} %scatter_custom_fusion), kind=kOutput, calls=%fused_computation.14 | convolution fusion | flops 9696706560 | bytes 31471616 | tf_op jit(solution)/shard_map/dot_general | solution.py:73
  159.7 15.9 %convolution_convert_fusion.2 = bf16[512,3072]{1,0:T(8,128)(2,1)} fusion(bf16[512,3072]{1,0:T(8,128)(2,1)} %fusion.3, bf16[3072,3072]{1,0:T(8,128)(2,1)} %param.12), kind=kOutput, calls=%fused_computation.23 | convolution fusion | flops 9665249280 | bytes 25165824 | tf_op jit(solution)/shard_map/dot_general | solution.py:77
  175.6 19.9 %convolution_convert_fusion = bf16[3072,3072]{1,0:T(8,128)(2,1)} fusion(bf16[512,3072]{1,0:T(8,128)(2,1)} %all-gather.5.cloned.1.call-done, f32[512,3072]{1,0:T(8,128)} %fusion.20, s32[3072]{0:T(1024)S(1)} %convert_add_fusion, s32[512]{0:T(512)S(1)} %scatter_custom_fusion), kind=kOutput, calls=%fused_computation.1 | convolution fusion | flops 9690415104 | bytes 28325888 | tf_op jit(solution)/shard_map/dot_general | solution.py:70
  195.5 0.0 reduce-scatter.6.cloned.1.call-start
  195.6 15.8 %convolution_convert_fusion.1 = bf16[3072,3072]{1,0:T(8,128)(2,1)} fusion(bf16[512,3072]{1,0:T(8,128)(2,1)} %fusion.3, f32[3072]{0:T(1024)S(1)} %copy-done.1, bf16[512,3072]{1,0:T(8,128)(2,1)S(1)} %copy-done, f32[512]{0:T(512)S(1)} %add_rsqrt_fusion, f32[512]{0:T(512)S(1)} %broadcast_multiply_fusion), kind=kOutput, calls=%fused_computation.2 | convolution fusion | flops 9680977920 | bytes 25182208 | tf_op jit(solution)/shard_map/dot_general | solution.py:80
  211.4 0.1 dynamic-slice.3
  211.5 3.8 fusion
  215.3 19.3 %reduce-scatter.4.cloned.1.call-done = bf16[128,3072]{1,0:T(8,128)(2,1)} async-done(((bf16[512,3072]{1,0:T(8,128)(2,1)}), bf16[128,3072]{1,0:T(8,128)(2,1)}) %reduce-scatter.4.cloned.1.call-update) | async-done | bytes 786448 | tf_op jit(solution)/shard_map/reduce_scatter | solution.py:98
  234.7 2.0 fusion.19
  236.7 3.3 add_convert_fusion
  240.0 136.6 %reduce-scatter.8.cloned.1.call-done = bf16[3072,768]{1,0:T(8,128)(2,1)} async-done(((bf16[3072,3072]{1,0:T(8,128)(2,1)}), bf16[3072,768]{1,0:T(8,128)(2,1)}) %reduce-scatter.8.cloned.1.call-update) | async-done | bytes 4718608 | tf_op jit(solution)/shard_map/reduce_scatter | solution.py:86
  376.6 5.4 %multiply_convert_fusion = bf16[3072,768]{1,0:T(8,128)(2,1)} fusion(bf16[3072,768]{1,0:T(8,128)(2,1)} %reduce-scatter.8.cloned.1.call-done), kind=kLoop, calls=%fused_computation.5 | loop fusion | flops 7077888 | bytes 9437184 | tf_op jit(solution)/shard_map/convert_element_type | solution.py:90
  382.0 136.7 %reduce-scatter.6.cloned.1.call-done = bf16[768,3072]{1,0:T(8,128)(2,1)} async-done(((bf16[3072,3072]{1,0:T(8,128)(2,1)}), bf16[768,3072]{1,0:T(8,128)(2,1)}) %reduce-scatter.6.cloned.1.call-update) | async-done | bytes 4718608 | tf_op jit(solution)/shard_map/reduce_scatter | solution.py:92
  518.7 5.6 %multiply_convert_fusion.1 = bf16[768,3072]{1,0:T(8,128)(2,1)} fusion(bf16[768,3072]{1,0:T(8,128)(2,1)} %reduce-scatter.6.cloned.1.call-done), kind=kLoop, calls=%fused_computation.6 | loop fusion | flops 7077888 | bytes 9437184 | tf_op jit(solution)/shard_map/convert_element_type | solution.py:96
  (16 shorter events, 0.2 us)
Async XLA Ops:
  7.2 74.0 %copy-start.1 = (f32[3072]{0:T(1024)S(1)}, f32[3072]{0:T(1024)}, u32[]{:S(2)}) copy-start(f32[3072]{0:T(1024)} %param.9) | copy-start | bytes 36868
  7.2 68.6 %all-gather.3.cloned.1.call-start = ((), (), s32[]{:S(2)}) async-start(), calls=%async_computation.3 | async-start | bytes 3932160 | tf_op jit(solution)/shard_map/all_gather | solution.py:55
  7.9 131.7 %all-gather.5.cloned.1.call-start = ((), (), s32[]{:S(2)}) async-start(), calls=%async_computation.4 | async-start | bytes 3932160 | tf_op jit(solution)/shard_map/all_gather | solution.py:56
  8.7 226.0 %reduce-scatter.4.cloned.1.call-start = ((), (), s32[]{:S(2)}) async-start(), calls=%async_computation.5 | async-start | bytes 3932160 | tf_op jit(solution)/shard_map/reduce_scatter | solution.py:98
  75.8 5.4 %copy-start = (bf16[512,3072]{1,0:T(8,128)(2,1)S(1)}, bf16[512,3072]{1,0:T(8,128)(2,1)}, u32[]{:S(2)}) copy-start(bf16[512,3072]{1,0:T(8,128)(2,1)} %all-gather.3.cloned.1.call-done) | copy-start | bytes 9437188
  175.6 201.0 %reduce-scatter.8.cloned.1.call-start = ((), (), s32[]{:S(2)}) async-start(), calls=%async_computation.7 | async-start | bytes 23592960 | tf_op jit(solution)/shard_map/reduce_scatter | solution.py:86
  195.5 323.2 %reduce-scatter.6.cloned.1.call-start = ((), (), s32[]{:S(2)}) async-start(), calls=%async_computation.6 | async-start | bytes 23592960 | tf_op jit(solution)/shard_map/reduce_scatter | solution.py:92
Sparse Core Ops, SparseCore 0:
  9.6 66.1 all-gather.2
  77.4 62.1 all-gather.4
  175.7 58.8 reduce-scatter.3
  237.1 139.4 reduce-scatter.7
  379.2 139.4 reduce-scatter.5
where the time goes:
time: 531 us
  waiting for transfers between devices  396 us (75%)
  matrix products  87.8 us (17%)
  other arithmetic  26.9 us (5%)
  between operations  15.8 us (3%)
    reduce_scatter x1, waiting for transfers between devices, shards(): lax.psum_scatter(in_term.astype(jnp.bfloat16), 'dp', scatter_dimension=0,...  137 us
    reduce_scatter x1, waiting for transfers between devices, shards(): lax.psum_scatter(out_term.astype(jnp.bfloat16), 'dp', scatter_dimension=1...  137 us
    all_gather x1, waiting for transfers between devices, shards(): lax.all_gather(inputs, 'tensor', axis=0, tiled=True)  60 us
    all_gather x1, waiting for transfers between devices, shards(): lax.all_gather(grad_out, 'tensor', axis=0, tiled=True)  42.2 us
    dot_general x1, matrix products, shards(): lax.dot_general(grad_rows, weight_out, (((1,), (1,)), ((), ())), preferre...  20.1 us
    dot_general x1, matrix products, shards(): lax.dot_general(hidden, grad_rows, (((0,), (0,)), ((), ())), preferred_el...  19.9 us
    reduce_scatter x1, waiting for transfers between devices, shards(): lax.psum_scatter(grad_normed_part.astype(jnp.bfloat16), 'tensor', scatter...  19.3 us
    dot_general x1, matrix products, shards(): pre_act = jnp.dot(normed, weight_in, preferred_element_type=jnp.float32)  16.2 us
  transfers between devices with their start and end apart: 5, of which 5 were waited for; matrix products, arithmetic and copies ran while one was open for 14% of the time, Pallas kernels for 0%

commit v1 on v0

v1 whole, which is shorter than its diff:
```python
import jax
import jax.numpy as jnp
from jax import lax
from jax.sharding import PartitionSpec as P

GELU_SCALE = 0.7978845608028654
GELU_CUBE = 0.044715
NORM_EPS = 1e-06


def gelu_parts(pre_act):
    tanh_val = jnp.tanh(GELU_SCALE * (pre_act + GELU_CUBE * pre_act * pre_act * pre_act))
    gelu_value = 0.5 * pre_act * (1.0 + tanh_val)
    gelu_slope = 0.5 * (1.0 + tanh_val) + 0.5 * pre_act * (
        1.0 - tanh_val * tanh_val
    ) * GELU_SCALE * (1.0 + 3.0 * GELU_CUBE * pre_act * pre_act)
    return (gelu_value, gelu_slope)


def token_levels(block_order, count_row):
    above_three = count_row[3]
    above_two = above_three + count_row[2]
    above_one = above_two + count_row[1]
    places = jnp.arange(block_order.shape[0], dtype=jnp.int32)
    ranked = (
        (places < above_three).astype(jnp.int32)
        + (places < above_two).astype(jnp.int32)
        + (places < above_one).astype(jnp.int32)
    )
    hits = block_order[None, :] == places[:, None]
    return jnp.sum(jnp.where(hits, ranked[None, :], 0), axis=1)


def column_bands(first_column, column_count, unit_total):
    columns = first_column + jnp.arange(column_count, dtype=jnp.int32)
    return (
        (columns >= unit_total // 8).astype(jnp.int32)
        + (columns >= unit_total // 4).astype(jnp.int32)
        + (columns >= unit_total // 2).astype(jnp.int32)
    )


def norm_backward(grad_normed, standard, row_scale, norm_gain):
    scaled = grad_normed * norm_gain[None, :]
    centre = jnp.mean(scaled, axis=1, keepdims=True)
    along = jnp.mean(scaled * standard, axis=1, keepdims=True)
    return row_scale * (scaled - centre - standard * along)


def shards(inputs, grad_out, norm_gain, level_order, level_counts, weight_in, weight_out):
    rows = inputs.shape[0]
    ring = lax.axis_size("tensor")
    place = lax.axis_index("tensor")
    blocks = lax.axis_size("dp")
    block = lax.axis_index("dp")
    chips = blocks // 2
    unit_local = weight_in.shape[1]
    unit_total = unit_local * ring
    features = inputs.shape[1]
    share = features // blocks

    from_next = [((i + 1) % ring, i) for i in range(ring)]
    from_chip = [((i + 2) % blocks, i) for i in range(blocks)]
    swap_cores = [(i, i ^ 1) for i in range(blocks)]

    as_float = inputs.astype(jnp.float32)
    row_mean = jnp.mean(as_float, axis=1, keepdims=True)
    centred = as_float - row_mean
    row_scale = lax.rsqrt(jnp.mean(centred * centred, axis=1, keepdims=True) + NORM_EPS)
    standard = centred * row_scale
    normed = (standard * norm_gain[None, :]).astype(jnp.bfloat16)

    levels = token_levels(level_order, level_counts[0])
    levels = lax.dynamic_slice_in_dim(jnp.concatenate([levels, levels]), place * rows, rows * ring, 0)
    level_sets = [levels]
    for _ in range(chips - 1):
        level_sets.append(lax.ppermute(level_sets[-1], "dp", from_chip))
    unit_band = column_bands(place * unit_local, unit_local, unit_total)

    own_cols = block * share
    swap_cols = (block ^ 1) * share

    def columns(value, first):
        return lax.dynamic_slice_in_dim(value, first, share, 1)

    grad_ring, normed_ring = grad_out, normed
    hiddens, grad_pres, grad_cols, normed_cols = [], [], [], []
    own_normed_grads = []
    for step in range(ring):
        if step > 0:
            grad_ring = lax.ppermute(grad_ring, "tensor", from_next)
            normed_ring = lax.ppermute(normed_ring, "tensor", from_next)
        grad_set, normed_set = [grad_ring], [normed_ring]
        for _ in range(chips - 1):
            grad_set.append(lax.ppermute(grad_set[-1], "dp", from_chip))
            normed_set.append(lax.ppermute(normed_set[-1], "dp", from_chip))
        grad_rows = jnp.concatenate(grad_set)
        normed_rows = jnp.concatenate(normed_set)
        row_level = jnp.concatenate([one[step * rows : (step + 1) * rows] for one in level_sets])
        unit_mask = unit_band[None, :] <= row_level[:, None]
        pre_act = jnp.dot(normed_rows, weight_in, preferred_element_type=jnp.float32)
        gelu_value, gelu_slope = gelu_parts(pre_act)
        hidden = jnp.where(unit_mask, gelu_value, 0.0).astype(jnp.bfloat16)
        grad_hidden = lax.dot_general(
            grad_rows, weight_out, (((1,), (1,)), ((), ())), preferred_element_type=jnp.float32
        )
        grad_pre = jnp.where(unit_mask, grad_hidden * gelu_slope, 0.0).astype(jnp.bfloat16)
        hiddens += [hidden, lax.ppermute(hidden, "dp", swap_cores)]
        grad_pres += [grad_pre, lax.ppermute(grad_pre, "dp", swap_cores)]
        grad_cols += [
            columns(grad_rows, own_cols),
            lax.ppermute(columns(grad_rows, swap_cols), "dp", swap_cores),
        ]
        normed_cols += [
            columns(normed_rows, own_cols),
            lax.ppermute(columns(normed_rows, swap_cols), "dp", swap_cores),
        ]
        own_normed_grads.append(
            lax.dot_general(
                grad_pre[:rows], weight_in, (((1,), (1,)), ((), ())), preferred_element_type=jnp.float32
            )
        )
    travelling = None
    for step in range(1, ring):
        total = own_normed_grads[step]
        if travelling is not None:
            total = total + travelling.astype(jnp.float32)
        travelling = lax.ppermute(total.astype(jnp.bfloat16), "tensor", from_next)
    own_grad = own_normed_grads[0]
    if travelling is not None:
        own_grad = own_grad + travelling.astype(jnp.float32)
    branch_grad = norm_backward(own_grad, standard, row_scale, norm_gain)
    grad_input = (grad_out.astype(jnp.float32) + branch_grad).astype(jnp.bfloat16)

    grad_weight_out = lax.dot_general(
        jnp.concatenate(hiddens),
        jnp.concatenate(grad_cols),
        (((0,), (0,)), ((), ())),
        preferred_element_type=jnp.float32,
    )
    grad_weight_in = lax.dot_general(
        jnp.concatenate(normed_cols),
        jnp.concatenate(grad_pres),
        (((0,), (0,)), ((), ())),
        preferred_element_type=jnp.float32,
    )
    grad_weight_out = (grad_weight_out / blocks).astype(jnp.bfloat16)
    grad_weight_in = (grad_weight_in / blocks).astype(jnp.bfloat16)
    return (grad_input, grad_weight_in, grad_weight_out)


def solution(mesh):
    in_specs = (
        P(("groups", "dp", "tensor"), None),
        P(("groups", "dp", "tensor"), None),
        P(),
        P(("groups", "dp")),
        P(("groups", "dp"), None),
        P(None, "tensor"),
        P("tensor", None),
    )
    out_specs = (
        P(("groups", "dp", "tensor"), None),
        P(("groups", "dp"), "tensor"),
        P(("groups", "tensor"), "dp"),
    )
    return jax.shard_map(shards, mesh=mesh, in_specs=in_specs, out_specs=out_specs, check_vma=False)
```

time: 531 us -> 364 us (0.69); the launches traced: 531 us -> 357 us
  waiting for transfers between devices: 396 us -> 103 us
  matrix products: 87.8 us -> 171 us
  local copies, waits for them, and re-layouts: 3.87 us -> 40.5 us
  starting transfers between devices: 0.2 us -> 25.5 us
  other arithmetic: 26.9 us -> 13.4 us
  between operations: 15.8 us -> 3.46 us
    reduce_scatter x3 -> x0, waiting for transfers between devices: 293 us -> none  [the longest x1 137 us: shards(): lax.psum_scatter(in_term.astype(jnp.bfloat16), 'dp', scatter_dimension=0,...]
    ppermute x0 -> x34, waiting for transfers between devices: none -> 103 us  [the longest x4 31 us: shards(): normed_set.append(lax.ppermute(normed_set[-1], 'dp', from_chip))]
    all_gather x2 -> x0, waiting for transfers between devices: 102 us -> none  [the longest x1 60 us: shards(): lax.all_gather(inputs, 'tensor', axis=0, tiled=True)]
    dot_general x4 -> x10, matrix products: 67.7 us -> 123 us  [the longest x4 49 us: shards(): lax.dot_general(grad_pre[:rows], weight_in, (((1,), (1,)), ((), ())), pre...]
    dot_general x1 -> x4, matrix products: 20.1 us -> 48.4 us  [shards(): lax.dot_general(grad_rows, weight_out, (((1,), (1,)), ((), ())), preferre...]
    ppermute x0 -> x34, starting transfers between devices: none -> 25.5 us  [the longest x3 7.86 us: shards(): normed_ring = lax.ppermute(normed_ring, 'tensor', from_next)]
    unnamed x4 -> x69, local copies, waits for them, and re-layouts: 0.01 us -> 23.8 us
    concatenate x0 -> x11, local copies, waits for them, and re-layouts: none -> 9.97 us  [the longest x1 2.88 us: shards(): jnp.concatenate(hiddens)]
  transfers between devices with their start and end apart: 5 -> 34, of which waited for: 5 -> 9; matrix products, arithmetic and copies ran while one was open for 14% -> 57% of each run, Pallas kernels for 0% -> 0%
where the time goes in v1:
time: 364 us; the launch traced here: 357 us
  matrix products  171 us (47%)
  waiting for transfers between devices  103 us (28%)
  local copies, waits for them, and re-layouts  40.5 us (11%)
  starting transfers between devices  25.5 us (7%)
  other arithmetic  13.4 us (4%)
    dot_general x4, matrix products, shards(): lax.dot_general(grad_pre[:rows], weight_in, (((1,), (1,)), ((), ())), pre...  49 us
    dot_general x4, matrix products, shards(): lax.dot_general(grad_rows, weight_out, (((1,), (1,)), ((), ())), preferre...  48.4 us
    dot_general x4, matrix products, shards(): jnp.dot(normed_rows, weight_in, preferred_element_type=jnp.float32)  47.2 us
    ppermute x4, waiting for transfers between devices, shards(): normed_set.append(lax.ppermute(normed_set[-1], 'dp', from_chip))  31 us
    ppermute x1, waiting for transfers between devices, shards(): level_sets.append(lax.ppermute(level_sets[-1], 'dp', from_chip))  28.4 us
    ppermute x4, waiting for transfers between devices, shards(): grad_set.append(lax.ppermute(grad_set[-1], 'dp', from_chip))  26.5 us
    unnamed x69, local copies, waits for them, and re-layouts  23.8 us
    dot_general x1, matrix products, shards(): lax.dot_general(jnp.concatenate(hiddens), jnp.concatenate(grad_cols), (((...  14.7 us
  transfers between devices with their start and end apart: 34, of which 9 were waited for; matrix products, arithmetic and copies ran while one was open for 57% of the time, Pallas kernels for 0%

profile of v1, /device:TPU:0, one launch (start us, length us, event | category | flops | bytes accessed | tf_op | source)
XLA Modules:
  0.0 356.7 jit_solution(16154375118709241340)
XLA Ops:
  5.0 5.1 %collective-permute-start.7 = (bf16[128,3072]{1,0:T(8,128)(2,1)S(1)}, bf16[128,3072]{1,0:T(8,128)(2,1)}, u32[]{:S(2)}, u32[]{:S(2)}) collective-permute-start(bf16[128,3072]{1,0:T(8,128)(2,1)S(1)} %fusion.37), channel_id=1, source_target_pairs={{1,0},{2,1},{3,2},{0,3},{5,4},{6,5},{7,6},{4,7},{9,8},{10,9},{11,1... | collective-permute-start | bytes 2359304 | tf_op jit(solution)/shard_map/ppermute | solution.py:92
  17.7 28.4 %collective-permute-done = s32[512]{0:T(512)S(1)} collective-permute-done((s32[512]{0:T(512)S(1)}, s32[512]{0:T(512)S(1)}, u32[]{:S(2)}, u32[]{:S(2)}) %collective-permute-start) | collective-permute-done | bytes 2080 | tf_op jit(solution)/shard_map/ppermute | solution.py:77
  52.4 11.3 %constant_dynamic-update-slice_fusion.33 = (bf16[2048,3072]{1,0:T(8,128)(2,1)}, bf16[256,3072]{1,0:T(8,128)(2,1)}, f32[256,3072]{1,0:T(8,128)}) fusion(s32[256]{0:T(256)S(1)} %pad_add_fusion.1, s32[3072]{0:T(1024)S(1)} %convert_add_fusion, bf16[3072,3072]{1,0:T(8,128)(2,1)} %param.12, bf16[128,3072]{1,0:T(8,128)(2,1)} %collective-permute-done.2, ...), kind=kOutput, calls=%fused_computation.127 | convolution fusion | flops 4843634688 | bytes 26752000 | tf_op jit(solution)/shard_map/dot_general | solution.py:101
  63.8 12.3 %constant_dynamic-update-slice_fusion.25 = (bf16[2048,3072]{1,0:T(8,128)(2,1)}, bf16[256,3072]{1,0:T(8,128)(2,1)}) fusion(f32[256,3072]{1,0:T(8,128)} %get-tuple-element.49, bf16[256,3072]{1,0:T(8,128)(2,1)S(1)} %constant_dynamic-update-slice_fusion, bf16[3072,3072]{1,0:T(8,128)(2,1)} %param.13, s32[256]{0:T(256)S(1)} %pad_add_fusion.1, ...), kind=kOutput, calls=%fused_computation.119 | convolution fusion | flops 4848353280 | bytes 26752000 | tf_op jit(solution)/shard_map/dot_general | solution.py:104
  84.5 12.2 %collective-permute-done.13 = bf16[128,3072]{1,0:T(8,128)(2,1)S(1)} collective-permute-done((bf16[128,3072]{1,0:T(8,128)(2,1)}, bf16[128,3072]{1,0:T(8,128)(2,1)S(1)}, u32[]{:S(2)}, u32[]{:S(2)}) %collective-permute-start.13) | collective-permute-done | bytes 786464 | tf_op jit(solution)/shard_map/ppermute | solution.py:95
  98.1 15.1 %collective-permute-done.14 = bf16[128,3072]{1,0:T(8,128)(2,1)S(1)} collective-permute-done((bf16[128,3072]{1,0:T(8,128)(2,1)}, bf16[128,3072]{1,0:T(8,128)(2,1)S(1)}, u32[]{:S(2)}, u32[]{:S(2)}) %collective-permute-start.14) | collective-permute-done | bytes 786464 | tf_op jit(solution)/shard_map/ppermute | solution.py:96
  115.8 4.6 %collective-permute-done.4 = bf16[128,3072]{1,0:T(8,128)(2,1)} collective-permute-done((bf16[128,3072]{1,0:T(8,128)(2,1)}, bf16[128,3072]{1,0:T(8,128)(2,1)}, u32[]{:S(2)}, u32[]{:S(2)}) %collective-permute-start.4) | collective-permute-done | bytes 786464 | tf_op jit(solution)/shard_map/ppermute | solution.py:91
  129.2 14.4 %constant_dynamic-update-slice_fusion.31 = (bf16[2048,3072]{1,0:T(8,128)(2,1)}, bf16[256,3072]{1,0:T(8,128)(2,1)}, f32[256,3072]{1,0:T(8,128)}) fusion(bf16[2048,3072]{1,0:T(8,128)(2,1)} %constant_dynamic-update-slice_fusion.32, s32[256]{0:T(256)S(1)} %copy-done.20, s32[3072]{0:T(1024)S(1)} %convert_add_fusion, ...), kind=kOutput, calls=%fused_computation.125 | convolution fusion | flops 4840488960 | bytes 26752000 | tf_op jit(solution)/shard_map/dot_general | solution.py:101
  144.9 12.2 %constant_dynamic-update-slice_fusion.23 = (bf16[2048,3072]{1,0:T(8,128)(2,1)}, bf16[256,3072]{1,0:T(8,128)(2,1)}) fusion(bf16[2048,3072]{1,0:T(8,128)(2,1)} %constant_dynamic-update-slice_fusion.24, f32[256,3072]{1,0:T(8,128)} %get-tuple-element.50, bf16[256,3072]{1,0:T(8,128)(2,1)S(1)} %constant_dynamic-update-slice_fusion.10, ...), kind=kOutput, calls=%fused_computation.117 | convolution fusion | flops 4848353280 | bytes 26752000 | tf_op jit(solution)/shard_map/dot_general | solution.py:104
  157.1 13.8 %convolution_convert_fusion = bf16[128,3072]{1,0:T(8,128)(2,1)} fusion(bf16[3072,3072]{1,0:T(8,128)(2,1)} %param.12, bf16[256,3072]{1,0:T(8,128)(2,1)} %get-tuple-element.44), kind=kOutput, calls=%fused_computation.26 | convolution fusion | flops 2416312320 | bytes 20447232 | tf_op jit(solution)/shard_map/dot_general | solution.py:119
  181.2 14.3 %collective-permute-done.6 = bf16[128,3072]{1,0:T(8,128)(2,1)S(1)} collective-permute-done((bf16[128,3072]{1,0:T(8,128)(2,1)}, bf16[128,3072]{1,0:T(8,128)(2,1)S(1)}, u32[]{:S(2)}, u32[]{:S(2)}) %collective-permute-start.6) | collective-permute-done | bytes 786464 | tf_op jit(solution)/shard_map/ppermute | solution.py:95
  195.9 15.9 %collective-permute-done.10 = bf16[128,3072]{1,0:T(8,128)(2,1)S(1)} collective-permute-done((bf16[128,3072]{1,0:T(8,128)(2,1)}, bf16[128,3072]{1,0:T(8,128)(2,1)S(1)}, u32[]{:S(2)}, u32[]{:S(2)}) %collective-permute-start.10) | collective-permute-done | bytes 786464 | tf_op jit(solution)/shard_map/ppermute | solution.py:96
  214.3 10.7 %constant_dynamic-update-slice_fusion.29 = (bf16[2048,3072]{1,0:T(8,128)(2,1)}, bf16[256,3072]{1,0:T(8,128)(2,1)}, f32[256,3072]{1,0:T(8,128)S(1)}) fusion(bf16[2048,3072]{1,0:T(8,128)(2,1)} %constant_dynamic-update-slice_fusion.30, s32[256]{0:T(256)S(1)} %copy-done.19, s32[3072]{0:T(1024)S(1)} %convert_add_fusion, ...), kind=kOutput, calls=%fused_computation.123 | convolution fusion | flops 4840488960 | bytes 26752000 | tf_op jit(solution)/shard_map/dot_general | solution.py:101
  226.3 12.0 %constant_dynamic-update-slice_fusion.21 = (bf16[2048,3072]{1,0:T(8,128)(2,1)}, bf16[256,3072]{1,0:T(8,128)(2,1)}) fusion(bf16[2048,3072]{1,0:T(8,128)(2,1)} %constant_dynamic-update-slice_fusion.22, f32[256,3072]{1,0:T(8,128)S(1)} %get-tuple-element.51, bf16[256,3072]{1,0:T(8,128)(2,1)S(1)} %constant_dynamic-update-slice_fusion.6, ...), kind=kOutput, calls=%fused_computation.115 | convolution fusion | flops 4848353280 | bytes 26752000 | tf_op jit(solution)/shard_map/dot_general | solution.py:104
  238.7 14.0 %add_convert_fusion.1 = bf16[128,3072]{1,0:T(8,128)(2,1)} fusion(bf16[128,3072]{1,0:T(8,128)(2,1)} %collective-permute-done.15, bf16[3072,3072]{1,0:T(8,128)(2,1)} %param.12, bf16[256,3072]{1,0:T(8,128)(2,1)} %get-tuple-element.46), kind=kOutput, calls=%fused_computation.73 | convolution fusion | flops 2417098752 | bytes 21233664 | tf_op jit(solution)/shard_map/dot_general | solution.py:119
  254.3 10.7 %constant_dynamic-update-slice_fusion.27 = (bf16[2048,3072]{1,0:T(8,128)(2,1)}, bf16[256,3072]{1,0:T(8,128)(2,1)}, f32[256,3072]{1,0:T(8,128)S(1)}) fusion(bf16[2048,3072]{1,0:T(8,128)(2,1)} %constant_dynamic-update-slice_fusion.28, s32[256]{0:T(256)S(1)} %copy-done.18, s32[3072]{0:T(1024)S(1)} %convert_add_fusion, bf16[256,3072]{1,0:T(8,128)(2,1)S(1)} %copy-done.6, ...), kind=kOutput, calls=%fused_computation.121 | convolution fusion | flops 4840488960 | bytes 26752000 | tf_op jit(solution)/shard_map/dot_general | solution.py:101
  267.0 11.9 %constant_dynamic-update-slice_fusion.19 = (bf16[2048,3072]{1,0:T(8,128)(2,1)}, bf16[256,3072]{1,0:T(8,128)(2,1)}) fusion(bf16[2048,3072]{1,0:T(8,128)(2,1)} %constant_dynamic-update-slice_fusion.20, f32[256,3072]{1,0:T(8,128)S(1)} %get-tuple-element.52, bf16[256,3072]{1,0:T(8,128)(2,1)S(1)} %copy-done.3, bf16[3072,3072]{1,0:T(8,128)(2,1)} %param.13, ...), kind=kOutput, calls=%fused_computation.113 | convolution fusion | flops 4848353280 | bytes 26752000 | tf_op jit(solution)/shard_map/dot_general | solution.py:104
  278.9 10.3 %fusion.50 = f32[128,3072]{1,0:T(8,128)S(1)} fusion(bf16[3072,3072]{1,0:T(8,128)(2,1)} %param.12, bf16[256,3072]{1,0:T(8,128)(2,1)} %get-tuple-element.48), kind=kOutput, calls=%fused_computation.79 | convolution fusion | flops 2415919104 | bytes 21233664 | tf_op jit(solution)/shard_map/dot_general | solution.py:119
  298.8 11.7 %collective-permute-done.17 = bf16[128,3072]{1,0:T(8,128)(2,1)S(1)} collective-permute-done((bf16[128,3072]{1,0:T(8,128)(2,1)S(1)}, bf16[128,3072]{1,0:T(8,128)(2,1)S(1)}, u32[]{:S(2)}, u32[]{:S(2)}) %collective-permute-start.17) | collective-permute-done | bytes 786464 | tf_op jit(solution)/shard_map/ppermute | solution.py:128
  310.6 10.9 %fusion.54 = (f32[128]{0:T(128)S(1)}, f32[128]{0:T(128)S(1)}, f32[128,3072]{1,0:T(8,128)S(1)}) fusion(f32[3072]{0:T(1024)S(1)} %copy-done.11, bf16[128,3072]{1,0:T(8,128)(2,1)S(1)} %collective-permute-done.17, f32[128]{0:T(128)} %copy-done.14, f32[128]{0:T(128)S(1)} %broadcast_multiply_fusion.2, bf16[128,3072]{1,0:T(8,128)(2,1)S(1)} %copy-done, ...), kind=kOutput, calls=%fused_computation.83 | convolution fusion | flops 2419458048 | bytes 22820864 | tf_op jit(solution)/shard_map/dot_general | solution.py:119
  321.5 3.0 fusion.42
  324.5 2.9 constant_dynamic-update-slice_fusion.26
  327.4 14.7 %multiply_convert_fusion = bf16[3072,768]{1,0:T(8,128)(2,1)} fusion(bf16[2048,3072]{1,0:T(8,128)(2,1)} %constant_dynamic-update-slice_fusion.26, bf16[2048,768]{1,0:T(8,128)(2,1)S(1)} %copy-done.12), kind=kOutput, calls=%fused_computation | convolution fusion | flops 9668395008 | bytes 20447232 | tf_op jit(solution)/shard_map/dot_general | solution.py:135
  344.5 11.8 %multiply_convert_fusion.1 = bf16[768,3072]{1,0:T(8,128)(2,1)} fusion(bf16[2048,768]{1,0:T(8,128)(2,1)S(1)} %copy-done.13, bf16[2048,3072]{1,0:T(8,128)(2,1)S(1)} %constant_dynamic-update-slice_fusion.18), kind=kOutput, calls=%fused_computation.1 | convolution fusion | flops 9668395008 | bytes 20447232 | tf_op jit(solution)/shard_map/dot_general | solution.py:141
  (167 shorter events, 69.0 us)
Async XLA Ops:
  5.0 73.9 %collective-permute-start.7 = (bf16[128,3072]{1,0:T(8,128)(2,1)S(1)}, bf16[128,3072]{1,0:T(8,128)(2,1)}, u32[]{:S(2)}, u32[]{:S(2)}) collective-permute-start(bf16[128,3072]{1,0:T(8,128)(2,1)S(1)} %fusion.37), channel_id=1, source_target_pairs={{1,0},{2,1},{3,2},{0,3},{5,4},{6,5},{7,6},{4,7},{9,8},{10,9},{11,1... | collective-permute-start | bytes 2359304 | tf_op jit(solution)/shard_map/ppermute | solution.py:92
  10.1 39.8 %collective-permute-start.2 = (bf16[128,3072]{1,0:T(8,128)(2,1)S(1)}, bf16[128,3072]{1,0:T(8,128)(2,1)}, u32[]{:S(2)}, u32[]{:S(2)}) collective-permute-start(bf16[128,3072]{1,0:T(8,128)(2,1)S(1)} %fusion.37), channel_id=1, source_target_pairs={{8,0},{12,4},{0,8},{4,12},{9,1},{13,5},{1,9},{5,13},{10,2},{14,6},... | collective-permute-start | bytes 2359304 | tf_op jit(solution)/shard_map/ppermute | solution.py:96
  11.6 36.3 %collective-permute-start.1 = (bf16[128,3072]{1,0:T(8,128)(2,1)S(1)}, bf16[128,3072]{1,0:T(8,128)(2,1)}, u32[]{:S(2)}, u32[]{:S(2)}) collective-permute-start(bf16[128,3072]{1,0:T(8,128)(2,1)S(1)} %copy-done.1), channel_id=1, source_target_pairs={{8,0},{12,4},{0,8},{4,12},{9,1},{13,5},{1,9},{5,13},{10,2},{14,6},... | collective-permute-start | bytes 2359304 | tf_op jit(solution)/shard_map/ppermute | solution.py:95
  12.2 63.9 %collective-permute-start.3 = (bf16[128,3072]{1,0:T(8,128)(2,1)S(1)}, bf16[128,3072]{1,0:T(8,128)(2,1)}, u32[]{:S(2)}, u32[]{:S(2)}) collective-permute-start(bf16[128,3072]{1,0:T(8,128)(2,1)S(1)} %copy-done.1), channel_id=1, source_target_pairs={{1,0},{2,1},{3,2},{0,3},{5,4},{6,5},{7,6},{4,7},{9,8},{10,9},{11,1... | collective-permute-start | bytes 2359304 | tf_op jit(solution)/shard_map/ppermute | solution.py:91
  16.1 30.0 %collective-permute-start = (s32[512]{0:T(512)S(1)}, s32[512]{0:T(512)S(1)}, u32[]{:S(2)}, u32[]{:S(2)}) collective-permute-start(s32[512]{0:T(512)S(1)} %dynamic_slice.51), channel_id=1, source_target_pairs={{8,0},{12,4},{0,8},{4,12},{9,1},{13,5},{1,9},{5,13},{10,2},{14,6},... | collective-permute-start | bytes 6152 | tf_op jit(solution)/shard_map/ppermute | solution.py:77
  50.0 30.8 %collective-permute-start.30 = (bf16[256,768]{1,0:T(8,128)(2,1)S(1)}, bf16[256,768]{1,0:T(8,128)(2,1)S(1)}, u32[]{:S(2)}, u32[]{:S(2)}) collective-permute-start(bf16[256,768]{1,0:T(8,128)(2,1)S(1)} %get-tuple-element.19), channel_id=1, source_target_pairs={{0,4},{4,0},{8,12},{12,8},{1,5},{5,1},{9,13},{13,9},{2,6},{6,2},{1... | collective-permute-start | bytes 1179656 | tf_op jit(solution)/shard_map/ppermute | solution.py:112
  51.9 31.4 %collective-permute-start.18 = (bf16[256,768]{1,0:T(8,128)(2,1)}, bf16[256,768]{1,0:T(8,128)(2,1)S(1)}, u32[]{:S(2)}, u32[]{:S(2)}) collective-permute-start(bf16[256,768]{1,0:T(8,128)(2,1)} %get-tuple-element.27), channel_id=1, source_target_pairs={{0,4},{4,0},{8,12},{12,8},{1,5},{5,1},{9,13},{13,9},{2,6},{6,2},{1... | collective-permute-start | bytes 1179656 | tf_op jit(solution)/shard_map/ppermute | solution.py:116
  63.7 63.7 %collective-permute-start.26 = (bf16[256,3072]{1,0:T(8,128)(2,1)}, bf16[256,3072]{1,0:T(8,128)(2,1)S(1)}, u32[]{:S(2)}, u32[]{:S(2)}) collective-permute-start(bf16[256,3072]{1,0:T(8,128)(2,1)} %get-tuple-element.12), channel_id=1, source_target_pairs={{0,4},{4,0},{8,12},{12,8},{1,5},{5,1},{9,13},{13,9},{2,6},{6,2},{1... | collective-permute-start | bytes 4718600 | tf_op jit(solution)/shard_map/ppermute | solution.py:108
  78.9 34.3 %collective-permute-start.14 = (bf16[128,3072]{1,0:T(8,128)(2,1)}, bf16[128,3072]{1,0:T(8,128)(2,1)S(1)}, u32[]{:S(2)}, u32[]{:S(2)}) collective-permute-start(bf16[128,3072]{1,0:T(8,128)(2,1)} %collective-permute-done.7), channel_id=1, source_target_pairs={{8,0},{12,4},{0,8},{4,12},{9,1},{13,5},{1,9},{5,13},{10,2},{14,6},... | collective-permute-start | bytes 2359304 | tf_op jit(solution)/shard_map/ppermute | solution.py:96
  81.5 62.2 %collective-permute-start.22 = (bf16[256,3072]{1,0:T(8,128)(2,1)S(1)}, bf16[256,3072]{1,0:T(8,128)(2,1)S(1)}, u32[]{:S(2)}, u32[]{:S(2)}) collective-permute-start(bf16[256,3072]{1,0:T(8,128)(2,1)S(1)} %copy-done.9), channel_id=1, source_target_pairs={{0,4},{4,0},{8,12},{12,8},{1,5},{5,1},{9,13},{13,9},{2,6},{6,2},{1... | collective-permute-start | bytes 4718600 | tf_op jit(solution)/shard_map/ppermute | solution.py:109
  83.3 30.8 %collective-permute-start.8 = (bf16[128,3072]{1,0:T(8,128)(2,1)}, bf16[128,3072]{1,0:T(8,128)(2,1)}, u32[]{:S(2)}, u32[]{:S(2)}) collective-permute-start(bf16[128,3072]{1,0:T(8,128)(2,1)} %collective-permute-done.7), channel_id=1, source_target_pairs={{1,0},{2,1},{3,2},{0,3},{5,4},{6,5},{7,6},{4,7},{9,8},{10,9},{11,1... | collective-permute-start | bytes 2359304 | tf_op jit(solution)/shard_map/ppermute | solution.py:92
  120.4 54.4 %collective-permute-start.12 = (bf16[128,3072]{1,0:T(8,128)(2,1)}, bf16[128,3072]{1,0:T(8,128)(2,1)}, u32[]{:S(2)}, u32[]{:S(2)}) collective-permute-start(bf16[128,3072]{1,0:T(8,128)(2,1)} %collective-permute-done.8), channel_id=1, source_target_pairs={{8,0},{12,4},{0,8},{4,12},{9,1},{13,5},{1,9},{5,13},{10,2},{14,6},... | collective-permute-start | bytes 2359304 | tf_op jit(solution)/shard_map/ppermute | solution.py:96
  123.1 55.5 %collective-permute-start.9 = (bf16[128,3072]{1,0:T(8,128)(2,1)}, bf16[128,3072]{1,0:T(8,128)(2,1)}, u32[]{:S(2)}, u32[]{:S(2)}) collective-permute-start(bf16[128,3072]{1,0:T(8,128)(2,1)} %collective-permute-done.8), channel_id=1, source_target_pairs={{1,0},{2,1},{3,2},{0,3},{5,4},{6,5},{7,6},{4,7},{9,8},{10,9},{11,1... | collective-permute-start | bytes 2359304 | tf_op jit(solution)/shard_map/ppermute | solution.py:92
  126.2 44.8 %collective-permute-start.11 = (bf16[128,3072]{1,0:T(8,128)(2,1)}, bf16[128,3072]{1,0:T(8,128)(2,1)}, u32[]{:S(2)}, u32[]{:S(2)}) collective-permute-start(bf16[128,3072]{1,0:T(8,128)(2,1)} %collective-permute-done.4), channel_id=1, source_target_pairs={{8,0},{12,4},{0,8},{4,12},{9,1},{13,5},{1,9},{5,13},{10,2},{14,6},... | collective-permute-start | bytes 2359304 | tf_op jit(solution)/shard_map/ppermute | solution.py:95
  127.5 46.0 %collective-permute-start.5 = (bf16[128,3072]{1,0:T(8,128)(2,1)}, bf16[128,3072]{1,0:T(8,128)(2,1)}, u32[]{:S(2)}, u32[]{:S(2)}) collective-permute-start(bf16[128,3072]{1,0:T(8,128)(2,1)} %collective-permute-done.4), channel_id=1, source_target_pairs={{1,0},{2,1},{3,2},{0,3},{5,4},{6,5},{7,6},{4,7},{9,8},{10,9},{11,1... | collective-permute-start | bytes 2359304 | tf_op jit(solution)/shard_map/ppermute | solution.py:91
  170.9 54.0 %collective-permute-start.23 = (bf16[256,3072]{1,0:T(8,128)(2,1)}, bf16[256,3072]{1,0:T(8,128)(2,1)S(1)}, u32[]{:S(2)}, u32[]{:S(2)}) collective-permute-start(bf16[256,3072]{1,0:T(8,128)(2,1)} %get-tuple-element.44), channel_id=1, source_target_pairs={{0,4},{4,0},{8,12},{12,8},{1,5},{5,1},{9,13},{13,9},{2,6},{6,2},{1... | collective-permute-start | bytes 4718600 | tf_op jit(solution)/shard_map/ppermute | solution.py:109
  173.5 38.4 %collective-permute-start.27 = (bf16[256,3072]{1,0:T(8,128)(2,1)S(1)}, bf16[256,3072]{1,0:T(8,128)(2,1)S(1)}, u32[]{:S(2)}, u32[]{:S(2)}) collective-permute-start(bf16[256,3072]{1,0:T(8,128)(2,1)S(1)} %copy-done.21), channel_id=1, source_target_pairs={{0,4},{4,0},{8,12},{12,8},{1,5},{5,1},{9,13},{13,9},{2,6},{6,2},{1... | collective-permute-start | bytes 4718600 | tf_op jit(solution)/shard_map/ppermute | solution.py:108
  178.6 33.2 %collective-permute-start.10 = (bf16[128,3072]{1,0:T(8,128)(2,1)}, bf16[128,3072]{1,0:T(8,128)(2,1)S(1)}, u32[]{:S(2)}, u32[]{:S(2)}) collective-permute-start(bf16[128,3072]{1,0:T(8,128)(2,1)} %collective-permute-done.9), channel_id=1, source_target_pairs={{8,0},{12,4},{0,8},{4,12},{9,1},{13,5},{1,9},{5,13},{10,2},{14,6},... | collective-permute-start | bytes 2359304 | tf_op jit(solution)/shard_map/ppermute | solution.py:96
  180.3 112.9 %collective-permute-start.20 = (bf16[256,768]{1,0:T(8,128)(2,1)}, bf16[256,768]{1,0:T(8,128)(2,1)S(1)}, u32[]{:S(2)}, u32[]{:S(2)}) collective-permute-start(bf16[256,768]{1,0:T(8,128)(2,1)} %get-tuple-element.23), channel_id=1, source_target_pairs={{0,4},{4,0},{8,12},{12,8},{1,5},{5,1},{9,13},{13,9},{2,6},{6,2},{1... | collective-permute-start | bytes 1179656 | tf_op jit(solution)/shard_map/ppermute | solution.py:116
  195.5 43.2 %collective-permute-start.15 = (bf16[128,3072]{1,0:T(8,128)(2,1)S(1)}, bf16[128,3072]{1,0:T(8,128)(2,1)}, u32[]{:S(2)}, u32[]{:S(2)}) collective-permute-start(bf16[128,3072]{1,0:T(8,128)(2,1)S(1)} %copy-done.8), channel_id=1, source_target_pairs={{1,0},{2,1},{3,2},{0,3},{5,4},{6,5},{7,6},{4,7},{9,8},{10,9},{11,1... | collective-permute-start | bytes 2359304 | tf_op jit(solution)/shard_map/ppermute | solution.py:128
  225.0 28.1 %collective-permute-start.28 = (bf16[256,3072]{1,0:T(8,128)(2,1)}, bf16[256,3072]{1,0:T(8,128)(2,1)S(1)}, u32[]{:S(2)}, u32[]{:S(2)}) collective-permute-start(bf16[256,3072]{1,0:T(8,128)(2,1)} %get-tuple-element.8), channel_id=1, source_target_pairs={{0,4},{4,0},{8,12},{12,8},{1,5},{5,1},{9,13},{13,9},{2,6},{6,2},{1... | collective-permute-start | bytes 4718600 | tf_op jit(solution)/shard_map/ppermute | solution.py:108
  238.2 26.8 %collective-permute-start.24 = (bf16[256,3072]{1,0:T(8,128)(2,1)}, bf16[256,3072]{1,0:T(8,128)(2,1)S(1)}, u32[]{:S(2)}, u32[]{:S(2)}) collective-permute-start(bf16[256,3072]{1,0:T(8,128)(2,1)} %get-tuple-element.46), channel_id=1, source_target_pairs={{0,4},{4,0},{8,12},{12,8},{1,5},{5,1},{9,13},{13,9},{2,6},{6,2},{1... | collective-permute-start | bytes 4718600 | tf_op jit(solution)/shard_map/ppermute | solution.py:109
  252.7 36.5 %collective-permute-start.16 = (bf16[128,3072]{1,0:T(8,128)(2,1)}, bf16[128,3072]{1,0:T(8,128)(2,1)}, u32[]{:S(2)}, u32[]{:S(2)}) collective-permute-start(bf16[128,3072]{1,0:T(8,128)(2,1)} %add_convert_fusion.1), channel_id=1, source_target_pairs={{1,0},{2,1},{3,2},{0,3},{5,4},{6,5},{7,6},{4,7},{9,8},{10,9},{11,1... | collective-permute-start | bytes 2359304 | tf_op jit(solution)/shard_map/ppermute | solution.py:128
  298.3 43.8 %collective-permute-start.25 = (bf16[256,3072]{1,0:T(8,128)(2,1)}, bf16[256,3072]{1,0:T(8,128)(2,1)}, u32[]{:S(2)}, u32[]{:S(2)}) collective-permute-start(bf16[256,3072]{1,0:T(8,128)(2,1)} %get-tuple-element.48), channel_id=1, source_target_pairs={{0,4},{4,0},{8,12},{12,8},{1,5},{5,1},{9,13},{13,9},{2,6},{6,2},{1... | collective-permute-start | bytes 4718600 | tf_op jit(solution)/shard_map/ppermute | solution.py:109
  (35 other events, 419.1 us)

commit v2 on v1

v2 whole, which is shorter than its diff:
```python
import functools

import jax
import jax.numpy as jnp
from jax import lax
from jax.experimental import pallas as pl
from jax.experimental.pallas import tpu as pltpu
from jax.sharding import PartitionSpec as P

GELU_SCALE = 0.7978845608028654
GELU_CUBE = 0.044715
NORM_EPS = 1e-06
GROUP_ROWS = 256
VMEM_LIMIT = 48 * 1024 * 1024


def gelu_parts(pre_act):
    tanh_val = jnp.tanh(GELU_SCALE * (pre_act + GELU_CUBE * pre_act * pre_act * pre_act))
    gelu_value = 0.5 * pre_act * (1.0 + tanh_val)
    gelu_slope = 0.5 * (1.0 + tanh_val) + 0.5 * pre_act * (
        1.0 - tanh_val * tanh_val
    ) * GELU_SCALE * (1.0 + 3.0 * GELU_CUBE * pre_act * pre_act)
    return (gelu_value, gelu_slope)


def token_levels(block_order, count_row):
    above_three = count_row[3]
    above_two = above_three + count_row[2]
    above_one = above_two + count_row[1]
    places = jnp.arange(block_order.shape[0], dtype=jnp.int32)
    ranked = (
        (places < above_three).astype(jnp.int32)
        + (places < above_two).astype(jnp.int32)
        + (places < above_one).astype(jnp.int32)
    )
    hits = block_order[None, :] == places[:, None]
    return jnp.sum(jnp.where(hits, ranked[None, :], 0), axis=1)


def norm_backward(grad_normed, standard, row_scale, norm_gain):
    scaled = grad_normed * norm_gain[None, :]
    centre = jnp.mean(scaled, axis=1, keepdims=True)
    along = jnp.mean(scaled * standard, axis=1, keepdims=True)
    return row_scale * (scaled - centre - standard * along)


def tile_of(extent, wanted):
    while extent % wanted:
        wanted //= 2
    return wanted


def group_kernel(spots, *refs, pieces, unit_total, share, with_grad):
    normed_refs = refs[:pieces]
    grad_refs = refs[pieces : 2 * pieces]
    level_ref, in_ref, out_ref = refs[2 * pieces : 2 * pieces + 3]
    outs = refs[2 * pieces + 3 :]
    acts_ref, own_ref, swap_ref = outs[:3]
    tile = pl.program_id(0)
    normed = jnp.concatenate([ref[...] for ref in normed_refs], axis=0)
    grads = jnp.concatenate([ref[...] for ref in grad_refs], axis=0)

    @pl.when(tile == 0)
    def _():
        own = pl.ds(pl.multiple_of(spots[1], 128), share)
        swap = pl.ds(pl.multiple_of(spots[2], 128), share)
        for kind, sources in enumerate((normed_refs, grad_refs)):
            for at, ref in enumerate(sources):
                size = ref.shape[0]
                own_ref[kind, at * size : (at + 1) * size, :] = ref[:, own]
                swap_ref[kind, at * size : (at + 1) * size, :] = ref[:, swap]

    pre_act = jnp.dot(normed, in_ref[...], preferred_element_type=jnp.float32)
    grad_hidden = lax.dot_general(
        grads, out_ref[...], (((1,), (1,)), ((), ())), preferred_element_type=jnp.float32
    )
    rows, units = pre_act.shape
    column = spots[0] + tile * units + lax.broadcasted_iota(jnp.int32, (rows, units), 1)
    band = (
        (column >= unit_total // 8).astype(jnp.int32)
        + (column >= unit_total // 4).astype(jnp.int32)
        + (column >= unit_total // 2).astype(jnp.int32)
    )
    mask = band <= level_ref[...]
    gelu_value, gelu_slope = gelu_parts(pre_act)
    hidden = jnp.where(mask, gelu_value, 0.0).astype(jnp.bfloat16)
    grad_pre = jnp.where(mask, grad_hidden * gelu_slope, 0.0).astype(jnp.bfloat16)
    acts_ref[0] = grad_pre
    acts_ref[1] = hidden
    if with_grad:
        back_ref = outs[3]
        term = lax.dot_general(
            grad_pre, in_ref[...], (((1,), (1,)), ((), ())), preferred_element_type=jnp.float32
        )

        @pl.when(tile == 0)
        def _():
            back_ref[...] = term

        @pl.when(tile != 0)
        def _():
            back_ref[...] += term


def group_call(spots, normed, grads, level, weight_in, weight_out, unit_total, share, with_grad):
    features, units = weight_in.shape
    pieces = len(normed)
    rows = sum(one.shape[0] for one in normed)
    tile = tile_of(units, 512)
    whole = lambda shape: pl.BlockSpec(shape, lambda i, spots: (0,) * len(shape))
    out_shape = [
        jax.ShapeDtypeStruct((2, rows, units), jnp.bfloat16),
        jax.ShapeDtypeStruct((2, rows, share), jnp.bfloat16),
        jax.ShapeDtypeStruct((2, rows, share), jnp.bfloat16),
    ]
    out_specs = [
        pl.BlockSpec((2, rows, tile), lambda i, spots: (0, 0, i)),
        whole((2, rows, share)),
        whole((2, rows, share)),
    ]
    if with_grad:
        out_shape.append(jax.ShapeDtypeStruct((rows, features), jnp.float32))
        out_specs.append(whole((rows, features)))
    return pl.pallas_call(
        functools.partial(
            group_kernel, pieces=pieces, unit_total=unit_total, share=share, with_grad=with_grad
        ),
        grid_spec=pltpu.PrefetchScalarGridSpec(
            num_scalar_prefetch=1,
            grid=(units // tile,),
            in_specs=[whole(one.shape) for one in (*normed, *grads)]
            + [
                whole((rows, 1)),
                pl.BlockSpec((features, tile), lambda i, spots: (0, i)),
                pl.BlockSpec((tile, features), lambda i, spots: (i, 0)),
            ],
            out_specs=out_specs,
        ),
        out_shape=out_shape,
        compiler_params=pltpu.CompilerParams(vmem_limit_bytes=VMEM_LIMIT),
        cost_estimate=pl.CostEstimate(
            flops=2 * rows * units * features, bytes_accessed=weight_in.size * 2, transcendentals=0
        ),
        name="group",
    )(spots, *normed, *grads, level, weight_in, weight_out)


def weights_kernel(*refs, groups, scale):
    act_refs = refs[:groups]
    col_refs = refs[groups : 2 * groups]
    in_ref, out_ref = refs[2 * groups :]

    def stack(sources, kind):
        return jnp.concatenate([ref[kind] for ref in sources], axis=0)

    def total(left, right):
        return lax.dot_general(
            left, right, (((0,), (0,)), ((), ())), preferred_element_type=jnp.float32
        )

    in_ref[...] = (total(stack(col_refs, 0), stack(act_refs, 0)) * scale).astype(jnp.bfloat16)
    out_ref[...] = (total(stack(act_refs, 1), stack(col_refs, 1)) * scale).astype(jnp.bfloat16)


def weights_call(acts, cols, blocks):
    units, share = acts[0].shape[2], cols[0].shape[2]
    tile = tile_of(units, 512)
    rows = sum(one.shape[1] for one in acts)
    return pl.pallas_call(
        functools.partial(weights_kernel, groups=len(acts), scale=1.0 / blocks),
        grid=(units // tile,),
        in_specs=[pl.BlockSpec((2, one.shape[1], tile), lambda i: (0, 0, i)) for one in acts]
        + [pl.BlockSpec(one.shape, lambda i: (0, 0, 0)) for one in cols],
        out_specs=[
            pl.BlockSpec((share, tile), lambda i: (0, i)),
            pl.BlockSpec((tile, share), lambda i: (i, 0)),
        ],
        out_shape=[
            jax.ShapeDtypeStruct((share, units), jnp.bfloat16),
            jax.ShapeDtypeStruct((units, share), jnp.bfloat16),
        ],
        compiler_params=pltpu.CompilerParams(vmem_limit_bytes=VMEM_LIMIT),
        cost_estimate=pl.CostEstimate(
            flops=4 * rows * units * share, bytes_accessed=2 * rows * units * 2, transcendentals=0
        ),
        name="weights",
    )(*acts, *cols)


def shards(inputs, grad_out, norm_gain, level_order, level_counts, weight_in, weight_out):
    rows = inputs.shape[0]
    ring = lax.axis_size("tensor")
    place = lax.axis_index("tensor")
    blocks = lax.axis_size("dp")
    block = lax.axis_index("dp")
    chips = blocks // 2
    unit_local = weight_in.shape[1]
    unit_total = unit_local * ring
    share = inputs.shape[1] // blocks
    pieces = max(1, min(ring, GROUP_ROWS // rows))

    from_next = [((i + 1) % ring, i) for i in range(ring)]
    from_chip = [((i + 2) % blocks, i) for i in range(blocks)]
    swap_cores = [(i, i ^ 1) for i in range(blocks)]

    as_float = inputs.astype(jnp.float32)
    row_mean = jnp.mean(as_float, axis=1, keepdims=True)
    centred = as_float - row_mean
    row_scale = lax.rsqrt(jnp.mean(centred * centred, axis=1, keepdims=True) + NORM_EPS)
    standard = centred * row_scale
    normed = (standard * norm_gain[None, :]).astype(jnp.bfloat16)

    levels = token_levels(level_order, level_counts[0])
    levels = lax.dynamic_slice_in_dim(jnp.concatenate([levels, levels]), place * rows, rows * ring, 0)
    level_sets = [levels]
    for _ in range(chips - 1):
        level_sets.append(lax.ppermute(level_sets[-1], "dp", from_chip))
    spots = jnp.stack([place * unit_local, block * share, (block ^ 1) * share]).astype(jnp.int32)

    grad_rings, normed_rings = [grad_out], [normed]
    for _ in range(ring - 1):
        grad_rings.append(lax.ppermute(grad_rings[-1], "tensor", from_next))
        normed_rings.append(lax.ppermute(normed_rings[-1], "tensor", from_next))
    grad_sets, normed_sets = [grad_rings], [normed_rings]
    for _ in range(chips - 1):
        grad_sets.append([lax.ppermute(one, "dp", from_chip) for one in grad_sets[-1]])
        normed_sets.append([lax.ppermute(one, "dp", from_chip) for one in normed_sets[-1]])

    acts, cols, own_grads = [], [], []
    for first in range(0, ring, pieces):
        span = slice(first, first + pieces)
        for chip in range(chips):
            level = level_sets[chip][first * rows : (first + pieces) * rows, None]
            act, own_cols, swap_cols, *back = group_call(
                spots,
                normed_sets[chip][span],
                grad_sets[chip][span],
                level,
                weight_in,
                weight_out,
                unit_total,
                share,
                chip == 0,
            )
            acts += [act, lax.ppermute(act, "dp", swap_cores)]
            cols += [own_cols, lax.ppermute(swap_cols, "dp", swap_cores)]
            own_grads += [back[0][i * rows : (i + 1) * rows] for i in range(pieces) if back]
    travelling = None
    for step in range(1, ring):
        total = own_grads[step]
        if travelling is not None:
            total = total + travelling.astype(jnp.float32)
        travelling = lax.ppermute(total.astype(jnp.bfloat16), "tensor", from_next)
    own_grad = own_grads[0]
    if travelling is not None:
        own_grad = own_grad + travelling.astype(jnp.float32)
    branch_grad = norm_backward(own_grad, standard, row_scale, norm_gain)
    grad_input = (grad_out.astype(jnp.float32) + branch_grad).astype(jnp.bfloat16)

    grad_weight_in, grad_weight_out = weights_call(acts, cols, blocks)
    return (grad_input, grad_weight_in, grad_weight_out)


def solution(mesh):
    in_specs = (
        P(("groups", "dp", "tensor"), None),
        P(("groups", "dp", "tensor"), None),
        P(),
        P(("groups", "dp")),
        P(("groups", "dp"), None),
        P(None, "tensor"),
        P("tensor", None),
    )
    out_specs = (
        P(("groups", "dp", "tensor"), None),
        P(("groups", "dp"), "tensor"),
        P(("groups", "tensor"), "dp"),
    )
    return jax.shard_map(shards, mesh=mesh, in_specs=in_specs, out_specs=out_specs, check_vma=False)
```

time: 364 us -> 286 us (0.79); the launches traced: 357 us -> 286 us
  matrix products: 171 us -> 0 us
  Pallas kernels: 0 us -> 116 us
  local copies, waits for them, and re-layouts: 40.5 us -> 6.12 us
  waiting for transfers between devices: 103 us -> 115 us
  starting transfers between devices: 25.5 us -> 33.7 us
    dot_general x14 -> x0, matrix products: 171 us -> none  [the longest x4 49 us: shards(): lax.dot_general(grad_pre[:rows], weight_in, (((1,), (1,)), ((), ())), pre...]
    pallas_call x0 -> x5, Pallas kernels: none -> 116 us  [the longest x4 91.6 us: group_call(): pl.pallas_call(functools.partial(group_kernel, pieces=pieces, unit_total=...]
    ppermute x30 -> x22, waiting for transfers between devices: 62.7 us -> 95.9 us  [the longest x8 46 us: shards(): lax.ppermute(one, 'dp', from_chip)]
    ppermute x1, waiting for transfers between devices: 28.4 us -> 0.01 us  [shards(): level_sets.append(lax.ppermute(level_sets[-1], 'dp', from_chip))]
    unnamed x69 -> x26, local copies, waits for them, and re-layouts: 23.8 us -> 1.95 us
    ppermute x30 -> x22, starting transfers between devices: 20.7 us -> 31.9 us  [the longest x3 13.8 us: shards(): normed_rings.append(lax.ppermute(normed_rings[-1], 'tensor', from_next))]
    concatenate x11 -> x0, local copies, waits for them, and re-layouts: 9.97 us -> none  [the longest x1 2.88 us: shards(): jnp.concatenate(hiddens)]
    ppermute x3, waiting for transfers between devices: 11.7 us -> 19.5 us  [shards(): travelling = lax.ppermute(total.astype(jnp.bfloat16), 'tensor', from_next)]
  transfers between devices with their start and end apart: 34 -> 26, of which waited for: 9 -> 11; matrix products, arithmetic and copies ran while one was open for 57% -> 4% of each run, Pallas kernels for 0% -> 32%
where the time goes in v2:
time: 286 us
  Pallas kernels  116 us (41%)
  waiting for transfers between devices  115 us (40%)
  starting transfers between devices  33.7 us (12%)
  other arithmetic  11.2 us (4%)
  local copies, waits for them, and re-layouts  6.12 us (2%)
    pallas_call x4, Pallas kernels, group_call(): pl.pallas_call(functools.partial(group_kernel, pieces=pieces, unit_total=...  91.6 us
    ppermute x8, waiting for transfers between devices, shards(): lax.ppermute(one, 'dp', from_chip)  46 us
    ppermute x3, waiting for transfers between devices, shards(): grad_rings.append(lax.ppermute(grad_rings[-1], 'tensor', from_next))  25 us
    pallas_call x1, Pallas kernels, weights_call(): pl.pallas_call(functools.partial(weights_kernel, groups=len(acts), scale=...  24.9 us
    ppermute x3, waiting for transfers between devices, shards(): normed_rings.append(lax.ppermute(normed_rings[-1], 'tensor', from_next))  22.8 us
    ppermute x3, waiting for transfers between devices, shards(): travelling = lax.ppermute(total.astype(jnp.bfloat16), 'tensor', from_next)  19.5 us
    ppermute x3, starting transfers between devices, shards(): normed_rings.append(lax.ppermute(normed_rings[-1], 'tensor', from_next))  13.8 us
    ppermute x3, starting transfers between devices, shards(): grad_rings.append(lax.ppermute(grad_rings[-1], 'tensor', from_next))  9.11 us
  transfers between devices with their start and end apart: 26, of which 11 were waited for; matrix products, arithmetic and copies ran while one was open for 4% of the time, Pallas kernels for 32%

profile of v2, /device:TPU:0, one launch (start us, length us, event | category | flops | bytes accessed | tf_op | source)
XLA Modules:
  0.0 285.8 jit_solution(15424381637976729290)
XLA Ops:
  4.0 5.1 %collective-permute-start = (bf16[128,3072]{1,0:T(8,128)(2,1)S(1)}, bf16[128,3072]{1,0:T(8,128)(2,1)}, u32[]{:S(2)}, u32[]{:S(2)}) collective-permute-start(bf16[128,3072]{1,0:T(8,128)(2,1)S(1)} %fusion.5.refs_0_), channel_id=1, source_target_pairs={{1,0},{2,1},{3,2},{0,3},{5,4},{6,5},{7,6},{4,7},{9,8},{10,9},{11,1... | collective-permute-start | bytes 2359304 | tf_op jit(solution)/shard_map/ppermute | solution.py:223
  11.6 15.5 %collective-permute-done.refs_1_ = bf16[128,3072]{1,0:T(8,128)(2,1)} collective-permute-done((bf16[128,3072]{1,0:T(8,128)(2,1)S(1)}, bf16[128,3072]{1,0:T(8,128)(2,1)}, u32[]{:S(2)}, u32[]{:S(2)}) %collective-permute-start) | collective-permute-done | bytes 786464 | tf_op jit(solution)/shard_map/ppermute | solution.py:223
  27.0 4.4 %collective-permute-start.2 = (bf16[128,3072]{1,0:T(8,128)(2,1)}, bf16[128,3072]{1,0:T(8,128)(2,1)}, u32[]{:S(2)}, u32[]{:S(2)}) collective-permute-start(bf16[128,3072]{1,0:T(8,128)(2,1)} %collective-permute-done.refs_1_), channel_id=1, source_target_pairs={{1,0},{2,1},{3,2},{0,3},{5,4},{6,5},{7,6},{4,7},{9,8},{10,9},{11,1... | collective-permute-start | bytes 2359304 | tf_op jit(solution)/shard_map/ppermute | solution.py:223
  31.4 12.5 %collective-permute-done.1.refs_3_ = bf16[128,3072]{1,0:T(8,128)(2,1)} collective-permute-done((bf16[128,3072]{1,0:T(8,128)(2,1)S(1)}, bf16[128,3072]{1,0:T(8,128)(2,1)}, u32[]{:S(2)}, u32[]{:S(2)}) %collective-permute-start.1) | collective-permute-done | bytes 786464 | tf_op jit(solution)/shard_map/ppermute | solution.py:222
  43.9 4.4 %collective-permute-start.4 = (bf16[128,3072]{1,0:T(8,128)(2,1)}, bf16[128,3072]{1,0:T(8,128)(2,1)}, u32[]{:S(2)}, u32[]{:S(2)}) collective-permute-start(bf16[128,3072]{1,0:T(8,128)(2,1)} %collective-permute-done.1.refs_3_), channel_id=1, source_target_pairs={{1,0},{2,1},{3,2},{0,3},{5,4},{6,5},{7,6},{4,7},{9,8},{10,9},{11,1... | collective-permute-start | bytes 2359304 | tf_op jit(solution)/shard_map/ppermute | solution.py:222
  53.5 7.4 %collective-permute-done.2.refs_0_ = bf16[128,3072]{1,0:T(8,128)(2,1)} collective-permute-done((bf16[128,3072]{1,0:T(8,128)(2,1)}, bf16[128,3072]{1,0:T(8,128)(2,1)}, u32[]{:S(2)}, u32[]{:S(2)}) %collective-permute-start.2) | collective-permute-done | bytes 786464 | tf_op jit(solution)/shard_map/ppermute | solution.py:223
  60.8 4.3 %collective-permute-start.3 = (bf16[128,3072]{1,0:T(8,128)(2,1)}, bf16[128,3072]{1,0:T(8,128)(2,1)}, u32[]{:S(2)}, u32[]{:S(2)}) collective-permute-start(bf16[128,3072]{1,0:T(8,128)(2,1)} %collective-permute-done.2.refs_0_), channel_id=1, source_target_pairs={{1,0},{2,1},{3,2},{0,3},{5,4},{6,5},{7,6},{4,7},{9,8},{10,9},{11,1... | collective-permute-start | bytes 2359304 | tf_op jit(solution)/shard_map/ppermute | solution.py:223
  65.1 12.6 %collective-permute-done.4.refs_2_ = bf16[128,3072]{1,0:T(8,128)(2,1)} collective-permute-done((bf16[128,3072]{1,0:T(8,128)(2,1)}, bf16[128,3072]{1,0:T(8,128)(2,1)}, u32[]{:S(2)}, u32[]{:S(2)}) %collective-permute-start.4) | collective-permute-done | bytes 786464 | tf_op jit(solution)/shard_map/ppermute | solution.py:222
  77.7 4.3 %collective-permute-start.5 = (bf16[128,3072]{1,0:T(8,128)(2,1)}, bf16[128,3072]{1,0:T(8,128)(2,1)}, u32[]{:S(2)}, u32[]{:S(2)}) collective-permute-start(bf16[128,3072]{1,0:T(8,128)(2,1)} %collective-permute-done.4.refs_2_), channel_id=1, source_target_pairs={{1,0},{2,1},{3,2},{0,3},{5,4},{6,5},{7,6},{4,7},{9,8},{10,9},{11,1... | collective-permute-start | bytes 2359304 | tf_op jit(solution)/shard_map/ppermute | solution.py:222
  82.0 26.2 %group.4 = (bf16[2,256,3072]{2,1,0:T(8,128)(2,1)}, bf16[2,256,768]{2,1,0:T(8,128)(2,1)S(1)}, bf16[2,256,768]{2,1,0:T(8,128)(2,1)S(1)}, f32[256,3072]{1,0:T(8,128)}) custom-call(s32[3]{0:T(128)S(1)} %pad_add_fusion.1.spots, bf16[128,3072]{1,0:T(8,128)(2,1)S(1)} %fusion.5.refs_0_, bf16[128,3072]{1,0:T(8,128)(2,1)} %collective-permute-done.refs_1_, ...), custom_call_target="tpu_custom_call" | custom-call | flops 4831838208 | bytes 18874368 | tf_op jit(solution)/shard_map/group/pallas_call | solution.py:124
  108.2 3.0 %slice.59 = bf16[128,3072]{1,0:T(8,128)(2,1)} slice(f32[256,3072]{1,0:T(8,128)} %get-tuple-element.19), slice={[128:256], [0:3072]} | slice | bytes 1572864 | tf_op jit(solution)/shard_map/slice | solution.py:247
  111.1 1.5 collective-permute-start.11
  115.2 26.7 %group.5 = (bf16[2,256,3072]{2,1,0:T(8,128)(2,1)}, bf16[2,256,768]{2,1,0:T(8,128)(2,1)S(1)}, bf16[2,256,768]{2,1,0:T(8,128)(2,1)S(1)}, f32[256,3072]{1,0:T(8,128)}) custom-call(s32[3]{0:T(128)S(1)} %pad_add_fusion.1.spots, bf16[128,3072]{1,0:T(8,128)(2,1)} %collective-permute-done.2.refs_0_, bf16[128,3072]{1,0:T(8,128)(2,1)} %collective-permute-done.3.refs_1_, ...), custom_call_target="tpu_custom_call" | custom-call | flops 4831838208 | bytes 18874368 | tf_op jit(solution)/shard_map/group/pallas_call | solution.py:124
  144.5 2.8 add_convert_fusion.1
  148.7 16.8 %collective-permute-done.17.refs_0_ = bf16[128,3072]{1,0:T(8,128)(2,1)S(1)} collective-permute-done((bf16[128,3072]{1,0:T(8,128)(2,1)}, bf16[128,3072]{1,0:T(8,128)(2,1)S(1)}, u32[]{:S(2)}, u32[]{:S(2)}) %collective-permute-start.17) | collective-permute-done | bytes 786464 | tf_op jit(solution)/shard_map/ppermute | solution.py:227
  165.5 19.3 %group.6 = (bf16[2,256,3072]{2,1,0:T(8,128)(2,1)}, bf16[2,256,768]{2,1,0:T(8,128)(2,1)S(1)}, bf16[2,256,768]{2,1,0:T(8,128)(2,1)S(1)}) custom-call(s32[3]{0:T(128)S(1)} %pad_add_fusion.1.spots, bf16[128,3072]{1,0:T(8,128)(2,1)S(1)} %collective-permute-done.10.refs_0_, bf16[128,3072]{1,0:T(8,128)(2,1)} %collective-permute-done.11.refs_1_, ...), custom_call_target="tpu_custom_call" | custom-call | flops 4831838208 | bytes 18874368 | tf_op jit(solution)/shard_map/group/pallas_call | solution.py:124
  184.8 14.4 %collective-permute-done.18.refs_1_ = bf16[128,3072]{1,0:T(8,128)(2,1)S(1)} collective-permute-done((bf16[128,3072]{1,0:T(8,128)(2,1)}, bf16[128,3072]{1,0:T(8,128)(2,1)S(1)}, u32[]{:S(2)}, u32[]{:S(2)}) %collective-permute-start.18) | collective-permute-done | bytes 786464 | tf_op jit(solution)/shard_map/ppermute | solution.py:227
  199.2 13.4 %collective-permute-done.20.refs_3_ = bf16[128,3072]{1,0:T(8,128)(2,1)S(1)} collective-permute-done((bf16[128,3072]{1,0:T(8,128)(2,1)}, bf16[128,3072]{1,0:T(8,128)(2,1)S(1)}, u32[]{:S(2)}, u32[]{:S(2)}) %collective-permute-start.20) | collective-permute-done | bytes 786464 | tf_op jit(solution)/shard_map/ppermute | solution.py:226
  212.6 19.4 %group.7 = (bf16[2,256,3072]{2,1,0:T(8,128)(2,1)}, bf16[2,256,768]{2,1,0:T(8,128)(2,1)S(1)}, bf16[2,256,768]{2,1,0:T(8,128)(2,1)S(1)}) custom-call(s32[3]{0:T(128)S(1)} %pad_add_fusion.1.spots, bf16[128,3072]{1,0:T(8,128)(2,1)S(1)} %collective-permute-done.17.refs_0_, bf16[128,3072]{1,0:T(8,128)(2,1)S(1)} %collective-permute-done.18.refs_1_, ...), custom_call_target="tpu_custom_call" | custom-call | flops 4831838208 | bytes 18874368 | tf_op jit(solution)/shard_map/group/pallas_call | solution.py:124
  232.6 1.9 add_convert_fusion
  234.8 19.5 %collective-permute-done.8 = bf16[128,3072]{1,0:T(8,128)(2,1)S(1)} collective-permute-done((bf16[128,3072]{1,0:T(8,128)(2,1)S(1)}, bf16[128,3072]{1,0:T(8,128)(2,1)S(1)}, u32[]{:S(2)}, u32[]{:S(2)}) %collective-permute-start.8) | collective-permute-done | bytes 786464 | tf_op jit(solution)/shard_map/ppermute | solution.py:253
  255.0 1.6 collective-permute-done.24.refs_13_
  256.8 1.8 fusion.10
  260.9 24.9 %weights.1 = (bf16[768,3072]{1,0:T(8,128)(2,1)}, bf16[3072,768]{1,0:T(8,128)(2,1)}) custom-call(bf16[2,256,3072]{2,1,0:T(8,128)(2,1)} %get-tuple-element.21.refs_0_, bf16[2,256,3072]{2,1,0:T(8,128)(2,1)} %collective-permute-done.9.refs_1_, bf16[2,256,3072]{2,1,0:T(8,128)(2,1)} %get-tuple-element.22.refs_2_, ...), custom_call_target="tpu_custom_call" | custom-call | flops 19327352832 | bytes 25165824 | tf_op jit(solution)/shard_map/weights/pallas_call | solution.py:169
  (82 shorter events, 19.5 us)
Async XLA Ops:
  4.0 23.0 %collective-permute-start = (bf16[128,3072]{1,0:T(8,128)(2,1)S(1)}, bf16[128,3072]{1,0:T(8,128)(2,1)}, u32[]{:S(2)}, u32[]{:S(2)}) collective-permute-start(bf16[128,3072]{1,0:T(8,128)(2,1)S(1)} %fusion.5.refs_0_), channel_id=1, source_target_pairs={{1,0},{2,1},{3,2},{0,3},{5,4},{6,5},{7,6},{4,7},{9,8},{10,9},{11,1... | collective-permute-start | bytes 2359304 | tf_op jit(solution)/shard_map/ppermute | solution.py:223
  9.1 34.8 %collective-permute-start.1 = (bf16[128,3072]{1,0:T(8,128)(2,1)S(1)}, bf16[128,3072]{1,0:T(8,128)(2,1)}, u32[]{:S(2)}, u32[]{:S(2)}) collective-permute-start(bf16[128,3072]{1,0:T(8,128)(2,1)S(1)} %copy-done), channel_id=1, source_target_pairs={{1,0},{2,1},{3,2},{0,3},{5,4},{6,5},{7,6},{4,7},{9,8},{10,9},{11,1... | collective-permute-start | bytes 2359304 | tf_op jit(solution)/shard_map/ppermute | solution.py:222
  9.5 103.1 %collective-permute-start.10 = (bf16[128,3072]{1,0:T(8,128)(2,1)S(1)}, bf16[128,3072]{1,0:T(8,128)(2,1)S(1)}, u32[]{:S(2)}, u32[]{:S(2)}) collective-permute-start(bf16[128,3072]{1,0:T(8,128)(2,1)S(1)} %fusion.5.refs_0_), channel_id=1, source_target_pairs={{8,0},{12,4},{0,8},{4,12},{9,1},{13,5},{1,9},{5,13},{10,2},{14,6},... | collective-permute-start | bytes 2359304 | tf_op jit(solution)/shard_map/ppermute | solution.py:227
  11.0 130.9 %collective-permute-start.12 = (bf16[128,3072]{1,0:T(8,128)(2,1)S(1)}, bf16[128,3072]{1,0:T(8,128)(2,1)S(1)}, u32[]{:S(2)}, u32[]{:S(2)}) collective-permute-start(bf16[128,3072]{1,0:T(8,128)(2,1)S(1)} %copy-done), channel_id=1, source_target_pairs={{8,0},{12,4},{0,8},{4,12},{9,1},{13,5},{1,9},{5,13},{10,2},{14,6},... | collective-permute-start | bytes 2359304 | tf_op jit(solution)/shard_map/ppermute | solution.py:226
  27.0 33.8 %collective-permute-start.2 = (bf16[128,3072]{1,0:T(8,128)(2,1)}, bf16[128,3072]{1,0:T(8,128)(2,1)}, u32[]{:S(2)}, u32[]{:S(2)}) collective-permute-start(bf16[128,3072]{1,0:T(8,128)(2,1)} %collective-permute-done.refs_1_), channel_id=1, source_target_pairs={{1,0},{2,1},{3,2},{0,3},{5,4},{6,5},{7,6},{4,7},{9,8},{10,9},{11,1... | collective-permute-start | bytes 2359304 | tf_op jit(solution)/shard_map/ppermute | solution.py:223
  43.9 33.8 %collective-permute-start.4 = (bf16[128,3072]{1,0:T(8,128)(2,1)}, bf16[128,3072]{1,0:T(8,128)(2,1)}, u32[]{:S(2)}, u32[]{:S(2)}) collective-permute-start(bf16[128,3072]{1,0:T(8,128)(2,1)} %collective-permute-done.1.refs_3_), channel_id=1, source_target_pairs={{1,0},{2,1},{3,2},{0,3},{5,4},{6,5},{7,6},{4,7},{9,8},{10,9},{11,1... | collective-permute-start | bytes 2359304 | tf_op jit(solution)/shard_map/ppermute | solution.py:222
  51.7 59.4 %collective-permute-start.14 = (s32[512]{0:T(512)S(1)}, s32[512]{0:T(512)S(1)}, u32[]{:S(2)}, u32[]{:S(2)}) collective-permute-start(s32[512]{0:T(512)S(1)} %dynamic_slice.3), channel_id=1, source_target_pairs={{8,0},{12,4},{0,8},{4,12},{9,1},{13,5},{1,9},{5,13},{10,2},{14,6},... | collective-permute-start | bytes 6152 | tf_op jit(solution)/shard_map/ppermute | solution.py:217
  60.8 52.3 %collective-permute-start.3 = (bf16[128,3072]{1,0:T(8,128)(2,1)}, bf16[128,3072]{1,0:T(8,128)(2,1)}, u32[]{:S(2)}, u32[]{:S(2)}) collective-permute-start(bf16[128,3072]{1,0:T(8,128)(2,1)} %collective-permute-done.2.refs_0_), channel_id=1, source_target_pairs={{1,0},{2,1},{3,2},{0,3},{5,4},{6,5},{7,6},{4,7},{9,8},{10,9},{11,1... | collective-permute-start | bytes 2359304 | tf_op jit(solution)/shard_map/ppermute | solution.py:223
  77.7 36.0 %collective-permute-start.5 = (bf16[128,3072]{1,0:T(8,128)(2,1)}, bf16[128,3072]{1,0:T(8,128)(2,1)}, u32[]{:S(2)}, u32[]{:S(2)}) collective-permute-start(bf16[128,3072]{1,0:T(8,128)(2,1)} %collective-permute-done.4.refs_2_), channel_id=1, source_target_pairs={{1,0},{2,1},{3,2},{0,3},{5,4},{6,5},{7,6},{4,7},{9,8},{10,9},{11,1... | collective-permute-start | bytes 2359304 | tf_op jit(solution)/shard_map/ppermute | solution.py:222
  111.1 31.4 %collective-permute-start.11 = (bf16[128,3072]{1,0:T(8,128)(2,1)}, bf16[128,3072]{1,0:T(8,128)(2,1)}, u32[]{:S(2)}, u32[]{:S(2)}) collective-permute-start(bf16[128,3072]{1,0:T(8,128)(2,1)} %collective-permute-done.refs_1_), channel_id=1, source_target_pairs={{8,0},{12,4},{0,8},{4,12},{9,1},{13,5},{1,9},{5,13},{10,2},{14,6},... | collective-permute-start | bytes 2359304 | tf_op jit(solution)/shard_map/ppermute | solution.py:227
  112.6 31.4 %collective-permute-start.6 = (bf16[128,3072]{1,0:T(8,128)(2,1)}, bf16[128,3072]{1,0:T(8,128)(2,1)}, u32[]{:S(2)}, u32[]{:S(2)}) collective-permute-start(bf16[128,3072]{1,0:T(8,128)(2,1)} %slice.59), channel_id=1, source_target_pairs={{1,0},{2,1},{3,2},{0,3},{5,4},{6,5},{7,6},{4,7},{9,8},{10,9},{11,1... | collective-permute-start | bytes 2359304 | tf_op jit(solution)/shard_map/ppermute | solution.py:253
  113.1 35.6 %collective-permute-start.13 = (bf16[128,3072]{1,0:T(8,128)(2,1)}, bf16[128,3072]{1,0:T(8,128)(2,1)S(1)}, u32[]{:S(2)}, u32[]{:S(2)}) collective-permute-start(bf16[128,3072]{1,0:T(8,128)(2,1)} %collective-permute-done.1.refs_3_), channel_id=1, source_target_pairs={{8,0},{12,4},{0,8},{4,12},{9,1},{13,5},{1,9},{5,13},{10,2},{14,6},... | collective-permute-start | bytes 2359304 | tf_op jit(solution)/shard_map/ppermute | solution.py:226
  113.7 51.8 %collective-permute-start.17 = (bf16[128,3072]{1,0:T(8,128)(2,1)}, bf16[128,3072]{1,0:T(8,128)(2,1)S(1)}, u32[]{:S(2)}, u32[]{:S(2)}) collective-permute-start(bf16[128,3072]{1,0:T(8,128)(2,1)} %collective-permute-done.2.refs_0_), channel_id=1, source_target_pairs={{8,0},{12,4},{0,8},{4,12},{9,1},{13,5},{1,9},{5,13},{10,2},{14,6},... | collective-permute-start | bytes 2359304 | tf_op jit(solution)/shard_map/ppermute | solution.py:227
  141.9 42.9 %collective-permute-start.19 = (bf16[128,3072]{1,0:T(8,128)(2,1)}, bf16[128,3072]{1,0:T(8,128)(2,1)S(1)}, u32[]{:S(2)}, u32[]{:S(2)}) collective-permute-start(bf16[128,3072]{1,0:T(8,128)(2,1)} %collective-permute-done.4.refs_2_), channel_id=1, source_target_pairs={{8,0},{12,4},{0,8},{4,12},{9,1},{13,5},{1,9},{5,13},{10,2},{14,6},... | collective-permute-start | bytes 2359304 | tf_op jit(solution)/shard_map/ppermute | solution.py:226
  142.5 56.7 %collective-permute-start.18 = (bf16[128,3072]{1,0:T(8,128)(2,1)}, bf16[128,3072]{1,0:T(8,128)(2,1)S(1)}, u32[]{:S(2)}, u32[]{:S(2)}) collective-permute-start(bf16[128,3072]{1,0:T(8,128)(2,1)} %collective-permute-done.3.refs_1_), channel_id=1, source_target_pairs={{8,0},{12,4},{0,8},{4,12},{9,1},{13,5},{1,9},{5,13},{10,2},{14,6},... | collective-permute-start | bytes 2359304 | tf_op jit(solution)/shard_map/ppermute | solution.py:227
  144.0 68.6 %collective-permute-start.20 = (bf16[128,3072]{1,0:T(8,128)(2,1)}, bf16[128,3072]{1,0:T(8,128)(2,1)S(1)}, u32[]{:S(2)}, u32[]{:S(2)}) collective-permute-start(bf16[128,3072]{1,0:T(8,128)(2,1)} %collective-permute-done.5.refs_3_), channel_id=1, source_target_pairs={{8,0},{12,4},{0,8},{4,12},{9,1},{13,5},{1,9},{5,13},{10,2},{14,6},... | collective-permute-start | bytes 2359304 | tf_op jit(solution)/shard_map/ppermute | solution.py:226
  148.7 83.3 %collective-permute-start.22 = (bf16[2,256,768]{2,1,0:T(8,128)(2,1)S(1)}, bf16[2,256,768]{2,1,0:T(8,128)(2,1)S(1)}, u32[]{:S(2)}, u32[]{:S(2)}) collective-permute-start(bf16[2,256,768]{2,1,0:T(8,128)(2,1)S(1)} %copy-done.4), channel_id=1, source_target_pairs={{0,4},{4,0},{8,12},{12,8},{1,5},{5,1},{9,13},{13,9},{2,6},{6,2},{1... | collective-permute-start | bytes 2359304 | tf_op jit(solution)/shard_map/ppermute | solution.py:246
  165.5 67.0 %collective-permute-start.7 = (bf16[128,3072]{1,0:T(8,128)(2,1)}, bf16[128,3072]{1,0:T(8,128)(2,1)}, u32[]{:S(2)}, u32[]{:S(2)}) collective-permute-start(bf16[128,3072]{1,0:T(8,128)(2,1)} %add_convert_fusion.1), channel_id=1, source_target_pairs={{1,0},{2,1},{3,2},{0,3},{5,4},{6,5},{7,6},{4,7},{9,8},{10,9},{11,1... | collective-permute-start | bytes 2359304 | tf_op jit(solution)/shard_map/ppermute | solution.py:253
  184.8 74.1 %collective-permute-start.9 = (bf16[2,256,3072]{2,1,0:T(8,128)(2,1)}, bf16[2,256,3072]{2,1,0:T(8,128)(2,1)}, u32[]{:S(2)}, u32[]{:S(2)}) collective-permute-start(bf16[2,256,3072]{2,1,0:T(8,128)(2,1)} %get-tuple-element.21.refs_0_), channel_id=1, source_target_pairs={{0,4},{4,0},{8,12},{12,8},{1,5},{5,1},{9,13},{13,9},{2,6},{6,2},{1... | collective-permute-start | bytes 9437192 | tf_op jit(solution)/shard_map/ppermute | solution.py:245
  199.2 35.2 %collective-permute-start.23 = (bf16[2,256,768]{2,1,0:T(8,128)(2,1)S(1)}, bf16[2,256,768]{2,1,0:T(8,128)(2,1)S(1)}, u32[]{:S(2)}, u32[]{:S(2)}) collective-permute-start(bf16[2,256,768]{2,1,0:T(8,128)(2,1)S(1)} %get-tuple-element.28), channel_id=1, source_target_pairs={{0,4},{4,0},{8,12},{12,8},{1,5},{5,1},{9,13},{13,9},{2,6},{6,2},{1... | collective-permute-start | bytes 2359304 | tf_op jit(solution)/shard_map/ppermute | solution.py:246
  212.6 46.3 %collective-permute-start.15 = (bf16[2,256,3072]{2,1,0:T(8,128)(2,1)}, bf16[2,256,3072]{2,1,0:T(8,128)(2,1)}, u32[]{:S(2)}, u32[]{:S(2)}) collective-permute-start(bf16[2,256,3072]{2,1,0:T(8,128)(2,1)} %get-tuple-element.22.refs_2_), channel_id=1, source_target_pairs={{0,4},{4,0},{8,12},{12,8},{1,5},{5,1},{9,13},{13,9},{2,6},{6,2},{1... | collective-permute-start | bytes 9437192 | tf_op jit(solution)/shard_map/ppermute | solution.py:245
  232.0 26.9 %collective-permute-start.16 = (bf16[2,256,3072]{2,1,0:T(8,128)(2,1)}, bf16[2,256,3072]{2,1,0:T(8,128)(2,1)S(1)}, u32[]{:S(2)}, u32[]{:S(2)}) collective-permute-start(bf16[2,256,3072]{2,1,0:T(8,128)(2,1)} %get-tuple-element.23.refs_4_), channel_id=1, source_target_pairs={{0,4},{4,0},{8,12},{12,8},{1,5},{5,1},{9,13},{13,9},{2,6},{6,2},{1... | collective-permute-start | bytes 9437192 | tf_op jit(solution)/shard_map/ppermute | solution.py:245
  232.5 26.4 %collective-permute-start.21 = (bf16[2,256,3072]{2,1,0:T(8,128)(2,1)}, bf16[2,256,3072]{2,1,0:T(8,128)(2,1)}, u32[]{:S(2)}, u32[]{:S(2)}) collective-permute-start(bf16[2,256,3072]{2,1,0:T(8,128)(2,1)} %get-tuple-element.24.refs_6_), channel_id=1, source_target_pairs={{0,4},{4,0},{8,12},{12,8},{1,5},{5,1},{9,13},{13,9},{2,6},{6,2},{1... | collective-permute-start | bytes 9437192 | tf_op jit(solution)/shard_map/ppermute | solution.py:245
  234.5 19.9 %collective-permute-start.8 = (bf16[128,3072]{1,0:T(8,128)(2,1)S(1)}, bf16[128,3072]{1,0:T(8,128)(2,1)S(1)}, u32[]{:S(2)}, u32[]{:S(2)}) collective-permute-start(bf16[128,3072]{1,0:T(8,128)(2,1)S(1)} %add_convert_fusion), channel_id=1, source_target_pairs={{1,0},{2,1},{3,2},{0,3},{5,4},{6,5},{7,6},{4,7},{9,8},{10,9},{11,1... | collective-permute-start | bytes 2359304 | tf_op jit(solution)/shard_map/ppermute | solution.py:253
  (15 other events, 200.9 us)

commit v3 on v2

v3 whole, which is shorter than its diff:
```python
import functools
import math

import jax
import jax.numpy as jnp
from jax import lax
from jax.experimental import pallas as pl
from jax.experimental.pallas import tpu as pltpu
from jax.sharding import PartitionSpec as P

GELU_SCALE = 0.7978845608028654
GELU_CUBE = 0.044715
NORM_EPS = 1e-06
GROUP_ROWS = 256
VMEM_LIMIT = 48 * 1024 * 1024
WORK = 0.3


def gelu_parts(pre_act):
    square = pre_act * pre_act
    tanh_val = jnp.tanh(pre_act * (GELU_SCALE + (GELU_SCALE * GELU_CUBE) * square))
    share = 0.5 + 0.5 * tanh_val
    gelu_value = pre_act * share
    gelu_slope = share + gelu_value * (1.0 - tanh_val) * (
        GELU_SCALE + (3.0 * GELU_SCALE * GELU_CUBE) * square
    )
    return (gelu_value, gelu_slope)


def token_levels(block_order, count_row):
    above_three = count_row[3]
    above_two = above_three + count_row[2]
    above_one = above_two + count_row[1]
    places = jnp.arange(block_order.shape[0], dtype=jnp.int32)
    ranked = (
        (places < above_three).astype(jnp.int32)
        + (places < above_two).astype(jnp.int32)
        + (places < above_one).astype(jnp.int32)
    )
    hits = block_order[None, :] == places[:, None]
    return jnp.sum(jnp.where(hits, ranked[None, :], 0), axis=1)


def norm_backward(grad_normed, standard, row_scale, norm_gain):
    scaled = grad_normed * norm_gain[None, :]
    centre = jnp.mean(scaled, axis=1, keepdims=True)
    along = jnp.mean(scaled * standard, axis=1, keepdims=True)
    return row_scale * (scaled - centre - standard * along)


def work_of(flops):
    return pl.CostEstimate(flops=int(WORK * flops), bytes_accessed=0, transcendentals=0)


def tile_of(extent, wanted):
    while extent % wanted:
        wanted //= 2
    return wanted


def group_kernel(spots, *refs, pieces, begun, share, with_grad):
    normed_refs = refs[:pieces]
    grad_refs = refs[pieces : 2 * pieces]
    limit_ref, in_ref, out_ref = refs[2 * pieces : 2 * pieces + 3]
    outs = refs[2 * pieces + 3 + begun :]
    acts_ref, own_ref, swap_ref = outs[:3]
    tile = pl.program_id(0)
    normed = jnp.concatenate([ref[...] for ref in normed_refs], axis=0)
    grads = jnp.concatenate([ref[...] for ref in grad_refs], axis=0)

    @pl.when(tile == 0)
    def _():
        own = pl.ds(pl.multiple_of(spots[1], 128), share)
        swap = pl.ds(pl.multiple_of(spots[2], 128), share)
        for kind, parts in enumerate((normed_refs, grad_refs)):
            for at, ref in enumerate(parts):
                size = ref.shape[0]
                own_ref[kind, at * size : (at + 1) * size, :] = ref[:, own]
                swap_ref[kind, at * size : (at + 1) * size, :] = ref[:, swap]

    pre_act = jnp.dot(normed, in_ref[...], preferred_element_type=jnp.float32)
    grad_hidden = lax.dot_general(
        grads, out_ref[...], (((1,), (1,)), ((), ())), preferred_element_type=jnp.float32
    )
    mask = spots[0] + tile * in_ref.shape[1] < limit_ref[...]
    gelu_value, gelu_slope = gelu_parts(pre_act)
    grad_pre = jnp.where(mask, grad_hidden * gelu_slope, 0.0).astype(jnp.bfloat16)
    acts_ref[0] = grad_pre
    acts_ref[1] = jnp.where(mask, gelu_value, 0.0).astype(jnp.bfloat16)
    if with_grad:
        back_refs, total_ref = outs[3:-1], outs[-1]
        term = lax.dot_general(
            grad_pre, in_ref[...], (((1,), (1,)), ((), ())), preferred_element_type=jnp.float32
        )

        @pl.when(tile == 0)
        def _():
            total_ref[...] = term

        @pl.when(tile != 0)
        def _():
            total_ref[...] += term

        @pl.when(tile == pl.num_programs(0) - 1)
        def _():
            for at, ref in enumerate(back_refs):
                size = ref.shape[0]
                ref[...] = total_ref[at * size : (at + 1) * size, :].astype(ref.dtype)


def group_call(
    spots, normed, grads, limit, weight_in, weight_out, tile, share, back_types, chip, chips, begun
):
    features, units = weight_in.shape
    piece_rows = normed[0].shape[0]
    rows = piece_rows * len(normed)
    whole = lambda shape: pl.BlockSpec(shape, lambda i, spots: (0,) * len(shape))
    out_shape = [
        jax.ShapeDtypeStruct((2, chips * rows, units), jnp.bfloat16),
        jax.ShapeDtypeStruct((2, chips * rows, share), jnp.bfloat16),
        jax.ShapeDtypeStruct((2, chips * rows, share), jnp.bfloat16),
    ]
    out_specs = [
        pl.BlockSpec((2, rows, tile), lambda i, spots: (0, chip, i)),
        pl.BlockSpec((2, rows, share), lambda i, spots: (0, chip, 0)),
        pl.BlockSpec((2, rows, share), lambda i, spots: (0, chip, 0)),
    ]
    operands = (spots, *normed, *grads, limit, weight_in, weight_out)
    for kind in back_types:
        out_shape.append(jax.ShapeDtypeStruct((piece_rows, features), kind))
        out_specs.append(whole((piece_rows, features)))
    return pl.pallas_call(
        functools.partial(
            group_kernel,
            pieces=len(normed),
            begun=len(begun),
            share=share,
            with_grad=bool(back_types),
        ),
        grid_spec=pltpu.PrefetchScalarGridSpec(
            num_scalar_prefetch=1,
            grid=(units // tile,),
            in_specs=[whole(one.shape) for one in (*normed, *grads)]
            + [
                whole((rows, 1)),
                pl.BlockSpec((features, tile), lambda i, spots: (0, i)),
                pl.BlockSpec((tile, features), lambda i, spots: (i, 0)),
            ]
            + [pl.BlockSpec(memory_space=pl.ANY) for _ in begun],
            out_specs=out_specs,
            scratch_shapes=[pltpu.VMEM((rows, features), jnp.float32)] if back_types else [],
        ),
        out_shape=out_shape,
        compiler_params=pltpu.CompilerParams(vmem_limit_bytes=VMEM_LIMIT),
        cost_estimate=work_of((6 if back_types else 4) * rows * units * features),
        input_output_aliases={len(operands) + at: at for at in range(len(begun))},
        name="group",
    )(*operands, *begun)


def weights_kernel(*refs, groups, scale, started):
    act_refs = refs[:groups]
    col_refs = refs[groups : 2 * groups]
    in_ref, out_ref = refs[-2:]

    def stack(sources, kind):
        return jnp.concatenate([ref[kind] for ref in sources], axis=0)

    def total(left, right):
        return lax.dot_general(
            left, right, (((0,), (0,)), ((), ())), preferred_element_type=jnp.float32
        )

    for_in = total(stack(col_refs, 0), stack(act_refs, 0))
    for_out = total(stack(act_refs, 1), stack(col_refs, 1))
    if started:
        for_in += refs[-4][...]
        for_out += refs[-3][...]
    in_ref[...] = (for_in * scale).astype(in_ref.dtype)
    out_ref[...] = (for_out * scale).astype(out_ref.dtype)


def weights_call(acts, cols, begun, scale, kind):
    units, share = acts[0].shape[2], cols[0].shape[2]
    tile = tile_of(units, 512)
    in_spec = pl.BlockSpec((share, tile), lambda i: (0, i))
    out_spec = pl.BlockSpec((tile, share), lambda i: (i, 0))
    return pl.pallas_call(
        functools.partial(weights_kernel, groups=len(acts), scale=scale, started=bool(begun)),
        grid=(units // tile,),
        in_specs=[pl.BlockSpec((2, one.shape[1], tile), lambda i: (0, 0, i)) for one in acts]
        + [pl.BlockSpec(one.shape, lambda i: (0, 0, 0)) for one in cols]
        + ([in_spec, out_spec] if begun else []),
        out_specs=[in_spec, out_spec],
        out_shape=[
            jax.ShapeDtypeStruct((share, units), kind),
            jax.ShapeDtypeStruct((units, share), kind),
        ],
        compiler_params=pltpu.CompilerParams(vmem_limit_bytes=VMEM_LIMIT),
        cost_estimate=work_of(4 * sum(one.shape[1] for one in acts) * units * share),
        name="weights",
    )(*acts, *cols, *begun)


def after(value, *others):
    return lax.optimization_barrier((value, others))[0] if others else value


def flat(pairs):
    return [one for pair in pairs for one in pair]


def shards(inputs, grad_out, norm_gain, level_order, level_counts, weight_in, weight_out):
    rows = inputs.shape[0]
    ring = lax.axis_size("tensor")
    place = lax.axis_index("tensor")
    blocks = lax.axis_size("dp")
    block = lax.axis_index("dp")
    chips = blocks // 2
    unit_local = weight_in.shape[1]
    unit_total = unit_local * ring
    share = inputs.shape[1] // blocks
    pieces = max(1, min(ring, GROUP_ROWS // rows))
    tile = tile_of(math.gcd(unit_local, unit_total // 8), 512)

    from_next = [((i + 1) % ring, i) for i in range(ring)]
    from_last = [(i, (i + 1) % ring) for i in range(ring)]
    from_chip = [((i + 2) % blocks, i) for i in range(blocks)]
    swap_cores = [(i, i ^ 1) for i in range(blocks)]
    half = ring // 2

    as_float = inputs.astype(jnp.float32)
    row_mean = jnp.mean(as_float, axis=1, keepdims=True)
    centred = as_float - row_mean
    row_scale = lax.rsqrt(jnp.mean(centred * centred, axis=1, keepdims=True) + NORM_EPS)
    standard = centred * row_scale
    normed = (standard * norm_gain[None, :]).astype(jnp.bfloat16)

    limits = unit_total // (1 << (3 - token_levels(level_order, level_counts[0])))
    limits = lax.dynamic_slice_in_dim(jnp.concatenate([limits, limits]), place * rows, rows * ring, 0)
    limit_sets = [limits]
    for _ in range(chips - 1):
        limit_sets.append(lax.ppermute(limit_sets[-1], "dp", from_chip))
    spots = jnp.stack([place * unit_local, block * share, (block ^ 1) * share]).astype(jnp.int32)

    def send(one, axis, pairs, name):
        with jax.named_scope(name):
            return lax.ppermute(one, axis, pairs)

    kinds = ("grad", "normed")

    def move(piece, axis, pairs, name, *gates):
        return tuple(
            send(after(one, *gates), axis, pairs, f"{name}_{kind}") for one, kind in zip(piece, kinds)
        )

    near = {0: (grad_out, normed)}
    for step in range(1, half + 1):
        near[step] = move(near[step - 1], "tensor", from_next, f"ring_{step}")
    for step in range(ring - 1, half, -1):
        gates = near[1] if step == ring - 1 else ()
        near[step] = move(near[(step + 1) % ring], "tensor", from_last, f"ring_{step}", *gates)
    sets = [[near[step] for step in range(ring)]] + [[None] * ring for _ in range(1, chips)]
    acts, cols, own_grads = [], [], []
    heads = {half, half + 1}

    def over_chips(step, *gates):
        for chip in range(1, chips):
            grads, rows_normed = sets[chip - 1][step]
            grads = send(grads, "dp", from_chip, f"chip_{step}_grad")
            if 0 < step == ring - 1:
                rows_normed = after(sets[chip][0][1], *gates)
                rows_normed = send(rows_normed, "tensor", from_last, f"ring_chip_{step}_normed")
            else:
                rows_normed = send(rows_normed, "dp", from_chip, f"chip_{step}_normed")
            sets[chip][step] = (grads, rows_normed)

    def run_group(first, chip, begun, *gates):
        span = slice(first, first + pieces)
        limit = limit_sets[chip][first * rows : (first + pieces) * rows, None]
        back_types = [
            jnp.bfloat16 if first + i in heads else jnp.float32
            for i in range(pieces if chip == 0 else 0)
        ]
        with jax.named_scope(f"group_{chip}_{first}"):
            act, own_cols, swap_cols, *back = group_call(
                after(spots, *gates),
                [piece[1] for piece in sets[chip][span]],
                [piece[0] for piece in sets[chip][span]],
                limit,
                weight_in,
                weight_out,
                tile,
                share,
                back_types,
                chip,
                chips,
                begun,
            )
        own_grads.extend(back)
        return [act, own_cols, swap_cols]

    def swap(first, results):
        act, own_cols, swap_cols = results
        acts.append([act, send(act, "dp", swap_cores, f"swap_acts_{first}")])
        cols.append([own_cols, send(swap_cols, "dp", swap_cores, f"swap_cols_{first}")])

    for step in range(ring - 1):
        over_chips(step)
    results = run_group(0, 0, [], *[one[0] for one in sets[1:]])
    if ring > 1:
        over_chips(ring - 1, results[2])
    for chip in range(1, chips):
        results = run_group(0, chip, results, *near.get(2, ()))
    swap(0, results)
    totals = []
    for first in range(pieces, ring, pieces):
        gates = []
        if first + pieces >= ring:
            gates = [one[ring - 2][0] for one in sets[1:]]
            totals = weights_call(
                [after(one, *gates) for one in flat(acts)], flat(cols), [], 1.0, jnp.float32
            )
            acts, cols = [], []
            gates = [totals[0]]
        results = []
        for chip in range(chips):
            results = run_group(first, chip, results, *gates)
        swap(first, results)

    def chain(steps, pairs, name):
        travelling = None
        for step in steps:
            total = own_grads[step]
            if travelling is not None:
                total = (total + travelling.astype(jnp.float32)).astype(jnp.bfloat16)
            travelling = send(total.astype(jnp.bfloat16), "tensor", pairs, f"{name}_{step}")
        return travelling

    own_grad = own_grads[0].astype(jnp.float32)
    if ring > 1:
        own_grad = own_grad + chain(range(half, 0, -1), from_last, "sum_up").astype(jnp.float32)
    if ring > 2:
        own_grad = own_grad + chain(range(half + 1, ring), from_next, "sum_down").astype(jnp.float32)
    branch_grad = norm_backward(own_grad, standard, row_scale, norm_gain)
    grad_input = (grad_out.astype(jnp.float32) + branch_grad).astype(jnp.bfloat16)

    grad_weight_in, grad_weight_out = weights_call(
        flat(acts), flat(cols), totals, 1.0 / blocks, jnp.bfloat16
    )
    return (grad_input, grad_weight_in, grad_weight_out)


def solution(mesh):
    in_specs = (
        P(("groups", "dp", "tensor"), None),
        P(("groups", "dp", "tensor"), None),
        P(),
        P(("groups", "dp")),
        P(("groups", "dp"), None),
        P(None, "tensor"),
        P("tensor", None),
    )
    out_specs = (
        P(("groups", "dp", "tensor"), None),
        P(("groups", "dp"), "tensor"),
        P(("groups", "tensor"), "dp"),
    )
    return jax.shard_map(shards, mesh=mesh, in_specs=in_specs, out_specs=out_specs, check_vma=False)
```

time: 286 us -> 277 us (0.969)
  starting transfers between devices: 33.7 us -> 22.7 us
  waiting for transfers between devices: 115 us -> 105 us
  Pallas kernels: 116 us -> 125 us
  local copies, waits for them, and re-layouts: 6.12 us -> 10.4 us
    ppermute x26 -> x22, starting transfers between devices: 33.7 us -> 22.7 us  [the longest x21 21.2 us: send(): return lax.ppermute(one, axis, pairs)]
    ppermute x26 -> x22, waiting for transfers between devices: 115 us -> 105 us  [the longest x21 87.1 us: send(): return lax.ppermute(one, axis, pairs)]
    pallas_call x1 -> x2, Pallas kernels: 24.9 us -> 32.8 us  [weights_call(): pl.pallas_call(functools.partial(weights_kernel, groups=len(acts), scale=...]
    unnamed x26 -> x32, local copies, waits for them, and re-layouts: 1.95 us -> 9.2 us
    slice x3 -> x2, local copies, waits for them, and re-layouts: 2.96 us -> 0.01 us  [run_group(): limit = limit_sets[chip][first * rows:(first + pieces) * rows, None]]
    convert_element_type x2 -> x1, other arithmetic: 4.61 us -> 1.74 us  [chain(): total = (total + travelling.astype(jnp.float32)).astype(jnp.bfloat16)]
  transfers between devices with their start and end apart: 26 -> 22, of which waited for: 11 -> 7; matrix products, arithmetic and copies ran while one was open for 4% -> 3% of each run, Pallas kernels for 32% -> 24%
where the time goes in v3:
time: 277 us
  Pallas kernels  125 us (45%)
  waiting for transfers between devices  105 us (38%)
  starting transfers between devices  22.7 us (8%)
  local copies, waits for them, and re-layouts  10.4 us (4%)
  other arithmetic  9.74 us (4%)
  between operations  2.88 us (1%)
    pallas_call x4, Pallas kernels, group_call(): pl.pallas_call(functools.partial(group_kernel, pieces=len(normed), begun=...  92.6 us
    ppermute x21, waiting for transfers between devices, send(): return lax.ppermute(one, axis, pairs)  87.1 us
    pallas_call x2, Pallas kernels, weights_call(): pl.pallas_call(functools.partial(weights_kernel, groups=len(acts), scale=...  32.8 us
    ppermute x21, starting transfers between devices, send(): return lax.ppermute(one, axis, pairs)  21.2 us
    ppermute x1, waiting for transfers between devices, shards(): limit_sets.append(lax.ppermute(limit_sets[-1], 'dp', from_chip))  18.4 us
    unnamed x32, local copies, waits for them, and re-layouts  9.2 us
  transfers between devices with their start and end apart: 22, of which 7 were waited for; matrix products, arithmetic and copies ran while one was open for 3% of the time, Pallas kernels for 24%

profile of v3, /device:TPU:0, one launch (start us, length us, event | category | flops | bytes accessed | tf_op | source)
XLA Modules:
  0.0 276.6 jit_solution(16373655382238903162)
XLA Ops:
  4.0 5.1 %collective-permute-start.2 = (bf16[128,3072]{1,0:T(8,128)(2,1)S(1)}, bf16[128,3072]{1,0:T(8,128)(2,1)}, u32[]{:S(2)}, u32[]{:S(2)}) collective-permute-start(bf16[128,3072]{1,0:T(8,128)(2,1)S(1)} %fusion.5.refs_0_), channel_id=1, source_target_pairs={{1,0},{2,1},{3,2},{0,3},{5,4},{6,5},{7,6},{4,7},{9,8},{10,9},{11,1... | collective-permute-start | bytes 2359304 | tf_op jit(solution)/shard_map/ring_1_normed/ppermute | solution.py:248
  15.2 1.5 collective-permute-start.8
  16.7 10.3 %collective-permute-done.2.refs_1_ = bf16[128,3072]{1,0:T(8,128)(2,1)} collective-permute-done((bf16[128,3072]{1,0:T(8,128)(2,1)S(1)}, bf16[128,3072]{1,0:T(8,128)(2,1)}, u32[]{:S(2)}, u32[]{:S(2)}) %collective-permute-start.2) | collective-permute-done | bytes 786464 | tf_op jit(solution)/shard_map/ring_1_normed/ppermute | solution.py:248
  28.5 18.4 %collective-permute-done.8 = s32[512]{0:T(512)S(1)} collective-permute-done((s32[512]{0:T(512)S(1)}, s32[512]{0:T(512)S(1)}, u32[]{:S(2)}, u32[]{:S(2)}) %collective-permute-start.8) | collective-permute-done | bytes 2080 | tf_op jit(solution)/shard_map/ppermute | solution.py:243
  47.4 1.5 collective-permute-start.7
  50.6 26.0 %group.4 = (bf16[2,512,3072]{2,1,0:T(8,128)(2,1)}, bf16[2,512,768]{2,1,0:T(8,128)(2,1)S(1)}, bf16[2,512,768]{2,1,0:T(8,128)(2,1)}, f32[128,3072]{1,0:T(8,128)}, f32[128,3072]{1,0:T(8,128)}) custom-call(s32[3]{0:T(128)S(1)} %pad_add_fusion.1.spots, bf16[128,3072]{1,0:T(8,128)(2,1)S(1)} %fusion.5.refs_0_, bf16[128,3072]{1,0:T(8,128)(2,1)} %collective-permute-done.2.refs_1_, ...), custom_call_target="tpu_custom_call" | custom-call | flops 4348654592 | tf_op jit(solution)/shard_map/group_0_0/group/pallas_call | solution.py:132
  76.5 3.6 %collective-permute-done.4.refs_2_ = bf16[128,3072]{1,0:T(8,128)(2,1)} collective-permute-done((bf16[128,3072]{1,0:T(8,128)(2,1)}, bf16[128,3072]{1,0:T(8,128)(2,1)}, u32[]{:S(2)}, u32[]{:S(2)}) %collective-permute-start.4) | collective-permute-done | bytes 786464 | tf_op jit(solution)/shard_map/ring_2_grad/ppermute | solution.py:248
  81.2 20.6 %group.5 = (bf16[2,512,3072]{2,1,0:T(8,128)(2,1)}, bf16[2,512,768]{2,1,0:T(8,128)(2,1)S(1)}, bf16[2,512,768]{2,1,0:T(8,128)(2,1)}) custom-call(s32[3]{0:T(128)S(1)} %pad_add_fusion.1.spots, bf16[128,3072]{1,0:T(8,128)(2,1)} %collective-permute-done.1.refs_0_, ...), custom_call_target="tpu_custom_call", output_to_operand_aliasing={{0}: (8, {}), {1}: (9, {}), {2}: (10, {})} | custom-call | flops 2899102976 | tf_op jit(solution)/shard_map/group_1_0/group/pallas_call | solution.py:132
  102.4 1.6 collective-permute-start.13
  103.9 1.5 collective-permute-start.9
  105.5 19.2 %collective-permute-done.13.refs_3_ = bf16[128,3072]{1,0:T(8,128)(2,1)} collective-permute-done((bf16[128,3072]{1,0:T(8,128)(2,1)S(1)}, bf16[128,3072]{1,0:T(8,128)(2,1)}, u32[]{:S(2)}, u32[]{:S(2)}) %collective-permute-start.13) | collective-permute-done | bytes 786464 | tf_op jit(solution)/shard_map/ring_3_grad/ppermute | solution.py:248
  127.6 2.1 copy-done.10
  130.0 15.1 %weights.2 = (f32[768,3072]{1,0:T(8,128)}, f32[3072,768]{1,0:T(8,128)}) custom-call(bf16[2,512,3072]{2,1,0:T(8,128)(2,1)} %get-tuple-element.39.refs_0_, bf16[2,512,3072]{2,1,0:T(8,128)(2,1)} %copy-done.10, bf16[2,512,768]{2,1,0:T(8,128)(2,1)S(1)} %get-tuple-element.41.refs_2_, bf16[2,512,768]{2,1,0:T(8,128)(2,1)} %collective-permute-done.11.refs_3_), custom_call_target="tpu_custom_call" | custom-call | flops 2899102976 | tf_op jit(solution)/shard_map/weights/pallas_call | solution.py:188
  145.1 25.7 %group.6 = (bf16[2,512,3072]{2,1,0:T(8,128)(2,1)}, bf16[2,512,768]{2,1,0:T(8,128)(2,1)}, bf16[2,512,768]{2,1,0:T(8,128)(2,1)}, bf16[128,3072]{1,0:T(8,128)(2,1)S(1)}, bf16[128,3072]{1,0:T(8,128)(2,1)S(1)}) custom-call(s32[3]{0:T(128)S(1)} %pad_add_fusion.1.spots, bf16[128,3072]{1,0:T(8,128)(2,1)} %collective-permute-done.5.refs_0_, ...), custom_call_target="tpu_custom_call" | custom-call | flops 4348654592 | tf_op jit(solution)/shard_map/group_0_2/group/pallas_call | solution.py:132
  172.2 20.4 %group.7 = (bf16[2,512,3072]{2,1,0:T(8,128)(2,1)}, bf16[2,512,768]{2,1,0:T(8,128)(2,1)S(1)}, bf16[2,512,768]{2,1,0:T(8,128)(2,1)}) custom-call(s32[3]{0:T(128)S(1)} %pad_add_fusion.1.spots, bf16[128,3072]{1,0:T(8,128)(2,1)} %collective-permute-done.17.refs_0_, ...), custom_call_target="tpu_custom_call", output_to_operand_aliasing={{0}: (8, {}), {1}: (9, {}), {2}: (10, {})} | custom-call | flops 2899102976 | tf_op jit(solution)/shard_map/group_1_2/group/pallas_call | solution.py:132
  192.8 3.9 %collective-permute-start.16 = (bf16[128,3072]{1,0:T(8,128)(2,1)S(1)}, bf16[128,3072]{1,0:T(8,128)(2,1)S(1)}, u32[]{:S(2)}, u32[]{:S(2)}) collective-permute-start(bf16[128,3072]{1,0:T(8,128)(2,1)S(1)} %get-tuple-element.48), channel_id=1, source_target_pairs={{1,0},{2,1},{3,2},{0,3},{5,4},{6,5},{7,6},{4,7},{9,8},{10,9},{11,1... | collective-permute-start | bytes 2359304 | tf_op jit(solution)/shard_map/sum_down_3/ppermute | solution.py:248
  196.7 18.4 %collective-permute-done.14 = bf16[128,3072]{1,0:T(8,128)(2,1)S(1)} collective-permute-done((bf16[128,3072]{1,0:T(8,128)(2,1)S(1)}, bf16[128,3072]{1,0:T(8,128)(2,1)S(1)}, u32[]{:S(2)}, u32[]{:S(2)}) %collective-permute-start.14) | collective-permute-done | bytes 786464 | tf_op jit(solution)/shard_map/sum_up_2/ppermute | solution.py:248
  215.0 1.7 add_convert_fusion
  217.0 12.6 %collective-permute-done.16 = bf16[128,3072]{1,0:T(8,128)(2,1)S(1)} collective-permute-done((bf16[128,3072]{1,0:T(8,128)(2,1)S(1)}, bf16[128,3072]{1,0:T(8,128)(2,1)S(1)}, u32[]{:S(2)}, u32[]{:S(2)}) %collective-permute-start.16) | collective-permute-done | bytes 786464 | tf_op jit(solution)/shard_map/sum_down_3/ppermute | solution.py:248
  229.5 23.0 %collective-permute-done.15 = bf16[128,3072]{1,0:T(8,128)(2,1)S(1)} collective-permute-done((bf16[128,3072]{1,0:T(8,128)(2,1)S(1)}, bf16[128,3072]{1,0:T(8,128)(2,1)S(1)}, u32[]{:S(2)}, u32[]{:S(2)}) %collective-permute-start.15) | collective-permute-done | bytes 786464 | tf_op jit(solution)/shard_map/sum_up_1/ppermute | solution.py:248
  252.5 2.1 fusion.13
  254.7 1.6 fusion.10
  256.2 2.7 copy-done.11
  258.9 17.7 %weights.3 = (bf16[768,3072]{1,0:T(8,128)(2,1)}, bf16[3072,768]{1,0:T(8,128)(2,1)}) custom-call(bf16[2,512,3072]{2,1,0:T(8,128)(2,1)} %get-tuple-element.53.refs_0_, bf16[2,512,3072]{2,1,0:T(8,128)(2,1)} %copy-done.11, bf16[2,512,768]{2,1,0:T(8,128)(2,1)S(1)} %copy-done.2, bf16[2,512,768]{2,1,0:T(8,128)(2,1)S(1)} %collective-permute-done.21.refs_3_, ...), custom_call_target="tpu_custom_call" | custom-call | flops 2899102976 | tf_op jit(solution)/shard_map/weights/pallas_call | solution.py:188
  (80 shorter events, 17.6 us)
Async XLA Ops:
  4.0 23.0 %collective-permute-start.2 = (bf16[128,3072]{1,0:T(8,128)(2,1)S(1)}, bf16[128,3072]{1,0:T(8,128)(2,1)}, u32[]{:S(2)}, u32[]{:S(2)}) collective-permute-start(bf16[128,3072]{1,0:T(8,128)(2,1)S(1)} %fusion.5.refs_0_), channel_id=1, source_target_pairs={{1,0},{2,1},{3,2},{0,3},{5,4},{6,5},{7,6},{4,7},{9,8},{10,9},{11,1... | collective-permute-start | bytes 2359304 | tf_op jit(solution)/shard_map/ring_1_normed/ppermute | solution.py:248
  9.1 38.3 %collective-permute-start.3 = (bf16[128,3072]{1,0:T(8,128)(2,1)S(1)}, bf16[128,3072]{1,0:T(8,128)(2,1)}, u32[]{:S(2)}, u32[]{:S(2)}) collective-permute-start(bf16[128,3072]{1,0:T(8,128)(2,1)S(1)} %copy-done.3), channel_id=1, source_target_pairs={{1,0},{2,1},{3,2},{0,3},{5,4},{6,5},{7,6},{4,7},{9,8},{10,9},{11,1... | collective-permute-start | bytes 2359304 | tf_op jit(solution)/shard_map/ring_1_grad/ppermute | solution.py:248
  9.5 39.3 %collective-permute-start.1 = (bf16[128,3072]{1,0:T(8,128)(2,1)S(1)}, bf16[128,3072]{1,0:T(8,128)(2,1)}, u32[]{:S(2)}, u32[]{:S(2)}) collective-permute-start(bf16[128,3072]{1,0:T(8,128)(2,1)S(1)} %fusion.5.refs_0_), channel_id=1, source_target_pairs={{8,0},{12,4},{0,8},{4,12},{9,1},{13,5},{1,9},{5,13},{10,2},{14,6},... | collective-permute-start | bytes 2359304 | tf_op jit(solution)/shard_map/chip_0_normed/ppermute | solution.py:248
  11.0 38.7 %collective-permute-start = (bf16[128,3072]{1,0:T(8,128)(2,1)S(1)}, bf16[128,3072]{1,0:T(8,128)(2,1)S(1)}, u32[]{:S(2)}, u32[]{:S(2)}) collective-permute-start(bf16[128,3072]{1,0:T(8,128)(2,1)S(1)} %copy-done.3), channel_id=1, source_target_pairs={{8,0},{12,4},{0,8},{4,12},{9,1},{13,5},{1,9},{5,13},{10,2},{14,6},... | collective-permute-start | bytes 2359304 | tf_op jit(solution)/shard_map/chip_0_grad/ppermute | solution.py:248
  15.2 31.7 %collective-permute-start.8 = (s32[512]{0:T(512)S(1)}, s32[512]{0:T(512)S(1)}, u32[]{:S(2)}, u32[]{:S(2)}) collective-permute-start(s32[512]{0:T(512)S(1)} %dynamic_slice.3), channel_id=1, source_target_pairs={{8,0},{12,4},{0,8},{4,12},{9,1},{13,5},{1,9},{5,13},{10,2},{14,6},... | collective-permute-start | bytes 6152 | tf_op jit(solution)/shard_map/ppermute | solution.py:243
  27.0 53.1 %collective-permute-start.6 = (bf16[128,3072]{1,0:T(8,128)(2,1)}, bf16[128,3072]{1,0:T(8,128)(2,1)}, u32[]{:S(2)}, u32[]{:S(2)}) collective-permute-start(bf16[128,3072]{1,0:T(8,128)(2,1)} %collective-permute-done.2.refs_1_), channel_id=1, source_target_pairs={{8,0},{12,4},{0,8},{4,12},{9,1},{13,5},{1,9},{5,13},{10,2},{14,6},... | collective-permute-start | bytes 2359304 | tf_op jit(solution)/shard_map/chip_1_normed/ppermute | solution.py:248
  46.9 29.6 %collective-permute-start.5 = (bf16[128,3072]{1,0:T(8,128)(2,1)}, bf16[128,3072]{1,0:T(8,128)(2,1)}, u32[]{:S(2)}, u32[]{:S(2)}) collective-permute-start(bf16[128,3072]{1,0:T(8,128)(2,1)} %collective-permute-done.2.refs_1_), channel_id=1, source_target_pairs={{1,0},{2,1},{3,2},{0,3},{5,4},{6,5},{7,6},{4,7},{9,8},{10,9},{11,1... | collective-permute-start | bytes 2359304 | tf_op jit(solution)/shard_map/ring_2_normed/ppermute | solution.py:248
  47.4 32.8 %collective-permute-start.7 = (bf16[128,3072]{1,0:T(8,128)(2,1)}, bf16[128,3072]{1,0:T(8,128)(2,1)}, u32[]{:S(2)}, u32[]{:S(2)}) collective-permute-start(bf16[128,3072]{1,0:T(8,128)(2,1)} %collective-permute-done.3.refs_3_), channel_id=1, source_target_pairs={{8,0},{12,4},{0,8},{4,12},{9,1},{13,5},{1,9},{5,13},{10,2},{14,6},... | collective-permute-start | bytes 2359304 | tf_op jit(solution)/shard_map/chip_1_grad/ppermute | solution.py:248
  48.9 31.3 %collective-permute-start.4 = (bf16[128,3072]{1,0:T(8,128)(2,1)}, bf16[128,3072]{1,0:T(8,128)(2,1)}, u32[]{:S(2)}, u32[]{:S(2)}) collective-permute-start(bf16[128,3072]{1,0:T(8,128)(2,1)} %collective-permute-done.3.refs_3_), channel_id=1, source_target_pairs={{1,0},{2,1},{3,2},{0,3},{5,4},{6,5},{7,6},{4,7},{9,8},{10,9},{11,1... | collective-permute-start | bytes 2359304 | tf_op jit(solution)/shard_map/ring_2_grad/ppermute | solution.py:248
  101.9 25.2 %collective-permute-start.10 = (bf16[2,512,3072]{2,1,0:T(8,128)(2,1)}, bf16[2,512,3072]{2,1,0:T(8,128)(2,1)S(1)}, u32[]{:S(2)}, u32[]{:S(2)}) collective-permute-start(bf16[2,512,3072]{2,1,0:T(8,128)(2,1)} %get-tuple-element.39.refs_0_), channel_id=1, source_target_pairs={{0,4},{4,0},{8,12},{12,8},{1,5},{5,1},{9,13},{13,9},{2,6},{6,2},{1... | collective-permute-start | bytes 18874376 | tf_op jit(solution)/shard_map/swap_acts_0/ppermute | solution.py:248
  101.9 28.1 %collective-permute-start.11 = (bf16[2,512,768]{2,1,0:T(8,128)(2,1)}, bf16[2,512,768]{2,1,0:T(8,128)(2,1)}, u32[]{:S(2)}, u32[]{:S(2)}) collective-permute-start(bf16[2,512,768]{2,1,0:T(8,128)(2,1)} %get-tuple-element.42), channel_id=1, source_target_pairs={{0,4},{4,0},{8,12},{12,8},{1,5},{5,1},{9,13},{13,9},{2,6},{6,2},{1... | collective-permute-start | bytes 4718600 | tf_op jit(solution)/shard_map/swap_cols_0/ppermute | solution.py:248
  102.4 22.3 %collective-permute-start.13 = (bf16[128,3072]{1,0:T(8,128)(2,1)S(1)}, bf16[128,3072]{1,0:T(8,128)(2,1)}, u32[]{:S(2)}, u32[]{:S(2)}) collective-permute-start(bf16[128,3072]{1,0:T(8,128)(2,1)S(1)} %copy-done.3), channel_id=1, source_target_pairs={{0,1},{1,2},{2,3},{3,0},{4,5},{5,6},{6,7},{7,4},{8,9},{9,10},{10,1... | collective-permute-start | bytes 2359304 | tf_op jit(solution)/shard_map/ring_3_grad/ppermute | solution.py:248
  103.9 20.7 %collective-permute-start.9 = (bf16[128,3072]{1,0:T(8,128)(2,1)}, bf16[128,3072]{1,0:T(8,128)(2,1)S(1)}, u32[]{:S(2)}, u32[]{:S(2)}) collective-permute-start(bf16[128,3072]{1,0:T(8,128)(2,1)} %collective-permute-done.4.refs_2_), channel_id=1, source_target_pairs={{8,0},{12,4},{0,8},{4,12},{9,1},{13,5},{1,9},{5,13},{10,2},{14,6},... | collective-permute-start | bytes 2359304 | tf_op jit(solution)/shard_map/chip_2_grad/ppermute | solution.py:248
  105.4 39.7 %collective-permute-start.12 = (bf16[128,3072]{1,0:T(8,128)(2,1)S(1)}, bf16[128,3072]{1,0:T(8,128)(2,1)}, u32[]{:S(2)}, u32[]{:S(2)}) collective-permute-start(bf16[128,3072]{1,0:T(8,128)(2,1)S(1)} %fusion.5.refs_0_), channel_id=1, source_target_pairs={{0,1},{1,2},{2,3},{3,0},{4,5},{5,6},{6,7},{7,4},{8,9},{9,10},{10,1... | collective-permute-start | bytes 2359304 | tf_op jit(solution)/shard_map/ring_3_normed/ppermute | solution.py:248
  124.7 46.1 %collective-permute-start.18 = (bf16[128,3072]{1,0:T(8,128)(2,1)}, bf16[128,3072]{1,0:T(8,128)(2,1)}, u32[]{:S(2)}, u32[]{:S(2)}) collective-permute-start(bf16[128,3072]{1,0:T(8,128)(2,1)} %collective-permute-done.1.refs_0_), channel_id=1, source_target_pairs={{0,1},{1,2},{2,3},{3,0},{4,5},{5,6},{6,7},{7,4},{8,9},{9,10},{10,1... | collective-permute-start | bytes 2359304 | tf_op jit(solution)/shard_map/ring_chip_3_normed/ppermute | solution.py:248
  125.6 45.2 %collective-permute-start.17 = (bf16[128,3072]{1,0:T(8,128)(2,1)}, bf16[128,3072]{1,0:T(8,128)(2,1)}, u32[]{:S(2)}, u32[]{:S(2)}) collective-permute-start(bf16[128,3072]{1,0:T(8,128)(2,1)} %collective-permute-done.5.refs_0_), channel_id=1, source_target_pairs={{8,0},{12,4},{0,8},{4,12},{9,1},{13,5},{1,9},{5,13},{10,2},{14,6},... | collective-permute-start | bytes 2359304 | tf_op jit(solution)/shard_map/chip_2_normed/ppermute | solution.py:248
  127.0 43.8 %collective-permute-start.19 = (bf16[128,3072]{1,0:T(8,128)(2,1)}, bf16[128,3072]{1,0:T(8,128)(2,1)}, u32[]{:S(2)}, u32[]{:S(2)}) collective-permute-start(bf16[128,3072]{1,0:T(8,128)(2,1)} %collective-permute-done.13.refs_3_), channel_id=1, source_target_pairs={{8,0},{12,4},{0,8},{4,12},{9,1},{13,5},{1,9},{5,13},{10,2},{14,6},... | collective-permute-start | bytes 2359304 | tf_op jit(solution)/shard_map/chip_3_grad/ppermute | solution.py:248
  145.1 25.7 %copy-start.7 = (bf16[128,3072]{1,0:T(8,128)(2,1)S(1)}, bf16[128,3072]{1,0:T(8,128)(2,1)}, u32[]{:S(2)}) copy-start(bf16[128,3072]{1,0:T(8,128)(2,1)} %copy-done.6) | copy-start | bytes 2359300
  192.6 63.6 %collective-permute-start.20 = (bf16[2,512,3072]{2,1,0:T(8,128)(2,1)}, bf16[2,512,3072]{2,1,0:T(8,128)(2,1)S(1)}, u32[]{:S(2)}, u32[]{:S(2)}) collective-permute-start(bf16[2,512,3072]{2,1,0:T(8,128)(2,1)} %get-tuple-element.53.refs_0_), channel_id=1, source_target_pairs={{0,4},{4,0},{8,12},{12,8},{1,5},{5,1},{9,13},{13,9},{2,6},{6,2},{1... | collective-permute-start | bytes 18874376 | tf_op jit(solution)/shard_map/swap_acts_2/ppermute | solution.py:248
  192.7 22.3 %collective-permute-start.14 = (bf16[128,3072]{1,0:T(8,128)(2,1)S(1)}, bf16[128,3072]{1,0:T(8,128)(2,1)S(1)}, u32[]{:S(2)}, u32[]{:S(2)}) collective-permute-start(bf16[128,3072]{1,0:T(8,128)(2,1)S(1)} %get-tuple-element.47), channel_id=1, source_target_pairs={{0,1},{1,2},{2,3},{3,0},{4,5},{5,6},{6,7},{7,4},{8,9},{9,10},{10,1... | collective-permute-start | bytes 2359304 | tf_op jit(solution)/shard_map/sum_up_2/ppermute | solution.py:248
  192.8 36.7 %collective-permute-start.16 = (bf16[128,3072]{1,0:T(8,128)(2,1)S(1)}, bf16[128,3072]{1,0:T(8,128)(2,1)S(1)}, u32[]{:S(2)}, u32[]{:S(2)}) collective-permute-start(bf16[128,3072]{1,0:T(8,128)(2,1)S(1)} %get-tuple-element.48), channel_id=1, source_target_pairs={{1,0},{2,1},{3,2},{0,3},{5,4},{6,5},{7,6},{4,7},{9,8},{10,9},{11,1... | collective-permute-start | bytes 2359304 | tf_op jit(solution)/shard_map/sum_down_3/ppermute | solution.py:248
  215.0 37.5 %copy-start.9 = (bf16[128,3072]{1,0:T(8,128)(2,1)S(1)}, bf16[128,3072]{1,0:T(8,128)(2,1)}, u32[]{:S(2)}) copy-start(bf16[128,3072]{1,0:T(8,128)(2,1)} %param.7) | copy-start | bytes 2359300
  216.8 35.7 %collective-permute-start.15 = (bf16[128,3072]{1,0:T(8,128)(2,1)S(1)}, bf16[128,3072]{1,0:T(8,128)(2,1)S(1)}, u32[]{:S(2)}, u32[]{:S(2)}) collective-permute-start(bf16[128,3072]{1,0:T(8,128)(2,1)S(1)} %add_convert_fusion), channel_id=1, source_target_pairs={{0,1},{1,2},{2,3},{3,0},{4,5},{5,6},{6,7},{7,4},{8,9},{9,10},{10,1... | collective-permute-start | bytes 2359304 | tf_op jit(solution)/shard_map/sum_up_1/ppermute | solution.py:248
  216.9 39.3 %collective-permute-start.21 = (bf16[2,512,768]{2,1,0:T(8,128)(2,1)S(1)}, bf16[2,512,768]{2,1,0:T(8,128)(2,1)S(1)}, u32[]{:S(2)}, u32[]{:S(2)}) collective-permute-start(bf16[2,512,768]{2,1,0:T(8,128)(2,1)S(1)} %copy-done.12), channel_id=1, source_target_pairs={{0,4},{4,0},{8,12},{12,8},{1,5},{5,1},{9,13},{13,9},{2,6},{6,2},{1... | collective-permute-start | bytes 4718600 | tf_op jit(solution)/shard_map/swap_cols_2/ppermute | solution.py:248
  (14 other events, 79.4 us)

commit v4 on v3

v4 whole, which is shorter than its diff:
```python
import functools
import math

import jax
import jax.numpy as jnp
from jax import lax
from jax.experimental import pallas as pl
from jax.experimental.pallas import tpu as pltpu
from jax.sharding import PartitionSpec as P

GELU_SCALE = 0.7978845608028654
GELU_CUBE = 0.044715
NORM_EPS = 1e-06
VMEM_LIMIT = 48 * 1024 * 1024
WORK = 4.0


def gelu_parts(pre_act):
    square = pre_act * pre_act
    tanh_val = jnp.tanh(pre_act * (GELU_SCALE + (GELU_SCALE * GELU_CUBE) * square))
    share = 0.5 + 0.5 * tanh_val
    gelu_value = pre_act * share
    gelu_slope = share + gelu_value * (1.0 - tanh_val) * (
        GELU_SCALE + (3.0 * GELU_SCALE * GELU_CUBE) * square
    )
    return (gelu_value, gelu_slope)


def token_levels(block_order, count_row):
    above_three = count_row[3]
    above_two = above_three + count_row[2]
    above_one = above_two + count_row[1]
    places = jnp.arange(block_order.shape[0], dtype=jnp.int32)
    ranked = (
        (places < above_three).astype(jnp.int32)
        + (places < above_two).astype(jnp.int32)
        + (places < above_one).astype(jnp.int32)
    )
    hits = block_order[None, :] == places[:, None]
    return jnp.sum(jnp.where(hits, ranked[None, :], 0), axis=1)


def norm_backward(grad_normed, standard, row_scale, norm_gain):
    scaled = grad_normed * norm_gain[None, :]
    centre = jnp.mean(scaled, axis=1, keepdims=True)
    along = jnp.mean(scaled * standard, axis=1, keepdims=True)
    return row_scale * (scaled - centre - standard * along)


def work_of(flops):
    return pl.CostEstimate(flops=int(WORK * flops), bytes_accessed=0, transcendentals=0)


def tile_of(extent, wanted):
    while extent % wanted:
        wanted //= 2
    return wanted


def group_kernel(spots, *refs, pieces, owned, share, tiles):
    normed_refs = refs[:pieces]
    grad_refs = refs[pieces : 2 * pieces]
    limit_ref, in_ref, out_ref = refs[2 * pieces : 2 * pieces + 3]
    acts_ref, own_ref = refs[2 * pieces + 3 : 2 * pieces + 5]
    rest = refs[2 * pieces + 5 :]
    tile = pl.program_id(0)

    def columns(target, first):
        span = pl.ds(pl.multiple_of(first, 128), share)
        for kind, sources in enumerate((normed_refs, grad_refs)):
            for at, ref in enumerate(sources):
                size = ref.shape[0]
                target[kind, at * size : (at + 1) * size, :] = ref[:, span]

    @pl.when(tile == 0)
    def _():
        columns(own_ref, spots[1])

    @pl.when(tile == tiles)
    def _():
        columns(acts_ref, spots[2])

    @pl.when(tile < tiles)
    def _():
        group_tile(spots[0], normed_refs, grad_refs, limit_ref, in_ref, out_ref, acts_ref, rest, owned, tiles)


def group_tile(first, normed_refs, grad_refs, limit_ref, in_ref, out_ref, acts_ref, rest, owned, tiles):
    tile = pl.program_id(0)
    units = in_ref.shape[1]
    width = 256 if units % 256 == 0 else units
    normed = jnp.concatenate([ref[...] for ref in normed_refs], axis=0)
    grads = jnp.concatenate([ref[...] for ref in grad_refs], axis=0)

    mask = first + tile * units < limit_ref[...]
    products = []
    for start in range(0, units, width):
        span = slice(start, start + width)
        pre_act = jnp.dot(normed, in_ref[:, span], preferred_element_type=jnp.float32)
        grad_hidden = lax.dot_general(
            grads, out_ref[span, :], (((1,), (1,)), ((), ())), preferred_element_type=jnp.float32
        )
        products.append((span, pre_act, grad_hidden))
    for span, pre_act, grad_hidden in products:
        gelu_value, gelu_slope = gelu_parts(pre_act)
        acts_ref[0, :, span] = jnp.where(mask, grad_hidden * gelu_slope, 0.0).astype(jnp.bfloat16)
        acts_ref[1, :, span] = jnp.where(mask, gelu_value, 0.0).astype(jnp.bfloat16)
    if owned:
        back_refs, total_ref = rest[:-1], rest[-1]
        term = lax.dot_general(
            acts_ref[0, : total_ref.shape[0], :],
            in_ref[...],
            (((1,), (1,)), ((), ())),
            preferred_element_type=jnp.float32,
        )

        @pl.when(tile == 0)
        def _():
            total_ref[...] = term

        @pl.when(tile != 0)
        def _():
            total_ref[...] += term

        @pl.when(tile == tiles - 1)
        def _():
            for at, ref in enumerate(back_refs):
                size = ref.shape[0]
                ref[...] = total_ref[at * size : (at + 1) * size, :].astype(ref.dtype)


def group_call(spots, normed, grads, limit, weight_in, weight_out, tile, share, back_types):
    features, units = weight_in.shape
    piece_rows = normed[0].shape[0]
    rows = piece_rows * len(normed)
    owned = len(back_types)
    tiles = units // tile
    whole = lambda shape: pl.BlockSpec(shape, lambda i, spots: (0,) * len(shape))
    out_shape = [
        jax.ShapeDtypeStruct((2, rows, units + share), jnp.bfloat16),
        jax.ShapeDtypeStruct((2, rows, share), jnp.bfloat16),
    ]
    out_specs = [
        pl.BlockSpec((2, rows, tile), lambda i, spots: (0, 0, i)),
        whole((2, rows, share)),
    ]
    for kind in back_types:
        out_shape.append(jax.ShapeDtypeStruct((piece_rows, features), kind))
        out_specs.append(whole((piece_rows, features)))
    return pl.pallas_call(
        functools.partial(
            group_kernel, pieces=len(normed), owned=owned, share=share, tiles=tiles
        ),
        grid_spec=pltpu.PrefetchScalarGridSpec(
            num_scalar_prefetch=1,
            grid=(tiles + share // tile,),
            in_specs=[whole(one.shape) for one in (*normed, *grads)]
            + [
                whole((rows, 1)),
                pl.BlockSpec((features, tile), lambda i, spots: (0, jnp.minimum(i, tiles - 1))),
                pl.BlockSpec((tile, features), lambda i, spots: (jnp.minimum(i, tiles - 1), 0)),
            ],
            out_specs=out_specs,
            scratch_shapes=[pltpu.VMEM((owned * piece_rows, features), jnp.float32)] if owned else [],
        ),
        out_shape=out_shape,
        compiler_params=pltpu.CompilerParams(vmem_limit_bytes=VMEM_LIMIT),
        cost_estimate=work_of((4 * rows + 2 * owned * piece_rows) * units * features),
        name="group",
    )(spots, *normed, *grads, limit, weight_in, weight_out)


def weights_kernel(*refs, groups, scale, started):
    act_refs = refs[:groups]
    col_refs = refs[groups : 2 * groups]
    in_ref, out_ref = refs[-2:]

    def stack(sources, kind):
        return jnp.concatenate([ref[kind] for ref in sources], axis=0)

    def total(left, right):
        return lax.dot_general(
            left, right, (((0,), (0,)), ((), ())), preferred_element_type=jnp.float32
        )

    for_in = total(stack(col_refs, 0), stack(act_refs, 0))
    for_out = total(stack(act_refs, 1), stack(col_refs, 1))
    if started:
        for_in += refs[-4][...].astype(jnp.float32)
        for_out += refs[-3][...].astype(jnp.float32)
    in_ref[...] = (for_in * scale).astype(in_ref.dtype)
    out_ref[...] = (for_out * scale).astype(out_ref.dtype)


def weights_call(groups, begun, scale):
    share = groups[0][1].shape[2]
    units = groups[0][0].shape[2] - share
    tile = tile_of(units, 512)
    acts, acts_specs, cols, cols_specs = [], [], [], []
    for own, own_cols, other in groups:
        rows = own.shape[1]
        acts += [own, other]
        acts_specs += [pl.BlockSpec((2, rows, tile), lambda i: (0, 0, i))] * 2
        cols += [own_cols, other]
        cols_specs += [
            pl.BlockSpec((2, rows, share), lambda i: (0, 0, 0)),
            pl.BlockSpec((2, rows, share), lambda i: (0, 0, units // share)),
        ]
    in_spec = pl.BlockSpec((share, tile), lambda i: (0, i))
    out_spec = pl.BlockSpec((tile, share), lambda i: (i, 0))
    return pl.pallas_call(
        functools.partial(weights_kernel, groups=len(acts), scale=scale, started=bool(begun)),
        grid=(units // tile,),
        in_specs=acts_specs + cols_specs + ([in_spec, out_spec] if begun else []),
        out_specs=[in_spec, out_spec],
        out_shape=[
            jax.ShapeDtypeStruct((share, units), jnp.bfloat16),
            jax.ShapeDtypeStruct((units, share), jnp.bfloat16),
        ],
        compiler_params=pltpu.CompilerParams(vmem_limit_bytes=VMEM_LIMIT),
        cost_estimate=work_of(4 * sum(one.shape[1] for one in acts) * units * share),
        name="weights",
    )(*acts, *cols, *begun)


def after(value, *others):
    return lax.optimization_barrier((value, others))[0] if others else value


def shards(inputs, grad_out, norm_gain, level_order, level_counts, weight_in, weight_out):
    rows = inputs.shape[0]
    ring = lax.axis_size("tensor")
    place = lax.axis_index("tensor")
    blocks = lax.axis_size("dp")
    block = lax.axis_index("dp")
    chips = blocks // 2
    unit_local = weight_in.shape[1]
    unit_total = unit_local * ring
    share = inputs.shape[1] // blocks
    tile = math.gcd(unit_local, unit_total // 8, share)

    from_next = [((i + 1) % ring, i) for i in range(ring)]
    from_last = [(i, (i + 1) % ring) for i in range(ring)]
    from_chip = [((i + 2) % blocks, i) for i in range(blocks)]
    swap_cores = [(i, i ^ 1) for i in range(blocks)]
    half = ring // 2

    as_float = inputs.astype(jnp.float32)
    row_mean = jnp.mean(as_float, axis=1, keepdims=True)
    centred = as_float - row_mean
    row_scale = lax.rsqrt(jnp.mean(centred * centred, axis=1, keepdims=True) + NORM_EPS)
    standard = centred * row_scale
    normed = (standard * norm_gain[None, :]).astype(jnp.bfloat16)

    def limits_of(order, counts):
        limits = unit_total // (1 << (3 - token_levels(order, counts)))
        limits = jnp.concatenate([limits, limits])
        return lax.dynamic_slice_in_dim(limits, place * rows, rows * ring, 0)

    spots = jnp.stack([place * unit_local, block * share, (block ^ 1) * share]).astype(jnp.int32)

    def send(one, axis, pairs, name):
        with jax.named_scope(name):
            return lax.ppermute(one, axis, pairs)

    kinds = ("grad", "normed")

    def move(piece, axis, pairs, name, *gates):
        return tuple(
            send(after(one, *gates), axis, pairs, f"{name}_{kind}") for one, kind in zip(piece, kinds)
        )

    near = {0: (grad_out, normed)}
    for step in range(1, ring):
        near[step] = move(near[step - 1], "tensor", from_next, f"ring_{step}")
    sets = [[near[step] for step in range(ring)]]
    limit_sets = [limits_of(level_order, level_counts[0])]
    levels = jnp.concatenate([level_order, level_counts[0]])
    for chip in range(1, chips):
        levels = send(levels, "dp", from_chip, "chip_levels")
        limit_sets.append(limits_of(levels[:-4], levels[-4:]))
        far = []
        for step, (grads, rows_normed) in enumerate(sets[-1]):
            grads = send(grads, "dp", from_chip, f"chip_{step}_grad")
            if step == 0:
                rows_normed = after(rows_normed, levels)
            far.append((grads, send(rows_normed, "dp", from_chip, f"chip_{step}_normed")))
        sets.append(far)

    groups, own_grads = [], []
    arrivals = [
        [(chip, slot - chip) for chip in range(chips) if 0 <= slot - chip < ring]
        for slot in range(ring + chips - 1)
    ]
    if len(arrivals) > 1:
        arrivals[:2] = [sorted(arrivals[0] + arrivals[1])]
    totals = []
    for at, entries in enumerate(arrivals):
        gates = []
        if at > 0 and at == len(arrivals) - 1:
            early = [sets[chip][step][0] for chip, step in entries]
            totals = weights_call(
                [(after(own, *early), *others) for own, *others in groups[:-1]], [], 1.0
            )
            gates = [totals[0]]
            groups = groups[-1:]
        own_steps = [step for chip, step in entries if chip == 0]
        back_types = [jnp.bfloat16 if step in (half, half + 1) else jnp.float32 for step in own_steps]
        limit = jnp.concatenate(
            [limit_sets[chip][step * rows : (step + 1) * rows, None] for chip, step in entries]
        )
        with jax.named_scope(f"group_{at}"):
            act, own_cols, *back = group_call(
                after(spots, *gates),
                [sets[chip][step][1] for chip, step in entries],
                [sets[chip][step][0] for chip, step in entries],
                limit,
                weight_in,
                weight_out,
                tile,
                share,
                back_types,
            )
        own_grads.extend(back)
        groups.append((act, own_cols, send(act, "dp", swap_cores, f"swap_{at}")))

    def chain(steps, pairs, name):
        travelling = None
        for step in steps:
            total = own_grads[step]
            if travelling is not None:
                total = (total + travelling.astype(jnp.float32)).astype(jnp.bfloat16)
            travelling = send(total.astype(jnp.bfloat16), "tensor", pairs, f"{name}_{step}")
        return travelling

    own_grad = own_grads[0].astype(jnp.float32)
    if ring > 1:
        own_grad = own_grad + chain(range(half, 0, -1), from_last, "sum_up").astype(jnp.float32)
    if ring > 2:
        own_grad = own_grad + chain(range(half + 1, ring), from_next, "sum_down").astype(jnp.float32)
    branch_grad = norm_backward(own_grad, standard, row_scale, norm_gain)
    grad_input = (grad_out.astype(jnp.float32) + branch_grad).astype(jnp.bfloat16)

    grad_weight_in, grad_weight_out = weights_call(groups, totals, 1.0 / blocks)
    return (grad_input, grad_weight_in, grad_weight_out)


def solution(mesh):
    in_specs = (
        P(("groups", "dp", "tensor"), None),
        P(("groups", "dp", "tensor"), None),
        P(),
        P(("groups", "dp")),
        P(("groups", "dp"), None),
        P(None, "tensor"),
        P("tensor", None),
    )
    out_specs = (
        P(("groups", "dp", "tensor"), None),
        P(("groups", "dp"), "tensor"),
        P(("groups", "tensor"), "dp"),
    )
    return jax.shard_map(shards, mesh=mesh, in_specs=in_specs, out_specs=out_specs, check_vma=False)
```

time: 277 us -> 198 us (0.71)
  waiting for transfers between devices: 105 us -> 32.2 us
  local copies, waits for them, and re-layouts: 10.4 us -> 3.18 us
  starting transfers between devices: 22.7 us -> 26.6 us
  Pallas kernels: 125 us -> 122 us
    ppermute x21 -> x22, waiting for transfers between devices: 87.1 us -> 32.2 us  [send(): return lax.ppermute(one, axis, pairs)]
    ppermute x1 -> x0, waiting for transfers between devices: 18.4 us -> none  [shards(): limit_sets.append(lax.ppermute(limit_sets[-1], 'dp', from_chip))]
    unnamed x32, local copies, waits for them, and re-layouts: 9.2 us -> 1.29 us
    ppermute x21 -> x22, starting transfers between devices: 21.2 us -> 26.6 us  [send(): return lax.ppermute(one, axis, pairs)]
    pallas_call x2, Pallas kernels: 32.8 us -> 30 us  [weights_call(): pl.pallas_call(functools.partial(weights_kernel, groups=len(acts), scale=...]
  transfers between devices with their start and end apart: 22 -> 22, of which waited for: 7 -> 6; matrix products, arithmetic and copies ran while one was open for 3% -> 5% of each run, Pallas kernels for 24% -> 55%
where the time goes in v4:
time: 198 us; the launch traced here: 197 us
  Pallas kernels  122 us (62%)
  waiting for transfers between devices  32.2 us (16%)
  starting transfers between devices  26.6 us (13%)
  other arithmetic  8.37 us (4%)
  between operations  4.84 us (2%)
  local copies, waits for them, and re-layouts  3.18 us (2%)
    pallas_call x4, Pallas kernels, group_call(): pl.pallas_call(functools.partial(group_kernel, pieces=len(normed), owned=...  92.1 us
    ppermute x22, waiting for transfers between devices, send(): return lax.ppermute(one, axis, pairs)  32.2 us
    pallas_call x2, Pallas kernels, weights_call(): pl.pallas_call(functools.partial(weights_kernel, groups=len(acts), scale=...  30 us
    ppermute x22, starting transfers between devices, send(): return lax.ppermute(one, axis, pairs)  26.6 us
  transfers between devices with their start and end apart: 22, of which 6 were waited for; matrix products, arithmetic and copies ran while one was open for 5% of the time, Pallas kernels for 55%

profile of v4, /device:TPU:0, one launch (start us, length us, event | category | flops | bytes accessed | tf_op | source)
XLA Modules:
  0.0 197.2 jit_solution(8929560074647605674)
XLA Ops:
  0.7 5.1 %collective-permute-start.3 = (bf16[128,3072]{1,0:T(8,128)(2,1)}, bf16[128,3072]{1,0:T(8,128)(2,1)S(1)}, u32[]{:S(2)}, u32[]{:S(2)}) collective-permute-start(bf16[128,3072]{1,0:T(8,128)(2,1)} %refs_3_.2), channel_id=1, source_target_pairs={{1,0},{2,1},{3,2},{0,3},{5,4},{6,5},{7,6},{4,7},{9,8},{10,9},{11,1... | collective-permute-start | bytes 2359304 | tf_op jit(solution)/shard_map/ring_1_grad/ppermute | solution.py:264
  5.8 1.5 collective-permute-start.4
  8.6 1.3 convert_reduce_fusion
  9.9 1.6 fusion.11
  16.2 8.9 %collective-permute-done.1 = s32[516]{0:T(1024)S(1)} collective-permute-done((s32[516]{0:T(1024)S(1)}, s32[516]{0:T(1024)S(1)}, u32[]{:S(2)}, u32[]{:S(2)}) %collective-permute-start.1) | collective-permute-done | bytes 2096 | tf_op jit(solution)/shard_map/chip_levels/ppermute | solution.py:264
  28.3 1.6 collective-permute-start.2
  30.9 8.8 %collective-permute-done.refs_1_ = bf16[128,3072]{1,0:T(8,128)(2,1)} collective-permute-done((bf16[128,3072]{1,0:T(8,128)(2,1)S(1)}, bf16[128,3072]{1,0:T(8,128)(2,1)}, u32[]{:S(2)}, u32[]{:S(2)}) %collective-permute-start) | collective-permute-done | bytes 786464 | tf_op jit(solution)/shard_map/ring_1_normed/ppermute | solution.py:264
  39.6 4.4 %collective-permute-start.5 = (bf16[128,3072]{1,0:T(8,128)(2,1)}, bf16[128,3072]{1,0:T(8,128)(2,1)S(1)}, u32[]{:S(2)}, u32[]{:S(2)}) collective-permute-start(bf16[128,3072]{1,0:T(8,128)(2,1)} %collective-permute-done.refs_1_), channel_id=1, source_target_pairs={{1,0},{2,1},{3,2},{0,3},{5,4},{6,5},{7,6},{4,7},{9,8},{10,9},{11,1... | collective-permute-start | bytes 2359304 | tf_op jit(solution)/shard_map/ring_2_normed/ppermute | solution.py:264
  44.0 1.5 collective-permute-start.6
  46.1 1.5 collective-permute-done.2.refs_2_
  47.6 30.3 %group.4 = (bf16[2,384,3840]{2,1,0:T(8,128)(2,1)}, bf16[2,384,768]{2,1,0:T(8,128)(2,1)S(1)}, f32[128,3072]{1,0:T(8,128)}, f32[128,3072]{1,0:T(8,128)}) custom-call(s32[3]{0:T(128)S(1)} %pad_add_fusion.6.spots, bf16[128,3072]{1,0:T(8,128)(2,1)S(1)} %fusion.5.refs_0_, bf16[128,3072]{1,0:T(8,128)(2,1)} %collective-permute-done.refs_1_, ...), custom_call_target="tpu_custom_call" | custom-call | flops 77309411328 | tf_op jit(solution)/shard_map/group_0/group/pallas_call | solution.py:150
  79.5 1.5 collective-permute-start.12
  81.0 1.8 collective-permute-start.13
  83.3 22.8 %group.5 = (bf16[2,256,3840]{2,1,0:T(8,128)(2,1)}, bf16[2,256,768]{2,1,0:T(8,128)(2,1)S(1)}, bf16[128,3072]{1,0:T(8,128)(2,1)S(1)}) custom-call(s32[3]{0:T(128)S(1)} %pad_add_fusion.6.spots, bf16[128,3072]{1,0:T(8,128)(2,1)S(1)} %collective-permute-done.5.refs_0_, bf16[128,3072]{1,0:T(8,128)(2,1)S(1)} %collective-permute-done.6.refs_1_, ...), custom_call_target="tpu_custom_call" | custom-call | flops 48318382080 | tf_op jit(solution)/shard_map/group_1/group/pallas_call | solution.py:150
  106.1 9.6 %collective-permute-done.13.refs_2_ = bf16[128,3072]{1,0:T(8,128)(2,1)S(1)} collective-permute-done((bf16[128,3072]{1,0:T(8,128)(2,1)S(1)}, bf16[128,3072]{1,0:T(8,128)(2,1)S(1)}, u32[]{:S(2)}, u32[]{:S(2)}) %collective-permute-start.13) | collective-permute-done | bytes 786464 | tf_op jit(solution)/shard_map/ring_3_grad/ppermute | solution.py:264
  116.2 1.5 collective-permute-start.17
  117.7 23.1 %group.6 = (bf16[2,256,3840]{2,1,0:T(8,128)(2,1)}, bf16[2,256,768]{2,1,0:T(8,128)(2,1)S(1)}, bf16[128,3072]{1,0:T(8,128)(2,1)S(1)}) custom-call(s32[3]{0:T(128)S(1)} %pad_add_fusion.6.spots, bf16[128,3072]{1,0:T(8,128)(2,1)S(1)} %collective-permute-done.11.refs_0_, bf16[128,3072]{1,0:T(8,128)(2,1)S(1)} %collective-permute-done.12.refs_1_, ...), custom_call_target="tpu_custom_call" | custom-call | flops 48318382080 | tf_op jit(solution)/shard_map/group_2/group/pallas_call | solution.py:150
  142.0 2.9 %collective-permute-start.15 = (bf16[128,3072]{1,0:T(8,128)(2,1)S(1)}, bf16[128,3072]{1,0:T(8,128)(2,1)S(1)}, u32[]{:S(2)}, u32[]{:S(2)}) collective-permute-start(bf16[128,3072]{1,0:T(8,128)(2,1)S(1)} %get-tuple-element.27), channel_id=1, source_target_pairs={{1,0},{2,1},{3,2},{0,3},{5,4},{6,5},{7,6},{4,7},{9,8},{10,9},{11,1... | collective-permute-start | bytes 2359304 | tf_op jit(solution)/shard_map/sum_down_3/ppermute | solution.py:264
  145.4 17.1 %weights.2 = (bf16[768,3072]{1,0:T(8,128)(2,1)}, bf16[3072,768]{1,0:T(8,128)(2,1)}) custom-call(bf16[2,384,3840]{2,1,0:T(8,128)(2,1)} %get-tuple-element.30.refs_0_, bf16[2,384,3840]{2,1,0:T(8,128)(2,1)} %collective-permute-done.18.refs_1_.refs_5_, bf16[2,256,3840]{2,1,0:T(8,128)(2,1)S(1)} %copy-done.1, ...), custom_call_target="tpu_custom_call" | custom-call | flops 48318382080 | tf_op jit(solution)/shard_map/weights/pallas_call | solution.py:211
  162.5 1.8 collective-permute-done.20.refs_0_
  164.3 15.9 %group.7 = (bf16[2,128,3840]{2,1,0:T(8,128)(2,1)S(1)}, bf16[2,128,768]{2,1,0:T(8,128)(2,1)S(1)}) custom-call(s32[3]{0:T(128)S(1)} %pad_add_fusion.6.spots, bf16[128,3072]{1,0:T(8,128)(2,1)S(1)} %collective-permute-done.20.refs_0_, bf16[128,3072]{1,0:T(8,128)(2,1)S(1)} %collective-permute-done.17.refs_1_, s32[128,1]{1,0:T(8,128)S(1)} %copy.25.refs_2_, ...), custom_call_target="tpu_custom_call" | custom-call | flops 19327352832 | tf_op jit(solution)/shard_map/group_3/group/pallas_call | solution.py:150
  181.1 1.6 fusion.10
  182.7 1.6 collective-permute-done.21.refs_3_.refs_7_
  184.3 12.9 %weights.3 = (bf16[768,3072]{1,0:T(8,128)(2,1)}, bf16[3072,768]{1,0:T(8,128)(2,1)}) custom-call(bf16[2,256,3840]{2,1,0:T(8,128)(2,1)} %get-tuple-element.28.refs_0_, bf16[2,256,3840]{2,1,0:T(8,128)(2,1)} %collective-permute-done.16.refs_1_.refs_5_, bf16[2,128,3840]{2,1,0:T(8,128)(2,1)S(1)} %get-tuple-element.37.refs_2_, ...), custom_call_target="tpu_custom_call" | custom-call | flops 28991029248 | tf_op jit(solution)/shard_map/weights/pallas_call | solution.py:211
  (91 shorter events, 12.0 us)
Async XLA Ops:
  0.7 44.8 %collective-permute-start.3 = (bf16[128,3072]{1,0:T(8,128)(2,1)}, bf16[128,3072]{1,0:T(8,128)(2,1)S(1)}, u32[]{:S(2)}, u32[]{:S(2)}) collective-permute-start(bf16[128,3072]{1,0:T(8,128)(2,1)} %refs_3_.2), channel_id=1, source_target_pairs={{1,0},{2,1},{3,2},{0,3},{5,4},{6,5},{7,6},{4,7},{9,8},{10,9},{11,1... | collective-permute-start | bytes 2359304 | tf_op jit(solution)/shard_map/ring_1_grad/ppermute | solution.py:264
  5.8 39.8 %collective-permute-start.4 = (bf16[128,3072]{1,0:T(8,128)(2,1)}, bf16[128,3072]{1,0:T(8,128)(2,1)}, u32[]{:S(2)}, u32[]{:S(2)}) collective-permute-start(bf16[128,3072]{1,0:T(8,128)(2,1)} %refs_3_.2), channel_id=1, source_target_pairs={{8,0},{12,4},{0,8},{4,12},{9,1},{13,5},{1,9},{5,13},{10,2},{14,6},... | collective-permute-start | bytes 2359304 | tf_op jit(solution)/shard_map/chip_0_grad/ppermute | solution.py:264
  8.0 17.2 %collective-permute-start.1 = (s32[516]{0:T(1024)S(1)}, s32[516]{0:T(1024)S(1)}, u32[]{:S(2)}, u32[]{:S(2)}) collective-permute-start(s32[516]{0:T(1024)S(1)} %pad_add_fusion), channel_id=1, source_target_pairs={{8,0},{12,4},{0,8},{4,12},{9,1},{13,5},{1,9},{5,13},{10,2},{14,6},... | collective-permute-start | bytes 6200 | tf_op jit(solution)/shard_map/chip_levels/ppermute | solution.py:264
  9.9 37.7 %copy-start = (bf16[128,3072]{1,0:T(8,128)(2,1)S(1)}, bf16[128,3072]{1,0:T(8,128)(2,1)}, u32[]{:S(2)}) copy-start(bf16[128,3072]{1,0:T(8,128)(2,1)} %refs_3_.2) | copy-start | bytes 2359300
  12.0 27.6 %collective-permute-start = (bf16[128,3072]{1,0:T(8,128)(2,1)S(1)}, bf16[128,3072]{1,0:T(8,128)(2,1)}, u32[]{:S(2)}, u32[]{:S(2)}) collective-permute-start(bf16[128,3072]{1,0:T(8,128)(2,1)S(1)} %fusion.5.refs_0_), channel_id=1, source_target_pairs={{1,0},{2,1},{3,2},{0,3},{5,4},{6,5},{7,6},{4,7},{9,8},{10,9},{11,1... | collective-permute-start | bytes 2359304 | tf_op jit(solution)/shard_map/ring_1_normed/ppermute | solution.py:264
  28.3 19.3 %collective-permute-start.2 = (bf16[128,3072]{1,0:T(8,128)(2,1)S(1)}, bf16[128,3072]{1,0:T(8,128)(2,1)}, u32[]{:S(2)}, u32[]{:S(2)}) collective-permute-start(bf16[128,3072]{1,0:T(8,128)(2,1)S(1)} %fusion.5.refs_0_), channel_id=1, source_target_pairs={{8,0},{12,4},{0,8},{4,12},{9,1},{13,5},{1,9},{5,13},{10,2},{14,6},... | collective-permute-start | bytes 2359304 | tf_op jit(solution)/shard_map/chip_0_normed/ppermute | solution.py:264
  39.6 39.2 %collective-permute-start.5 = (bf16[128,3072]{1,0:T(8,128)(2,1)}, bf16[128,3072]{1,0:T(8,128)(2,1)S(1)}, u32[]{:S(2)}, u32[]{:S(2)}) collective-permute-start(bf16[128,3072]{1,0:T(8,128)(2,1)} %collective-permute-done.refs_1_), channel_id=1, source_target_pairs={{1,0},{2,1},{3,2},{0,3},{5,4},{6,5},{7,6},{4,7},{9,8},{10,9},{11,1... | collective-permute-start | bytes 2359304 | tf_op jit(solution)/shard_map/ring_2_normed/ppermute | solution.py:264
  44.0 37.0 %collective-permute-start.6 = (bf16[128,3072]{1,0:T(8,128)(2,1)}, bf16[128,3072]{1,0:T(8,128)(2,1)S(1)}, u32[]{:S(2)}, u32[]{:S(2)}) collective-permute-start(bf16[128,3072]{1,0:T(8,128)(2,1)} %collective-permute-done.refs_1_), channel_id=1, source_target_pairs={{8,0},{12,4},{0,8},{4,12},{9,1},{13,5},{1,9},{5,13},{10,2},{14,6},... | collective-permute-start | bytes 2359304 | tf_op jit(solution)/shard_map/chip_1_normed/ppermute | solution.py:264
  45.5 34.0 %collective-permute-start.7 = (bf16[128,3072]{1,0:T(8,128)(2,1)S(1)}, bf16[128,3072]{1,0:T(8,128)(2,1)S(1)}, u32[]{:S(2)}, u32[]{:S(2)}) collective-permute-start(bf16[128,3072]{1,0:T(8,128)(2,1)S(1)} %collective-permute-done.3.refs_4_), channel_id=1, source_target_pairs={{1,0},{2,1},{3,2},{0,3},{5,4},{6,5},{7,6},{4,7},{9,8},{10,9},{11,1... | collective-permute-start | bytes 2359304 | tf_op jit(solution)/shard_map/ring_2_grad/ppermute | solution.py:264
  45.5 37.3 %collective-permute-start.8 = (bf16[128,3072]{1,0:T(8,128)(2,1)S(1)}, bf16[128,3072]{1,0:T(8,128)(2,1)S(1)}, u32[]{:S(2)}, u32[]{:S(2)}) collective-permute-start(bf16[128,3072]{1,0:T(8,128)(2,1)S(1)} %collective-permute-done.3.refs_4_), channel_id=1, source_target_pairs={{8,0},{12,4},{0,8},{4,12},{9,1},{13,5},{1,9},{5,13},{10,2},{14,6},... | collective-permute-start | bytes 2359304 | tf_op jit(solution)/shard_map/chip_1_grad/ppermute | solution.py:264
  78.9 66.6 %collective-permute-start.18 = (bf16[2,384,3840]{2,1,0:T(8,128)(2,1)}, bf16[2,384,3840]{2,1,0:T(8,128)(2,1)}, u32[]{:S(2)}, u32[]{:S(2)}) collective-permute-start(bf16[2,384,3840]{2,1,0:T(8,128)(2,1)} %get-tuple-element.30.refs_0_), channel_id=1, source_target_pairs={{0,4},{4,0},{8,12},{12,8},{1,5},{5,1},{9,13},{13,9},{2,6},{6,2},{1... | collective-permute-start | bytes 17694728 | tf_op jit(solution)/shard_map/swap_0/ppermute | solution.py:264
  78.9 36.8 %collective-permute-start.11 = (bf16[128,3072]{1,0:T(8,128)(2,1)S(1)}, bf16[128,3072]{1,0:T(8,128)(2,1)S(1)}, u32[]{:S(2)}, u32[]{:S(2)}) collective-permute-start(bf16[128,3072]{1,0:T(8,128)(2,1)S(1)} %collective-permute-done.5.refs_0_), channel_id=1, source_target_pairs={{1,0},{2,1},{3,2},{0,3},{5,4},{6,5},{7,6},{4,7},{9,8},{10,9},{11,1... | collective-permute-start | bytes 2359304 | tf_op jit(solution)/shard_map/ring_3_normed/ppermute | solution.py:264
  79.5 36.8 %collective-permute-start.12 = (bf16[128,3072]{1,0:T(8,128)(2,1)S(1)}, bf16[128,3072]{1,0:T(8,128)(2,1)S(1)}, u32[]{:S(2)}, u32[]{:S(2)}) collective-permute-start(bf16[128,3072]{1,0:T(8,128)(2,1)S(1)} %collective-permute-done.5.refs_0_), channel_id=1, source_target_pairs={{8,0},{12,4},{0,8},{4,12},{9,1},{13,5},{1,9},{5,13},{10,2},{14,6},... | collective-permute-start | bytes 2359304 | tf_op jit(solution)/shard_map/chip_2_normed/ppermute | solution.py:264
  81.0 34.7 %collective-permute-start.13 = (bf16[128,3072]{1,0:T(8,128)(2,1)S(1)}, bf16[128,3072]{1,0:T(8,128)(2,1)S(1)}, u32[]{:S(2)}, u32[]{:S(2)}) collective-permute-start(bf16[128,3072]{1,0:T(8,128)(2,1)S(1)} %collective-permute-done.7.refs_2_), channel_id=1, source_target_pairs={{1,0},{2,1},{3,2},{0,3},{5,4},{6,5},{7,6},{4,7},{9,8},{10,9},{11,1... | collective-permute-start | bytes 2359304 | tf_op jit(solution)/shard_map/ring_3_grad/ppermute | solution.py:264
  82.8 35.0 %collective-permute-start.14 = (bf16[128,3072]{1,0:T(8,128)(2,1)S(1)}, bf16[128,3072]{1,0:T(8,128)(2,1)S(1)}, u32[]{:S(2)}, u32[]{:S(2)}) collective-permute-start(bf16[128,3072]{1,0:T(8,128)(2,1)S(1)} %collective-permute-done.7.refs_2_), channel_id=1, source_target_pairs={{8,0},{12,4},{0,8},{4,12},{9,1},{13,5},{1,9},{5,13},{10,2},{14,6},... | collective-permute-start | bytes 2359304 | tf_op jit(solution)/shard_map/chip_2_grad/ppermute | solution.py:264
  115.7 29.2 %collective-permute-start.19 = (bf16[2,256,3840]{2,1,0:T(8,128)(2,1)}, bf16[2,256,3840]{2,1,0:T(8,128)(2,1)}, u32[]{:S(2)}, u32[]{:S(2)}) collective-permute-start(bf16[2,256,3840]{2,1,0:T(8,128)(2,1)} %get-tuple-element.32.refs_2_), channel_id=1, source_target_pairs={{0,4},{4,0},{8,12},{12,8},{1,5},{5,1},{9,13},{13,9},{2,6},{6,2},{1... | collective-permute-start | bytes 11796488 | tf_op jit(solution)/shard_map/swap_1/ppermute | solution.py:264
  115.7 25.1 %collective-permute-start.9 = (bf16[128,3072]{1,0:T(8,128)(2,1)S(1)}, bf16[128,3072]{1,0:T(8,128)(2,1)S(1)}, u32[]{:S(2)}, u32[]{:S(2)}) collective-permute-start(bf16[128,3072]{1,0:T(8,128)(2,1)S(1)} %get-tuple-element.26), channel_id=1, source_target_pairs={{0,1},{1,2},{2,3},{3,0},{4,5},{5,6},{6,7},{7,4},{8,9},{9,10},{10,1... | collective-permute-start | bytes 2359304 | tf_op jit(solution)/shard_map/sum_up_2/ppermute | solution.py:264
  116.2 25.7 %collective-permute-start.17 = (bf16[128,3072]{1,0:T(8,128)(2,1)S(1)}, bf16[128,3072]{1,0:T(8,128)(2,1)S(1)}, u32[]{:S(2)}, u32[]{:S(2)}) collective-permute-start(bf16[128,3072]{1,0:T(8,128)(2,1)S(1)} %collective-permute-done.13.refs_2_), channel_id=1, source_target_pairs={{8,0},{12,4},{0,8},{4,12},{9,1},{13,5},{1,9},{5,13},{10,2},{14,6},... | collective-permute-start | bytes 2359304 | tf_op jit(solution)/shard_map/chip_3_grad/ppermute | solution.py:264
  117.7 27.7 %copy-start.1 = (bf16[2,256,3840]{2,1,0:T(8,128)(2,1)S(1)}, bf16[2,256,3840]{2,1,0:T(8,128)(2,1)}, u32[]{:S(2)}) copy-start(bf16[2,256,3840]{2,1,0:T(8,128)(2,1)} %get-tuple-element.32.refs_2_) | copy-start | bytes 11796484
  140.8 41.9 %collective-permute-start.16 = (bf16[2,256,3840]{2,1,0:T(8,128)(2,1)}, bf16[2,256,3840]{2,1,0:T(8,128)(2,1)}, u32[]{:S(2)}, u32[]{:S(2)}) collective-permute-start(bf16[2,256,3840]{2,1,0:T(8,128)(2,1)} %get-tuple-element.28.refs_0_), channel_id=1, source_target_pairs={{0,4},{4,0},{8,12},{12,8},{1,5},{5,1},{9,13},{13,9},{2,6},{6,2},{1... | collective-permute-start | bytes 11796488 | tf_op jit(solution)/shard_map/swap_2/ppermute | solution.py:264
  141.0 39.4 %collective-permute-start.10 = (bf16[128,3072]{1,0:T(8,128)(2,1)S(1)}, bf16[128,3072]{1,0:T(8,128)(2,1)S(1)}, u32[]{:S(2)}, u32[]{:S(2)}) collective-permute-start(bf16[128,3072]{1,0:T(8,128)(2,1)S(1)} %add_convert_fusion), channel_id=1, source_target_pairs={{0,1},{1,2},{2,3},{3,0},{4,5},{5,6},{6,7},{7,4},{8,9},{9,10},{10,1... | collective-permute-start | bytes 2359304 | tf_op jit(solution)/shard_map/sum_up_1/ppermute | solution.py:264
  142.0 38.4 %collective-permute-start.15 = (bf16[128,3072]{1,0:T(8,128)(2,1)S(1)}, bf16[128,3072]{1,0:T(8,128)(2,1)S(1)}, u32[]{:S(2)}, u32[]{:S(2)}) collective-permute-start(bf16[128,3072]{1,0:T(8,128)(2,1)S(1)} %get-tuple-element.27), channel_id=1, source_target_pairs={{1,0},{2,1},{3,2},{0,3},{5,4},{6,5},{7,6},{4,7},{9,8},{10,9},{11,1... | collective-permute-start | bytes 2359304 | tf_op jit(solution)/shard_map/sum_down_3/ppermute | solution.py:264
  144.9 19.5 %collective-permute-start.20 = (bf16[128,3072]{1,0:T(8,128)(2,1)S(1)}, bf16[128,3072]{1,0:T(8,128)(2,1)S(1)}, u32[]{:S(2)}, u32[]{:S(2)}) collective-permute-start(bf16[128,3072]{1,0:T(8,128)(2,1)S(1)} %collective-permute-done.11.refs_0_), channel_id=1, source_target_pairs={{8,0},{12,4},{0,8},{4,12},{9,1},{13,5},{1,9},{5,13},{10,2},{14,6},... | collective-permute-start | bytes 2359304 | tf_op jit(solution)/shard_map/chip_3_normed/ppermute | solution.py:264
  180.3 4.0 %collective-permute-start.21 = (bf16[2,128,3840]{2,1,0:T(8,128)(2,1)S(1)}, bf16[2,128,3840]{2,1,0:T(8,128)(2,1)S(1)}, u32[]{:S(2)}, u32[]{:S(2)}) collective-permute-start(bf16[2,128,3840]{2,1,0:T(8,128)(2,1)S(1)} %get-tuple-element.37.refs_2_), channel_id=1, source_target_pairs={{0,4},{4,0},{8,12},{12,8},{1,5},{5,1},{9,13},{13,9},{2,6},{6,2},{1... | collective-permute-start | bytes 5898248 | tf_op jit(solution)/shard_map/swap_3/ppermute | solution.py:264
  (14 other events, 161.0 us)

commit v5 on v4

--- a/solution.py
+++ b/solution.py
@@ -12,7 +12,8 @@
 GELU_CUBE = 0.044715
 NORM_EPS = 1e-06
 VMEM_LIMIT = 48 * 1024 * 1024
-WORK = 4.0
+WORK = 3.0
+WEIGHTS = {2: 3.0}
 
 
 def gelu_parts(pre_act):
@@ -57,12 +58,11 @@
     return wanted
 
 
-def group_kernel(spots, *refs, pieces, owned, share, tiles):
+def group_kernel(spots, *refs, pieces, begun, owned, share, tiles):
     normed_refs = refs[:pieces]
     grad_refs = refs[pieces : 2 * pieces]
     limit_ref, in_ref, out_ref = refs[2 * pieces : 2 * pieces + 3]
-    acts_ref, own_ref = refs[2 * pieces + 3 : 2 * pieces + 5]
-    rest = refs[2 * pieces + 5 :]
+    acts_ref, own_ref, *rest = refs[2 * pieces + 3 + begun :]
     tile = pl.program_id(0)
 
     def columns(target, first):
@@ -72,9 +72,15 @@
                 size = ref.shape[0]
                 target[kind, at * size : (at + 1) * size, :] = ref[:, span]
 
+    rows_ref, rest = rest[-1], rest[:-1]
+
     @pl.when(tile == 0)
     def _():
         columns(own_ref, spots[1])
+        for kind, sources in enumerate((normed_refs, grad_refs)):
+            for at, ref in enumerate(sources):
+                size = ref.shape[0]
+                rows_ref[kind, at * size : (at + 1) * size, :] = ref[...]
 
     @pl.when(tile == tiles)
     def _():
@@ -82,23 +88,21 @@
 
     @pl.when(tile < tiles)
     def _():
-        group_tile(spots[0], normed_refs, grad_refs, limit_ref, in_ref, out_ref, acts_ref, rest, owned, tiles)
-
-
-def group_tile(first, normed_refs, grad_refs, limit_ref, in_ref, out_ref, acts_ref, rest, owned, tiles):
+        group_tile(spots[0], rows_ref, limit_ref, in_ref, out_ref, acts_ref, rest, owned, tiles)
+
+
+def group_tile(first, rows_ref, limit_ref, in_ref, out_ref, acts_ref, rest, owned, tiles):
     tile = pl.program_id(0)
     units = in_ref.shape[1]
     width = 256 if units % 256 == 0 else units
-    normed = jnp.concatenate([ref[...] for ref in normed_refs], axis=0)
-    grads = jnp.concatenate([ref[...] for ref in grad_refs], axis=0)
 
     mask = first + tile * units < limit_ref[...]
     products = []
     for start in range(0, units, width):
         span = slice(start, start + width)
-        pre_act = jnp.dot(normed, in_ref[:, span], preferred_element_type=jnp.float32)
+        pre_act = jnp.dot(rows_ref[0], in_ref[:, span], preferred_element_type=jnp.float32)
         grad_hidden = lax.dot_general(
-            grads, out_ref[span, :], (((1,), (1,)), ((), ())), preferred_element_type=jnp.float32
+            rows_ref[1], out_ref[span, :], (((1,), (1,)), ((), ())), preferred_element_type=jnp.float32
         )
         products.append((span, pre_act, grad_hidden))
     for span, pre_act, grad_hidden in products:
@@ -129,27 +133,36 @@
                 ref[...] = total_ref[at * size : (at + 1) * size, :].astype(ref.dtype)
 
 
-def group_call(spots, normed, grads, limit, weight_in, weight_out, tile, share, back_types):
+def group_call(
+    spots, normed, grads, limit, weight_in, weight_out, tile, share, back_types, begun, rows_after, weight
+):
     features, units = weight_in.shape
     piece_rows = normed[0].shape[0]
     rows = piece_rows * len(normed)
     owned = len(back_types)
     tiles = units // tile
+    total = begun[0].shape[1] if begun else rows + rows_after
     whole = lambda shape: pl.BlockSpec(shape, lambda i, spots: (0,) * len(shape))
     out_shape = [
-        jax.ShapeDtypeStruct((2, rows, units + share), jnp.bfloat16),
-        jax.ShapeDtypeStruct((2, rows, share), jnp.bfloat16),
+        jax.ShapeDtypeStruct((2, total, units + share), jnp.bfloat16),
+        jax.ShapeDtypeStruct((2, total, share), jnp.bfloat16),
     ]
     out_specs = [
-        pl.BlockSpec((2, rows, tile), lambda i, spots: (0, 0, i)),
-        whole((2, rows, share)),
+        pl.BlockSpec((2, rows, tile), lambda i, spots: (0, rows_after // rows, i)),
+        pl.BlockSpec((2, rows, share), lambda i, spots: (0, rows_after // rows, 0)),
     ]
+    operands = (spots, *normed, *grads, limit, weight_in, weight_out)
     for kind in back_types:
         out_shape.append(jax.ShapeDtypeStruct((piece_rows, features), kind))
         out_specs.append(whole((piece_rows, features)))
     return pl.pallas_call(
         functools.partial(
-            group_kernel, pieces=len(normed), owned=owned, share=share, tiles=tiles
+            group_kernel,
+            pieces=len(normed),
+            begun=len(begun),
+            owned=owned,
+            share=share,
+            tiles=tiles,
         ),
         grid_spec=pltpu.PrefetchScalarGridSpec(
             num_scalar_prefetch=1,
@@ -159,15 +172,18 @@
                 whole((rows, 1)),
                 pl.BlockSpec((features, tile), lambda i, spots: (0, jnp.minimum(i, tiles - 1))),
                 pl.BlockSpec((tile, features), lambda i, spots: (jnp.minimum(i, tiles - 1), 0)),
-            ],
+            ]
+            + [pl.BlockSpec(memory_space=pl.ANY) for _ in begun],
             out_specs=out_specs,
-            scratch_shapes=[pltpu.VMEM((owned * piece_rows, features), jnp.float32)] if owned else [],
+            scratch_shapes=[pltpu.VMEM((owned * piece_rows, features), jnp.float32)] * bool(owned)
+            + [pltpu.VMEM((2, rows, features), jnp.bfloat16)],
         ),
         out_shape=out_shape,
         compiler_params=pltpu.CompilerParams(vmem_limit_bytes=VMEM_LIMIT),
-        cost_estimate=work_of((4 * rows + 2 * owned * piece_rows) * units * features),
+        cost_estimate=work_of(weight * (4 * rows + 2 * owned * piece_rows) * units * features),
+        input_output_aliases={len(operands) + at: at for at in range(len(begun))},
         name="group",
-    )(spots, *normed, *grads, limit, weight_in, weight_out)
+    )(*operands, *begun)
 
 
 def weights_kernel(*refs, groups, scale, started):
@@ -218,7 +234,7 @@
             jax.ShapeDtypeStruct((units, share), jnp.bfloat16),
         ],
         compiler_params=pltpu.CompilerParams(vmem_limit_bytes=VMEM_LIMIT),
-        cost_estimate=work_of(4 * sum(one.shape[1] for one in acts) * units * share),
+        cost_estimate=work_of(0),
         name="weights",
     )(*acts, *cols, *begun)
 
@@ -263,28 +279,27 @@
         with jax.named_scope(name):
             return lax.ppermute(one, axis, pairs)
 
-    kinds = ("grad", "normed")
+    kinds = ("normed", "grad")
 
     def move(piece, axis, pairs, name, *gates):
         return tuple(
             send(after(one, *gates), axis, pairs, f"{name}_{kind}") for one, kind in zip(piece, kinds)
         )
 
-    near = {0: (grad_out, normed)}
+    near = {0: (normed, grad_out)}
     for step in range(1, ring):
         near[step] = move(near[step - 1], "tensor", from_next, f"ring_{step}")
     sets = [[near[step] for step in range(ring)]]
     limit_sets = [limits_of(level_order, level_counts[0])]
     levels = jnp.concatenate([level_order, level_counts[0]])
+
     for chip in range(1, chips):
         levels = send(levels, "dp", from_chip, "chip_levels")
         limit_sets.append(limits_of(levels[:-4], levels[-4:]))
         far = []
-        for step, (grads, rows_normed) in enumerate(sets[-1]):
-            grads = send(grads, "dp", from_chip, f"chip_{step}_grad")
-            if step == 0:
-                rows_normed = after(rows_normed, levels)
-            far.append((grads, send(rows_normed, "dp", from_chip, f"chip_{step}_normed")))
+        for step, piece in enumerate(sets[-1]):
+            held = [levels] if step == 0 else []
+            far.append(move(piece, "dp", from_chip, f"chip_{step}", *held))
         sets.append(far)
 
     groups, own_grads = [], []
@@ -292,15 +307,18 @@
         [(chip, slot - chip) for chip in range(chips) if 0 <= slot - chip < ring]
         for slot in range(ring + chips - 1)
     ]
-    if len(arrivals) > 1:
-        arrivals[:2] = [sorted(arrivals[0] + arrivals[1])]
+    last = len(arrivals) - 1
     totals = []
     for at, entries in enumerate(arrivals):
-        gates = []
-        if at > 0 and at == len(arrivals) - 1:
-            early = [sets[chip][step][0] for chip, step in entries]
+        gates, begun, rows_after = [], [], 0
+        if at == 0 and last > 0:
+            rows_after = rows * len(arrivals[1])
+        elif at == 1:
+            begun = groups.pop()[:2]
+        if last > 2 and at >= last - 1:
+            early = [sets[chip][step][1] for chip, step in entries]
             totals = weights_call(
-                [(after(own, *early), *others) for own, *others in groups[:-1]], [], 1.0
+                [(after(own, *early), *others) for own, *others in groups[:-1]], totals, 1.0
             )
             gates = [totals[0]]
             groups = groups[-1:]
@@ -312,17 +330,23 @@
         with jax.named_scope(f"group_{at}"):
             act, own_cols, *back = group_call(
                 after(spots, *gates),
+                [sets[chip][step][0] for chip, step in entries],
                 [sets[chip][step][1] for chip, step in entries],
-                [sets[chip][step][0] for chip, step in entries],
                 limit,
                 weight_in,
                 weight_out,
                 tile,
                 share,
                 back_types,
+                begun,
+                rows_after,
+                WEIGHTS.get(at, 1.0),
             )
         own_grads.extend(back)
-        groups.append((act, own_cols, send(act, "dp", swap_cores, f"swap_{at}")))
+        if at == 0 and last > 0:
+            groups.append((act, own_cols))
+        else:
+            groups.append((act, own_cols, send(act, "dp", swap_cores, f"swap_{at}")))
 
     def chain(steps, pairs, name):
         travelling = None

time: 198 us -> 219 us (1.11)
  Pallas kernels: 122 us -> 144 us
  waiting for transfers between devices: 32.2 us -> 20.4 us
  local copies, waits for them, and re-layouts: 3.18 us -> 13.8 us
  starting transfers between devices: 26.6 us -> 23.2 us
  other arithmetic: 8.37 us -> 11.6 us
    pallas_call x4 -> x5, Pallas kernels: 92.1 us -> 108 us  [group_call(): pl.pallas_call(functools.partial(group_kernel, pieces=len(normed), begun=...]
    ppermute x22, waiting for transfers between devices: 32.2 us -> 20.4 us  [send(): return lax.ppermute(one, axis, pairs)]
    unnamed x32 -> x48, local copies, waits for them, and re-layouts: 1.29 us -> 8.05 us
    pallas_call x2 -> x3, Pallas kernels: 30 us -> 36.1 us  [weights_call(): pl.pallas_call(functools.partial(weights_kernel, groups=len(acts), scale=...]
    ppermute x22, starting transfers between devices: 26.6 us -> 23.2 us  [send(): return lax.ppermute(one, axis, pairs)]
  transfers between devices with their start and end apart: 22 -> 22, of which waited for: 6 -> 5; matrix products, arithmetic and copies ran while one was open for 5% -> 8% of each run, Pallas kernels for 55% -> 60%
where the time goes in v5:
time: 219 us; the launch traced here: 218 us
  Pallas kernels  144 us (66%)
  starting transfers between devices  23.2 us (11%)
  waiting for transfers between devices  20.4 us (9%)
  local copies, waits for them, and re-layouts  13.8 us (6%)
  other arithmetic  11.6 us (5%)
  between operations  4.67 us (2%)
    pallas_call x5, Pallas kernels, group_call(): pl.pallas_call(functools.partial(group_kernel, pieces=len(normed), begun=...  108 us
    pallas_call x3, Pallas kernels, weights_call(): pl.pallas_call(functools.partial(weights_kernel, groups=len(acts), scale=...  36.1 us
    ppermute x22, starting transfers between devices, send(): return lax.ppermute(one, axis, pairs)  23.2 us
    ppermute x22, waiting for transfers between devices, send(): return lax.ppermute(one, axis, pairs)  20.4 us
    unnamed x48, local copies, waits for them, and re-layouts  8.05 us
  transfers between devices with their start and end apart: 22, of which 5 were waited for; matrix products, arithmetic and copies ran while one was open for 8% of the time, Pallas kernels for 60%

profile of v5, /device:TPU:0, one launch (start us, length us, event | category | flops | bytes accessed | tf_op | source)
XLA Modules:
  0.0 217.8 jit_solution(15845024399883675542)
XLA Ops:
  1.5 3.0 %collective-permute-start.1 = (s32[516]{0:T(1024)S(1)}, s32[516]{0:T(1024)S(1)}, u32[]{:S(2)}, u32[]{:S(2)}) collective-permute-start(s32[516]{0:T(1024)S(1)} %pad_add_fusion.1), channel_id=1, source_target_pairs={{8,0},{12,4},{0,8},{4,12},{9,1},{13,5},{1,9},{5,13},{10,2},{14,6},... | collective-permute-start | bytes 6200 | tf_op jit(solution)/shard_map/chip_levels/ppermute | solution.py:280
  5.8 1.5 fusion.11
  8.5 3.6 %collective-permute-start = (bf16[128,3072]{1,0:T(8,128)(2,1)}, bf16[128,3072]{1,0:T(8,128)(2,1)}, u32[]{:S(2)}, u32[]{:S(2)}) collective-permute-start(bf16[128,3072]{1,0:T(8,128)(2,1)} %fusion.5.refs_0_), channel_id=1, source_target_pairs={{1,0},{2,1},{3,2},{0,3},{5,4},{6,5},{7,6},{4,7},{9,8},{10,9},{11,1... | collective-permute-start | bytes 2359304 | tf_op jit(solution)/shard_map/ring_1_normed/ppermute | solution.py:280
  21.5 1.5 collective-permute-start.4
  23.8 21.7 %group.5 = (bf16[2,384,3840]{2,1,0:T(8,128)(2,1)}, bf16[2,384,768]{2,1,0:T(8,128)(2,1)S(1)}, f32[128,3072]{1,0:T(8,128)S(1)}) custom-call(s32[3]{0:T(128)S(1)} %pad_add_fusion.6.spots, bf16[128,3072]{1,0:T(8,128)(2,1)} %fusion.5.refs_0_, bf16[128,3072]{1,0:T(8,128)(2,1)S(1)} %copy-done.2, s32[128,1]{1,0:T(8,128)S(1)} %copy-done.7, ...), custom_call_target="tpu_custom_call" | custom-call | flops 21743271936 | tf_op jit(solution)/shard_map/group_0/group/pallas_call | solution.py:158
  51.0 1.9 collective-permute-start.8
  52.9 5.7 %collective-permute-done.4.refs_3_ = bf16[128,3072]{1,0:T(8,128)(2,1)} collective-permute-done((bf16[128,3072]{1,0:T(8,128)(2,1)S(1)}, bf16[128,3072]{1,0:T(8,128)(2,1)}, u32[]{:S(2)}, u32[]{:S(2)}) %collective-permute-start.4) | collective-permute-done | bytes 786464 | tf_op jit(solution)/shard_map/chip_0_grad/ppermute | solution.py:280
  59.5 23.6 %group.6 = (bf16[2,384,3840]{2,1,0:T(8,128)(2,1)}, bf16[2,384,768]{2,1,0:T(8,128)(2,1)S(1)}, f32[128,3072]{1,0:T(8,128)S(1)}) custom-call(s32[3]{0:T(128)S(1)} %pad_add_fusion.6.spots, bf16[128,3072]{1,0:T(8,128)(2,1)} %collective-permute-done.refs_0_, ...), custom_call_target="tpu_custom_call", output_to_operand_aliasing={{0}: (8, {}), {1}: (9, {})} | custom-call | flops 36238786560 | tf_op jit(solution)/shard_map/group_1/group/pallas_call | solution.py:158
  83.1 1.8 collective-permute-done.7.refs_2_
  84.9 2.2 %collective-permute-start.11 = (bf16[128,3072]{1,0:T(8,128)(2,1)S(1)}, bf16[128,3072]{1,0:T(8,128)(2,1)}, u32[]{:S(2)}, u32[]{:S(2)}) collective-permute-start(bf16[128,3072]{1,0:T(8,128)(2,1)S(1)} %collective-permute-done.7.refs_2_), channel_id=1, source_target_pairs={{1,0},{2,1},{3,2},{0,3},{5,4},{6,5},{7,6},{4,7},{9,8},{10,9},{11,1... | collective-permute-start | bytes 2359304 | tf_op jit(solution)/shard_map/ring_3_grad/ppermute | solution.py:280
  87.7 4.5 %collective-permute-done.8.refs_3_ = bf16[128,3072]{1,0:T(8,128)(2,1)S(1)} collective-permute-done((bf16[128,3072]{1,0:T(8,128)(2,1)}, bf16[128,3072]{1,0:T(8,128)(2,1)S(1)}, u32[]{:S(2)}, u32[]{:S(2)}) %collective-permute-start.8) | collective-permute-done | bytes 786464 | tf_op jit(solution)/shard_map/chip_1_grad/ppermute | solution.py:280
  92.7 23.1 %group.7 = (bf16[2,256,3840]{2,1,0:T(8,128)(2,1)}, bf16[2,256,768]{2,1,0:T(8,128)(2,1)S(1)}, bf16[128,3072]{1,0:T(8,128)(2,1)}) custom-call(s32[3]{0:T(128)S(1)} %pad_add_fusion.6.spots, bf16[128,3072]{1,0:T(8,128)(2,1)S(1)} %collective-permute-done.5.refs_0_, bf16[128,3072]{1,0:T(8,128)(2,1)S(1)} %collective-permute-done.6.refs_1_, ...), custom_call_target="tpu_custom_call" | custom-call | flops 108716359680 | tf_op jit(solution)/shard_map/group_2/group/pallas_call | solution.py:158
  116.8 1.6 collective-permute-start.9
  118.4 1.6 collective-permute-done.14.refs_0_
  122.0 12.1 %weights.3 = (bf16[768,3072]{1,0:T(8,128)(2,1)S(1)}, bf16[3072,768]{1,0:T(8,128)(2,1)}) custom-call(bf16[2,384,3840]{2,1,0:T(8,128)(2,1)} %get-tuple-element.37.refs_0_, bf16[2,384,3840]{2,1,0:T(8,128)(2,1)} %collective-permute-done.13.refs_1_.refs_3_, bf16[2,384,768]{2,1,0:T(8,128)(2,1)S(1)} %get-tuple-element.38.refs_2_, ...), custom_call_target="tpu_custom_call" | custom-call | tf_op jit(solution)/shard_map/weights/pallas_call | solution.py:227
  134.0 2.2 %copy-done = bf16[768,3072]{1,0:T(8,128)(2,1)} copy-done((bf16[768,3072]{1,0:T(8,128)(2,1)}, bf16[768,3072]{1,0:T(8,128)(2,1)S(1)}, u32[]{:S(2)}) %copy-start) | copy-done | bytes 4718616
  139.4 23.2 %group.8 = (bf16[2,256,3840]{2,1,0:T(8,128)(2,1)}, bf16[2,256,768]{2,1,0:T(8,128)(2,1)S(1)}, bf16[128,3072]{1,0:T(8,128)(2,1)S(1)}) custom-call(s32[3]{0:T(128)S(1)} %pad_add_fusion.6.spots, bf16[128,3072]{1,0:T(8,128)(2,1)S(1)} %collective-permute-done.14.refs_0_, bf16[128,3072]{1,0:T(8,128)(2,1)S(1)} %copy-done.11, ...), custom_call_target="tpu_custom_call" | custom-call | flops 36238786560 | tf_op jit(solution)/shard_map/group_3/group/pallas_call | solution.py:158
  163.9 1.6 collective-permute-start.10
  165.5 11.2 %weights.4 = (bf16[768,3072]{1,0:T(8,128)(2,1)}, bf16[3072,768]{1,0:T(8,128)(2,1)}) custom-call(bf16[2,256,3840]{2,1,0:T(8,128)(2,1)S(1)} %copy-done.1, bf16[2,256,3840]{2,1,0:T(8,128)(2,1)} %collective-permute-done.19.refs_1_.refs_3_, bf16[2,256,768]{2,1,0:T(8,128)(2,1)S(1)} %get-tuple-element.45.refs_2_, ...), custom_call_target="tpu_custom_call" | custom-call | tf_op jit(solution)/shard_map/weights/pallas_call | solution.py:227
  176.7 2.5 %collective-permute-start.16 = (bf16[128,3072]{1,0:T(8,128)(2,1)S(1)}, bf16[128,3072]{1,0:T(8,128)(2,1)S(1)}, u32[]{:S(2)}, u32[]{:S(2)}) collective-permute-start(bf16[128,3072]{1,0:T(8,128)(2,1)S(1)} %get-tuple-element.41), channel_id=1, source_target_pairs={{1,0},{2,1},{3,2},{0,3},{5,4},{6,5},{7,6},{4,7},{9,8},{10,9},{11,1... | collective-permute-start | bytes 2359304 | tf_op jit(solution)/shard_map/sum_down_3/ppermute | solution.py:280
  179.3 16.4 %group.9 = (bf16[2,128,3840]{2,1,0:T(8,128)(2,1)S(1)}, bf16[2,128,768]{2,1,0:T(8,128)(2,1)S(1)}) custom-call(s32[3]{0:T(128)S(1)} %pad_add_fusion.6.spots, bf16[128,3072]{1,0:T(8,128)(2,1)} %collective-permute-done.20.refs_0_, bf16[128,3072]{1,0:T(8,128)(2,1)} %collective-permute-done.18.refs_1_, s32[128,1]{1,0:T(8,128)S(1)} %copy-done.6, ...), custom_call_target="tpu_custom_call" | custom-call | flops 14495514624 | tf_op jit(solution)/shard_map/group_4/group/pallas_call | solution.py:158
  195.7 6.8 %collective-permute-done.16 = bf16[128,3072]{1,0:T(8,128)(2,1)S(1)} collective-permute-done((bf16[128,3072]{1,0:T(8,128)(2,1)S(1)}, bf16[128,3072]{1,0:T(8,128)(2,1)S(1)}, u32[]{:S(2)}, u32[]{:S(2)}) %collective-permute-start.16) | collective-permute-done | bytes 786464 | tf_op jit(solution)/shard_map/sum_down_3/ppermute | solution.py:280
  203.3 1.6 fusion.10
  204.9 12.9 %weights.5 = (bf16[768,3072]{1,0:T(8,128)(2,1)}, bf16[3072,768]{1,0:T(8,128)(2,1)}) custom-call(bf16[2,256,3840]{2,1,0:T(8,128)(2,1)} %get-tuple-element.42.refs_0_, bf16[2,256,3840]{2,1,0:T(8,128)(2,1)} %collective-permute-done.17.refs_1_.refs_5_, bf16[2,128,3840]{2,1,0:T(8,128)(2,1)S(1)} %get-tuple-element.49.refs_2_, ...), custom_call_target="tpu_custom_call" | custom-call | tf_op jit(solution)/shard_map/weights/pallas_call | solution.py:227
  (110 shorter events, 25.5 us)
Async XLA Ops:
  1.5 14.7 %collective-permute-start.1 = (s32[516]{0:T(1024)S(1)}, s32[516]{0:T(1024)S(1)}, u32[]{:S(2)}, u32[]{:S(2)}) collective-permute-start(s32[516]{0:T(1024)S(1)} %pad_add_fusion.1), channel_id=1, source_target_pairs={{8,0},{12,4},{0,8},{4,12},{9,1},{13,5},{1,9},{5,13},{10,2},{14,6},... | collective-permute-start | bytes 6200 | tf_op jit(solution)/shard_map/chip_levels/ppermute | solution.py:280
  8.5 41.5 %collective-permute-start = (bf16[128,3072]{1,0:T(8,128)(2,1)}, bf16[128,3072]{1,0:T(8,128)(2,1)}, u32[]{:S(2)}, u32[]{:S(2)}) collective-permute-start(bf16[128,3072]{1,0:T(8,128)(2,1)} %fusion.5.refs_0_), channel_id=1, source_target_pairs={{1,0},{2,1},{3,2},{0,3},{5,4},{6,5},{7,6},{4,7},{9,8},{10,9},{11,1... | collective-permute-start | bytes 2359304 | tf_op jit(solution)/shard_map/ring_1_normed/ppermute | solution.py:280
  12.1 38.9 %collective-permute-start.3 = (bf16[128,3072]{1,0:T(8,128)(2,1)S(1)}, bf16[128,3072]{1,0:T(8,128)(2,1)}, u32[]{:S(2)}, u32[]{:S(2)}) collective-permute-start(bf16[128,3072]{1,0:T(8,128)(2,1)S(1)} %copy-done.2), channel_id=1, source_target_pairs={{1,0},{2,1},{3,2},{0,3},{5,4},{6,5},{7,6},{4,7},{9,8},{10,9},{11,1... | collective-permute-start | bytes 2359304 | tf_op jit(solution)/shard_map/ring_1_grad/ppermute | solution.py:280
  20.9 30.1 %collective-permute-start.2 = (bf16[128,3072]{1,0:T(8,128)(2,1)}, bf16[128,3072]{1,0:T(8,128)(2,1)}, u32[]{:S(2)}, u32[]{:S(2)}) collective-permute-start(bf16[128,3072]{1,0:T(8,128)(2,1)} %fusion.5.refs_0_), channel_id=1, source_target_pairs={{8,0},{12,4},{0,8},{4,12},{9,1},{13,5},{1,9},{5,13},{10,2},{14,6},... | collective-permute-start | bytes 2359304 | tf_op jit(solution)/shard_map/chip_0_normed/ppermute | solution.py:280
  21.5 37.1 %collective-permute-start.4 = (bf16[128,3072]{1,0:T(8,128)(2,1)S(1)}, bf16[128,3072]{1,0:T(8,128)(2,1)}, u32[]{:S(2)}, u32[]{:S(2)}) collective-permute-start(bf16[128,3072]{1,0:T(8,128)(2,1)S(1)} %copy-done.2), channel_id=1, source_target_pairs={{8,0},{12,4},{0,8},{4,12},{9,1},{13,5},{1,9},{5,13},{10,2},{14,6},... | collective-permute-start | bytes 2359304 | tf_op jit(solution)/shard_map/chip_0_grad/ppermute | solution.py:280
  50.0 37.2 %collective-permute-start.5 = (bf16[128,3072]{1,0:T(8,128)(2,1)}, bf16[128,3072]{1,0:T(8,128)(2,1)S(1)}, u32[]{:S(2)}, u32[]{:S(2)}) collective-permute-start(bf16[128,3072]{1,0:T(8,128)(2,1)} %collective-permute-done.refs_0_), channel_id=1, source_target_pairs={{1,0},{2,1},{3,2},{0,3},{5,4},{6,5},{7,6},{4,7},{9,8},{10,9},{11,1... | collective-permute-start | bytes 2359304 | tf_op jit(solution)/shard_map/ring_2_normed/ppermute | solution.py:280
  50.4 37.3 %collective-permute-start.6 = (bf16[128,3072]{1,0:T(8,128)(2,1)}, bf16[128,3072]{1,0:T(8,128)(2,1)S(1)}, u32[]{:S(2)}, u32[]{:S(2)}) collective-permute-start(bf16[128,3072]{1,0:T(8,128)(2,1)} %collective-permute-done.refs_0_), channel_id=1, source_target_pairs={{8,0},{12,4},{0,8},{4,12},{9,1},{13,5},{1,9},{5,13},{10,2},{14,6},... | collective-permute-start | bytes 2359304 | tf_op jit(solution)/shard_map/chip_1_normed/ppermute | solution.py:280
  51.0 34.0 %collective-permute-start.7 = (bf16[128,3072]{1,0:T(8,128)(2,1)}, bf16[128,3072]{1,0:T(8,128)(2,1)S(1)}, u32[]{:S(2)}, u32[]{:S(2)}) collective-permute-start(bf16[128,3072]{1,0:T(8,128)(2,1)} %collective-permute-done.3.refs_2_), channel_id=1, source_target_pairs={{1,0},{2,1},{3,2},{0,3},{5,4},{6,5},{7,6},{4,7},{9,8},{10,9},{11,1... | collective-permute-start | bytes 2359304 | tf_op jit(solution)/shard_map/ring_2_grad/ppermute | solution.py:280
  51.0 41.1 %collective-permute-start.8 = (bf16[128,3072]{1,0:T(8,128)(2,1)}, bf16[128,3072]{1,0:T(8,128)(2,1)S(1)}, u32[]{:S(2)}, u32[]{:S(2)}) collective-permute-start(bf16[128,3072]{1,0:T(8,128)(2,1)} %collective-permute-done.3.refs_2_), channel_id=1, source_target_pairs={{8,0},{12,4},{0,8},{4,12},{9,1},{13,5},{1,9},{5,13},{10,2},{14,6},... | collective-permute-start | bytes 2359304 | tf_op jit(solution)/shard_map/chip_1_grad/ppermute | solution.py:280
  59.5 33.2 %copy-start.4 = (s32[256,1]{1,0:T(8,128)S(1)}, s32[256,1]{1,0:T(8,128)}, u32[]{:S(2)}) copy-start(s32[256,1]{1,0:T(8,128)} %copy.27.refs_4_) | copy-start | bytes 3076
  83.1 37.4 %collective-permute-start.13 = (bf16[2,384,3840]{2,1,0:T(8,128)(2,1)}, bf16[2,384,3840]{2,1,0:T(8,128)(2,1)}, u32[]{:S(2)}, u32[]{:S(2)}) collective-permute-start(bf16[2,384,3840]{2,1,0:T(8,128)(2,1)} %get-tuple-element.37.refs_0_), channel_id=1, source_target_pairs={{0,4},{4,0},{8,12},{12,8},{1,5},{5,1},{9,13},{13,9},{2,6},{6,2},{1... | collective-permute-start | bytes 17694728 | tf_op jit(solution)/shard_map/swap_1/ppermute | solution.py:280
  84.9 30.9 %collective-permute-start.11 = (bf16[128,3072]{1,0:T(8,128)(2,1)S(1)}, bf16[128,3072]{1,0:T(8,128)(2,1)}, u32[]{:S(2)}, u32[]{:S(2)}) collective-permute-start(bf16[128,3072]{1,0:T(8,128)(2,1)S(1)} %collective-permute-done.7.refs_2_), channel_id=1, source_target_pairs={{1,0},{2,1},{3,2},{0,3},{5,4},{6,5},{7,6},{4,7},{9,8},{10,9},{11,1... | collective-permute-start | bytes 2359304 | tf_op jit(solution)/shard_map/ring_3_grad/ppermute | solution.py:280
  87.2 28.7 %collective-permute-start.12 = (bf16[128,3072]{1,0:T(8,128)(2,1)S(1)}, bf16[128,3072]{1,0:T(8,128)(2,1)S(1)}, u32[]{:S(2)}, u32[]{:S(2)}) collective-permute-start(bf16[128,3072]{1,0:T(8,128)(2,1)S(1)} %collective-permute-done.7.refs_2_), channel_id=1, source_target_pairs={{8,0},{12,4},{0,8},{4,12},{9,1},{13,5},{1,9},{5,13},{10,2},{14,6},... | collective-permute-start | bytes 2359304 | tf_op jit(solution)/shard_map/chip_2_grad/ppermute | solution.py:280
  87.7 32.2 %collective-permute-start.14 = (bf16[128,3072]{1,0:T(8,128)(2,1)S(1)}, bf16[128,3072]{1,0:T(8,128)(2,1)S(1)}, u32[]{:S(2)}, u32[]{:S(2)}) collective-permute-start(bf16[128,3072]{1,0:T(8,128)(2,1)S(1)} %collective-permute-done.5.refs_0_), channel_id=1, source_target_pairs={{1,0},{2,1},{3,2},{0,3},{5,4},{6,5},{7,6},{4,7},{9,8},{10,9},{11,1... | collective-permute-start | bytes 2359304 | tf_op jit(solution)/shard_map/ring_3_normed/ppermute | solution.py:280
  92.2 44.0 %collective-permute-start.15 = (bf16[128,3072]{1,0:T(8,128)(2,1)S(1)}, bf16[128,3072]{1,0:T(8,128)(2,1)S(1)}, u32[]{:S(2)}, u32[]{:S(2)}) collective-permute-start(bf16[128,3072]{1,0:T(8,128)(2,1)S(1)} %collective-permute-done.5.refs_0_), channel_id=1, source_target_pairs={{8,0},{12,4},{0,8},{4,12},{9,1},{13,5},{1,9},{5,13},{10,2},{14,6},... | collective-permute-start | bytes 2359304 | tf_op jit(solution)/shard_map/chip_2_normed/ppermute | solution.py:280
  115.8 49.7 %collective-permute-start.19 = (bf16[2,256,3840]{2,1,0:T(8,128)(2,1)}, bf16[2,256,3840]{2,1,0:T(8,128)(2,1)}, u32[]{:S(2)}, u32[]{:S(2)}) collective-permute-start(bf16[2,256,3840]{2,1,0:T(8,128)(2,1)} %get-tuple-element.44.refs_0_), channel_id=1, source_target_pairs={{0,4},{4,0},{8,12},{12,8},{1,5},{5,1},{9,13},{13,9},{2,6},{6,2},{1... | collective-permute-start | bytes 11796488 | tf_op jit(solution)/shard_map/swap_2/ppermute | solution.py:280
  116.8 45.8 %collective-permute-start.9 = (bf16[128,3072]{1,0:T(8,128)(2,1)}, bf16[128,3072]{1,0:T(8,128)(2,1)}, u32[]{:S(2)}, u32[]{:S(2)}) collective-permute-start(bf16[128,3072]{1,0:T(8,128)(2,1)} %get-tuple-element.35), channel_id=1, source_target_pairs={{0,1},{1,2},{2,3},{3,0},{4,5},{5,6},{6,7},{7,4},{8,9},{9,10},{10,1... | collective-permute-start | bytes 2359304 | tf_op jit(solution)/shard_map/sum_up_2/ppermute | solution.py:280
  119.9 45.6 %collective-permute-start.18 = (bf16[128,3072]{1,0:T(8,128)(2,1)}, bf16[128,3072]{1,0:T(8,128)(2,1)}, u32[]{:S(2)}, u32[]{:S(2)}) collective-permute-start(bf16[128,3072]{1,0:T(8,128)(2,1)} %collective-permute-done.11.refs_2_), channel_id=1, source_target_pairs={{8,0},{12,4},{0,8},{4,12},{9,1},{13,5},{1,9},{5,13},{10,2},{14,6},... | collective-permute-start | bytes 2359304 | tf_op jit(solution)/shard_map/chip_3_grad/ppermute | solution.py:280
  120.5 58.8 %collective-permute-start.20 = (bf16[128,3072]{1,0:T(8,128)(2,1)S(1)}, bf16[128,3072]{1,0:T(8,128)(2,1)}, u32[]{:S(2)}, u32[]{:S(2)}) collective-permute-start(bf16[128,3072]{1,0:T(8,128)(2,1)S(1)} %collective-permute-done.14.refs_0_), channel_id=1, source_target_pairs={{8,0},{12,4},{0,8},{4,12},{9,1},{13,5},{1,9},{5,13},{10,2},{14,6},... | collective-permute-start | bytes 2359304 | tf_op jit(solution)/shard_map/chip_3_normed/ppermute | solution.py:280
  139.4 26.2 %copy-start.1 = (bf16[2,256,3840]{2,1,0:T(8,128)(2,1)S(1)}, bf16[2,256,3840]{2,1,0:T(8,128)(2,1)}, u32[]{:S(2)}) copy-start(bf16[2,256,3840]{2,1,0:T(8,128)(2,1)} %get-tuple-element.44.refs_0_) | copy-start | bytes 11796484
  162.6 42.3 %collective-permute-start.17 = (bf16[2,256,3840]{2,1,0:T(8,128)(2,1)}, bf16[2,256,3840]{2,1,0:T(8,128)(2,1)}, u32[]{:S(2)}, u32[]{:S(2)}) collective-permute-start(bf16[2,256,3840]{2,1,0:T(8,128)(2,1)} %get-tuple-element.42.refs_0_), channel_id=1, source_target_pairs={{0,4},{4,0},{8,12},{12,8},{1,5},{5,1},{9,13},{13,9},{2,6},{6,2},{1... | collective-permute-start | bytes 11796488 | tf_op jit(solution)/shard_map/swap_3/ppermute | solution.py:280
  163.9 31.8 %collective-permute-start.10 = (bf16[128,3072]{1,0:T(8,128)(2,1)S(1)}, bf16[128,3072]{1,0:T(8,128)(2,1)S(1)}, u32[]{:S(2)}, u32[]{:S(2)}) collective-permute-start(bf16[128,3072]{1,0:T(8,128)(2,1)S(1)} %add_convert_fusion), channel_id=1, source_target_pairs={{0,1},{1,2},{2,3},{3,0},{4,5},{5,6},{6,7},{7,4},{8,9},{9,10},{10,1... | collective-permute-start | bytes 2359304 | tf_op jit(solution)/shard_map/sum_up_1/ppermute | solution.py:280
  176.7 25.8 %collective-permute-start.16 = (bf16[128,3072]{1,0:T(8,128)(2,1)S(1)}, bf16[128,3072]{1,0:T(8,128)(2,1)S(1)}, u32[]{:S(2)}, u32[]{:S(2)}) collective-permute-start(bf16[128,3072]{1,0:T(8,128)(2,1)S(1)} %get-tuple-element.41), channel_id=1, source_target_pairs={{1,0},{2,1},{3,2},{0,3},{5,4},{6,5},{7,6},{4,7},{9,8},{10,9},{11,1... | collective-permute-start | bytes 2359304 | tf_op jit(solution)/shard_map/sum_down_3/ppermute | solution.py:280
  195.6 9.3 %collective-permute-start.21 = (bf16[2,128,3840]{2,1,0:T(8,128)(2,1)S(1)}, bf16[2,128,3840]{2,1,0:T(8,128)(2,1)S(1)}, u32[]{:S(2)}, u32[]{:S(2)}) collective-permute-start(bf16[2,128,3840]{2,1,0:T(8,128)(2,1)S(1)} %get-tuple-element.49.refs_2_), channel_id=1, source_target_pairs={{0,4},{4,0},{8,12},{12,8},{1,5},{5,1},{9,13},{13,9},{2,6},{6,2},{1... | collective-permute-start | bytes 5898248 | tf_op jit(solution)/shard_map/swap_4/ppermute | solution.py:280
  (22 other events, 244.1 us)

commit v6 on v5

--- a/solution.py
+++ b/solution.py
@@ -13,7 +13,7 @@
 NORM_EPS = 1e-06
 VMEM_LIMIT = 48 * 1024 * 1024
 WORK = 3.0
-WEIGHTS = {2: 3.0}
+WEIGHTS = {1: 3.0}
 
 
 def gelu_parts(pre_act):
@@ -27,18 +27,21 @@
     return (gelu_value, gelu_slope)
 
 
-def token_levels(block_order, count_row):
+def unit_limits(block_order, count_row, first, unit_total):
     above_three = count_row[3]
     above_two = above_three + count_row[2]
     above_one = above_two + count_row[1]
-    places = jnp.arange(block_order.shape[0], dtype=jnp.int32)
+    count = block_order.shape[0]
+    places = jnp.arange(count, dtype=jnp.int32)
     ranked = (
         (places < above_three).astype(jnp.int32)
         + (places < above_two).astype(jnp.int32)
         + (places < above_one).astype(jnp.int32)
     )
-    hits = block_order[None, :] == places[:, None]
-    return jnp.sum(jnp.where(hits, ranked[None, :], 0), axis=1)
+    tokens = (first + places) % count
+    hits = block_order[None, :] == tokens[:, None]
+    limits = unit_total // (1 << (3 - ranked))
+    return jnp.sum(jnp.where(hits, limits[None, :], 0), axis=1, keepdims=True)
 
 
 def norm_backward(grad_normed, standard, row_scale, norm_gain):
@@ -58,11 +61,12 @@
     return wanted
 
 
-def group_kernel(spots, *refs, pieces, begun, owned, share, tiles):
+def group_kernel(spots, *refs, limit_at, owned, share, tiles):
+    pieces, sets = len(limit_at), 1 + max(at for at, _ in limit_at)
     normed_refs = refs[:pieces]
     grad_refs = refs[pieces : 2 * pieces]
-    limit_ref, in_ref, out_ref = refs[2 * pieces : 2 * pieces + 3]
-    acts_ref, own_ref, *rest = refs[2 * pieces + 3 + begun :]
+    limit_refs = refs[2 * pieces : 2 * pieces + sets]
+    in_ref, out_ref, acts_ref, own_ref, *rest = refs[2 * pieces + sets :]
     tile = pl.program_id(0)
 
     def columns(target, first):
@@ -73,6 +77,8 @@
                 target[kind, at * size : (at + 1) * size, :] = ref[:, span]
 
     rows_ref, rest = rest[-1], rest[:-1]
+    size = normed_refs[0].shape[0]
+    limit = jnp.concatenate([limit_refs[at][step * size : (step + 1) * size, :] for at, step in limit_at])
 
     @pl.when(tile == 0)
     def _():
@@ -88,15 +94,15 @@
 
     @pl.when(tile < tiles)
     def _():
-        group_tile(spots[0], rows_ref, limit_ref, in_ref, out_ref, acts_ref, rest, owned, tiles)
-
-
-def group_tile(first, rows_ref, limit_ref, in_ref, out_ref, acts_ref, rest, owned, tiles):
+        group_tile(spots[0], rows_ref, limit, in_ref, out_ref, acts_ref, rest, owned, tiles)
+
+
+def group_tile(first, rows_ref, limit, in_ref, out_ref, acts_ref, rest, owned, tiles):
     tile = pl.program_id(0)
     units = in_ref.shape[1]
     width = 256 if units % 256 == 0 else units
 
-    mask = first + tile * units < limit_ref[...]
+    mask = first + tile * units < limit
     products = []
     for start in range(0, units, width):
         span = slice(start, start + width)
@@ -134,46 +140,37 @@
 
 
 def group_call(
-    spots, normed, grads, limit, weight_in, weight_out, tile, share, back_types, begun, rows_after, weight
+    spots, normed, grads, limits, limit_at, weight_in, weight_out, tile, share, back_types, weight
 ):
     features, units = weight_in.shape
     piece_rows = normed[0].shape[0]
     rows = piece_rows * len(normed)
     owned = len(back_types)
     tiles = units // tile
-    total = begun[0].shape[1] if begun else rows + rows_after
     whole = lambda shape: pl.BlockSpec(shape, lambda i, spots: (0,) * len(shape))
     out_shape = [
-        jax.ShapeDtypeStruct((2, total, units + share), jnp.bfloat16),
-        jax.ShapeDtypeStruct((2, total, share), jnp.bfloat16),
+        jax.ShapeDtypeStruct((2, rows, units + share), jnp.bfloat16),
+        jax.ShapeDtypeStruct((2, rows, share), jnp.bfloat16),
     ]
     out_specs = [
-        pl.BlockSpec((2, rows, tile), lambda i, spots: (0, rows_after // rows, i)),
-        pl.BlockSpec((2, rows, share), lambda i, spots: (0, rows_after // rows, 0)),
+        pl.BlockSpec((2, rows, tile), lambda i, spots: (0, 0, i)),
+        whole((2, rows, share)),
     ]
-    operands = (spots, *normed, *grads, limit, weight_in, weight_out)
     for kind in back_types:
         out_shape.append(jax.ShapeDtypeStruct((piece_rows, features), kind))
         out_specs.append(whole((piece_rows, features)))
     return pl.pallas_call(
         functools.partial(
-            group_kernel,
-            pieces=len(normed),
-            begun=len(begun),
-            owned=owned,
-            share=share,
-            tiles=tiles,
+            group_kernel, limit_at=limit_at, owned=owned, share=share, tiles=tiles
         ),
         grid_spec=pltpu.PrefetchScalarGridSpec(
             num_scalar_prefetch=1,
             grid=(tiles + share // tile,),
-            in_specs=[whole(one.shape) for one in (*normed, *grads)]
+            in_specs=[whole(one.shape) for one in (*normed, *grads, *limits)]
             + [
-                whole((rows, 1)),
                 pl.BlockSpec((features, tile), lambda i, spots: (0, jnp.minimum(i, tiles - 1))),
                 pl.BlockSpec((tile, features), lambda i, spots: (jnp.minimum(i, tiles - 1), 0)),
-            ]
-            + [pl.BlockSpec(memory_space=pl.ANY) for _ in begun],
+            ],
             out_specs=out_specs,
             scratch_shapes=[pltpu.VMEM((owned * piece_rows, features), jnp.float32)] * bool(owned)
             + [pltpu.VMEM((2, rows, features), jnp.bfloat16)],
@@ -181,9 +178,8 @@
         out_shape=out_shape,
         compiler_params=pltpu.CompilerParams(vmem_limit_bytes=VMEM_LIMIT),
         cost_estimate=work_of(weight * (4 * rows + 2 * owned * piece_rows) * units * features),
-        input_output_aliases={len(operands) + at: at for at in range(len(begun))},
         name="group",
-    )(*operands, *begun)
+    )(spots, *normed, *grads, *limits, weight_in, weight_out)
 
 
 def weights_kernel(*refs, groups, scale, started):
@@ -261,23 +257,23 @@
     swap_cores = [(i, i ^ 1) for i in range(blocks)]
     half = ring // 2
 
-    as_float = inputs.astype(jnp.float32)
+    def send(one, axis, pairs, name):
+        with jax.named_scope(name):
+            return lax.ppermute(one, axis, pairs)
+
+    level_sets = [jnp.concatenate([level_order, level_counts[0]])]
+    for _ in range(1, chips):
+        level_sets.append(send(level_sets[-1], "dp", from_chip, "chip_levels"))
+
+    as_float = after(inputs, *level_sets[1:]).astype(jnp.float32)
     row_mean = jnp.mean(as_float, axis=1, keepdims=True)
     centred = as_float - row_mean
     row_scale = lax.rsqrt(jnp.mean(centred * centred, axis=1, keepdims=True) + NORM_EPS)
     standard = centred * row_scale
     normed = (standard * norm_gain[None, :]).astype(jnp.bfloat16)
 
-    def limits_of(order, counts):
-        limits = unit_total // (1 << (3 - token_levels(order, counts)))
-        limits = jnp.concatenate([limits, limits])
-        return lax.dynamic_slice_in_dim(limits, place * rows, rows * ring, 0)
-
+    limits = [unit_limits(one[:-4], one[-4:], place * rows, unit_total) for one in level_sets]
     spots = jnp.stack([place * unit_local, block * share, (block ^ 1) * share]).astype(jnp.int32)
-
-    def send(one, axis, pairs, name):
-        with jax.named_scope(name):
-            return lax.ppermute(one, axis, pairs)
 
     kinds = ("normed", "grad")
 
@@ -290,32 +286,23 @@
     for step in range(1, ring):
         near[step] = move(near[step - 1], "tensor", from_next, f"ring_{step}")
     sets = [[near[step] for step in range(ring)]]
-    limit_sets = [limits_of(level_order, level_counts[0])]
-    levels = jnp.concatenate([level_order, level_counts[0]])
-
     for chip in range(1, chips):
-        levels = send(levels, "dp", from_chip, "chip_levels")
-        limit_sets.append(limits_of(levels[:-4], levels[-4:]))
-        far = []
-        for step, piece in enumerate(sets[-1]):
-            held = [levels] if step == 0 else []
-            far.append(move(piece, "dp", from_chip, f"chip_{step}", *held))
-        sets.append(far)
+        sets.append(
+            [move(piece, "dp", from_chip, f"chip_{step}") for step, piece in enumerate(sets[-1])]
+        )
 
     groups, own_grads = [], []
     arrivals = [
         [(chip, slot - chip) for chip in range(chips) if 0 <= slot - chip < ring]
         for slot in range(ring + chips - 1)
     ]
+    if len(arrivals) > 1:
+        arrivals[:2] = [sorted(arrivals[0] + arrivals[1])]
     last = len(arrivals) - 1
     totals = []
     for at, entries in enumerate(arrivals):
-        gates, begun, rows_after = [], [], 0
-        if at == 0 and last > 0:
-            rows_after = rows * len(arrivals[1])
-        elif at == 1:
-            begun = groups.pop()[:2]
-        if last > 2 and at >= last - 1:
+        gates = []
+        if last > 1 and at >= last - 1:
             early = [sets[chip][step][1] for chip, step in entries]
             totals = weights_call(
                 [(after(own, *early), *others) for own, *others in groups[:-1]], totals, 1.0
@@ -324,29 +311,22 @@
             groups = groups[-1:]
         own_steps = [step for chip, step in entries if chip == 0]
         back_types = [jnp.bfloat16 if step in (half, half + 1) else jnp.float32 for step in own_steps]
-        limit = jnp.concatenate(
-            [limit_sets[chip][step * rows : (step + 1) * rows, None] for chip, step in entries]
-        )
         with jax.named_scope(f"group_{at}"):
             act, own_cols, *back = group_call(
                 after(spots, *gates),
                 [sets[chip][step][0] for chip, step in entries],
                 [sets[chip][step][1] for chip, step in entries],
-                limit,
+                limits[: 1 + max(chip for chip, _ in entries)],
+                entries,
                 weight_in,
                 weight_out,
                 tile,
                 share,
                 back_types,
-                begun,
-                rows_after,
                 WEIGHTS.get(at, 1.0),
             )
         own_grads.extend(back)
-        if at == 0 and last > 0:
-            groups.append((act, own_cols))
-        else:
-            groups.append((act, own_cols, send(act, "dp", swap_cores, f"swap_{at}")))
+        groups.append((act, own_cols, send(act, "dp", swap_cores, f"swap_{at}")))
 
     def chain(steps, pairs, name):
         travelling = None

time: 219 us -> 232 us (1.059)
  waiting for transfers between devices: 20.4 us -> 51.4 us
  Pallas kernels: 144 us -> 129 us
  starting transfers between devices: 23.2 us -> 31.4 us
  local copies, waits for them, and re-layouts: 13.8 us -> 5.81 us
  other arithmetic: 11.6 us -> 8.36 us
    ppermute x22, waiting for transfers between devices: 20.4 us -> 51.4 us  [send(): return lax.ppermute(one, axis, pairs)]
    pallas_call x5 -> x4, Pallas kernels: 108 us -> 93 us  [group_call(): pl.pallas_call(functools.partial(group_kernel, limit_at=limit_at, owned=o...]
    ppermute x22, starting transfers between devices: 23.2 us -> 31.4 us  [send(): return lax.ppermute(one, axis, pairs)]
    unnamed x48 -> x36, local copies, waits for them, and re-layouts: 8.05 us -> 4.26 us
    concatenate x3 -> x0, local copies, waits for them, and re-layouts: 2.41 us -> none  [shards(): jnp.concatenate([limit_sets[chip][step * rows:(step + 1) * rows, None] fo...]
  transfers between devices with their start and end apart: 22 -> 22, of which waited for: 5 -> 5; matrix products, arithmetic and copies ran while one was open for 8% -> 4% of each run, Pallas kernels for 60% -> 50%
where the time goes in v6:
time: 232 us; the launch traced here: 231 us
  Pallas kernels  129 us (56%)
  waiting for transfers between devices  51.4 us (22%)
  starting transfers between devices  31.4 us (14%)
  other arithmetic  8.36 us (4%)
  local copies, waits for them, and re-layouts  5.81 us (3%)
  between operations  4.81 us (2%)
    pallas_call x4, Pallas kernels, group_call(): pl.pallas_call(functools.partial(group_kernel, limit_at=limit_at, owned=o...  93 us
    ppermute x22, waiting for transfers between devices, send(): return lax.ppermute(one, axis, pairs)  51.4 us
    pallas_call x3, Pallas kernels, weights_call(): pl.pallas_call(functools.partial(weights_kernel, groups=len(acts), scale=...  36.2 us
    ppermute x22, starting transfers between devices, send(): return lax.ppermute(one, axis, pairs)  31.4 us
  transfers between devices with their start and end apart: 22, of which 5 were waited for; matrix products, arithmetic and copies ran while one was open for 4% of the time, Pallas kernels for 50%

profile of v6, /device:TPU:0, one launch (start us, length us, event | category | flops | bytes accessed | tf_op | source)
XLA Modules:
  0.0 230.9 jit_solution(16172991810580548025)
XLA Ops:
  1.5 3.0 %collective-permute-start = (s32[516]{0:T(1024)S(1)}, s32[516]{0:T(1024)S(1)}, u32[]{:S(2)}, u32[]{:S(2)}) collective-permute-start(s32[516]{0:T(1024)S(1)} %pad_add_fusion), channel_id=1, source_target_pairs={{8,0},{12,4},{0,8},{4,12},{9,1},{13,5},{1,9},{5,13},{10,2},{14,6},... | collective-permute-start | bytes 6200 | tf_op jit(solution)/shard_map/chip_levels/ppermute | solution.py:262
  4.5 3.6 %collective-permute-start.3 = (bf16[128,3072]{1,0:T(8,128)(2,1)}, bf16[128,3072]{1,0:T(8,128)(2,1)S(1)}, u32[]{:S(2)}, u32[]{:S(2)}) collective-permute-start(bf16[128,3072]{1,0:T(8,128)(2,1)} %refs_3_.1), channel_id=1, source_target_pairs={{1,0},{2,1},{3,2},{0,3},{5,4},{6,5},{7,6},{4,7},{9,8},{10,9},{11,1... | collective-permute-start | bytes 2359304 | tf_op jit(solution)/shard_map/ring_1_grad/ppermute | solution.py:262
  9.4 1.5 fusion.11
  11.3 2.2 collective-permute-start.1
  13.4 1.5 collective-permute-start.4
  22.9 3.4 %collective-permute-done.3.refs_4_ = bf16[128,3072]{1,0:T(8,128)(2,1)S(1)} collective-permute-done((bf16[128,3072]{1,0:T(8,128)(2,1)}, bf16[128,3072]{1,0:T(8,128)(2,1)S(1)}, u32[]{:S(2)}, u32[]{:S(2)}) %collective-permute-start.3) | collective-permute-done | bytes 786464 | tf_op jit(solution)/shard_map/ring_1_grad/ppermute | solution.py:262
  26.4 4.2 %collective-permute-start.7 = (bf16[128,3072]{1,0:T(8,128)(2,1)S(1)}, bf16[128,3072]{1,0:T(8,128)(2,1)S(1)}, u32[]{:S(2)}, u32[]{:S(2)}) collective-permute-start(bf16[128,3072]{1,0:T(8,128)(2,1)S(1)} %collective-permute-done.3.refs_4_), channel_id=1, source_target_pairs={{1,0},{2,1},{3,2},{0,3},{5,4},{6,5},{7,6},{4,7},{9,8},{10,9},{11,1... | collective-permute-start | bytes 2359304 | tf_op jit(solution)/shard_map/ring_2_grad/ppermute | solution.py:262
  31.1 12.0 %collective-permute-done.1.refs_1_ = bf16[128,3072]{1,0:T(8,128)(2,1)} collective-permute-done((bf16[128,3072]{1,0:T(8,128)(2,1)S(1)}, bf16[128,3072]{1,0:T(8,128)(2,1)}, u32[]{:S(2)}, u32[]{:S(2)}) %collective-permute-start.1) | collective-permute-done | bytes 786464 | tf_op jit(solution)/shard_map/ring_1_normed/ppermute | solution.py:262
  43.1 4.4 %collective-permute-start.5 = (bf16[128,3072]{1,0:T(8,128)(2,1)}, bf16[128,3072]{1,0:T(8,128)(2,1)S(1)}, u32[]{:S(2)}, u32[]{:S(2)}) collective-permute-start(bf16[128,3072]{1,0:T(8,128)(2,1)} %collective-permute-done.1.refs_1_), channel_id=1, source_target_pairs={{1,0},{2,1},{3,2},{0,3},{5,4},{6,5},{7,6},{4,7},{9,8},{10,9},{11,1... | collective-permute-start | bytes 2359304 | tf_op jit(solution)/shard_map/ring_2_normed/ppermute | solution.py:262
  48.0 2.8 %collective-permute-done.2.refs_2_ = bf16[128,3072]{1,0:T(8,128)(2,1)} collective-permute-done((bf16[128,3072]{1,0:T(8,128)(2,1)S(1)}, bf16[128,3072]{1,0:T(8,128)(2,1)}, u32[]{:S(2)}, u32[]{:S(2)}) %collective-permute-start.2) | collective-permute-done | bytes 786464 | tf_op jit(solution)/shard_map/chip_0_normed/ppermute | solution.py:262
  50.9 30.8 %group.4 = (bf16[2,384,3840]{2,1,0:T(8,128)(2,1)}, bf16[2,384,768]{2,1,0:T(8,128)(2,1)}, f32[128,3072]{1,0:T(8,128)}, f32[128,3072]{1,0:T(8,128)}) custom-call(s32[3]{0:T(128)S(1)} %pad_add_fusion.1.spots, bf16[128,3072]{1,0:T(8,128)(2,1)S(1)} %fusion.5.refs_0_, bf16[128,3072]{1,0:T(8,128)(2,1)} %collective-permute-done.1.refs_1_, ...), custom_call_target="tpu_custom_call" | custom-call | flops 57982058496 | tf_op jit(solution)/shard_map/group_0/group/pallas_call | solution.py:162
  84.8 23.1 %group.5 = (bf16[2,256,3840]{2,1,0:T(8,128)(2,1)}, bf16[2,256,768]{2,1,0:T(8,128)(2,1)S(1)}, bf16[128,3072]{1,0:T(8,128)(2,1)}) custom-call(s32[3]{0:T(128)S(1)} %pad_add_fusion.1.spots, bf16[128,3072]{1,0:T(8,128)(2,1)S(1)} %collective-permute-done.5.refs_0_, bf16[128,3072]{1,0:T(8,128)(2,1)S(1)} %collective-permute-done.6.refs_1_, ...), custom_call_target="tpu_custom_call" | custom-call | flops 108716359680 | tf_op jit(solution)/shard_map/group_1/group/pallas_call | solution.py:162
  107.9 1.6 collective-permute-start.9
  109.5 25.9 %collective-permute-done.14.refs_0_ = bf16[128,3072]{1,0:T(8,128)(2,1)S(1)} collective-permute-done((bf16[128,3072]{1,0:T(8,128)(2,1)S(1)}, bf16[128,3072]{1,0:T(8,128)(2,1)S(1)}, u32[]{:S(2)}, u32[]{:S(2)}) %collective-permute-start.14) | collective-permute-done | bytes 786464 | tf_op jit(solution)/shard_map/ring_3_normed/ppermute | solution.py:262
  135.4 1.5 collective-permute-start.18
  137.4 12.0 %weights.3 = (bf16[768,3072]{1,0:T(8,128)(2,1)S(1)}, bf16[3072,768]{1,0:T(8,128)(2,1)}) custom-call(bf16[2,384,3840]{2,1,0:T(8,128)(2,1)} %get-tuple-element.31.refs_0_, bf16[2,384,3840]{2,1,0:T(8,128)(2,1)} %collective-permute-done.13.refs_1_.refs_3_, bf16[2,384,768]{2,1,0:T(8,128)(2,1)S(1)} %copy-done.2, ...), custom_call_target="tpu_custom_call" | custom-call | tf_op jit(solution)/shard_map/weights/pallas_call | solution.py:223
  149.5 2.2 copy-done
  153.7 23.1 %group.6 = (bf16[2,256,3840]{2,1,0:T(8,128)(2,1)}, bf16[2,256,768]{2,1,0:T(8,128)(2,1)S(1)}, bf16[128,3072]{1,0:T(8,128)(2,1)S(1)}) custom-call(s32[3]{0:T(128)S(1)} %pad_add_fusion.1.spots, bf16[128,3072]{1,0:T(8,128)(2,1)S(1)} %collective-permute-done.14.refs_0_, bf16[128,3072]{1,0:T(8,128)(2,1)S(1)} %copy-done.5, ...), custom_call_target="tpu_custom_call" | custom-call | flops 36238786560 | tf_op jit(solution)/shard_map/group_2/group/pallas_call | solution.py:162
  177.1 11.2 %weights.4 = (bf16[768,3072]{1,0:T(8,128)(2,1)}, bf16[3072,768]{1,0:T(8,128)(2,1)}) custom-call(bf16[2,256,3840]{2,1,0:T(8,128)(2,1)S(1)} %copy-done.1, bf16[2,256,3840]{2,1,0:T(8,128)(2,1)} %collective-permute-done.19.refs_1_.refs_3_, bf16[2,256,768]{2,1,0:T(8,128)(2,1)S(1)} %get-tuple-element.39.refs_2_, ...), custom_call_target="tpu_custom_call" | custom-call | tf_op jit(solution)/shard_map/weights/pallas_call | solution.py:223
  188.3 4.1 %collective-permute-start.16 = (bf16[128,3072]{1,0:T(8,128)(2,1)S(1)}, bf16[128,3072]{1,0:T(8,128)(2,1)S(1)}, u32[]{:S(2)}, u32[]{:S(2)}) collective-permute-start(bf16[128,3072]{1,0:T(8,128)(2,1)S(1)} %get-tuple-element.35), channel_id=1, source_target_pairs={{1,0},{2,1},{3,2},{0,3},{5,4},{6,5},{7,6},{4,7},{9,8},{10,9},{11,1... | collective-permute-start | bytes 2359304 | tf_op jit(solution)/shard_map/sum_down_3/ppermute | solution.py:262
  192.4 16.0 %group.7 = (bf16[2,128,3840]{2,1,0:T(8,128)(2,1)S(1)}, bf16[2,128,768]{2,1,0:T(8,128)(2,1)S(1)}) custom-call(s32[3]{0:T(128)S(1)} %pad_add_fusion.1.spots, bf16[128,3072]{1,0:T(8,128)(2,1)S(1)} %collective-permute-done.20.refs_0_, bf16[128,3072]{1,0:T(8,128)(2,1)S(1)} %collective-permute-done.18.refs_1_, s32[512,1]{1,0:T(8,128)S(1)} %copy.18.refs_6_.refs_4_.refs_2_, ...), custom_call_target="tpu_custom_call" | custom-call | flops 14495514624 | tf_op jit(solution)/shard_map/group_3/group/pallas_call | solution.py:162
  208.5 7.2 %collective-permute-done.16 = bf16[128,3072]{1,0:T(8,128)(2,1)S(1)} collective-permute-done((bf16[128,3072]{1,0:T(8,128)(2,1)S(1)}, bf16[128,3072]{1,0:T(8,128)(2,1)S(1)}, u32[]{:S(2)}, u32[]{:S(2)}) %collective-permute-start.16) | collective-permute-done | bytes 786464 | tf_op jit(solution)/shard_map/sum_down_3/ppermute | solution.py:262
  216.4 1.6 fusion.10
  218.0 12.9 %weights.5 = (bf16[768,3072]{1,0:T(8,128)(2,1)}, bf16[3072,768]{1,0:T(8,128)(2,1)}) custom-call(bf16[2,256,3840]{2,1,0:T(8,128)(2,1)} %get-tuple-element.36.refs_0_, bf16[2,256,3840]{2,1,0:T(8,128)(2,1)} %collective-permute-done.17.refs_1_.refs_5_, bf16[2,128,3840]{2,1,0:T(8,128)(2,1)S(1)} %get-tuple-element.43.refs_2_, ...), custom_call_target="tpu_custom_call" | custom-call | tf_op jit(solution)/shard_map/weights/pallas_call | solution.py:223
  (83 shorter events, 14.3 us)
Async XLA Ops:
  1.5 6.6 %collective-permute-start = (s32[516]{0:T(1024)S(1)}, s32[516]{0:T(1024)S(1)}, u32[]{:S(2)}, u32[]{:S(2)}) collective-permute-start(s32[516]{0:T(1024)S(1)} %pad_add_fusion), channel_id=1, source_target_pairs={{8,0},{12,4},{0,8},{4,12},{9,1},{13,5},{1,9},{5,13},{10,2},{14,6},... | collective-permute-start | bytes 6200 | tf_op jit(solution)/shard_map/chip_levels/ppermute | solution.py:262
  4.5 21.9 %collective-permute-start.3 = (bf16[128,3072]{1,0:T(8,128)(2,1)}, bf16[128,3072]{1,0:T(8,128)(2,1)S(1)}, u32[]{:S(2)}, u32[]{:S(2)}) collective-permute-start(bf16[128,3072]{1,0:T(8,128)(2,1)} %refs_3_.1), channel_id=1, source_target_pairs={{1,0},{2,1},{3,2},{0,3},{5,4},{6,5},{7,6},{4,7},{9,8},{10,9},{11,1... | collective-permute-start | bytes 2359304 | tf_op jit(solution)/shard_map/ring_1_grad/ppermute | solution.py:262
  11.3 31.9 %collective-permute-start.1 = (bf16[128,3072]{1,0:T(8,128)(2,1)S(1)}, bf16[128,3072]{1,0:T(8,128)(2,1)}, u32[]{:S(2)}, u32[]{:S(2)}) collective-permute-start(bf16[128,3072]{1,0:T(8,128)(2,1)S(1)} %fusion.5.refs_0_), channel_id=1, source_target_pairs={{1,0},{2,1},{3,2},{0,3},{5,4},{6,5},{7,6},{4,7},{9,8},{10,9},{11,1... | collective-permute-start | bytes 2359304 | tf_op jit(solution)/shard_map/ring_1_normed/ppermute | solution.py:262
  13.4 34.1 %collective-permute-start.4 = (bf16[128,3072]{1,0:T(8,128)(2,1)S(1)}, bf16[128,3072]{1,0:T(8,128)(2,1)}, u32[]{:S(2)}, u32[]{:S(2)}) collective-permute-start(bf16[128,3072]{1,0:T(8,128)(2,1)S(1)} %copy-done.3), channel_id=1, source_target_pairs={{8,0},{12,4},{0,8},{4,12},{9,1},{13,5},{1,9},{5,13},{10,2},{14,6},... | collective-permute-start | bytes 2359304 | tf_op jit(solution)/shard_map/chip_0_grad/ppermute | solution.py:262
  14.9 35.9 %collective-permute-start.2 = (bf16[128,3072]{1,0:T(8,128)(2,1)S(1)}, bf16[128,3072]{1,0:T(8,128)(2,1)}, u32[]{:S(2)}, u32[]{:S(2)}) collective-permute-start(bf16[128,3072]{1,0:T(8,128)(2,1)S(1)} %fusion.5.refs_0_), channel_id=1, source_target_pairs={{8,0},{12,4},{0,8},{4,12},{9,1},{13,5},{1,9},{5,13},{10,2},{14,6},... | collective-permute-start | bytes 2359304 | tf_op jit(solution)/shard_map/chip_0_normed/ppermute | solution.py:262
  26.4 55.4 %collective-permute-start.7 = (bf16[128,3072]{1,0:T(8,128)(2,1)S(1)}, bf16[128,3072]{1,0:T(8,128)(2,1)S(1)}, u32[]{:S(2)}, u32[]{:S(2)}) collective-permute-start(bf16[128,3072]{1,0:T(8,128)(2,1)S(1)} %collective-permute-done.3.refs_4_), channel_id=1, source_target_pairs={{1,0},{2,1},{3,2},{0,3},{5,4},{6,5},{7,6},{4,7},{9,8},{10,9},{11,1... | collective-permute-start | bytes 2359304 | tf_op jit(solution)/shard_map/ring_2_grad/ppermute | solution.py:262
  30.5 51.7 %collective-permute-start.8 = (bf16[128,3072]{1,0:T(8,128)(2,1)S(1)}, bf16[128,3072]{1,0:T(8,128)(2,1)S(1)}, u32[]{:S(2)}, u32[]{:S(2)}) collective-permute-start(bf16[128,3072]{1,0:T(8,128)(2,1)S(1)} %collective-permute-done.3.refs_4_), channel_id=1, source_target_pairs={{8,0},{12,4},{0,8},{4,12},{9,1},{13,5},{1,9},{5,13},{10,2},{14,6},... | collective-permute-start | bytes 2359304 | tf_op jit(solution)/shard_map/chip_1_grad/ppermute | solution.py:262
  43.1 40.7 %collective-permute-start.5 = (bf16[128,3072]{1,0:T(8,128)(2,1)}, bf16[128,3072]{1,0:T(8,128)(2,1)S(1)}, u32[]{:S(2)}, u32[]{:S(2)}) collective-permute-start(bf16[128,3072]{1,0:T(8,128)(2,1)} %collective-permute-done.1.refs_1_), channel_id=1, source_target_pairs={{1,0},{2,1},{3,2},{0,3},{5,4},{6,5},{7,6},{4,7},{9,8},{10,9},{11,1... | collective-permute-start | bytes 2359304 | tf_op jit(solution)/shard_map/ring_2_normed/ppermute | solution.py:262
  47.5 36.7 %collective-permute-start.6 = (bf16[128,3072]{1,0:T(8,128)(2,1)}, bf16[128,3072]{1,0:T(8,128)(2,1)S(1)}, u32[]{:S(2)}, u32[]{:S(2)}) collective-permute-start(bf16[128,3072]{1,0:T(8,128)(2,1)} %collective-permute-done.1.refs_1_), channel_id=1, source_target_pairs={{8,0},{12,4},{0,8},{4,12},{9,1},{13,5},{1,9},{5,13},{10,2},{14,6},... | collective-permute-start | bytes 2359304 | tf_op jit(solution)/shard_map/chip_1_normed/ppermute | solution.py:262
  81.7 55.8 %copy-start.2 = (bf16[2,384,768]{2,1,0:T(8,128)(2,1)S(1)}, bf16[2,384,768]{2,1,0:T(8,128)(2,1)}, u32[]{:S(2)}) copy-start(bf16[2,384,768]{2,1,0:T(8,128)(2,1)} %get-tuple-element.32.refs_2_) | copy-start | bytes 3538948
  81.7 55.2 %collective-permute-start.13 = (bf16[2,384,3840]{2,1,0:T(8,128)(2,1)}, bf16[2,384,3840]{2,1,0:T(8,128)(2,1)}, u32[]{:S(2)}, u32[]{:S(2)}) collective-permute-start(bf16[2,384,3840]{2,1,0:T(8,128)(2,1)} %get-tuple-element.31.refs_0_), channel_id=1, source_target_pairs={{0,4},{4,0},{8,12},{12,8},{1,5},{5,1},{9,13},{13,9},{2,6},{6,2},{1... | collective-permute-start | bytes 17694728 | tf_op jit(solution)/shard_map/swap_0/ppermute | solution.py:262
  81.8 26.0 %collective-permute-start.11 = (bf16[128,3072]{1,0:T(8,128)(2,1)S(1)}, bf16[128,3072]{1,0:T(8,128)(2,1)S(1)}, u32[]{:S(2)}, u32[]{:S(2)}) collective-permute-start(bf16[128,3072]{1,0:T(8,128)(2,1)S(1)} %collective-permute-done.7.refs_2_), channel_id=1, source_target_pairs={{1,0},{2,1},{3,2},{0,3},{5,4},{6,5},{7,6},{4,7},{9,8},{10,9},{11,1... | collective-permute-start | bytes 2359304 | tf_op jit(solution)/shard_map/ring_3_grad/ppermute | solution.py:262
  82.3 25.6 %collective-permute-start.12 = (bf16[128,3072]{1,0:T(8,128)(2,1)S(1)}, bf16[128,3072]{1,0:T(8,128)(2,1)S(1)}, u32[]{:S(2)}, u32[]{:S(2)}) collective-permute-start(bf16[128,3072]{1,0:T(8,128)(2,1)S(1)} %collective-permute-done.7.refs_2_), channel_id=1, source_target_pairs={{8,0},{12,4},{0,8},{4,12},{9,1},{13,5},{1,9},{5,13},{10,2},{14,6},... | collective-permute-start | bytes 2359304 | tf_op jit(solution)/shard_map/chip_2_grad/ppermute | solution.py:262
  83.8 51.6 %collective-permute-start.14 = (bf16[128,3072]{1,0:T(8,128)(2,1)S(1)}, bf16[128,3072]{1,0:T(8,128)(2,1)S(1)}, u32[]{:S(2)}, u32[]{:S(2)}) collective-permute-start(bf16[128,3072]{1,0:T(8,128)(2,1)S(1)} %collective-permute-done.5.refs_0_), channel_id=1, source_target_pairs={{1,0},{2,1},{3,2},{0,3},{5,4},{6,5},{7,6},{4,7},{9,8},{10,9},{11,1... | collective-permute-start | bytes 2359304 | tf_op jit(solution)/shard_map/ring_3_normed/ppermute | solution.py:262
  84.2 67.5 %collective-permute-start.15 = (bf16[128,3072]{1,0:T(8,128)(2,1)S(1)}, bf16[128,3072]{1,0:T(8,128)(2,1)S(1)}, u32[]{:S(2)}, u32[]{:S(2)}) collective-permute-start(bf16[128,3072]{1,0:T(8,128)(2,1)S(1)} %collective-permute-done.5.refs_0_), channel_id=1, source_target_pairs={{8,0},{12,4},{0,8},{4,12},{9,1},{13,5},{1,9},{5,13},{10,2},{14,6},... | collective-permute-start | bytes 2359304 | tf_op jit(solution)/shard_map/chip_2_normed/ppermute | solution.py:262
  107.8 69.3 %collective-permute-start.19 = (bf16[2,256,3840]{2,1,0:T(8,128)(2,1)}, bf16[2,256,3840]{2,1,0:T(8,128)(2,1)}, u32[]{:S(2)}, u32[]{:S(2)}) collective-permute-start(bf16[2,256,3840]{2,1,0:T(8,128)(2,1)} %get-tuple-element.38.refs_0_), channel_id=1, source_target_pairs={{0,4},{4,0},{8,12},{12,8},{1,5},{5,1},{9,13},{13,9},{2,6},{6,2},{1... | collective-permute-start | bytes 11796488 | tf_op jit(solution)/shard_map/swap_1/ppermute | solution.py:262
  107.9 68.9 %collective-permute-start.9 = (bf16[128,3072]{1,0:T(8,128)(2,1)}, bf16[128,3072]{1,0:T(8,128)(2,1)S(1)}, u32[]{:S(2)}, u32[]{:S(2)}) collective-permute-start(bf16[128,3072]{1,0:T(8,128)(2,1)} %get-tuple-element.29), channel_id=1, source_target_pairs={{0,1},{1,2},{2,3},{3,0},{4,5},{5,6},{6,7},{7,4},{8,9},{9,10},{10,1... | collective-permute-start | bytes 2359304 | tf_op jit(solution)/shard_map/sum_up_2/ppermute | solution.py:262
  135.4 41.6 %collective-permute-start.18 = (bf16[128,3072]{1,0:T(8,128)(2,1)S(1)}, bf16[128,3072]{1,0:T(8,128)(2,1)S(1)}, u32[]{:S(2)}, u32[]{:S(2)}) collective-permute-start(bf16[128,3072]{1,0:T(8,128)(2,1)S(1)} %collective-permute-done.11.refs_2_), channel_id=1, source_target_pairs={{8,0},{12,4},{0,8},{4,12},{9,1},{13,5},{1,9},{5,13},{10,2},{14,6},... | collective-permute-start | bytes 2359304 | tf_op jit(solution)/shard_map/chip_3_grad/ppermute | solution.py:262
  136.9 55.5 %collective-permute-start.20 = (bf16[128,3072]{1,0:T(8,128)(2,1)S(1)}, bf16[128,3072]{1,0:T(8,128)(2,1)S(1)}, u32[]{:S(2)}, u32[]{:S(2)}) collective-permute-start(bf16[128,3072]{1,0:T(8,128)(2,1)S(1)} %collective-permute-done.14.refs_0_), channel_id=1, source_target_pairs={{8,0},{12,4},{0,8},{4,12},{9,1},{13,5},{1,9},{5,13},{10,2},{14,6},... | collective-permute-start | bytes 2359304 | tf_op jit(solution)/shard_map/chip_3_normed/ppermute | solution.py:262
  176.8 41.2 %collective-permute-start.17 = (bf16[2,256,3840]{2,1,0:T(8,128)(2,1)}, bf16[2,256,3840]{2,1,0:T(8,128)(2,1)}, u32[]{:S(2)}, u32[]{:S(2)}) collective-permute-start(bf16[2,256,3840]{2,1,0:T(8,128)(2,1)} %get-tuple-element.36.refs_0_), channel_id=1, source_target_pairs={{0,4},{4,0},{8,12},{12,8},{1,5},{5,1},{9,13},{13,9},{2,6},{6,2},{1... | collective-permute-start | bytes 11796488 | tf_op jit(solution)/shard_map/swap_2/ppermute | solution.py:262
  177.0 31.5 %collective-permute-start.10 = (bf16[128,3072]{1,0:T(8,128)(2,1)S(1)}, bf16[128,3072]{1,0:T(8,128)(2,1)S(1)}, u32[]{:S(2)}, u32[]{:S(2)}) collective-permute-start(bf16[128,3072]{1,0:T(8,128)(2,1)S(1)} %add_convert_fusion), channel_id=1, source_target_pairs={{0,1},{1,2},{2,3},{3,0},{4,5},{5,6},{6,7},{7,4},{8,9},{9,10},{10,1... | collective-permute-start | bytes 2359304 | tf_op jit(solution)/shard_map/sum_up_1/ppermute | solution.py:262
  188.3 27.4 %copy-start.9 = (f32[128,3072]{1,0:T(8,128)S(1)}, f32[128,3072]{1,0:T(8,128)}, u32[]{:S(2)}) copy-start(f32[128,3072]{1,0:T(8,128)} %get-tuple-element.27) | copy-start | bytes 4718596
  188.3 27.4 %collective-permute-start.16 = (bf16[128,3072]{1,0:T(8,128)(2,1)S(1)}, bf16[128,3072]{1,0:T(8,128)(2,1)S(1)}, u32[]{:S(2)}, u32[]{:S(2)}) collective-permute-start(bf16[128,3072]{1,0:T(8,128)(2,1)S(1)} %get-tuple-element.35), channel_id=1, source_target_pairs={{1,0},{2,1},{3,2},{0,3},{5,4},{6,5},{7,6},{4,7},{9,8},{10,9},{11,1... | collective-permute-start | bytes 2359304 | tf_op jit(solution)/shard_map/sum_down_3/ppermute | solution.py:262
  208.4 9.6 %collective-permute-start.21 = (bf16[2,128,3840]{2,1,0:T(8,128)(2,1)S(1)}, bf16[2,128,3840]{2,1,0:T(8,128)(2,1)S(1)}, u32[]{:S(2)}, u32[]{:S(2)}) collective-permute-start(bf16[2,128,3840]{2,1,0:T(8,128)(2,1)S(1)} %get-tuple-element.43.refs_2_), channel_id=1, source_target_pairs={{0,4},{4,0},{8,12},{12,8},{1,5},{5,1},{9,13},{13,9},{2,6},{6,2},{1... | collective-permute-start | bytes 5898248 | tf_op jit(solution)/shard_map/swap_3/ppermute | solution.py:262
  (16 other events, 248.1 us)

commit v7 on v6

--- a/solution.py
+++ b/solution.py
@@ -288,8 +288,19 @@
     sets = [[near[step] for step in range(ring)]]
     for chip in range(1, chips):
         sets.append(
-            [move(piece, "dp", from_chip, f"chip_{step}") for step, piece in enumerate(sets[-1])]
-        )
+            [
+                None if step == ring - 1 else move(piece, "dp", from_chip, f"chip_{step}")
+                for step, piece in enumerate(sets[-1])
+            ]
+        )
+
+    def last_over_chips(*gates):
+        for chip in range(1, chips):
+            normed_rows, grads = sets[chip - 1][-1]
+            name = f"chip_{ring - 1}"
+            grads = send(after(grads, *gates), "dp", from_chip, f"{name}_grad")
+            normed_rows = send(after(normed_rows, *gates), "dp", from_chip, f"{name}_normed")
+            sets[chip][-1] = (normed_rows, grads)
 
     groups, own_grads = [], []
     arrivals = [
@@ -299,15 +310,18 @@
     if len(arrivals) > 1:
         arrivals[:2] = [sorted(arrivals[0] + arrivals[1])]
     last = len(arrivals) - 1
-    totals = []
+    totals, hold = [], []
     for at, entries in enumerate(arrivals):
         gates = []
+        if any(sets[chip][step] is None for chip, step in entries):
+            last_over_chips(*hold)
         if last > 1 and at >= last - 1:
-            early = [sets[chip][step][1] for chip, step in entries]
+            early = [sets[chip][step][1] for chip, step in entries] if hold else []
             totals = weights_call(
                 [(after(own, *early), *others) for own, *others in groups[:-1]], totals, 1.0
             )
             gates = [totals[0]]
+            hold = hold or gates
             groups = groups[-1:]
         own_steps = [step for chip, step in entries if chip == 0]
         back_types = [jnp.bfloat16 if step in (half, half + 1) else jnp.float32 for step in own_steps]
@@ -331,7 +345,7 @@
     def chain(steps, pairs, name):
         travelling = None
         for step in steps:
-            total = own_grads[step]
+            total = after(own_grads[step], *hold)
             if travelling is not None:
                 total = (total + travelling.astype(jnp.float32)).astype(jnp.bfloat16)
             travelling = send(total.astype(jnp.bfloat16), "tensor", pairs, f"{name}_{step}")

time: 232 us -> 202 us (0.87)
  waiting for transfers between devices: 51.4 us -> 24.8 us
    ppermute x22, waiting for transfers between devices: 51.4 us -> 24.8 us  [send(): return lax.ppermute(one, axis, pairs)]
  transfers between devices with their start and end apart: 22 -> 22, of which waited for: 5 -> 4; matrix products, arithmetic and copies ran while one was open for 4% -> 4% of each run, Pallas kernels for 50% -> 58%
where the time goes in v7:
time: 202 us; the launch traced here: 201 us
  Pallas kernels  129 us (64%)
  starting transfers between devices  30.3 us (15%)
  waiting for transfers between devices  24.8 us (12%)
  other arithmetic  8.24 us (4%)
  between operations  4.71 us (2%)
  local copies, waits for them, and re-layouts  3.79 us (2%)
    pallas_call x4, Pallas kernels, group_call(): pl.pallas_call(functools.partial(group_kernel, limit_at=limit_at, owned=o...  93 us
    pallas_call x3, Pallas kernels, weights_call(): pl.pallas_call(functools.partial(weights_kernel, groups=len(acts), scale=...  36.2 us
    ppermute x22, starting transfers between devices, send(): return lax.ppermute(one, axis, pairs)  30.3 us
    ppermute x22, waiting for transfers between devices, send(): return lax.ppermute(one, axis, pairs)  24.8 us
  transfers between devices with their start and end apart: 22, of which 4 were waited for; matrix products, arithmetic and copies ran while one was open for 4% of the time, Pallas kernels for 58%

profile of v7, /device:TPU:0, one launch (start us, length us, event | category | flops | bytes accessed | tf_op | source)
XLA Modules:
  0.0 201.0 jit_solution(13236415463298953560)
XLA Ops:
  1.5 3.0 %collective-permute-start = (s32[516]{0:T(1024)S(1)}, s32[516]{0:T(1024)S(1)}, u32[]{:S(2)}, u32[]{:S(2)}) collective-permute-start(s32[516]{0:T(1024)S(1)} %pad_add_fusion), channel_id=1, source_target_pairs={{8,0},{12,4},{0,8},{4,12},{9,1},{13,5},{1,9},{5,13},{10,2},{14,6},... | collective-permute-start | bytes 6200 | tf_op jit(solution)/shard_map/chip_levels/ppermute | solution.py:262
  4.5 3.6 %collective-permute-start.3 = (bf16[128,3072]{1,0:T(8,128)(2,1)}, bf16[128,3072]{1,0:T(8,128)(2,1)S(1)}, u32[]{:S(2)}, u32[]{:S(2)}) collective-permute-start(bf16[128,3072]{1,0:T(8,128)(2,1)} %refs_3_.1), channel_id=1, source_target_pairs={{1,0},{2,1},{3,2},{0,3},{5,4},{6,5},{7,6},{4,7},{9,8},{10,9},{11,1... | collective-permute-start | bytes 2359304 | tf_op jit(solution)/shard_map/ring_1_grad/ppermute | solution.py:262
  9.4 1.5 fusion.11
  11.3 2.2 %collective-permute-start.1 = (bf16[128,3072]{1,0:T(8,128)(2,1)S(1)}, bf16[128,3072]{1,0:T(8,128)(2,1)}, u32[]{:S(2)}, u32[]{:S(2)}) collective-permute-start(bf16[128,3072]{1,0:T(8,128)(2,1)S(1)} %fusion.5.refs_0_), channel_id=1, source_target_pairs={{1,0},{2,1},{3,2},{0,3},{5,4},{6,5},{7,6},{4,7},{9,8},{10,9},{11,1... | collective-permute-start | bytes 2359304 | tf_op jit(solution)/shard_map/ring_1_normed/ppermute | solution.py:262
  13.4 1.5 collective-permute-start.4
  22.7 3.6 %collective-permute-done.3.refs_4_ = bf16[128,3072]{1,0:T(8,128)(2,1)S(1)} collective-permute-done((bf16[128,3072]{1,0:T(8,128)(2,1)}, bf16[128,3072]{1,0:T(8,128)(2,1)S(1)}, u32[]{:S(2)}, u32[]{:S(2)}) %collective-permute-start.3) | collective-permute-done | bytes 786464 | tf_op jit(solution)/shard_map/ring_1_grad/ppermute | solution.py:262
  26.9 4.2 %collective-permute-start.8 = (bf16[128,3072]{1,0:T(8,128)(2,1)S(1)}, bf16[128,3072]{1,0:T(8,128)(2,1)S(1)}, u32[]{:S(2)}, u32[]{:S(2)}) collective-permute-start(bf16[128,3072]{1,0:T(8,128)(2,1)S(1)} %collective-permute-done.3.refs_4_), channel_id=1, source_target_pairs={{1,0},{2,1},{3,2},{0,3},{5,4},{6,5},{7,6},{4,7},{9,8},{10,9},{11,1... | collective-permute-start | bytes 2359304 | tf_op jit(solution)/shard_map/ring_2_grad/ppermute | solution.py:262
  31.1 12.0 %collective-permute-done.1.refs_1_ = bf16[128,3072]{1,0:T(8,128)(2,1)} collective-permute-done((bf16[128,3072]{1,0:T(8,128)(2,1)S(1)}, bf16[128,3072]{1,0:T(8,128)(2,1)}, u32[]{:S(2)}, u32[]{:S(2)}) %collective-permute-start.1) | collective-permute-done | bytes 786464 | tf_op jit(solution)/shard_map/ring_1_normed/ppermute | solution.py:262
  43.6 4.4 %collective-permute-start.6 = (bf16[128,3072]{1,0:T(8,128)(2,1)}, bf16[128,3072]{1,0:T(8,128)(2,1)S(1)}, u32[]{:S(2)}, u32[]{:S(2)}) collective-permute-start(bf16[128,3072]{1,0:T(8,128)(2,1)} %collective-permute-done.1.refs_1_), channel_id=1, source_target_pairs={{1,0},{2,1},{3,2},{0,3},{5,4},{6,5},{7,6},{4,7},{9,8},{10,9},{11,1... | collective-permute-start | bytes 2359304 | tf_op jit(solution)/shard_map/ring_2_normed/ppermute | solution.py:262
  48.0 2.8 %collective-permute-done.2.refs_2_ = bf16[128,3072]{1,0:T(8,128)(2,1)} collective-permute-done((bf16[128,3072]{1,0:T(8,128)(2,1)S(1)}, bf16[128,3072]{1,0:T(8,128)(2,1)}, u32[]{:S(2)}, u32[]{:S(2)}) %collective-permute-start.2) | collective-permute-done | bytes 786464 | tf_op jit(solution)/shard_map/chip_0_normed/ppermute | solution.py:262
  50.9 30.8 %group.4 = (bf16[2,384,3840]{2,1,0:T(8,128)(2,1)}, bf16[2,384,768]{2,1,0:T(8,128)(2,1)}, f32[128,3072]{1,0:T(8,128)}, f32[128,3072]{1,0:T(8,128)}) custom-call(s32[3]{0:T(128)S(1)} %pad_add_fusion.1.spots, bf16[128,3072]{1,0:T(8,128)(2,1)S(1)} %fusion.5.refs_0_, bf16[128,3072]{1,0:T(8,128)(2,1)} %collective-permute-done.1.refs_1_, ...), custom_call_target="tpu_custom_call" | custom-call | flops 57982058496 | tf_op jit(solution)/shard_map/group_0/group/pallas_call | solution.py:162
  81.8 1.6 collective-permute-start.15
  84.8 23.0 %group.5 = (bf16[2,256,3840]{2,1,0:T(8,128)(2,1)}, bf16[2,256,768]{2,1,0:T(8,128)(2,1)S(1)}, bf16[128,3072]{1,0:T(8,128)(2,1)}) custom-call(s32[3]{0:T(128)S(1)} %pad_add_fusion.1.spots, bf16[128,3072]{1,0:T(8,128)(2,1)S(1)} %collective-permute-done.6.refs_0_, bf16[128,3072]{1,0:T(8,128)(2,1)S(1)} %collective-permute-done.7.refs_1_, ...), custom_call_target="tpu_custom_call" | custom-call | flops 108716359680 | tf_op jit(solution)/shard_map/group_1/group/pallas_call | solution.py:162
  107.9 12.1 %weights.3 = (bf16[768,3072]{1,0:T(8,128)(2,1)S(1)}, bf16[3072,768]{1,0:T(8,128)(2,1)}) custom-call(bf16[2,384,3840]{2,1,0:T(8,128)(2,1)} %get-tuple-element.33.refs_0_, bf16[2,384,3840]{2,1,0:T(8,128)(2,1)} %collective-permute-done.5.refs_1_.refs_3_, bf16[2,384,768]{2,1,0:T(8,128)(2,1)S(1)} %copy-done.2, ...), custom_call_target="tpu_custom_call" | custom-call | tf_op jit(solution)/shard_map/weights/pallas_call | solution.py:223
  120.0 2.2 %copy-done = bf16[768,3072]{1,0:T(8,128)(2,1)} copy-done((bf16[768,3072]{1,0:T(8,128)(2,1)}, bf16[768,3072]{1,0:T(8,128)(2,1)S(1)}, u32[]{:S(2)}) %copy-start) | copy-done | bytes 4718616
  122.2 1.6 collective-permute-start.10
  123.8 1.5 collective-permute-start.18
  125.8 23.0 %group.6 = (bf16[2,256,3840]{2,1,0:T(8,128)(2,1)}, bf16[2,256,768]{2,1,0:T(8,128)(2,1)S(1)}, bf16[128,3072]{1,0:T(8,128)(2,1)S(1)}) custom-call(s32[3]{0:T(128)S(1)} %pad_add_fusion.1.spots, bf16[128,3072]{1,0:T(8,128)(2,1)S(1)} %collective-permute-done.12.refs_0_, bf16[128,3072]{1,0:T(8,128)(2,1)S(1)} %collective-permute-done.13.refs_1_, ...), custom_call_target="tpu_custom_call" | custom-call | flops 36238786560 | tf_op jit(solution)/shard_map/group_2/group/pallas_call | solution.py:162
  148.9 2.3 %collective-permute-start.16 = (bf16[128,3072]{1,0:T(8,128)(2,1)S(1)}, bf16[128,3072]{1,0:T(8,128)(2,1)S(1)}, u32[]{:S(2)}, u32[]{:S(2)}) collective-permute-start(bf16[128,3072]{1,0:T(8,128)(2,1)S(1)} %get-tuple-element.41), channel_id=1, source_target_pairs={{1,0},{2,1},{3,2},{0,3},{5,4},{6,5},{7,6},{4,7},{9,8},{10,9},{11,1... | collective-permute-start | bytes 2359304 | tf_op jit(solution)/shard_map/sum_down_3/ppermute | solution.py:262
  151.6 11.1 %weights.4 = (bf16[768,3072]{1,0:T(8,128)(2,1)}, bf16[3072,768]{1,0:T(8,128)(2,1)}) custom-call(bf16[2,256,3840]{2,1,0:T(8,128)(2,1)S(1)} %copy-done.1, bf16[2,256,3840]{2,1,0:T(8,128)(2,1)} %collective-permute-done.19.refs_1_.refs_3_, bf16[2,256,768]{2,1,0:T(8,128)(2,1)S(1)} %get-tuple-element.46.refs_2_, ...), custom_call_target="tpu_custom_call" | custom-call | tf_op jit(solution)/shard_map/weights/pallas_call | solution.py:223
  162.8 16.1 %group.7 = (bf16[2,128,3840]{2,1,0:T(8,128)(2,1)S(1)}, bf16[2,128,768]{2,1,0:T(8,128)(2,1)S(1)}) custom-call(s32[3]{0:T(128)S(1)} %pad_add_fusion.1.spots, bf16[128,3072]{1,0:T(8,128)(2,1)S(1)} %collective-permute-done.20.refs_0_, bf16[128,3072]{1,0:T(8,128)(2,1)S(1)} %collective-permute-done.18.refs_1_, s32[512,1]{1,0:T(8,128)S(1)} %copy.18.refs_6_.refs_4_.refs_2_, ...), custom_call_target="tpu_custom_call" | custom-call | flops 14495514624 | tf_op jit(solution)/shard_map/group_3/group/pallas_call | solution.py:162
  179.5 6.2 %collective-permute-done.11 = bf16[128,3072]{1,0:T(8,128)(2,1)S(1)} collective-permute-done((bf16[128,3072]{1,0:T(8,128)(2,1)S(1)}, bf16[128,3072]{1,0:T(8,128)(2,1)S(1)}, u32[]{:S(2)}, u32[]{:S(2)}) %collective-permute-start.11) | collective-permute-done | bytes 786464 | tf_op jit(solution)/shard_map/sum_up_1/ppermute | solution.py:262
  186.4 1.6 fusion.10
  188.0 12.9 %weights.5 = (bf16[768,3072]{1,0:T(8,128)(2,1)}, bf16[3072,768]{1,0:T(8,128)(2,1)}) custom-call(bf16[2,256,3840]{2,1,0:T(8,128)(2,1)} %get-tuple-element.42.refs_0_, bf16[2,256,3840]{2,1,0:T(8,128)(2,1)} %collective-permute-done.17.refs_1_.refs_5_, bf16[2,128,3840]{2,1,0:T(8,128)(2,1)S(1)} %get-tuple-element.51.refs_2_, ...), custom_call_target="tpu_custom_call" | custom-call | tf_op jit(solution)/shard_map/weights/pallas_call | solution.py:223
  (79 shorter events, 11.4 us)
Async XLA Ops:
  1.5 6.6 %collective-permute-start = (s32[516]{0:T(1024)S(1)}, s32[516]{0:T(1024)S(1)}, u32[]{:S(2)}, u32[]{:S(2)}) collective-permute-start(s32[516]{0:T(1024)S(1)} %pad_add_fusion), channel_id=1, source_target_pairs={{8,0},{12,4},{0,8},{4,12},{9,1},{13,5},{1,9},{5,13},{10,2},{14,6},... | collective-permute-start | bytes 6200 | tf_op jit(solution)/shard_map/chip_levels/ppermute | solution.py:262
  4.5 21.9 %collective-permute-start.3 = (bf16[128,3072]{1,0:T(8,128)(2,1)}, bf16[128,3072]{1,0:T(8,128)(2,1)S(1)}, u32[]{:S(2)}, u32[]{:S(2)}) collective-permute-start(bf16[128,3072]{1,0:T(8,128)(2,1)} %refs_3_.1), channel_id=1, source_target_pairs={{1,0},{2,1},{3,2},{0,3},{5,4},{6,5},{7,6},{4,7},{9,8},{10,9},{11,1... | collective-permute-start | bytes 2359304 | tf_op jit(solution)/shard_map/ring_1_grad/ppermute | solution.py:262
  11.3 31.9 %collective-permute-start.1 = (bf16[128,3072]{1,0:T(8,128)(2,1)S(1)}, bf16[128,3072]{1,0:T(8,128)(2,1)}, u32[]{:S(2)}, u32[]{:S(2)}) collective-permute-start(bf16[128,3072]{1,0:T(8,128)(2,1)S(1)} %fusion.5.refs_0_), channel_id=1, source_target_pairs={{1,0},{2,1},{3,2},{0,3},{5,4},{6,5},{7,6},{4,7},{9,8},{10,9},{11,1... | collective-permute-start | bytes 2359304 | tf_op jit(solution)/shard_map/ring_1_normed/ppermute | solution.py:262
  13.4 30.2 %collective-permute-start.4 = (bf16[128,3072]{1,0:T(8,128)(2,1)S(1)}, bf16[128,3072]{1,0:T(8,128)(2,1)}, u32[]{:S(2)}, u32[]{:S(2)}) collective-permute-start(bf16[128,3072]{1,0:T(8,128)(2,1)S(1)} %copy-done.3), channel_id=1, source_target_pairs={{8,0},{12,4},{0,8},{4,12},{9,1},{13,5},{1,9},{5,13},{10,2},{14,6},... | collective-permute-start | bytes 2359304 | tf_op jit(solution)/shard_map/chip_0_grad/ppermute | solution.py:262
  14.9 35.9 %collective-permute-start.2 = (bf16[128,3072]{1,0:T(8,128)(2,1)S(1)}, bf16[128,3072]{1,0:T(8,128)(2,1)}, u32[]{:S(2)}, u32[]{:S(2)}) collective-permute-start(bf16[128,3072]{1,0:T(8,128)(2,1)S(1)} %fusion.5.refs_0_), channel_id=1, source_target_pairs={{8,0},{12,4},{0,8},{4,12},{9,1},{13,5},{1,9},{5,13},{10,2},{14,6},... | collective-permute-start | bytes 2359304 | tf_op jit(solution)/shard_map/chip_0_normed/ppermute | solution.py:262
  26.4 57.0 %collective-permute-start.9 = (bf16[128,3072]{1,0:T(8,128)(2,1)S(1)}, bf16[128,3072]{1,0:T(8,128)(2,1)S(1)}, u32[]{:S(2)}, u32[]{:S(2)}) collective-permute-start(bf16[128,3072]{1,0:T(8,128)(2,1)S(1)} %collective-permute-done.3.refs_4_), channel_id=1, source_target_pairs={{8,0},{12,4},{0,8},{4,12},{9,1},{13,5},{1,9},{5,13},{10,2},{14,6},... | collective-permute-start | bytes 2359304 | tf_op jit(solution)/shard_map/chip_1_grad/ppermute | solution.py:262
  26.9 54.9 %collective-permute-start.8 = (bf16[128,3072]{1,0:T(8,128)(2,1)S(1)}, bf16[128,3072]{1,0:T(8,128)(2,1)S(1)}, u32[]{:S(2)}, u32[]{:S(2)}) collective-permute-start(bf16[128,3072]{1,0:T(8,128)(2,1)S(1)} %collective-permute-done.3.refs_4_), channel_id=1, source_target_pairs={{1,0},{2,1},{3,2},{0,3},{5,4},{6,5},{7,6},{4,7},{9,8},{10,9},{11,1... | collective-permute-start | bytes 2359304 | tf_op jit(solution)/shard_map/ring_2_grad/ppermute | solution.py:262
  43.1 41.2 %collective-permute-start.7 = (bf16[128,3072]{1,0:T(8,128)(2,1)}, bf16[128,3072]{1,0:T(8,128)(2,1)S(1)}, u32[]{:S(2)}, u32[]{:S(2)}) collective-permute-start(bf16[128,3072]{1,0:T(8,128)(2,1)} %collective-permute-done.1.refs_1_), channel_id=1, source_target_pairs={{8,0},{12,4},{0,8},{4,12},{9,1},{13,5},{1,9},{5,13},{10,2},{14,6},... | collective-permute-start | bytes 2359304 | tf_op jit(solution)/shard_map/chip_1_normed/ppermute | solution.py:262
  43.6 40.1 %collective-permute-start.6 = (bf16[128,3072]{1,0:T(8,128)(2,1)}, bf16[128,3072]{1,0:T(8,128)(2,1)S(1)}, u32[]{:S(2)}, u32[]{:S(2)}) collective-permute-start(bf16[128,3072]{1,0:T(8,128)(2,1)} %collective-permute-done.1.refs_1_), channel_id=1, source_target_pairs={{1,0},{2,1},{3,2},{0,3},{5,4},{6,5},{7,6},{4,7},{9,8},{10,9},{11,1... | collective-permute-start | bytes 2359304 | tf_op jit(solution)/shard_map/ring_2_normed/ppermute | solution.py:262
  81.7 26.2 %copy-start.2 = (bf16[2,384,768]{2,1,0:T(8,128)(2,1)S(1)}, bf16[2,384,768]{2,1,0:T(8,128)(2,1)}, u32[]{:S(2)}) copy-start(bf16[2,384,768]{2,1,0:T(8,128)(2,1)} %get-tuple-element.34.refs_2_) | copy-start | bytes 3538948
  81.7 26.1 %collective-permute-start.5 = (bf16[2,384,3840]{2,1,0:T(8,128)(2,1)}, bf16[2,384,3840]{2,1,0:T(8,128)(2,1)}, u32[]{:S(2)}, u32[]{:S(2)}) collective-permute-start(bf16[2,384,3840]{2,1,0:T(8,128)(2,1)} %get-tuple-element.33.refs_0_), channel_id=1, source_target_pairs={{0,4},{4,0},{8,12},{12,8},{1,5},{5,1},{9,13},{13,9},{2,6},{6,2},{1... | collective-permute-start | bytes 17694728 | tf_op jit(solution)/shard_map/swap_0/ppermute | solution.py:262
  81.8 43.5 %collective-permute-start.15 = (bf16[128,3072]{1,0:T(8,128)(2,1)S(1)}, bf16[128,3072]{1,0:T(8,128)(2,1)S(1)}, u32[]{:S(2)}, u32[]{:S(2)}) collective-permute-start(bf16[128,3072]{1,0:T(8,128)(2,1)S(1)} %collective-permute-done.8.refs_2_), channel_id=1, source_target_pairs={{8,0},{12,4},{0,8},{4,12},{9,1},{13,5},{1,9},{5,13},{10,2},{14,6},... | collective-permute-start | bytes 2359304 | tf_op jit(solution)/shard_map/chip_2_grad/ppermute | solution.py:262
  83.3 38.8 %collective-permute-start.14 = (bf16[128,3072]{1,0:T(8,128)(2,1)S(1)}, bf16[128,3072]{1,0:T(8,128)(2,1)S(1)}, u32[]{:S(2)}, u32[]{:S(2)}) collective-permute-start(bf16[128,3072]{1,0:T(8,128)(2,1)S(1)} %collective-permute-done.8.refs_2_), channel_id=1, source_target_pairs={{1,0},{2,1},{3,2},{0,3},{5,4},{6,5},{7,6},{4,7},{9,8},{10,9},{11,1... | collective-permute-start | bytes 2359304 | tf_op jit(solution)/shard_map/ring_3_grad/ppermute | solution.py:262
  83.8 42.0 %collective-permute-start.13 = (bf16[128,3072]{1,0:T(8,128)(2,1)S(1)}, bf16[128,3072]{1,0:T(8,128)(2,1)S(1)}, u32[]{:S(2)}, u32[]{:S(2)}) collective-permute-start(bf16[128,3072]{1,0:T(8,128)(2,1)S(1)} %collective-permute-done.6.refs_0_), channel_id=1, source_target_pairs={{8,0},{12,4},{0,8},{4,12},{9,1},{13,5},{1,9},{5,13},{10,2},{14,6},... | collective-permute-start | bytes 2359304 | tf_op jit(solution)/shard_map/chip_2_normed/ppermute | solution.py:262
  84.3 37.8 %collective-permute-start.12 = (bf16[128,3072]{1,0:T(8,128)(2,1)S(1)}, bf16[128,3072]{1,0:T(8,128)(2,1)S(1)}, u32[]{:S(2)}, u32[]{:S(2)}) collective-permute-start(bf16[128,3072]{1,0:T(8,128)(2,1)S(1)} %collective-permute-done.6.refs_0_), channel_id=1, source_target_pairs={{1,0},{2,1},{3,2},{0,3},{5,4},{6,5},{7,6},{4,7},{9,8},{10,9},{11,1... | collective-permute-start | bytes 2359304 | tf_op jit(solution)/shard_map/ring_3_normed/ppermute | solution.py:262
  107.8 43.8 %collective-permute-start.19 = (bf16[2,256,3840]{2,1,0:T(8,128)(2,1)}, bf16[2,256,3840]{2,1,0:T(8,128)(2,1)}, u32[]{:S(2)}, u32[]{:S(2)}) collective-permute-start(bf16[2,256,3840]{2,1,0:T(8,128)(2,1)} %get-tuple-element.45.refs_0_), channel_id=1, source_target_pairs={{0,4},{4,0},{8,12},{12,8},{1,5},{5,1},{9,13},{13,9},{2,6},{6,2},{1... | collective-permute-start | bytes 11796488 | tf_op jit(solution)/shard_map/swap_1/ppermute | solution.py:262
  122.2 29.0 %copy-start.6 = (f32[128,3072]{1,0:T(8,128)S(1)}, f32[128,3072]{1,0:T(8,128)}, u32[]{:S(2)}) copy-start(f32[128,3072]{1,0:T(8,128)} %get-tuple-element.36) | copy-start | bytes 4718596
  122.2 29.0 %collective-permute-start.10 = (bf16[128,3072]{1,0:T(8,128)(2,1)}, bf16[128,3072]{1,0:T(8,128)(2,1)S(1)}, u32[]{:S(2)}, u32[]{:S(2)}) collective-permute-start(bf16[128,3072]{1,0:T(8,128)(2,1)} %get-tuple-element.38), channel_id=1, source_target_pairs={{0,1},{1,2},{2,3},{3,0},{4,5},{5,6},{6,7},{7,4},{8,9},{9,10},{10,1... | collective-permute-start | bytes 2359304 | tf_op jit(solution)/shard_map/sum_up_2/ppermute | solution.py:262
  123.8 27.5 %collective-permute-start.18 = (bf16[128,3072]{1,0:T(8,128)(2,1)S(1)}, bf16[128,3072]{1,0:T(8,128)(2,1)S(1)}, u32[]{:S(2)}, u32[]{:S(2)}) collective-permute-start(bf16[128,3072]{1,0:T(8,128)(2,1)S(1)} %collective-permute-done.14.refs_2_), channel_id=1, source_target_pairs={{8,0},{12,4},{0,8},{4,12},{9,1},{13,5},{1,9},{5,13},{10,2},{14,6},... | collective-permute-start | bytes 2359304 | tf_op jit(solution)/shard_map/chip_3_grad/ppermute | solution.py:262
  125.3 37.5 %collective-permute-start.20 = (bf16[128,3072]{1,0:T(8,128)(2,1)S(1)}, bf16[128,3072]{1,0:T(8,128)(2,1)S(1)}, u32[]{:S(2)}, u32[]{:S(2)}) collective-permute-start(bf16[128,3072]{1,0:T(8,128)(2,1)S(1)} %collective-permute-done.12.refs_0_), channel_id=1, source_target_pairs={{8,0},{12,4},{0,8},{4,12},{9,1},{13,5},{1,9},{5,13},{10,2},{14,6},... | collective-permute-start | bytes 2359304 | tf_op jit(solution)/shard_map/chip_3_normed/ppermute | solution.py:262
  148.9 30.6 %collective-permute-start.16 = (bf16[128,3072]{1,0:T(8,128)(2,1)S(1)}, bf16[128,3072]{1,0:T(8,128)(2,1)S(1)}, u32[]{:S(2)}, u32[]{:S(2)}) collective-permute-start(bf16[128,3072]{1,0:T(8,128)(2,1)S(1)} %get-tuple-element.41), channel_id=1, source_target_pairs={{1,0},{2,1},{3,2},{0,3},{5,4},{6,5},{7,6},{4,7},{9,8},{10,9},{11,1... | collective-permute-start | bytes 2359304 | tf_op jit(solution)/shard_map/sum_down_3/ppermute | solution.py:262
  151.1 36.9 %collective-permute-start.17 = (bf16[2,256,3840]{2,1,0:T(8,128)(2,1)}, bf16[2,256,3840]{2,1,0:T(8,128)(2,1)}, u32[]{:S(2)}, u32[]{:S(2)}) collective-permute-start(bf16[2,256,3840]{2,1,0:T(8,128)(2,1)} %get-tuple-element.42.refs_0_), channel_id=1, source_target_pairs={{0,4},{4,0},{8,12},{12,8},{1,5},{5,1},{9,13},{13,9},{2,6},{6,2},{1... | collective-permute-start | bytes 11796488 | tf_op jit(solution)/shard_map/swap_2/ppermute | solution.py:262
  151.3 34.4 %collective-permute-start.11 = (bf16[128,3072]{1,0:T(8,128)(2,1)S(1)}, bf16[128,3072]{1,0:T(8,128)(2,1)S(1)}, u32[]{:S(2)}, u32[]{:S(2)}) collective-permute-start(bf16[128,3072]{1,0:T(8,128)(2,1)S(1)} %add_convert_fusion), channel_id=1, source_target_pairs={{0,1},{1,2},{2,3},{3,0},{4,5},{5,6},{6,7},{7,4},{8,9},{9,10},{10,1... | collective-permute-start | bytes 2359304 | tf_op jit(solution)/shard_map/sum_up_1/ppermute | solution.py:262
  178.9 9.1 %collective-permute-start.21 = (bf16[2,128,3840]{2,1,0:T(8,128)(2,1)S(1)}, bf16[2,128,3840]{2,1,0:T(8,128)(2,1)S(1)}, u32[]{:S(2)}, u32[]{:S(2)}) collective-permute-start(bf16[2,128,3840]{2,1,0:T(8,128)(2,1)S(1)} %get-tuple-element.51.refs_2_), channel_id=1, source_target_pairs={{0,4},{4,0},{8,12},{12,8},{1,5},{5,1},{9,13},{13,9},{2,6},{6,2},{1... | collective-permute-start | bytes 5898248 | tf_op jit(solution)/shard_map/swap_3/ppermute | solution.py:262
  (14 other events, 229.9 us)

commit v8 on v7

--- a/solution.py
+++ b/solution.py
@@ -13,7 +13,7 @@
 NORM_EPS = 1e-06
 VMEM_LIMIT = 48 * 1024 * 1024
 WORK = 3.0
-WEIGHTS = {1: 3.0}
+WEIGHTS = {1: 3.0, 3: 3.0}
 
 
 def gelu_parts(pre_act):
@@ -265,7 +265,7 @@
     for _ in range(1, chips):
         level_sets.append(send(level_sets[-1], "dp", from_chip, "chip_levels"))
 
-    as_float = after(inputs, *level_sets[1:]).astype(jnp.float32)
+    as_float = inputs.astype(jnp.float32)
     row_mean = jnp.mean(as_float, axis=1, keepdims=True)
     centred = as_float - row_mean
     row_scale = lax.rsqrt(jnp.mean(centred * centred, axis=1, keepdims=True) + NORM_EPS)
@@ -294,15 +294,25 @@
             ]
         )
 
-    def last_over_chips(*gates):
+    def last_over_chips(early, gates):
         for chip in range(1, chips):
             normed_rows, grads = sets[chip - 1][-1]
             name = f"chip_{ring - 1}"
             grads = send(after(grads, *gates), "dp", from_chip, f"{name}_grad")
-            normed_rows = send(after(normed_rows, *gates), "dp", from_chip, f"{name}_normed")
+            normed_rows = send(after(normed_rows, *early), "dp", from_chip, f"{name}_normed")
             sets[chip][-1] = (normed_rows, grads)
 
-    groups, own_grads = [], []
+    groups, own_grads, hops, hold = [], [], [], []
+
+    def chain(steps, pairs, name):
+        travelling = None
+        for step in steps:
+            total = after(own_grads[step], *hold)
+            if travelling is not None:
+                total = (total + travelling.astype(jnp.float32)).astype(jnp.bfloat16)
+            travelling = send(total.astype(jnp.bfloat16), "tensor", pairs, f"{name}_{step}")
+        return travelling
+
     arrivals = [
         [(chip, slot - chip) for chip in range(chips) if 0 <= slot - chip < ring]
         for slot in range(ring + chips - 1)
@@ -310,19 +320,17 @@
     if len(arrivals) > 1:
         arrivals[:2] = [sorted(arrivals[0] + arrivals[1])]
     last = len(arrivals) - 1
-    totals, hold = [], []
+    totals = []
     for at, entries in enumerate(arrivals):
         gates = []
-        if any(sets[chip][step] is None for chip, step in entries):
-            last_over_chips(*hold)
-        if last > 1 and at >= last - 1:
-            early = [sets[chip][step][1] for chip, step in entries] if hold else []
-            totals = weights_call(
-                [(after(own, *early), *others) for own, *others in groups[:-1]], totals, 1.0
-            )
-            gates = [totals[0]]
-            hold = hold or gates
+        if at == len(arrivals) - 2 and at > 1:
+            totals = weights_call(groups[:-1], [], 1.0)
+            gates = hold = [totals[0]]
             groups = groups[-1:]
+        if not hold and at > 1:
+            hold = [own_cols]
+        if any(sets[chip][step] is None for chip, step in arrivals[min(at + 1, last)]):
+            last_over_chips([own_cols], hold)
         own_steps = [step for chip, step in entries if chip == 0]
         back_types = [jnp.bfloat16 if step in (half, half + 1) else jnp.float32 for step in own_steps]
         with jax.named_scope(f"group_{at}"):
@@ -340,26 +348,19 @@
                 WEIGHTS.get(at, 1.0),
             )
         own_grads.extend(back)
-        groups.append((act, own_cols, send(act, "dp", swap_cores, f"swap_{at}")))
-
-    def chain(steps, pairs, name):
-        travelling = None
-        for step in steps:
-            total = after(own_grads[step], *hold)
-            if travelling is not None:
-                total = (total + travelling.astype(jnp.float32)).astype(jnp.bfloat16)
-            travelling = send(total.astype(jnp.bfloat16), "tensor", pairs, f"{name}_{step}")
-        return travelling
-
-    own_grad = own_grads[0].astype(jnp.float32)
+        if at == last and ring > 2:
+            hops.append(chain(range(half + 1, ring), from_next, "sum_down"))
+        groups.append((act, own_cols, send(after(act, *hops), "dp", swap_cores, f"swap_{at}")))
+
     if ring > 1:
-        own_grad = own_grad + chain(range(half, 0, -1), from_last, "sum_up").astype(jnp.float32)
-    if ring > 2:
-        own_grad = own_grad + chain(range(half + 1, ring), from_next, "sum_down").astype(jnp.float32)
+        hops.append(chain(range(half, 0, -1), from_last, "sum_up"))
+    grad_weight_in, grad_weight_out = weights_call(groups, totals, 1.0 / blocks)
+    own_grad = after(own_grads[0], grad_weight_in).astype(jnp.float32)
+    for hop in hops:
+        own_grad = own_grad + hop.astype(jnp.float32)
     branch_grad = norm_backward(own_grad, standard, row_scale, norm_gain)
     grad_input = (grad_out.astype(jnp.float32) + branch_grad).astype(jnp.bfloat16)
 
-    grad_weight_in, grad_weight_out = weights_call(groups, totals, 1.0 / blocks)
     return (grad_input, grad_weight_in, grad_weight_out)
 
 

time: 202 us -> 199 us (0.985)
  Pallas kernels: 129 us -> 122 us
  waiting for transfers between devices: 24.8 us -> 28.2 us
  starting transfers between devices: 30.3 us -> 27.5 us
  local copies, waits for them, and re-layouts: 3.79 us -> 6.55 us
    pallas_call x3 -> x2, Pallas kernels: 36.2 us -> 29.9 us  [weights_call(): pl.pallas_call(functools.partial(weights_kernel, groups=len(acts), scale=...]
    ppermute x22, waiting for transfers between devices: 24.8 us -> 28.2 us  [send(): return lax.ppermute(one, axis, pairs)]
    ppermute x22, starting transfers between devices: 30.3 us -> 27.5 us  [send(): return lax.ppermute(one, axis, pairs)]
    unnamed x32 -> x34, local copies, waits for them, and re-layouts: 2.25 us -> 5.01 us
  transfers between devices with their start and end apart: 22 -> 22, of which waited for: 4 -> 4; matrix products, arithmetic and copies ran while one was open for 4% -> 3% of each run, Pallas kernels for 58% -> 62%
where the time goes in v8:
time: 199 us
  Pallas kernels  122 us (61%)
  waiting for transfers between devices  28.2 us (14%)
  starting transfers between devices  27.5 us (14%)
  other arithmetic  9.28 us (5%)
  local copies, waits for them, and re-layouts  6.55 us (3%)
  between operations  4.68 us (2%)
    pallas_call x4, Pallas kernels, group_call(): pl.pallas_call(functools.partial(group_kernel, limit_at=limit_at, owned=o...  92.5 us
    pallas_call x2, Pallas kernels, weights_call(): pl.pallas_call(functools.partial(weights_kernel, groups=len(acts), scale=...  29.9 us
    ppermute x22, waiting for transfers between devices, send(): return lax.ppermute(one, axis, pairs)  28.2 us
    ppermute x22, starting transfers between devices, send(): return lax.ppermute(one, axis, pairs)  27.5 us
    unnamed x34, local copies, waits for them, and re-layouts  5.01 us
  transfers between devices with their start and end apart: 22, of which 4 were waited for; matrix products, arithmetic and copies ran while one was open for 3% of the time, Pallas kernels for 62%

profile of v8, /device:TPU:0, one launch (start us, length us, event | category | flops | bytes accessed | tf_op | source)
XLA Modules:
  0.0 198.6 jit_solution(8173652542383118492)
XLA Ops:
  0.7 1.4 convert_reduce_fusion
  2.1 1.5 fusion.11
  4.0 3.0 %collective-permute-start.1 = (bf16[128,3072]{1,0:T(8,128)(2,1)S(1)}, bf16[128,3072]{1,0:T(8,128)(2,1)}, u32[]{:S(2)}, u32[]{:S(2)}) collective-permute-start(bf16[128,3072]{1,0:T(8,128)(2,1)S(1)} %fusion.5.refs_0_), channel_id=1, source_target_pairs={{8,0},{12,4},{0,8},{4,12},{9,1},{13,5},{1,9},{5,13},{10,2},{14,6},... | collective-permute-start | bytes 2359304 | tf_op jit(solution)/shard_map/chip_0_normed/ppermute | solution.py:262
  7.0 3.6 %collective-permute-start = (bf16[128,3072]{1,0:T(8,128)(2,1)S(1)}, bf16[128,3072]{1,0:T(8,128)(2,1)}, u32[]{:S(2)}, u32[]{:S(2)}) collective-permute-start(bf16[128,3072]{1,0:T(8,128)(2,1)S(1)} %fusion.5.refs_0_), channel_id=1, source_target_pairs={{1,0},{2,1},{3,2},{0,3},{5,4},{6,5},{7,6},{4,7},{9,8},{10,9},{11,1... | collective-permute-start | bytes 2359304 | tf_op jit(solution)/shard_map/ring_1_normed/ppermute | solution.py:262
  11.6 1.6 collective-permute-start.4
  16.5 25.0 %collective-permute-done.4 = s32[516]{0:T(1024)S(1)} collective-permute-done((s32[516]{0:T(1024)S(1)}, s32[516]{0:T(1024)S(1)}, u32[]{:S(2)}, u32[]{:S(2)}) %collective-permute-start.4) | collective-permute-done | bytes 2096 | tf_op jit(solution)/shard_map/chip_levels/ppermute | solution.py:262
  45.5 1.8 collective-permute-start.6
  47.3 3.6 %collective-permute-start.5 = (bf16[128,3072]{1,0:T(8,128)(2,1)}, bf16[128,3072]{1,0:T(8,128)(2,1)S(1)}, u32[]{:S(2)}, u32[]{:S(2)}) collective-permute-start(bf16[128,3072]{1,0:T(8,128)(2,1)} %collective-permute-done.refs_1_), channel_id=1, source_target_pairs={{1,0},{2,1},{3,2},{0,3},{5,4},{6,5},{7,6},{4,7},{9,8},{10,9},{11,1... | collective-permute-start | bytes 2359304 | tf_op jit(solution)/shard_map/ring_2_normed/ppermute | solution.py:262
  52.0 30.8 %group.4 = (bf16[2,384,3840]{2,1,0:T(8,128)(2,1)}, bf16[2,384,768]{2,1,0:T(8,128)(2,1)}, f32[128,3072]{1,0:T(8,128)}, f32[128,3072]{1,0:T(8,128)}) custom-call(s32[3]{0:T(128)S(1)} %pad_add_fusion.1.spots, bf16[128,3072]{1,0:T(8,128)(2,1)S(1)} %fusion.5.refs_0_, bf16[128,3072]{1,0:T(8,128)(2,1)} %collective-permute-done.refs_1_, ...), custom_call_target="tpu_custom_call" | custom-call | flops 57982058496 | tf_op jit(solution)/shard_map/group_0/group/pallas_call | solution.py:162
  82.9 1.5 collective-permute-start.12
  85.4 3.1 %collective-permute-start.13 = (bf16[128,3072]{1,0:T(8,128)(2,1)S(1)}, bf16[128,3072]{1,0:T(8,128)(2,1)S(1)}, u32[]{:S(2)}, u32[]{:S(2)}) collective-permute-start(bf16[128,3072]{1,0:T(8,128)(2,1)S(1)} %collective-permute-done.7.refs_2_), channel_id=1, source_target_pairs={{1,0},{2,1},{3,2},{0,3},{5,4},{6,5},{7,6},{4,7},{9,8},{10,9},{11,1... | collective-permute-start | bytes 2359304 | tf_op jit(solution)/shard_map/ring_3_grad/ppermute | solution.py:262
  88.5 22.8 %group.5 = (bf16[2,256,3840]{2,1,0:T(8,128)(2,1)}, bf16[2,256,768]{2,1,0:T(8,128)(2,1)S(1)}, bf16[128,3072]{1,0:T(8,128)(2,1)S(1)}) custom-call(s32[3]{0:T(128)S(1)} %pad_add_fusion.1.spots, bf16[128,3072]{1,0:T(8,128)(2,1)S(1)} %collective-permute-done.5.refs_0_, bf16[128,3072]{1,0:T(8,128)(2,1)S(1)} %collective-permute-done.6.refs_1_, ...), custom_call_target="tpu_custom_call" | custom-call | flops 108716359680 | tf_op jit(solution)/shard_map/group_1/group/pallas_call | solution.py:162
  111.4 1.6 collective-permute-start.16
  112.9 12.0 %weights.2 = (bf16[768,3072]{1,0:T(8,128)(2,1)S(1)}, bf16[3072,768]{1,0:T(8,128)(2,1)}) custom-call(bf16[2,384,3840]{2,1,0:T(8,128)(2,1)} %get-tuple-element.29.refs_0_, bf16[2,384,3840]{2,1,0:T(8,128)(2,1)} %collective-permute-done.10.refs_1_.refs_3_, bf16[2,384,768]{2,1,0:T(8,128)(2,1)S(1)} %copy-done.1, ...), custom_call_target="tpu_custom_call" | custom-call | tf_op jit(solution)/shard_map/weights/pallas_call | solution.py:223
  125.0 2.1 %copy-done = bf16[768,3072]{1,0:T(8,128)(2,1)} copy-done((bf16[768,3072]{1,0:T(8,128)(2,1)}, bf16[768,3072]{1,0:T(8,128)(2,1)S(1)}, u32[]{:S(2)}) %copy-start) | copy-done | bytes 4718616
  127.7 22.9 %group.6 = (bf16[2,256,3840]{2,1,0:T(8,128)(2,1)}, bf16[2,256,768]{2,1,0:T(8,128)(2,1)S(1)}, bf16[128,3072]{1,0:T(8,128)(2,1)S(1)}) custom-call(s32[3]{0:T(128)S(1)} %pad_add_fusion.1.spots, bf16[128,3072]{1,0:T(8,128)(2,1)S(1)} %collective-permute-done.11.refs_0_, bf16[128,3072]{1,0:T(8,128)(2,1)S(1)} %collective-permute-done.12.refs_1_, ...), custom_call_target="tpu_custom_call" | custom-call | flops 36238786560 | tf_op jit(solution)/shard_map/group_2/group/pallas_call | solution.py:162
  150.5 3.8 %collective-permute-start.18 = (bf16[128,3072]{1,0:T(8,128)(2,1)S(1)}, bf16[128,3072]{1,0:T(8,128)(2,1)S(1)}, u32[]{:S(2)}, u32[]{:S(2)}) collective-permute-start(bf16[128,3072]{1,0:T(8,128)(2,1)S(1)} %get-tuple-element.39), channel_id=1, source_target_pairs={{1,0},{2,1},{3,2},{0,3},{5,4},{6,5},{7,6},{4,7},{9,8},{10,9},{11,1... | collective-permute-start | bytes 2359304 | tf_op jit(solution)/shard_map/sum_down_3/ppermute | solution.py:262
  154.3 16.0 %group.7 = (bf16[2,128,3840]{2,1,0:T(8,128)(2,1)S(1)}, bf16[2,128,768]{2,1,0:T(8,128)(2,1)S(1)}) custom-call(s32[3]{0:T(128)S(1)} %pad_add_fusion.1.spots, bf16[128,3072]{1,0:T(8,128)(2,1)S(1)} %collective-permute-done.16.refs_0_, bf16[128,3072]{1,0:T(8,128)(2,1)S(1)} %collective-permute-done.17.refs_1_, s32[512,1]{1,0:T(8,128)S(1)} %copy.18.refs_6_.refs_4_.refs_2_, ...), custom_call_target="tpu_custom_call" | custom-call | flops 43486543872 | tf_op jit(solution)/shard_map/group_3/group/pallas_call | solution.py:162
  170.9 0.9 copy-done.7
  171.8 1.8 add_convert_fusion
  173.9 1.9 collective-permute-done.19.refs_5_.refs_11_
  175.8 1.9 copy-done.5
  177.7 17.8 %weights.3 = (bf16[768,3072]{1,0:T(8,128)(2,1)}, bf16[3072,768]{1,0:T(8,128)(2,1)}) custom-call(bf16[2,256,3840]{2,1,0:T(8,128)(2,1)} %get-tuple-element.28.refs_0_, bf16[2,256,3840]{2,1,0:T(8,128)(2,1)} %collective-permute-done.9.refs_1_.refs_7_, bf16[2,256,3840]{2,1,0:T(8,128)(2,1)} %get-tuple-element.33.refs_2_, bf16[2,256,3840]{2,1,0:T(8,128)(2,1)} %copy-done.5, ...), custom_call_target="tpu_custom_call" | custom-call | tf_op jit(solution)/shard_map/weights/pallas_call | solution.py:223
  197.1 1.6 fusion.10
  (80 shorter events, 10.0 us)
Async XLA Ops:
  3.6 41.6 %copy-start.15 = (f32[128]{0:T(128)}, f32[128]{0:T(128)S(1)}, u32[]{:S(2)}) copy-start(f32[128]{0:T(128)S(1)} %add_rsqrt_fusion) | copy-start | bytes 1540
  4.0 47.5 %collective-permute-start.1 = (bf16[128,3072]{1,0:T(8,128)(2,1)S(1)}, bf16[128,3072]{1,0:T(8,128)(2,1)}, u32[]{:S(2)}, u32[]{:S(2)}) collective-permute-start(bf16[128,3072]{1,0:T(8,128)(2,1)S(1)} %fusion.5.refs_0_), channel_id=1, source_target_pairs={{8,0},{12,4},{0,8},{4,12},{9,1},{13,5},{1,9},{5,13},{10,2},{14,6},... | collective-permute-start | bytes 2359304 | tf_op jit(solution)/shard_map/chip_0_normed/ppermute | solution.py:262
  7.0 38.5 %collective-permute-start = (bf16[128,3072]{1,0:T(8,128)(2,1)S(1)}, bf16[128,3072]{1,0:T(8,128)(2,1)}, u32[]{:S(2)}, u32[]{:S(2)}) collective-permute-start(bf16[128,3072]{1,0:T(8,128)(2,1)S(1)} %fusion.5.refs_0_), channel_id=1, source_target_pairs={{1,0},{2,1},{3,2},{0,3},{5,4},{6,5},{7,6},{4,7},{9,8},{10,9},{11,1... | collective-permute-start | bytes 2359304 | tf_op jit(solution)/shard_map/ring_1_normed/ppermute | solution.py:262
  10.6 40.4 %collective-permute-start.2 = (bf16[128,3072]{1,0:T(8,128)(2,1)S(1)}, bf16[128,3072]{1,0:T(8,128)(2,1)S(1)}, u32[]{:S(2)}, u32[]{:S(2)}) collective-permute-start(bf16[128,3072]{1,0:T(8,128)(2,1)S(1)} %copy-done.2), channel_id=1, source_target_pairs={{1,0},{2,1},{3,2},{0,3},{5,4},{6,5},{7,6},{4,7},{9,8},{10,9},{11,1... | collective-permute-start | bytes 2359304 | tf_op jit(solution)/shard_map/ring_1_grad/ppermute | solution.py:262
  11.1 40.9 %collective-permute-start.3 = (bf16[128,3072]{1,0:T(8,128)(2,1)S(1)}, bf16[128,3072]{1,0:T(8,128)(2,1)}, u32[]{:S(2)}, u32[]{:S(2)}) collective-permute-start(bf16[128,3072]{1,0:T(8,128)(2,1)S(1)} %copy-done.2), channel_id=1, source_target_pairs={{8,0},{12,4},{0,8},{4,12},{9,1},{13,5},{1,9},{5,13},{10,2},{14,6},... | collective-permute-start | bytes 2359304 | tf_op jit(solution)/shard_map/chip_0_grad/ppermute | solution.py:262
  11.6 29.9 %collective-permute-start.4 = (s32[516]{0:T(1024)S(1)}, s32[516]{0:T(1024)S(1)}, u32[]{:S(2)}, u32[]{:S(2)}) collective-permute-start(s32[516]{0:T(1024)S(1)} %pad_add_fusion), channel_id=1, source_target_pairs={{8,0},{12,4},{0,8},{4,12},{9,1},{13,5},{1,9},{5,13},{10,2},{14,6},... | collective-permute-start | bytes 6200 | tf_op jit(solution)/shard_map/chip_levels/ppermute | solution.py:262
  45.5 38.9 %collective-permute-start.6 = (bf16[128,3072]{1,0:T(8,128)(2,1)}, bf16[128,3072]{1,0:T(8,128)(2,1)S(1)}, u32[]{:S(2)}, u32[]{:S(2)}) collective-permute-start(bf16[128,3072]{1,0:T(8,128)(2,1)} %collective-permute-done.refs_1_), channel_id=1, source_target_pairs={{8,0},{12,4},{0,8},{4,12},{9,1},{13,5},{1,9},{5,13},{10,2},{14,6},... | collective-permute-start | bytes 2359304 | tf_op jit(solution)/shard_map/chip_1_normed/ppermute | solution.py:262
  47.3 35.5 %collective-permute-start.5 = (bf16[128,3072]{1,0:T(8,128)(2,1)}, bf16[128,3072]{1,0:T(8,128)(2,1)S(1)}, u32[]{:S(2)}, u32[]{:S(2)}) collective-permute-start(bf16[128,3072]{1,0:T(8,128)(2,1)} %collective-permute-done.refs_1_), channel_id=1, source_target_pairs={{1,0},{2,1},{3,2},{0,3},{5,4},{6,5},{7,6},{4,7},{9,8},{10,9},{11,1... | collective-permute-start | bytes 2359304 | tf_op jit(solution)/shard_map/ring_2_normed/ppermute | solution.py:262
  51.0 34.5 %collective-permute-start.8 = (bf16[128,3072]{1,0:T(8,128)(2,1)S(1)}, bf16[128,3072]{1,0:T(8,128)(2,1)S(1)}, u32[]{:S(2)}, u32[]{:S(2)}) collective-permute-start(bf16[128,3072]{1,0:T(8,128)(2,1)S(1)} %collective-permute-done.2.refs_4_), channel_id=1, source_target_pairs={{8,0},{12,4},{0,8},{4,12},{9,1},{13,5},{1,9},{5,13},{10,2},{14,6},... | collective-permute-start | bytes 2359304 | tf_op jit(solution)/shard_map/chip_1_grad/ppermute | solution.py:262
  51.5 33.3 %collective-permute-start.7 = (bf16[128,3072]{1,0:T(8,128)(2,1)S(1)}, bf16[128,3072]{1,0:T(8,128)(2,1)S(1)}, u32[]{:S(2)}, u32[]{:S(2)}) collective-permute-start(bf16[128,3072]{1,0:T(8,128)(2,1)S(1)} %collective-permute-done.2.refs_4_), channel_id=1, source_target_pairs={{1,0},{2,1},{3,2},{0,3},{5,4},{6,5},{7,6},{4,7},{9,8},{10,9},{11,1... | collective-permute-start | bytes 2359304 | tf_op jit(solution)/shard_map/ring_2_grad/ppermute | solution.py:262
  82.8 30.2 %copy-start.1 = (bf16[2,384,768]{2,1,0:T(8,128)(2,1)S(1)}, bf16[2,384,768]{2,1,0:T(8,128)(2,1)}, u32[]{:S(2)}) copy-start(bf16[2,384,768]{2,1,0:T(8,128)(2,1)} %get-tuple-element.30.refs_2_) | copy-start | bytes 3538948
  82.8 28.6 %collective-permute-start.10 = (bf16[2,384,3840]{2,1,0:T(8,128)(2,1)}, bf16[2,384,3840]{2,1,0:T(8,128)(2,1)}, u32[]{:S(2)}, u32[]{:S(2)}) collective-permute-start(bf16[2,384,3840]{2,1,0:T(8,128)(2,1)} %get-tuple-element.29.refs_0_), channel_id=1, source_target_pairs={{0,4},{4,0},{8,12},{12,8},{1,5},{5,1},{9,13},{13,9},{2,6},{6,2},{1... | collective-permute-start | bytes 17694728 | tf_op jit(solution)/shard_map/swap_0/ppermute | solution.py:262
  82.9 44.8 %collective-permute-start.12 = (bf16[128,3072]{1,0:T(8,128)(2,1)S(1)}, bf16[128,3072]{1,0:T(8,128)(2,1)S(1)}, u32[]{:S(2)}, u32[]{:S(2)}) collective-permute-start(bf16[128,3072]{1,0:T(8,128)(2,1)S(1)} %collective-permute-done.5.refs_0_), channel_id=1, source_target_pairs={{8,0},{12,4},{0,8},{4,12},{9,1},{13,5},{1,9},{5,13},{10,2},{14,6},... | collective-permute-start | bytes 2359304 | tf_op jit(solution)/shard_map/chip_2_normed/ppermute | solution.py:262
  84.4 26.9 %collective-permute-start.11 = (bf16[128,3072]{1,0:T(8,128)(2,1)S(1)}, bf16[128,3072]{1,0:T(8,128)(2,1)S(1)}, u32[]{:S(2)}, u32[]{:S(2)}) collective-permute-start(bf16[128,3072]{1,0:T(8,128)(2,1)S(1)} %collective-permute-done.5.refs_0_), channel_id=1, source_target_pairs={{1,0},{2,1},{3,2},{0,3},{5,4},{6,5},{7,6},{4,7},{9,8},{10,9},{11,1... | collective-permute-start | bytes 2359304 | tf_op jit(solution)/shard_map/ring_3_normed/ppermute | solution.py:262
  84.9 42.8 %collective-permute-start.14 = (bf16[128,3072]{1,0:T(8,128)(2,1)S(1)}, bf16[128,3072]{1,0:T(8,128)(2,1)S(1)}, u32[]{:S(2)}, u32[]{:S(2)}) collective-permute-start(bf16[128,3072]{1,0:T(8,128)(2,1)S(1)} %collective-permute-done.7.refs_2_), channel_id=1, source_target_pairs={{8,0},{12,4},{0,8},{4,12},{9,1},{13,5},{1,9},{5,13},{10,2},{14,6},... | collective-permute-start | bytes 2359304 | tf_op jit(solution)/shard_map/chip_2_grad/ppermute | solution.py:262
  85.4 41.7 %collective-permute-start.13 = (bf16[128,3072]{1,0:T(8,128)(2,1)S(1)}, bf16[128,3072]{1,0:T(8,128)(2,1)S(1)}, u32[]{:S(2)}, u32[]{:S(2)}) collective-permute-start(bf16[128,3072]{1,0:T(8,128)(2,1)S(1)} %collective-permute-done.7.refs_2_), channel_id=1, source_target_pairs={{1,0},{2,1},{3,2},{0,3},{5,4},{6,5},{7,6},{4,7},{9,8},{10,9},{11,1... | collective-permute-start | bytes 2359304 | tf_op jit(solution)/shard_map/ring_3_grad/ppermute | solution.py:262
  111.4 62.5 %collective-permute-start.9 = (bf16[2,256,3840]{2,1,0:T(8,128)(2,1)}, bf16[2,256,3840]{2,1,0:T(8,128)(2,1)}, u32[]{:S(2)}, u32[]{:S(2)}) collective-permute-start(bf16[2,256,3840]{2,1,0:T(8,128)(2,1)} %get-tuple-element.28.refs_0_), channel_id=1, source_target_pairs={{0,4},{4,0},{8,12},{12,8},{1,5},{5,1},{9,13},{13,9},{2,6},{6,2},{1... | collective-permute-start | bytes 11796488 | tf_op jit(solution)/shard_map/swap_1/ppermute | solution.py:262
  111.4 43.0 %collective-permute-start.16 = (bf16[128,3072]{1,0:T(8,128)(2,1)S(1)}, bf16[128,3072]{1,0:T(8,128)(2,1)S(1)}, u32[]{:S(2)}, u32[]{:S(2)}) collective-permute-start(bf16[128,3072]{1,0:T(8,128)(2,1)S(1)} %collective-permute-done.11.refs_0_), channel_id=1, source_target_pairs={{8,0},{12,4},{0,8},{4,12},{9,1},{13,5},{1,9},{5,13},{10,2},{14,6},... | collective-permute-start | bytes 2359304 | tf_op jit(solution)/shard_map/chip_3_normed/ppermute | solution.py:262
  127.1 27.2 %collective-permute-start.17 = (bf16[128,3072]{1,0:T(8,128)(2,1)S(1)}, bf16[128,3072]{1,0:T(8,128)(2,1)S(1)}, u32[]{:S(2)}, u32[]{:S(2)}) collective-permute-start(bf16[128,3072]{1,0:T(8,128)(2,1)S(1)} %collective-permute-done.13.refs_2_), channel_id=1, source_target_pairs={{8,0},{12,4},{0,8},{4,12},{9,1},{13,5},{1,9},{5,13},{10,2},{14,6},... | collective-permute-start | bytes 2359304 | tf_op jit(solution)/shard_map/chip_3_grad/ppermute | solution.py:262
  127.6 44.2 %collective-permute-start.20 = (bf16[128,3072]{1,0:T(8,128)(2,1)S(1)}, bf16[128,3072]{1,0:T(8,128)(2,1)}, u32[]{:S(2)}, u32[]{:S(2)}) collective-permute-start(bf16[128,3072]{1,0:T(8,128)(2,1)S(1)} %get-tuple-element.49), channel_id=1, source_target_pairs={{0,1},{1,2},{2,3},{3,0},{4,5},{5,6},{6,7},{7,4},{8,9},{9,10},{10,1... | collective-permute-start | bytes 2359304 | tf_op jit(solution)/shard_map/sum_up_2/ppermute | solution.py:262
  150.5 20.4 %collective-permute-start.18 = (bf16[128,3072]{1,0:T(8,128)(2,1)S(1)}, bf16[128,3072]{1,0:T(8,128)(2,1)S(1)}, u32[]{:S(2)}, u32[]{:S(2)}) collective-permute-start(bf16[128,3072]{1,0:T(8,128)(2,1)S(1)} %get-tuple-element.39), channel_id=1, source_target_pairs={{1,0},{2,1},{3,2},{0,3},{5,4},{6,5},{7,6},{4,7},{9,8},{10,9},{11,1... | collective-permute-start | bytes 2359304 | tf_op jit(solution)/shard_map/sum_down_3/ppermute | solution.py:262
  154.3 21.4 %collective-permute-start.15 = (bf16[2,256,3840]{2,1,0:T(8,128)(2,1)}, bf16[2,256,3840]{2,1,0:T(8,128)(2,1)S(1)}, u32[]{:S(2)}, u32[]{:S(2)}) collective-permute-start(bf16[2,256,3840]{2,1,0:T(8,128)(2,1)} %get-tuple-element.33.refs_2_), channel_id=1, source_target_pairs={{0,4},{4,0},{8,12},{12,8},{1,5},{5,1},{9,13},{13,9},{2,6},{6,2},{1... | collective-permute-start | bytes 11796488 | tf_op jit(solution)/shard_map/swap_2/ppermute | solution.py:262
  171.8 4.0 %collective-permute-start.19 = (bf16[2,128,3840]{2,1,0:T(8,128)(2,1)S(1)}, bf16[2,128,3840]{2,1,0:T(8,128)(2,1)S(1)}, u32[]{:S(2)}, u32[]{:S(2)}) collective-permute-start(bf16[2,128,3840]{2,1,0:T(8,128)(2,1)S(1)} %get-tuple-element.40.refs_4_), channel_id=1, source_target_pairs={{0,4},{4,0},{8,12},{12,8},{1,5},{5,1},{9,13},{13,9},{2,6},{6,2},{1... | collective-permute-start | bytes 5898248 | tf_op jit(solution)/shard_map/swap_3/ppermute | solution.py:262
  173.6 22.8 %collective-permute-start.21 = (bf16[128,3072]{1,0:T(8,128)(2,1)S(1)}, bf16[128,3072]{1,0:T(8,128)(2,1)S(1)}, u32[]{:S(2)}, u32[]{:S(2)}) collective-permute-start(bf16[128,3072]{1,0:T(8,128)(2,1)S(1)} %add_convert_fusion), channel_id=1, source_target_pairs={{0,1},{1,2},{2,3},{3,0},{4,5},{5,6},{6,7},{7,4},{8,9},{9,10},{10,1... | collective-permute-start | bytes 2359304 | tf_op jit(solution)/shard_map/sum_up_1/ppermute | solution.py:262
  (15 other events, 163.0 us)

commit v9 on v8

--- a/solution.py
+++ b/solution.py
@@ -13,7 +13,7 @@
 NORM_EPS = 1e-06
 VMEM_LIMIT = 48 * 1024 * 1024
 WORK = 3.0
-WEIGHTS = {1: 3.0, 3: 3.0}
+WEIGHTS = {2: 3.0, 4: 3.0}
 
 
 def gelu_parts(pre_act):
@@ -61,12 +61,13 @@
     return wanted
 
 
-def group_kernel(spots, *refs, limit_at, owned, share, tiles):
+def group_kernel(spots, *refs, limit_at, owned, extra, share, tiles):
     pieces, sets = len(limit_at), 1 + max(at for at, _ in limit_at)
     normed_refs = refs[:pieces]
     grad_refs = refs[pieces : 2 * pieces]
     limit_refs = refs[2 * pieces : 2 * pieces + sets]
-    in_ref, out_ref, acts_ref, own_ref, *rest = refs[2 * pieces + sets :]
+    extra_refs = refs[2 * pieces + sets : 2 * pieces + sets + extra]
+    in_ref, out_ref, acts_ref, own_ref, *rest = refs[2 * pieces + sets + extra :]
     tile = pl.program_id(0)
 
     def columns(target, first):
@@ -94,10 +95,12 @@
 
     @pl.when(tile < tiles)
     def _():
-        group_tile(spots[0], rows_ref, limit, in_ref, out_ref, acts_ref, rest, owned, tiles)
-
-
-def group_tile(first, rows_ref, limit, in_ref, out_ref, acts_ref, rest, owned, tiles):
+        group_tile(spots[0], rows_ref, limit, in_ref, out_ref, acts_ref, rest, owned * size, extra_refs, tiles)
+
+
+def group_tile(
+    first, rows_ref, limit, in_ref, out_ref, acts_ref, rest, own_rows, extra_refs, tiles
+):
     tile = pl.program_id(0)
     units = in_ref.shape[1]
     width = 256 if units % 256 == 0 else units
@@ -115,10 +118,11 @@
         gelu_value, gelu_slope = gelu_parts(pre_act)
         acts_ref[0, :, span] = jnp.where(mask, grad_hidden * gelu_slope, 0.0).astype(jnp.bfloat16)
         acts_ref[1, :, span] = jnp.where(mask, gelu_value, 0.0).astype(jnp.bfloat16)
-    if owned:
+    if rest:
         back_refs, total_ref = rest[:-1], rest[-1]
+        parts = [acts_ref[0, :own_rows, :]] if own_rows else []
         term = lax.dot_general(
-            acts_ref[0, : total_ref.shape[0], :],
+            jnp.concatenate(parts + [ref[0] for ref in extra_refs]),
             in_ref[...],
             (((1,), (1,)), ((), ())),
             preferred_element_type=jnp.float32,
@@ -140,12 +144,12 @@
 
 
 def group_call(
-    spots, normed, grads, limits, limit_at, weight_in, weight_out, tile, share, back_types, weight
+    spots, normed, grads, limits, limit_at, weight_in, weight_out, tile, share, back_types, extra, weight
 ):
     features, units = weight_in.shape
     piece_rows = normed[0].shape[0]
     rows = piece_rows * len(normed)
-    owned = len(back_types)
+    owned = len(back_types) - len(extra)
     tiles = units // tile
     whole = lambda shape: pl.BlockSpec(shape, lambda i, spots: (0,) * len(shape))
     out_shape = [
@@ -161,25 +165,35 @@
         out_specs.append(whole((piece_rows, features)))
     return pl.pallas_call(
         functools.partial(
-            group_kernel, limit_at=limit_at, owned=owned, share=share, tiles=tiles
+            group_kernel,
+            limit_at=limit_at,
+            owned=owned,
+            extra=len(extra),
+            share=share,
+            tiles=tiles,
         ),
         grid_spec=pltpu.PrefetchScalarGridSpec(
             num_scalar_prefetch=1,
             grid=(tiles + share // tile,),
             in_specs=[whole(one.shape) for one in (*normed, *grads, *limits)]
             + [
+                pl.BlockSpec((1, piece_rows, tile), lambda i, spots: (0, 0, jnp.minimum(i, tiles - 1)))
+                for _ in extra
+            ]
+            + [
                 pl.BlockSpec((features, tile), lambda i, spots: (0, jnp.minimum(i, tiles - 1))),
                 pl.BlockSpec((tile, features), lambda i, spots: (jnp.minimum(i, tiles - 1), 0)),
             ],
             out_specs=out_specs,
-            scratch_shapes=[pltpu.VMEM((owned * piece_rows, features), jnp.float32)] * bool(owned)
+            scratch_shapes=[pltpu.VMEM((len(back_types) * piece_rows, features), jnp.float32)]
+            * bool(back_types)
             + [pltpu.VMEM((2, rows, features), jnp.bfloat16)],
         ),
         out_shape=out_shape,
         compiler_params=pltpu.CompilerParams(vmem_limit_bytes=VMEM_LIMIT),
-        cost_estimate=work_of(weight * (4 * rows + 2 * owned * piece_rows) * units * features),
+        cost_estimate=work_of(weight * (4 * rows + 2 * len(back_types) * piece_rows) * units * features),
         name="group",
-    )(spots, *normed, *grads, *limits, weight_in, weight_out)
+    )(spots, *normed, *grads, *limits, *extra, weight_in, weight_out)
 
 
 def weights_kernel(*refs, groups, scale, started):
@@ -261,10 +275,6 @@
         with jax.named_scope(name):
             return lax.ppermute(one, axis, pairs)
 
-    level_sets = [jnp.concatenate([level_order, level_counts[0]])]
-    for _ in range(1, chips):
-        level_sets.append(send(level_sets[-1], "dp", from_chip, "chip_levels"))
-
     as_float = inputs.astype(jnp.float32)
     row_mean = jnp.mean(as_float, axis=1, keepdims=True)
     centred = as_float - row_mean
@@ -272,7 +282,10 @@
     standard = centred * row_scale
     normed = (standard * norm_gain[None, :]).astype(jnp.bfloat16)
 
-    limits = [unit_limits(one[:-4], one[-4:], place * rows, unit_total) for one in level_sets]
+    limits = [unit_limits(level_order, level_counts[0], place * rows, unit_total)]
+    for _ in range(1, chips):
+        limits.append(send(limits[-1], "dp", from_chip, "chip_limits"))
+
     spots = jnp.stack([place * unit_local, block * share, (block ^ 1) * share]).astype(jnp.int32)
 
     kinds = ("normed", "grad")
@@ -284,15 +297,20 @@
 
     near = {0: (normed, grad_out)}
     for step in range(1, ring):
-        near[step] = move(near[step - 1], "tensor", from_next, f"ring_{step}")
+        near[step] = None if 2 < step == ring - 1 else move(near[step - 1], "tensor", from_next, f"ring_{step}")
     sets = [[near[step] for step in range(ring)]]
     for chip in range(1, chips):
         sets.append(
             [
-                None if step == ring - 1 else move(piece, "dp", from_chip, f"chip_{step}")
+                None if step == ring - 1 or 1 < step == ring - 2 else move(piece, "dp", from_chip, f"chip_{step}")
                 for step, piece in enumerate(sets[-1])
             ]
         )
+
+    def second_over_chips(*gates):
+        for chip in range(1, chips):
+            sets[chip][-2] = move(sets[chip - 1][-2], "dp", from_chip, f"chip_{ring - 2}", *gates)
+        sets[0][-1] = move(sets[0][-2], "tensor", from_next, f"ring_{ring - 1}", *gates)
 
     def last_over_chips(early, gates):
         for chip in range(1, chips):
@@ -302,7 +320,7 @@
             normed_rows = send(after(normed_rows, *early), "dp", from_chip, f"{name}_normed")
             sets[chip][-1] = (normed_rows, grads)
 
-    groups, own_grads, hops, hold = [], [], [], []
+    groups, own_grads, hops, hold = [], {}, [], []
 
     def chain(steps, pairs, name):
         travelling = None
@@ -317,8 +335,6 @@
         [(chip, slot - chip) for chip in range(chips) if 0 <= slot - chip < ring]
         for slot in range(ring + chips - 1)
     ]
-    if len(arrivals) > 1:
-        arrivals[:2] = [sorted(arrivals[0] + arrivals[1])]
     last = len(arrivals) - 1
     totals = []
     for at, entries in enumerate(arrivals):
@@ -332,6 +348,12 @@
         if any(sets[chip][step] is None for chip, step in arrivals[min(at + 1, last)]):
             last_over_chips([own_cols], hold)
         own_steps = [step for chip, step in entries if chip == 0]
+        extra = []
+        if at == 1 and ring > 2:
+            own_steps, later = [], own_steps
+            gates = [groups[0][1]]
+        elif at == 2 and ring > 2:
+            own_steps, extra = own_steps + later, [groups[1][0]]
         back_types = [jnp.bfloat16 if step in (half, half + 1) else jnp.float32 for step in own_steps]
         with jax.named_scope(f"group_{at}"):
             act, own_cols, *back = group_call(
@@ -345,11 +367,14 @@
                 tile,
                 share,
                 back_types,
+                extra,
                 WEIGHTS.get(at, 1.0),
             )
-        own_grads.extend(back)
+        own_grads.update(zip(own_steps, back))
         if at == last and ring > 2:
             hops.append(chain(range(half + 1, ring), from_next, "sum_down"))
+        if at == 1 and ring > 3:
+            second_over_chips(own_cols, groups[0][2])
         groups.append((act, own_cols, send(after(act, *hops), "dp", swap_cores, f"swap_{at}")))
 
     if ring > 1:

time: 199 us -> 203 us (1.020)
  Pallas kernels: 122 us -> 133 us
  other arithmetic: 9.28 us -> 6.74 us
    pallas_call x4 -> x5, Pallas kernels: 92.5 us -> 104 us  [group_call(): pl.pallas_call(functools.partial(group_kernel, limit_at=limit_at, owned=o...]
    ppermute x22 -> x23, waiting for transfers between devices: 28.2 us -> 26.8 us  [send(): return lax.ppermute(one, axis, pairs)]
    unnamed x34 -> x32, local copies, waits for them, and re-layouts: 5.01 us -> 4.08 us
    ppermute x22 -> x23, starting transfers between devices: 27.5 us -> 28.2 us  [send(): return lax.ppermute(one, axis, pairs)]
  transfers between devices with their start and end apart: 22 -> 23, of which waited for: 4 -> 5; matrix products, arithmetic and copies ran while one was open for 3% -> 1% of each run, Pallas kernels for 62% -> 66%
where the time goes in v9:
time: 203 us
  Pallas kernels  133 us (66%)
  starting transfers between devices  28.2 us (14%)
  waiting for transfers between devices  26.8 us (13%)
  other arithmetic  6.74 us (3%)
  local copies, waits for them, and re-layouts  4.82 us (2%)
  between operations  2.81 us (1%)
    pallas_call x5, Pallas kernels, group_call(): pl.pallas_call(functools.partial(group_kernel, limit_at=limit_at, owned=o...  104 us
    pallas_call x2, Pallas kernels, weights_call(): pl.pallas_call(functools.partial(weights_kernel, groups=len(acts), scale=...  29.4 us
    ppermute x23, starting transfers between devices, send(): return lax.ppermute(one, axis, pairs)  28.2 us
    ppermute x23, waiting for transfers between devices, send(): return lax.ppermute(one, axis, pairs)  26.8 us
    unnamed x32, local copies, waits for them, and re-layouts  4.08 us
  transfers between devices with their start and end apart: 23, of which 5 were waited for; matrix products, arithmetic and copies ran while one was open for 1% of the time, Pallas kernels for 66%

profile of v9, /device:TPU:0, one launch (start us, length us, event | category | flops | bytes accessed | tf_op | source)
XLA Modules:
  0.0 202.6 jit_solution(16123674589194300507)
XLA Ops:
  0.7 1.4 convert_reduce_fusion
  2.1 1.5 fusion.11
  4.0 3.0 %collective-permute-start.7 = (bf16[128,3072]{1,0:T(8,128)(2,1)S(1)}, bf16[128,3072]{1,0:T(8,128)(2,1)}, u32[]{:S(2)}, u32[]{:S(2)}) collective-permute-start(bf16[128,3072]{1,0:T(8,128)(2,1)S(1)} %fusion.5.refs_0_), channel_id=1, source_target_pairs={{8,0},{12,4},{0,8},{4,12},{9,1},{13,5},{1,9},{5,13},{10,2},{14,6},... | collective-permute-start | bytes 2359304 | tf_op jit(solution)/shard_map/chip_0_normed/ppermute | solution.py:276
  7.0 3.6 %collective-permute-start = (bf16[128,3072]{1,0:T(8,128)(2,1)S(1)}, bf16[128,3072]{1,0:T(8,128)(2,1)S(1)}, u32[]{:S(2)}, u32[]{:S(2)}) collective-permute-start(bf16[128,3072]{1,0:T(8,128)(2,1)S(1)} %fusion.5.refs_0_), channel_id=1, source_target_pairs={{1,0},{2,1},{3,2},{0,3},{5,4},{6,5},{7,6},{4,7},{9,8},{10,9},{11,1... | collective-permute-start | bytes 2359304 | tf_op jit(solution)/shard_map/ring_1_normed/ppermute | solution.py:276
  15.3 1.6 collective-permute-start.6
  17.0 20.9 %group.5 = (bf16[2,128,3840]{2,1,0:T(8,128)(2,1)S(1)}, bf16[2,128,768]{2,1,0:T(8,128)(2,1)S(1)}, f32[128,3072]{1,0:T(8,128)S(1)}) custom-call(s32[3]{0:T(128)S(1)} %pad_add_fusion.spots, bf16[128,3072]{1,0:T(8,128)(2,1)S(1)} %fusion.5.refs_0_, bf16[128,3072]{1,0:T(8,128)(2,1)S(1)} %copy-done, s32[512,1]{1,0:T(8,128)S(1)} %copy.16.refs_2_.refs_4_, ...), custom_call_target="tpu_custom_call" | custom-call | flops 21743271936 | tf_op jit(solution)/shard_map/group_0/group/pallas_call | solution.py:166
  37.8 9.3 %collective-permute-done.6.refs_5_.refs_3_ = s32[512,1]{1,0:T(8,128)} collective-permute-done((s32[512,1]{1,0:T(8,128)S(1)}, s32[512,1]{1,0:T(8,128)}, u32[]{:S(2)}, u32[]{:S(2)}) %collective-permute-start.6) | collective-permute-done | bytes 2080 | tf_op jit(solution)/shard_map/chip_limits/ppermute | solution.py:276
  47.1 1.7 collective-permute-start.2
  48.9 3.6 %collective-permute-start.1 = (bf16[128,3072]{1,0:T(8,128)(2,1)S(1)}, bf16[128,3072]{1,0:T(8,128)(2,1)S(1)}, u32[]{:S(2)}, u32[]{:S(2)}) collective-permute-start(bf16[128,3072]{1,0:T(8,128)(2,1)S(1)} %collective-permute-done.refs_0_), channel_id=1, source_target_pairs={{1,0},{2,1},{3,2},{0,3},{5,4},{6,5},{7,6},{4,7},{9,8},{10,9},{11,1... | collective-permute-start | bytes 2359304 | tf_op jit(solution)/shard_map/ring_2_normed/ppermute | solution.py:276
  53.5 18.9 %group.6 = (bf16[2,256,3840]{2,1,0:T(8,128)(2,1)}, bf16[2,256,768]{2,1,0:T(8,128)(2,1)S(1)}) custom-call(s32[3]{0:T(128)S(1)} %pad_add_fusion.spots, bf16[128,3072]{1,0:T(8,128)(2,1)S(1)} %collective-permute-done.refs_0_, bf16[128,3072]{1,0:T(8,128)(2,1)} %collective-permute-done.7.refs_1_, bf16[128,3072]{1,0:T(8,128)(2,1)S(1)} %collective-permute-done.3.refs_2_, ...), custom_call_target="tpu_custom_call" | custom-call | flops 28991029248 | tf_op jit(solution)/shard_map/group_1/group/pallas_call | solution.py:166
  72.4 1.6 collective-permute-start.13
  73.9 12.6 %collective-permute-done.4.refs_2_ = bf16[128,3072]{1,0:T(8,128)(2,1)S(1)} collective-permute-done((bf16[128,3072]{1,0:T(8,128)(2,1)S(1)}, bf16[128,3072]{1,0:T(8,128)(2,1)S(1)}, u32[]{:S(2)}, u32[]{:S(2)}) %collective-permute-start.4) | collective-permute-done | bytes 786464 | tf_op jit(solution)/shard_map/ring_2_grad/ppermute | solution.py:276
  86.5 4.3 %collective-permute-start.12 = (bf16[128,3072]{1,0:T(8,128)(2,1)S(1)}, bf16[128,3072]{1,0:T(8,128)(2,1)}, u32[]{:S(2)}, u32[]{:S(2)}) collective-permute-start(bf16[128,3072]{1,0:T(8,128)(2,1)S(1)} %collective-permute-done.1.refs_0_), channel_id=1, source_target_pairs={{1,0},{2,1},{3,2},{0,3},{5,4},{6,5},{7,6},{4,7},{9,8},{10,9},{11,1... | collective-permute-start | bytes 2359304 | tf_op jit(solution)/shard_map/ring_3_normed/ppermute | solution.py:276
  93.3 25.0 %group.7 = (bf16[2,256,3840]{2,1,0:T(8,128)(2,1)}, bf16[2,256,768]{2,1,0:T(8,128)(2,1)S(1)}, bf16[128,3072]{1,0:T(8,128)(2,1)S(1)}, f32[128,3072]{1,0:T(8,128)}) custom-call(s32[3]{0:T(128)S(1)} %pad_add_fusion.spots, bf16[128,3072]{1,0:T(8,128)(2,1)S(1)} %collective-permute-done.1.refs_0_, bf16[128,3072]{1,0:T(8,128)(2,1)S(1)} %collective-permute-done.2.refs_1_, ...), custom_call_target="tpu_custom_call" | custom-call | flops 130459631616 | tf_op jit(solution)/shard_map/group_2/group/pallas_call | solution.py:166
  118.5 1.6 collective-permute-start.17
  120.0 11.7 %weights.2 = (bf16[768,3072]{1,0:T(8,128)(2,1)}, bf16[3072,768]{1,0:T(8,128)(2,1)}) custom-call(bf16[2,128,3840]{2,1,0:T(8,128)(2,1)S(1)} %get-tuple-element.37.refs_0_, bf16[2,128,3840]{2,1,0:T(8,128)(2,1)S(1)} %collective-permute-done.10.refs_1_.refs_5_, bf16[2,256,3840]{2,1,0:T(8,128)(2,1)} %get-tuple-element.35.refs_6_.refs_2_, ...), custom_call_target="tpu_custom_call" | custom-call | tf_op jit(solution)/shard_map/weights/pallas_call | solution.py:237
  133.1 2.0 collective-permute-start.21
  136.3 23.0 %group.8 = (bf16[2,256,3840]{2,1,0:T(8,128)(2,1)}, bf16[2,256,768]{2,1,0:T(8,128)(2,1)S(1)}, bf16[128,3072]{1,0:T(8,128)(2,1)S(1)}) custom-call(s32[3]{0:T(128)S(1)} %pad_add_fusion.spots, bf16[128,3072]{1,0:T(8,128)(2,1)} %collective-permute-done.12.refs_0_, bf16[128,3072]{1,0:T(8,128)(2,1)S(1)} %copy-done.2, ...), custom_call_target="tpu_custom_call" | custom-call | flops 36238786560 | tf_op jit(solution)/shard_map/group_3/group/pallas_call | solution.py:166
  159.3 1.8 collective-permute-start.19
  161.1 16.0 %group.9 = (bf16[2,128,3840]{2,1,0:T(8,128)(2,1)S(1)}, bf16[2,128,768]{2,1,0:T(8,128)(2,1)S(1)}) custom-call(s32[3]{0:T(128)S(1)} %pad_add_fusion.spots, bf16[128,3072]{1,0:T(8,128)(2,1)S(1)} %collective-permute-done.17.refs_0_, bf16[128,3072]{1,0:T(8,128)(2,1)S(1)} %collective-permute-done.18.refs_1_, s32[512,1]{1,0:T(8,128)S(1)} %copy.16.refs_2_.refs_4_, ...), custom_call_target="tpu_custom_call" | custom-call | flops 43486543872 | tf_op jit(solution)/shard_map/group_4/group/pallas_call | solution.py:166
  177.2 1.2 collective-permute-done.19
  178.9 3.5 %collective-permute-done.20.refs_5_.refs_11_ = bf16[2,128,3840]{2,1,0:T(8,128)(2,1)S(1)} collective-permute-done((bf16[2,128,3840]{2,1,0:T(8,128)(2,1)S(1)}, bf16[2,128,3840]{2,1,0:T(8,128)(2,1)S(1)}, u32[]{:S(2)}, u32[]{:S(2)}) %collective-permute-start.20) | collective-permute-done | bytes 1966112 | tf_op jit(solution)/shard_map/swap_4/ppermute | solution.py:276
  182.3 17.8 %weights.3 = (bf16[768,3072]{1,0:T(8,128)(2,1)}, bf16[3072,768]{1,0:T(8,128)(2,1)}) custom-call(bf16[2,256,3840]{2,1,0:T(8,128)(2,1)} %get-tuple-element.36.refs_0_, bf16[2,256,3840]{2,1,0:T(8,128)(2,1)} %collective-permute-done.9.refs_1_.refs_7_, bf16[2,256,3840]{2,1,0:T(8,128)(2,1)} %get-tuple-element.43.refs_2_, ...), custom_call_target="tpu_custom_call" | custom-call | tf_op jit(solution)/shard_map/weights/pallas_call | solution.py:237
  201.1 1.5 fusion.10
  (76 shorter events, 10.9 us)
Async XLA Ops:
  4.0 44.9 %collective-permute-start.7 = (bf16[128,3072]{1,0:T(8,128)(2,1)S(1)}, bf16[128,3072]{1,0:T(8,128)(2,1)}, u32[]{:S(2)}, u32[]{:S(2)}) collective-permute-start(bf16[128,3072]{1,0:T(8,128)(2,1)S(1)} %fusion.5.refs_0_), channel_id=1, source_target_pairs={{8,0},{12,4},{0,8},{4,12},{9,1},{13,5},{1,9},{5,13},{10,2},{14,6},... | collective-permute-start | bytes 2359304 | tf_op jit(solution)/shard_map/chip_0_normed/ppermute | solution.py:276
  7.0 40.1 %collective-permute-start = (bf16[128,3072]{1,0:T(8,128)(2,1)S(1)}, bf16[128,3072]{1,0:T(8,128)(2,1)S(1)}, u32[]{:S(2)}, u32[]{:S(2)}) collective-permute-start(bf16[128,3072]{1,0:T(8,128)(2,1)S(1)} %fusion.5.refs_0_), channel_id=1, source_target_pairs={{1,0},{2,1},{3,2},{0,3},{5,4},{6,5},{7,6},{4,7},{9,8},{10,9},{11,1... | collective-permute-start | bytes 2359304 | tf_op jit(solution)/shard_map/ring_1_normed/ppermute | solution.py:276
  10.6 42.4 %collective-permute-start.8 = (bf16[128,3072]{1,0:T(8,128)(2,1)S(1)}, bf16[128,3072]{1,0:T(8,128)(2,1)}, u32[]{:S(2)}, u32[]{:S(2)}) collective-permute-start(bf16[128,3072]{1,0:T(8,128)(2,1)S(1)} %copy-done), channel_id=1, source_target_pairs={{8,0},{12,4},{0,8},{4,12},{9,1},{13,5},{1,9},{5,13},{10,2},{14,6},... | collective-permute-start | bytes 2359304 | tf_op jit(solution)/shard_map/chip_0_grad/ppermute | solution.py:276
  11.1 41.3 %collective-permute-start.3 = (bf16[128,3072]{1,0:T(8,128)(2,1)S(1)}, bf16[128,3072]{1,0:T(8,128)(2,1)S(1)}, u32[]{:S(2)}, u32[]{:S(2)}) collective-permute-start(bf16[128,3072]{1,0:T(8,128)(2,1)S(1)} %copy-done), channel_id=1, source_target_pairs={{1,0},{2,1},{3,2},{0,3},{5,4},{6,5},{7,6},{4,7},{9,8},{10,9},{11,1... | collective-permute-start | bytes 2359304 | tf_op jit(solution)/shard_map/ring_1_grad/ppermute | solution.py:276
  15.3 31.8 %collective-permute-start.6 = (s32[512,1]{1,0:T(8,128)S(1)}, s32[512,1]{1,0:T(8,128)}, u32[]{:S(2)}, u32[]{:S(2)}) collective-permute-start(s32[512,1]{1,0:T(8,128)S(1)} %copy.16.refs_2_.refs_4_), channel_id=1, source_target_pairs={{8,0},{12,4},{0,8},{4,12},{9,1},{13,5},{1,9},{5,13},{10,2},{14,6},... | collective-permute-start | bytes 6152 | tf_op jit(solution)/shard_map/chip_limits/ppermute | solution.py:276
  47.1 25.3 %collective-permute-start.10 = (bf16[2,128,3840]{2,1,0:T(8,128)(2,1)S(1)}, bf16[2,128,3840]{2,1,0:T(8,128)(2,1)S(1)}, u32[]{:S(2)}, u32[]{:S(2)}) collective-permute-start(bf16[2,128,3840]{2,1,0:T(8,128)(2,1)S(1)} %get-tuple-element.37.refs_0_), channel_id=1, source_target_pairs={{0,4},{4,0},{8,12},{12,8},{1,5},{5,1},{9,13},{13,9},{2,6},{6,2},{1... | collective-permute-start | bytes 5898248 | tf_op jit(solution)/shard_map/swap_0/ppermute | solution.py:276
  47.1 43.7 %collective-permute-start.2 = (bf16[128,3072]{1,0:T(8,128)(2,1)S(1)}, bf16[128,3072]{1,0:T(8,128)(2,1)S(1)}, u32[]{:S(2)}, u32[]{:S(2)}) collective-permute-start(bf16[128,3072]{1,0:T(8,128)(2,1)S(1)} %collective-permute-done.refs_0_), channel_id=1, source_target_pairs={{8,0},{12,4},{0,8},{4,12},{9,1},{13,5},{1,9},{5,13},{10,2},{14,6},... | collective-permute-start | bytes 2359304 | tf_op jit(solution)/shard_map/chip_1_normed/ppermute | solution.py:276
  48.9 23.5 %collective-permute-start.1 = (bf16[128,3072]{1,0:T(8,128)(2,1)S(1)}, bf16[128,3072]{1,0:T(8,128)(2,1)S(1)}, u32[]{:S(2)}, u32[]{:S(2)}) collective-permute-start(bf16[128,3072]{1,0:T(8,128)(2,1)S(1)} %collective-permute-done.refs_0_), channel_id=1, source_target_pairs={{1,0},{2,1},{3,2},{0,3},{5,4},{6,5},{7,6},{4,7},{9,8},{10,9},{11,1... | collective-permute-start | bytes 2359304 | tf_op jit(solution)/shard_map/ring_2_normed/ppermute | solution.py:276
  52.5 38.9 %collective-permute-start.5 = (bf16[128,3072]{1,0:T(8,128)(2,1)S(1)}, bf16[128,3072]{1,0:T(8,128)(2,1)S(1)}, u32[]{:S(2)}, u32[]{:S(2)}) collective-permute-start(bf16[128,3072]{1,0:T(8,128)(2,1)S(1)} %collective-permute-done.3.refs_2_), channel_id=1, source_target_pairs={{8,0},{12,4},{0,8},{4,12},{9,1},{13,5},{1,9},{5,13},{10,2},{14,6},... | collective-permute-start | bytes 2359304 | tf_op jit(solution)/shard_map/chip_1_grad/ppermute | solution.py:276
  53.0 33.5 %collective-permute-start.4 = (bf16[128,3072]{1,0:T(8,128)(2,1)S(1)}, bf16[128,3072]{1,0:T(8,128)(2,1)S(1)}, u32[]{:S(2)}, u32[]{:S(2)}) collective-permute-start(bf16[128,3072]{1,0:T(8,128)(2,1)S(1)} %collective-permute-done.3.refs_2_), channel_id=1, source_target_pairs={{1,0},{2,1},{3,2},{0,3},{5,4},{6,5},{7,6},{4,7},{9,8},{10,9},{11,1... | collective-permute-start | bytes 2359304 | tf_op jit(solution)/shard_map/ring_2_grad/ppermute | solution.py:276
  72.4 46.1 %collective-permute-start.11 = (bf16[2,256,3840]{2,1,0:T(8,128)(2,1)}, bf16[2,256,3840]{2,1,0:T(8,128)(2,1)}, u32[]{:S(2)}, u32[]{:S(2)}) collective-permute-start(bf16[2,256,3840]{2,1,0:T(8,128)(2,1)} %get-tuple-element.35.refs_6_.refs_2_), channel_id=1, source_target_pairs={{0,4},{4,0},{8,12},{12,8},{1,5},{5,1},{9,13},{13,9},{2,6},{6,2},{1... | collective-permute-start | bytes 11796488 | tf_op jit(solution)/shard_map/swap_1/ppermute | solution.py:276
  72.4 59.9 %collective-permute-start.13 = (bf16[128,3072]{1,0:T(8,128)(2,1)S(1)}, bf16[128,3072]{1,0:T(8,128)(2,1)S(1)}, u32[]{:S(2)}, u32[]{:S(2)}) collective-permute-start(bf16[128,3072]{1,0:T(8,128)(2,1)S(1)} %collective-permute-done.1.refs_0_), channel_id=1, source_target_pairs={{8,0},{12,4},{0,8},{4,12},{9,1},{13,5},{1,9},{5,13},{10,2},{14,6},... | collective-permute-start | bytes 2359304 | tf_op jit(solution)/shard_map/chip_2_normed/ppermute | solution.py:276
  86.5 31.9 %collective-permute-start.12 = (bf16[128,3072]{1,0:T(8,128)(2,1)S(1)}, bf16[128,3072]{1,0:T(8,128)(2,1)}, u32[]{:S(2)}, u32[]{:S(2)}) collective-permute-start(bf16[128,3072]{1,0:T(8,128)(2,1)S(1)} %collective-permute-done.1.refs_0_), channel_id=1, source_target_pairs={{1,0},{2,1},{3,2},{0,3},{5,4},{6,5},{7,6},{4,7},{9,8},{10,9},{11,1... | collective-permute-start | bytes 2359304 | tf_op jit(solution)/shard_map/ring_3_normed/ppermute | solution.py:276
  90.8 44.4 %collective-permute-start.15 = (bf16[128,3072]{1,0:T(8,128)(2,1)S(1)}, bf16[128,3072]{1,0:T(8,128)(2,1)S(1)}, u32[]{:S(2)}, u32[]{:S(2)}) collective-permute-start(bf16[128,3072]{1,0:T(8,128)(2,1)S(1)} %collective-permute-done.4.refs_2_), channel_id=1, source_target_pairs={{8,0},{12,4},{0,8},{4,12},{9,1},{13,5},{1,9},{5,13},{10,2},{14,6},... | collective-permute-start | bytes 2359304 | tf_op jit(solution)/shard_map/chip_2_grad/ppermute | solution.py:276
  92.2 39.5 %collective-permute-start.14 = (bf16[128,3072]{1,0:T(8,128)(2,1)S(1)}, bf16[128,3072]{1,0:T(8,128)(2,1)S(1)}, u32[]{:S(2)}, u32[]{:S(2)}) collective-permute-start(bf16[128,3072]{1,0:T(8,128)(2,1)S(1)} %collective-permute-done.4.refs_2_), channel_id=1, source_target_pairs={{1,0},{2,1},{3,2},{0,3},{5,4},{6,5},{7,6},{4,7},{9,8},{10,9},{11,1... | collective-permute-start | bytes 2359304 | tf_op jit(solution)/shard_map/ring_3_grad/ppermute | solution.py:276
  118.4 60.5 %collective-permute-start.9 = (bf16[2,256,3840]{2,1,0:T(8,128)(2,1)}, bf16[2,256,3840]{2,1,0:T(8,128)(2,1)}, u32[]{:S(2)}, u32[]{:S(2)}) collective-permute-start(bf16[2,256,3840]{2,1,0:T(8,128)(2,1)} %get-tuple-element.36.refs_0_), channel_id=1, source_target_pairs={{0,4},{4,0},{8,12},{12,8},{1,5},{5,1},{9,13},{13,9},{2,6},{6,2},{1... | collective-permute-start | bytes 11796488 | tf_op jit(solution)/shard_map/swap_2/ppermute | solution.py:276
  118.5 42.6 %collective-permute-start.17 = (bf16[128,3072]{1,0:T(8,128)(2,1)}, bf16[128,3072]{1,0:T(8,128)(2,1)S(1)}, u32[]{:S(2)}, u32[]{:S(2)}) collective-permute-start(bf16[128,3072]{1,0:T(8,128)(2,1)} %collective-permute-done.12.refs_0_), channel_id=1, source_target_pairs={{8,0},{12,4},{0,8},{4,12},{9,1},{13,5},{1,9},{5,13},{10,2},{14,6},... | collective-permute-start | bytes 2359304 | tf_op jit(solution)/shard_map/chip_3_normed/ppermute | solution.py:276
  131.7 29.4 %collective-permute-start.18 = (bf16[128,3072]{1,0:T(8,128)(2,1)S(1)}, bf16[128,3072]{1,0:T(8,128)(2,1)S(1)}, u32[]{:S(2)}, u32[]{:S(2)}) collective-permute-start(bf16[128,3072]{1,0:T(8,128)(2,1)S(1)} %collective-permute-done.14.refs_2_), channel_id=1, source_target_pairs={{8,0},{12,4},{0,8},{4,12},{9,1},{13,5},{1,9},{5,13},{10,2},{14,6},... | collective-permute-start | bytes 2359304 | tf_op jit(solution)/shard_map/chip_3_grad/ppermute | solution.py:276
  133.1 45.2 %collective-permute-start.21 = (bf16[128,3072]{1,0:T(8,128)(2,1)S(1)}, bf16[128,3072]{1,0:T(8,128)(2,1)S(1)}, u32[]{:S(2)}, u32[]{:S(2)}) collective-permute-start(bf16[128,3072]{1,0:T(8,128)(2,1)S(1)} %get-tuple-element.59), channel_id=1, source_target_pairs={{0,1},{1,2},{2,3},{3,0},{4,5},{5,6},{6,7},{7,4},{8,9},{9,10},{10,1... | collective-permute-start | bytes 2359304 | tf_op jit(solution)/shard_map/sum_up_2/ppermute | solution.py:276
  159.3 19.0 %collective-permute-start.19 = (bf16[128,3072]{1,0:T(8,128)(2,1)S(1)}, bf16[128,3072]{1,0:T(8,128)(2,1)S(1)}, u32[]{:S(2)}, u32[]{:S(2)}) collective-permute-start(bf16[128,3072]{1,0:T(8,128)(2,1)S(1)} %get-tuple-element.49), channel_id=1, source_target_pairs={{1,0},{2,1},{3,2},{0,3},{5,4},{6,5},{7,6},{4,7},{9,8},{10,9},{11,1... | collective-permute-start | bytes 2359304 | tf_op jit(solution)/shard_map/sum_down_3/ppermute | solution.py:276
  161.1 21.2 %collective-permute-start.16 = (bf16[2,256,3840]{2,1,0:T(8,128)(2,1)}, bf16[2,256,3840]{2,1,0:T(8,128)(2,1)}, u32[]{:S(2)}, u32[]{:S(2)}) collective-permute-start(bf16[2,256,3840]{2,1,0:T(8,128)(2,1)} %get-tuple-element.43.refs_2_), channel_id=1, source_target_pairs={{0,4},{4,0},{8,12},{12,8},{1,5},{5,1},{9,13},{13,9},{2,6},{6,2},{1... | collective-permute-start | bytes 11796488 | tf_op jit(solution)/shard_map/swap_3/ppermute | solution.py:276
  178.3 4.0 %collective-permute-start.20 = (bf16[2,128,3840]{2,1,0:T(8,128)(2,1)S(1)}, bf16[2,128,3840]{2,1,0:T(8,128)(2,1)S(1)}, u32[]{:S(2)}, u32[]{:S(2)}) collective-permute-start(bf16[2,128,3840]{2,1,0:T(8,128)(2,1)S(1)} %get-tuple-element.50.refs_4_), channel_id=1, source_target_pairs={{0,4},{4,0},{8,12},{12,8},{1,5},{5,1},{9,13},{13,9},{2,6},{6,2},{1... | collective-permute-start | bytes 5898248 | tf_op jit(solution)/shard_map/swap_4/ppermute | solution.py:276
  178.5 21.9 %collective-permute-start.22 = (bf16[128,3072]{1,0:T(8,128)(2,1)S(1)}, bf16[128,3072]{1,0:T(8,128)(2,1)S(1)}, u32[]{:S(2)}, u32[]{:S(2)}) collective-permute-start(bf16[128,3072]{1,0:T(8,128)(2,1)S(1)} %add_convert_fusion), channel_id=1, source_target_pairs={{0,1},{1,2},{2,3},{3,0},{4,5},{5,6},{6,7},{7,4},{8,9},{9,10},{10,1... | collective-permute-start | bytes 2359304 | tf_op jit(solution)/shard_map/sum_up_1/ppermute | solution.py:276
  182.3 18.1 %copy-start.11 = (f32[128]{0:T(128)S(1)}, f32[128]{0:T(128)}, u32[]{:S(2)}) copy-start(f32[128]{0:T(128)} %copy-done.10) | copy-start | bytes 1540
  (15 other events, 132.5 us)

commit v10 on v9

--- a/solution.py
+++ b/solution.py
@@ -375,7 +375,8 @@
             hops.append(chain(range(half + 1, ring), from_next, "sum_down"))
         if at == 1 and ring > 3:
             second_over_chips(own_cols, groups[0][2])
-        groups.append((act, own_cols, send(after(act, *hops), "dp", swap_cores, f"swap_{at}")))
+        wait = [one[0][1] for one in sets[1:]] if at == 0 else hops
+        groups.append((act, own_cols, send(after(act, *wait), "dp", swap_cores, f"swap_{at}")))
 
     if ring > 1:
         hops.append(chain(range(half, 0, -1), from_last, "sum_up"))

time: 203 us -> 201 us (level)
  waiting for transfers between devices: 26.8 us -> 23.2 us
    ppermute x23, waiting for transfers between devices: 26.8 us -> 23.2 us  [send(): return lax.ppermute(one, axis, pairs)]
  transfers between devices with their start and end apart: 23 -> 23, of which waited for: 5 -> 6; matrix products, arithmetic and copies ran while one was open for 1% -> 1% of each run, Pallas kernels for 66% -> 66%
where the time goes in v10:
time: 201 us
  Pallas kernels  133 us (66%)
  starting transfers between devices  30 us (15%)
  waiting for transfers between devices  23.2 us (12%)
  other arithmetic  6.74 us (3%)
  local copies, waits for them, and re-layouts  4.82 us (2%)
  between operations  2.81 us (1%)
    pallas_call x5, Pallas kernels, group_call(): pl.pallas_call(functools.partial(group_kernel, limit_at=limit_at, owned=o...  104 us
    ppermute x23, starting transfers between devices, send(): return lax.ppermute(one, axis, pairs)  30 us
    pallas_call x2, Pallas kernels, weights_call(): pl.pallas_call(functools.partial(weights_kernel, groups=len(acts), scale=...  29.4 us
    ppermute x23, waiting for transfers between devices, send(): return lax.ppermute(one, axis, pairs)  23.2 us
    unnamed x32, local copies, waits for them, and re-layouts  4.08 us
  transfers between devices with their start and end apart: 23, of which 6 were waited for; matrix products, arithmetic and copies ran while one was open for 1% of the time, Pallas kernels for 66%

profile of v10, /device:TPU:0, one launch (start us, length us, event | category | flops | bytes accessed | tf_op | source)
XLA Modules:
  0.0 200.8 jit_solution(12516235388079880052)
XLA Ops:
  2.1 1.5 fusion.11
  4.0 3.0 %collective-permute-start.7 = (bf16[128,3072]{1,0:T(8,128)(2,1)S(1)}, bf16[128,3072]{1,0:T(8,128)(2,1)}, u32[]{:S(2)}, u32[]{:S(2)}) collective-permute-start(bf16[128,3072]{1,0:T(8,128)(2,1)S(1)} %fusion.5.refs_0_), channel_id=1, source_target_pairs={{8,0},{12,4},{0,8},{4,12},{9,1},{13,5},{1,9},{5,13},{10,2},{14,6},... | collective-permute-start | bytes 2359304 | tf_op jit(solution)/shard_map/chip_0_normed/ppermute | solution.py:276
  7.0 3.6 %collective-permute-start = (bf16[128,3072]{1,0:T(8,128)(2,1)S(1)}, bf16[128,3072]{1,0:T(8,128)(2,1)S(1)}, u32[]{:S(2)}, u32[]{:S(2)}) collective-permute-start(bf16[128,3072]{1,0:T(8,128)(2,1)S(1)} %fusion.5.refs_0_), channel_id=1, source_target_pairs={{1,0},{2,1},{3,2},{0,3},{5,4},{6,5},{7,6},{4,7},{9,8},{10,9},{11,1... | collective-permute-start | bytes 2359304 | tf_op jit(solution)/shard_map/ring_1_normed/ppermute | solution.py:276
  15.3 1.6 collective-permute-start.6
  17.0 20.9 %group.5 = (bf16[2,128,3840]{2,1,0:T(8,128)(2,1)S(1)}, bf16[2,128,768]{2,1,0:T(8,128)(2,1)S(1)}, f32[128,3072]{1,0:T(8,128)S(1)}) custom-call(s32[3]{0:T(128)S(1)} %pad_add_fusion.spots, bf16[128,3072]{1,0:T(8,128)(2,1)S(1)} %fusion.5.refs_0_, bf16[128,3072]{1,0:T(8,128)(2,1)S(1)} %copy-done, s32[512,1]{1,0:T(8,128)S(1)} %copy.16.refs_2_.refs_4_, ...), custom_call_target="tpu_custom_call" | custom-call | flops 21743271936 | tf_op jit(solution)/shard_map/group_0/group/pallas_call | solution.py:166
  37.8 4.5 %collective-permute-done.8.refs_3_ = bf16[128,3072]{1,0:T(8,128)(2,1)} collective-permute-done((bf16[128,3072]{1,0:T(8,128)(2,1)S(1)}, bf16[128,3072]{1,0:T(8,128)(2,1)}, u32[]{:S(2)}, u32[]{:S(2)}) %collective-permute-start.8) | collective-permute-done | bytes 786464 | tf_op jit(solution)/shard_map/chip_0_grad/ppermute | solution.py:276
  42.3 2.1 %collective-permute-start.2 = (bf16[128,3072]{1,0:T(8,128)(2,1)S(1)}, bf16[128,3072]{1,0:T(8,128)(2,1)S(1)}, u32[]{:S(2)}, u32[]{:S(2)}) collective-permute-start(bf16[128,3072]{1,0:T(8,128)(2,1)S(1)} %collective-permute-done.refs_0_), channel_id=1, source_target_pairs={{8,0},{12,4},{0,8},{4,12},{9,1},{13,5},{1,9},{5,13},{10,2},{14,6},... | collective-permute-start | bytes 2359304 | tf_op jit(solution)/shard_map/chip_1_normed/ppermute | solution.py:276
  44.4 3.6 %collective-permute-done.6.refs_5_.refs_3_ = s32[512,1]{1,0:T(8,128)} collective-permute-done((s32[512,1]{1,0:T(8,128)S(1)}, s32[512,1]{1,0:T(8,128)}, u32[]{:S(2)}, u32[]{:S(2)}) %collective-permute-start.6) | collective-permute-done | bytes 2080 | tf_op jit(solution)/shard_map/chip_limits/ppermute | solution.py:276
  47.9 4.2 %collective-permute-start.1 = (bf16[128,3072]{1,0:T(8,128)(2,1)S(1)}, bf16[128,3072]{1,0:T(8,128)(2,1)S(1)}, u32[]{:S(2)}, u32[]{:S(2)}) collective-permute-start(bf16[128,3072]{1,0:T(8,128)(2,1)S(1)} %collective-permute-done.refs_0_), channel_id=1, source_target_pairs={{1,0},{2,1},{3,2},{0,3},{5,4},{6,5},{7,6},{4,7},{9,8},{10,9},{11,1... | collective-permute-start | bytes 2359304 | tf_op jit(solution)/shard_map/ring_2_normed/ppermute | solution.py:276
  52.1 1.5 collective-permute-start.5
  54.1 18.9 %group.6 = (bf16[2,256,3840]{2,1,0:T(8,128)(2,1)}, bf16[2,256,768]{2,1,0:T(8,128)(2,1)S(1)}) custom-call(s32[3]{0:T(128)S(1)} %pad_add_fusion.spots, bf16[128,3072]{1,0:T(8,128)(2,1)S(1)} %collective-permute-done.refs_0_, bf16[128,3072]{1,0:T(8,128)(2,1)} %collective-permute-done.7.refs_1_, bf16[128,3072]{1,0:T(8,128)(2,1)S(1)} %collective-permute-done.3.refs_2_, ...), custom_call_target="tpu_custom_call" | custom-call | flops 28991029248 | tf_op jit(solution)/shard_map/group_1/group/pallas_call | solution.py:166
  73.6 10.2 %collective-permute-done.4.refs_2_ = bf16[128,3072]{1,0:T(8,128)(2,1)S(1)} collective-permute-done((bf16[128,3072]{1,0:T(8,128)(2,1)S(1)}, bf16[128,3072]{1,0:T(8,128)(2,1)S(1)}, u32[]{:S(2)}, u32[]{:S(2)}) %collective-permute-start.4) | collective-permute-done | bytes 786464 | tf_op jit(solution)/shard_map/ring_2_grad/ppermute | solution.py:276
  83.7 4.3 %collective-permute-start.12 = (bf16[128,3072]{1,0:T(8,128)(2,1)S(1)}, bf16[128,3072]{1,0:T(8,128)(2,1)}, u32[]{:S(2)}, u32[]{:S(2)}) collective-permute-start(bf16[128,3072]{1,0:T(8,128)(2,1)S(1)} %collective-permute-done.1.refs_0_), channel_id=1, source_target_pairs={{1,0},{2,1},{3,2},{0,3},{5,4},{6,5},{7,6},{4,7},{9,8},{10,9},{11,1... | collective-permute-start | bytes 2359304 | tf_op jit(solution)/shard_map/ring_3_normed/ppermute | solution.py:276
  88.0 1.5 collective-permute-start.15
  91.5 25.0 %group.7 = (bf16[2,256,3840]{2,1,0:T(8,128)(2,1)}, bf16[2,256,768]{2,1,0:T(8,128)(2,1)S(1)}, bf16[128,3072]{1,0:T(8,128)(2,1)S(1)}, f32[128,3072]{1,0:T(8,128)}) custom-call(s32[3]{0:T(128)S(1)} %pad_add_fusion.spots, bf16[128,3072]{1,0:T(8,128)(2,1)S(1)} %collective-permute-done.1.refs_0_, bf16[128,3072]{1,0:T(8,128)(2,1)S(1)} %collective-permute-done.2.refs_1_, ...), custom_call_target="tpu_custom_call" | custom-call | flops 130459631616 | tf_op jit(solution)/shard_map/group_2/group/pallas_call | solution.py:166
  117.3 11.7 %weights.2 = (bf16[768,3072]{1,0:T(8,128)(2,1)}, bf16[3072,768]{1,0:T(8,128)(2,1)}) custom-call(bf16[2,128,3840]{2,1,0:T(8,128)(2,1)S(1)} %get-tuple-element.39.refs_0_, bf16[2,128,3840]{2,1,0:T(8,128)(2,1)S(1)} %collective-permute-done.10.refs_1_.refs_5_, bf16[2,256,3840]{2,1,0:T(8,128)(2,1)} %get-tuple-element.36.refs_6_.refs_2_, ...), custom_call_target="tpu_custom_call" | custom-call | tf_op jit(solution)/shard_map/weights/pallas_call | solution.py:237
  128.9 1.5 collective-permute-start.18
  131.3 2.0 %collective-permute-start.21 = (bf16[128,3072]{1,0:T(8,128)(2,1)S(1)}, bf16[128,3072]{1,0:T(8,128)(2,1)S(1)}, u32[]{:S(2)}, u32[]{:S(2)}) collective-permute-start(bf16[128,3072]{1,0:T(8,128)(2,1)S(1)} %get-tuple-element.61), channel_id=1, source_target_pairs={{0,1},{1,2},{2,3},{3,0},{4,5},{5,6},{6,7},{7,4},{8,9},{9,10},{10,1... | collective-permute-start | bytes 2359304 | tf_op jit(solution)/shard_map/sum_up_2/ppermute | solution.py:276
  134.5 23.0 %group.8 = (bf16[2,256,3840]{2,1,0:T(8,128)(2,1)}, bf16[2,256,768]{2,1,0:T(8,128)(2,1)S(1)}, bf16[128,3072]{1,0:T(8,128)(2,1)S(1)}) custom-call(s32[3]{0:T(128)S(1)} %pad_add_fusion.spots, bf16[128,3072]{1,0:T(8,128)(2,1)} %collective-permute-done.12.refs_0_, bf16[128,3072]{1,0:T(8,128)(2,1)S(1)} %copy-done.2, ...), custom_call_target="tpu_custom_call" | custom-call | flops 36238786560 | tf_op jit(solution)/shard_map/group_3/group/pallas_call | solution.py:166
  157.5 1.8 collective-permute-start.19
  159.3 16.0 %group.9 = (bf16[2,128,3840]{2,1,0:T(8,128)(2,1)S(1)}, bf16[2,128,768]{2,1,0:T(8,128)(2,1)S(1)}) custom-call(s32[3]{0:T(128)S(1)} %pad_add_fusion.spots, bf16[128,3072]{1,0:T(8,128)(2,1)S(1)} %collective-permute-done.17.refs_0_, bf16[128,3072]{1,0:T(8,128)(2,1)S(1)} %collective-permute-done.18.refs_1_, s32[512,1]{1,0:T(8,128)S(1)} %copy.16.refs_2_.refs_4_, ...), custom_call_target="tpu_custom_call" | custom-call | flops 43486543872 | tf_op jit(solution)/shard_map/group_4/group/pallas_call | solution.py:166
  177.1 3.5 %collective-permute-done.20.refs_5_.refs_11_ = bf16[2,128,3840]{2,1,0:T(8,128)(2,1)S(1)} collective-permute-done((bf16[2,128,3840]{2,1,0:T(8,128)(2,1)S(1)}, bf16[2,128,3840]{2,1,0:T(8,128)(2,1)S(1)}, u32[]{:S(2)}, u32[]{:S(2)}) %collective-permute-start.20) | collective-permute-done | bytes 1966112 | tf_op jit(solution)/shard_map/swap_4/ppermute | solution.py:276
  180.5 17.8 %weights.3 = (bf16[768,3072]{1,0:T(8,128)(2,1)}, bf16[3072,768]{1,0:T(8,128)(2,1)}) custom-call(bf16[2,256,3840]{2,1,0:T(8,128)(2,1)} %get-tuple-element.37.refs_0_, bf16[2,256,3840]{2,1,0:T(8,128)(2,1)} %collective-permute-done.9.refs_1_.refs_7_, bf16[2,256,3840]{2,1,0:T(8,128)(2,1)} %get-tuple-element.45.refs_2_, ...), custom_call_target="tpu_custom_call" | custom-call | tf_op jit(solution)/shard_map/weights/pallas_call | solution.py:237
  199.3 1.5 fusion.10
  (76 shorter events, 13.1 us)
Async XLA Ops:
  4.0 49.6 %collective-permute-start.7 = (bf16[128,3072]{1,0:T(8,128)(2,1)S(1)}, bf16[128,3072]{1,0:T(8,128)(2,1)}, u32[]{:S(2)}, u32[]{:S(2)}) collective-permute-start(bf16[128,3072]{1,0:T(8,128)(2,1)S(1)} %fusion.5.refs_0_), channel_id=1, source_target_pairs={{8,0},{12,4},{0,8},{4,12},{9,1},{13,5},{1,9},{5,13},{10,2},{14,6},... | collective-permute-start | bytes 2359304 | tf_op jit(solution)/shard_map/chip_0_normed/ppermute | solution.py:276
  7.0 35.3 %collective-permute-start = (bf16[128,3072]{1,0:T(8,128)(2,1)S(1)}, bf16[128,3072]{1,0:T(8,128)(2,1)S(1)}, u32[]{:S(2)}, u32[]{:S(2)}) collective-permute-start(bf16[128,3072]{1,0:T(8,128)(2,1)S(1)} %fusion.5.refs_0_), channel_id=1, source_target_pairs={{1,0},{2,1},{3,2},{0,3},{5,4},{6,5},{7,6},{4,7},{9,8},{10,9},{11,1... | collective-permute-start | bytes 2359304 | tf_op jit(solution)/shard_map/ring_1_normed/ppermute | solution.py:276
  10.6 31.7 %collective-permute-start.8 = (bf16[128,3072]{1,0:T(8,128)(2,1)S(1)}, bf16[128,3072]{1,0:T(8,128)(2,1)}, u32[]{:S(2)}, u32[]{:S(2)}) collective-permute-start(bf16[128,3072]{1,0:T(8,128)(2,1)S(1)} %copy-done), channel_id=1, source_target_pairs={{8,0},{12,4},{0,8},{4,12},{9,1},{13,5},{1,9},{5,13},{10,2},{14,6},... | collective-permute-start | bytes 2359304 | tf_op jit(solution)/shard_map/chip_0_grad/ppermute | solution.py:276
  11.1 41.0 %collective-permute-start.3 = (bf16[128,3072]{1,0:T(8,128)(2,1)S(1)}, bf16[128,3072]{1,0:T(8,128)(2,1)S(1)}, u32[]{:S(2)}, u32[]{:S(2)}) collective-permute-start(bf16[128,3072]{1,0:T(8,128)(2,1)S(1)} %copy-done), channel_id=1, source_target_pairs={{1,0},{2,1},{3,2},{0,3},{5,4},{6,5},{7,6},{4,7},{9,8},{10,9},{11,1... | collective-permute-start | bytes 2359304 | tf_op jit(solution)/shard_map/ring_1_grad/ppermute | solution.py:276
  15.3 32.6 %collective-permute-start.6 = (s32[512,1]{1,0:T(8,128)S(1)}, s32[512,1]{1,0:T(8,128)}, u32[]{:S(2)}, u32[]{:S(2)}) collective-permute-start(s32[512,1]{1,0:T(8,128)S(1)} %copy.16.refs_2_.refs_4_), channel_id=1, source_target_pairs={{8,0},{12,4},{0,8},{4,12},{9,1},{13,5},{1,9},{5,13},{10,2},{14,6},... | collective-permute-start | bytes 6152 | tf_op jit(solution)/shard_map/chip_limits/ppermute | solution.py:276
  42.3 30.6 %collective-permute-start.10 = (bf16[2,128,3840]{2,1,0:T(8,128)(2,1)S(1)}, bf16[2,128,3840]{2,1,0:T(8,128)(2,1)S(1)}, u32[]{:S(2)}, u32[]{:S(2)}) collective-permute-start(bf16[2,128,3840]{2,1,0:T(8,128)(2,1)S(1)} %get-tuple-element.39.refs_0_), channel_id=1, source_target_pairs={{0,4},{4,0},{8,12},{12,8},{1,5},{5,1},{9,13},{13,9},{2,6},{6,2},{1... | collective-permute-start | bytes 5898248 | tf_op jit(solution)/shard_map/swap_0/ppermute | solution.py:276
  42.3 45.7 %collective-permute-start.2 = (bf16[128,3072]{1,0:T(8,128)(2,1)S(1)}, bf16[128,3072]{1,0:T(8,128)(2,1)S(1)}, u32[]{:S(2)}, u32[]{:S(2)}) collective-permute-start(bf16[128,3072]{1,0:T(8,128)(2,1)S(1)} %collective-permute-done.refs_0_), channel_id=1, source_target_pairs={{8,0},{12,4},{0,8},{4,12},{9,1},{13,5},{1,9},{5,13},{10,2},{14,6},... | collective-permute-start | bytes 2359304 | tf_op jit(solution)/shard_map/chip_1_normed/ppermute | solution.py:276
  47.9 25.0 %collective-permute-start.1 = (bf16[128,3072]{1,0:T(8,128)(2,1)S(1)}, bf16[128,3072]{1,0:T(8,128)(2,1)S(1)}, u32[]{:S(2)}, u32[]{:S(2)}) collective-permute-start(bf16[128,3072]{1,0:T(8,128)(2,1)S(1)} %collective-permute-done.refs_0_), channel_id=1, source_target_pairs={{1,0},{2,1},{3,2},{0,3},{5,4},{6,5},{7,6},{4,7},{9,8},{10,9},{11,1... | collective-permute-start | bytes 2359304 | tf_op jit(solution)/shard_map/ring_2_normed/ppermute | solution.py:276
  52.1 37.4 %collective-permute-start.5 = (bf16[128,3072]{1,0:T(8,128)(2,1)S(1)}, bf16[128,3072]{1,0:T(8,128)(2,1)S(1)}, u32[]{:S(2)}, u32[]{:S(2)}) collective-permute-start(bf16[128,3072]{1,0:T(8,128)(2,1)S(1)} %collective-permute-done.3.refs_2_), channel_id=1, source_target_pairs={{8,0},{12,4},{0,8},{4,12},{9,1},{13,5},{1,9},{5,13},{10,2},{14,6},... | collective-permute-start | bytes 2359304 | tf_op jit(solution)/shard_map/chip_1_grad/ppermute | solution.py:276
  53.6 30.1 %collective-permute-start.4 = (bf16[128,3072]{1,0:T(8,128)(2,1)S(1)}, bf16[128,3072]{1,0:T(8,128)(2,1)S(1)}, u32[]{:S(2)}, u32[]{:S(2)}) collective-permute-start(bf16[128,3072]{1,0:T(8,128)(2,1)S(1)} %collective-permute-done.3.refs_2_), channel_id=1, source_target_pairs={{1,0},{2,1},{3,2},{0,3},{5,4},{6,5},{7,6},{4,7},{9,8},{10,9},{11,1... | collective-permute-start | bytes 2359304 | tf_op jit(solution)/shard_map/ring_2_grad/ppermute | solution.py:276
  73.0 43.7 %collective-permute-start.11 = (bf16[2,256,3840]{2,1,0:T(8,128)(2,1)}, bf16[2,256,3840]{2,1,0:T(8,128)(2,1)}, u32[]{:S(2)}, u32[]{:S(2)}) collective-permute-start(bf16[2,256,3840]{2,1,0:T(8,128)(2,1)} %get-tuple-element.36.refs_6_.refs_2_), channel_id=1, source_target_pairs={{0,4},{4,0},{8,12},{12,8},{1,5},{5,1},{9,13},{13,9},{2,6},{6,2},{1... | collective-permute-start | bytes 11796488 | tf_op jit(solution)/shard_map/swap_1/ppermute | solution.py:276
  73.0 57.5 %collective-permute-start.13 = (bf16[128,3072]{1,0:T(8,128)(2,1)S(1)}, bf16[128,3072]{1,0:T(8,128)(2,1)S(1)}, u32[]{:S(2)}, u32[]{:S(2)}) collective-permute-start(bf16[128,3072]{1,0:T(8,128)(2,1)S(1)} %collective-permute-done.1.refs_0_), channel_id=1, source_target_pairs={{8,0},{12,4},{0,8},{4,12},{9,1},{13,5},{1,9},{5,13},{10,2},{14,6},... | collective-permute-start | bytes 2359304 | tf_op jit(solution)/shard_map/chip_2_normed/ppermute | solution.py:276
  83.7 32.8 %collective-permute-start.12 = (bf16[128,3072]{1,0:T(8,128)(2,1)S(1)}, bf16[128,3072]{1,0:T(8,128)(2,1)}, u32[]{:S(2)}, u32[]{:S(2)}) collective-permute-start(bf16[128,3072]{1,0:T(8,128)(2,1)S(1)} %collective-permute-done.1.refs_0_), channel_id=1, source_target_pairs={{1,0},{2,1},{3,2},{0,3},{5,4},{6,5},{7,6},{4,7},{9,8},{10,9},{11,1... | collective-permute-start | bytes 2359304 | tf_op jit(solution)/shard_map/ring_3_normed/ppermute | solution.py:276
  88.0 45.3 %collective-permute-start.15 = (bf16[128,3072]{1,0:T(8,128)(2,1)S(1)}, bf16[128,3072]{1,0:T(8,128)(2,1)S(1)}, u32[]{:S(2)}, u32[]{:S(2)}) collective-permute-start(bf16[128,3072]{1,0:T(8,128)(2,1)S(1)} %collective-permute-done.4.refs_2_), channel_id=1, source_target_pairs={{8,0},{12,4},{0,8},{4,12},{9,1},{13,5},{1,9},{5,13},{10,2},{14,6},... | collective-permute-start | bytes 2359304 | tf_op jit(solution)/shard_map/chip_2_grad/ppermute | solution.py:276
  90.4 38.5 %collective-permute-start.14 = (bf16[128,3072]{1,0:T(8,128)(2,1)S(1)}, bf16[128,3072]{1,0:T(8,128)(2,1)S(1)}, u32[]{:S(2)}, u32[]{:S(2)}) collective-permute-start(bf16[128,3072]{1,0:T(8,128)(2,1)S(1)} %collective-permute-done.4.refs_2_), channel_id=1, source_target_pairs={{1,0},{2,1},{3,2},{0,3},{5,4},{6,5},{7,6},{4,7},{9,8},{10,9},{11,1... | collective-permute-start | bytes 2359304 | tf_op jit(solution)/shard_map/ring_3_grad/ppermute | solution.py:276
  116.6 60.5 %collective-permute-start.9 = (bf16[2,256,3840]{2,1,0:T(8,128)(2,1)}, bf16[2,256,3840]{2,1,0:T(8,128)(2,1)}, u32[]{:S(2)}, u32[]{:S(2)}) collective-permute-start(bf16[2,256,3840]{2,1,0:T(8,128)(2,1)} %get-tuple-element.37.refs_0_), channel_id=1, source_target_pairs={{0,4},{4,0},{8,12},{12,8},{1,5},{5,1},{9,13},{13,9},{2,6},{6,2},{1... | collective-permute-start | bytes 11796488 | tf_op jit(solution)/shard_map/swap_2/ppermute | solution.py:276
  116.7 42.6 %collective-permute-start.17 = (bf16[128,3072]{1,0:T(8,128)(2,1)}, bf16[128,3072]{1,0:T(8,128)(2,1)S(1)}, u32[]{:S(2)}, u32[]{:S(2)}) collective-permute-start(bf16[128,3072]{1,0:T(8,128)(2,1)} %collective-permute-done.12.refs_0_), channel_id=1, source_target_pairs={{8,0},{12,4},{0,8},{4,12},{9,1},{13,5},{1,9},{5,13},{10,2},{14,6},... | collective-permute-start | bytes 2359304 | tf_op jit(solution)/shard_map/chip_3_normed/ppermute | solution.py:276
  128.9 30.4 %collective-permute-start.18 = (bf16[128,3072]{1,0:T(8,128)(2,1)S(1)}, bf16[128,3072]{1,0:T(8,128)(2,1)S(1)}, u32[]{:S(2)}, u32[]{:S(2)}) collective-permute-start(bf16[128,3072]{1,0:T(8,128)(2,1)S(1)} %collective-permute-done.14.refs_2_), channel_id=1, source_target_pairs={{8,0},{12,4},{0,8},{4,12},{9,1},{13,5},{1,9},{5,13},{10,2},{14,6},... | collective-permute-start | bytes 2359304 | tf_op jit(solution)/shard_map/chip_3_grad/ppermute | solution.py:276
  131.3 45.2 %collective-permute-start.21 = (bf16[128,3072]{1,0:T(8,128)(2,1)S(1)}, bf16[128,3072]{1,0:T(8,128)(2,1)S(1)}, u32[]{:S(2)}, u32[]{:S(2)}) collective-permute-start(bf16[128,3072]{1,0:T(8,128)(2,1)S(1)} %get-tuple-element.61), channel_id=1, source_target_pairs={{0,1},{1,2},{2,3},{3,0},{4,5},{5,6},{6,7},{7,4},{8,9},{9,10},{10,1... | collective-permute-start | bytes 2359304 | tf_op jit(solution)/shard_map/sum_up_2/ppermute | solution.py:276
  157.5 19.1 %collective-permute-start.19 = (bf16[128,3072]{1,0:T(8,128)(2,1)S(1)}, bf16[128,3072]{1,0:T(8,128)(2,1)S(1)}, u32[]{:S(2)}, u32[]{:S(2)}) collective-permute-start(bf16[128,3072]{1,0:T(8,128)(2,1)S(1)} %get-tuple-element.51), channel_id=1, source_target_pairs={{1,0},{2,1},{3,2},{0,3},{5,4},{6,5},{7,6},{4,7},{9,8},{10,9},{11,1... | collective-permute-start | bytes 2359304 | tf_op jit(solution)/shard_map/sum_down_3/ppermute | solution.py:276
  159.3 21.2 %collective-permute-start.16 = (bf16[2,256,3840]{2,1,0:T(8,128)(2,1)}, bf16[2,256,3840]{2,1,0:T(8,128)(2,1)}, u32[]{:S(2)}, u32[]{:S(2)}) collective-permute-start(bf16[2,256,3840]{2,1,0:T(8,128)(2,1)} %get-tuple-element.45.refs_2_), channel_id=1, source_target_pairs={{0,4},{4,0},{8,12},{12,8},{1,5},{5,1},{9,13},{13,9},{2,6},{6,2},{1... | collective-permute-start | bytes 11796488 | tf_op jit(solution)/shard_map/swap_3/ppermute | solution.py:276
  176.6 4.0 %collective-permute-start.20 = (bf16[2,128,3840]{2,1,0:T(8,128)(2,1)S(1)}, bf16[2,128,3840]{2,1,0:T(8,128)(2,1)S(1)}, u32[]{:S(2)}, u32[]{:S(2)}) collective-permute-start(bf16[2,128,3840]{2,1,0:T(8,128)(2,1)S(1)} %get-tuple-element.52.refs_4_), channel_id=1, source_target_pairs={{0,4},{4,0},{8,12},{12,8},{1,5},{5,1},{9,13},{13,9},{2,6},{6,2},{1... | collective-permute-start | bytes 5898248 | tf_op jit(solution)/shard_map/swap_4/ppermute | solution.py:276
  176.7 21.9 %collective-permute-start.22 = (bf16[128,3072]{1,0:T(8,128)(2,1)S(1)}, bf16[128,3072]{1,0:T(8,128)(2,1)S(1)}, u32[]{:S(2)}, u32[]{:S(2)}) collective-permute-start(bf16[128,3072]{1,0:T(8,128)(2,1)S(1)} %add_convert_fusion), channel_id=1, source_target_pairs={{0,1},{1,2},{2,3},{3,0},{4,5},{5,6},{6,7},{7,4},{8,9},{9,10},{10,1... | collective-permute-start | bytes 2359304 | tf_op jit(solution)/shard_map/sum_up_1/ppermute | solution.py:276
  180.5 18.1 %copy-start.11 = (f32[128]{0:T(128)S(1)}, f32[128]{0:T(128)}, u32[]{:S(2)}) copy-start(f32[128]{0:T(128)} %copy-done.10) | copy-start | bytes 1540
  (15 other events, 132.5 us)

commit v11 on v9

--- a/solution.py
+++ b/solution.py
@@ -13,7 +13,7 @@
 NORM_EPS = 1e-06
 VMEM_LIMIT = 48 * 1024 * 1024
 WORK = 3.0
-WEIGHTS = {2: 3.0, 4: 3.0}
+WEIGHTS = {1: 3.0, 3: 3.0}
 
 
 def gelu_parts(pre_act):
@@ -177,8 +177,8 @@
             grid=(tiles + share // tile,),
             in_specs=[whole(one.shape) for one in (*normed, *grads, *limits)]
             + [
-                pl.BlockSpec((1, piece_rows, tile), lambda i, spots: (0, 0, jnp.minimum(i, tiles - 1)))
-                for _ in extra
+                pl.BlockSpec((1, piece_rows, tile), lambda i, spots, at=at: (0, at, jnp.minimum(i, tiles - 1)))
+                for _, at in extra
             ]
             + [
                 pl.BlockSpec((features, tile), lambda i, spots: (0, jnp.minimum(i, tiles - 1))),
@@ -193,7 +193,7 @@
         compiler_params=pltpu.CompilerParams(vmem_limit_bytes=VMEM_LIMIT),
         cost_estimate=work_of(weight * (4 * rows + 2 * len(back_types) * piece_rows) * units * features),
         name="group",
-    )(spots, *normed, *grads, *limits, *extra, weight_in, weight_out)
+    )(spots, *normed, *grads, *limits, *(one for one, _ in extra), weight_in, weight_out)
 
 
 def weights_kernel(*refs, groups, scale, started):
@@ -297,20 +297,15 @@
 
     near = {0: (normed, grad_out)}
     for step in range(1, ring):
-        near[step] = None if 2 < step == ring - 1 else move(near[step - 1], "tensor", from_next, f"ring_{step}")
+        near[step] = move(near[step - 1], "tensor", from_next, f"ring_{step}")
     sets = [[near[step] for step in range(ring)]]
     for chip in range(1, chips):
-        sets.append(
-            [
-                None if step == ring - 1 or 1 < step == ring - 2 else move(piece, "dp", from_chip, f"chip_{step}")
-                for step, piece in enumerate(sets[-1])
-            ]
-        )
-
-    def second_over_chips(*gates):
-        for chip in range(1, chips):
-            sets[chip][-2] = move(sets[chip - 1][-2], "dp", from_chip, f"chip_{ring - 2}", *gates)
-        sets[0][-1] = move(sets[0][-2], "tensor", from_next, f"ring_{ring - 1}", *gates)
+        far = []
+        for step, piece in enumerate(sets[-1]):
+            if step == 0:
+                piece = (piece[0], after(piece[1], *limits[1:]))
+            far.append(None if step == ring - 1 else move(piece, "dp", from_chip, f"chip_{step}"))
+        sets.append(far)
 
     def last_over_chips(early, gates):
         for chip in range(1, chips):
@@ -335,6 +330,8 @@
         [(chip, slot - chip) for chip in range(chips) if 0 <= slot - chip < ring]
         for slot in range(ring + chips - 1)
     ]
+    if len(arrivals) > 1:
+        arrivals[:2] = [sorted(arrivals[0] + arrivals[1])]
     last = len(arrivals) - 1
     totals = []
     for at, entries in enumerate(arrivals):
@@ -349,11 +346,10 @@
             last_over_chips([own_cols], hold)
         own_steps = [step for chip, step in entries if chip == 0]
         extra = []
-        if at == 1 and ring > 2:
-            own_steps, later = [], own_steps
-            gates = [groups[0][1]]
-        elif at == 2 and ring > 2:
-            own_steps, extra = own_steps + later, [groups[1][0]]
+        if at == 0 and ring > 2:
+            own_steps = own_steps[:1]
+        elif at == 1 and ring > 2:
+            own_steps, extra = own_steps + [1], [(groups[0][0], 1)]
         back_types = [jnp.bfloat16 if step in (half, half + 1) else jnp.float32 for step in own_steps]
         with jax.named_scope(f"group_{at}"):
             act, own_cols, *back = group_call(
@@ -373,8 +369,6 @@
         own_grads.update(zip(own_steps, back))
         if at == last and ring > 2:
             hops.append(chain(range(half + 1, ring), from_next, "sum_down"))
-        if at == 1 and ring > 3:
-            second_over_chips(own_cols, groups[0][2])
         groups.append((act, own_cols, send(after(act, *hops), "dp", swap_cores, f"swap_{at}")))
 
     if ring > 1:

time: 203 us -> 199 us (0.980)
  Pallas kernels: 133 us -> 122 us
  starting transfers between devices: 28.2 us -> 31.2 us
  local copies, waits for them, and re-layouts: 4.82 us -> 7.53 us
  waiting for transfers between devices: 26.8 us -> 29.3 us
    pallas_call x5 -> x4, Pallas kernels: 104 us -> 91.8 us  [group_call(): pl.pallas_call(functools.partial(group_kernel, limit_at=limit_at, owned=o...]
    ppermute x23 -> x22, starting transfers between devices: 28.2 us -> 31.2 us  [send(): return lax.ppermute(one, axis, pairs)]
    ppermute x23 -> x22, waiting for transfers between devices: 26.8 us -> 29.3 us  [send(): return lax.ppermute(one, axis, pairs)]
    unnamed x32 -> x38, local copies, waits for them, and re-layouts: 4.08 us -> 6.02 us
  transfers between devices with their start and end apart: 23 -> 22, of which waited for: 5 -> 6; matrix products, arithmetic and copies ran while one was open for 1% -> 1% of each run, Pallas kernels for 66% -> 61%
where the time goes in v11:
time: 199 us
  Pallas kernels  122 us (61%)
  starting transfers between devices  31.2 us (16%)
  waiting for transfers between devices  29.3 us (15%)
  local copies, waits for them, and re-layouts  7.53 us (4%)
  other arithmetic  6.24 us (3%)
  between operations  2.82 us (1%)
    pallas_call x4, Pallas kernels, group_call(): pl.pallas_call(functools.partial(group_kernel, limit_at=limit_at, owned=o...  91.8 us
    ppermute x22, starting transfers between devices, send(): return lax.ppermute(one, axis, pairs)  31.2 us
    pallas_call x2, Pallas kernels, weights_call(): pl.pallas_call(functools.partial(weights_kernel, groups=len(acts), scale=...  29.9 us
    ppermute x22, waiting for transfers between devices, send(): return lax.ppermute(one, axis, pairs)  29.3 us
    unnamed x38, local copies, waits for them, and re-layouts  6.02 us
  transfers between devices with their start and end apart: 22, of which 6 were waited for; matrix products, arithmetic and copies ran while one was open for 1% of the time, Pallas kernels for 61%

profile of v11, /device:TPU:0, one launch (start us, length us, event | category | flops | bytes accessed | tf_op | source)
XLA Modules:
  0.0 198.9 jit_solution(1142814392431407907)
XLA Ops:
  5.8 3.0 %collective-permute-start.3 = (s32[512,1]{1,0:T(8,128)S(1)}, s32[512,1]{1,0:T(8,128)S(1)}, u32[]{:S(2)}, u32[]{:S(2)}) collective-permute-start(s32[512,1]{1,0:T(8,128)S(1)} %copy.15.refs_6_.refs_4_.refs_2_), channel_id=1, source_target_pairs={{8,0},{12,4},{0,8},{4,12},{9,1},{13,5},{1,9},{5,13},{10,2},{14,6},... | collective-permute-start | bytes 6152 | tf_op jit(solution)/shard_map/chip_limits/ppermute | solution.py:276
  11.1 4.1 %collective-permute-start = (bf16[128,3072]{1,0:T(8,128)(2,1)S(1)}, bf16[128,3072]{1,0:T(8,128)(2,1)S(1)}, u32[]{:S(2)}, u32[]{:S(2)}) collective-permute-start(bf16[128,3072]{1,0:T(8,128)(2,1)S(1)} %fusion.5.refs_0_), channel_id=1, source_target_pairs={{1,0},{2,1},{3,2},{0,3},{5,4},{6,5},{7,6},{4,7},{9,8},{10,9},{11,1... | collective-permute-start | bytes 2359304 | tf_op jit(solution)/shard_map/ring_1_normed/ppermute | solution.py:276
  16.7 2.1 %collective-permute-start.4 = (bf16[128,3072]{1,0:T(8,128)(2,1)S(1)}, bf16[128,3072]{1,0:T(8,128)(2,1)}, u32[]{:S(2)}, u32[]{:S(2)}) collective-permute-start(bf16[128,3072]{1,0:T(8,128)(2,1)S(1)} %copy-done.2), channel_id=1, source_target_pairs={{8,0},{12,4},{0,8},{4,12},{9,1},{13,5},{1,9},{5,13},{10,2},{14,6},... | collective-permute-start | bytes 2359304 | tf_op jit(solution)/shard_map/chip_0_grad/ppermute | solution.py:276
  18.8 14.4 %collective-permute-done.refs_1_ = bf16[128,3072]{1,0:T(8,128)(2,1)S(1)} collective-permute-done((bf16[128,3072]{1,0:T(8,128)(2,1)S(1)}, bf16[128,3072]{1,0:T(8,128)(2,1)S(1)}, u32[]{:S(2)}, u32[]{:S(2)}) %collective-permute-start) | collective-permute-done | bytes 786464 | tf_op jit(solution)/shard_map/ring_1_normed/ppermute | solution.py:276
  33.2 1.5 collective-permute-start.6
  34.7 4.3 %collective-permute-start.5 = (bf16[128,3072]{1,0:T(8,128)(2,1)S(1)}, bf16[128,3072]{1,0:T(8,128)(2,1)S(1)}, u32[]{:S(2)}, u32[]{:S(2)}) collective-permute-start(bf16[128,3072]{1,0:T(8,128)(2,1)S(1)} %collective-permute-done.refs_1_), channel_id=1, source_target_pairs={{1,0},{2,1},{3,2},{0,3},{5,4},{6,5},{7,6},{4,7},{9,8},{10,9},{11,1... | collective-permute-start | bytes 2359304 | tf_op jit(solution)/shard_map/ring_2_normed/ppermute | solution.py:276
  39.0 11.1 %collective-permute-done.2.refs_4_ = bf16[128,3072]{1,0:T(8,128)(2,1)S(1)} collective-permute-done((bf16[128,3072]{1,0:T(8,128)(2,1)S(1)}, bf16[128,3072]{1,0:T(8,128)(2,1)S(1)}, u32[]{:S(2)}, u32[]{:S(2)}) %collective-permute-start.2) | collective-permute-done | bytes 786464 | tf_op jit(solution)/shard_map/ring_1_grad/ppermute | solution.py:276
  50.1 1.5 collective-permute-start.8
  51.6 4.3 %collective-permute-start.7 = (bf16[128,3072]{1,0:T(8,128)(2,1)S(1)}, bf16[128,3072]{1,0:T(8,128)(2,1)S(1)}, u32[]{:S(2)}, u32[]{:S(2)}) collective-permute-start(bf16[128,3072]{1,0:T(8,128)(2,1)S(1)} %collective-permute-done.2.refs_4_), channel_id=1, source_target_pairs={{1,0},{2,1},{3,2},{0,3},{5,4},{6,5},{7,6},{4,7},{9,8},{10,9},{11,1... | collective-permute-start | bytes 2359304 | tf_op jit(solution)/shard_map/ring_2_grad/ppermute | solution.py:276
  56.8 29.3 %group.4 = (bf16[2,384,3840]{2,1,0:T(8,128)(2,1)}, bf16[2,384,768]{2,1,0:T(8,128)(2,1)}, f32[128,3072]{1,0:T(8,128)}) custom-call(s32[3]{0:T(128)S(1)} %pad_add_fusion.spots, bf16[128,3072]{1,0:T(8,128)(2,1)S(1)} %fusion.5.refs_0_, bf16[128,3072]{1,0:T(8,128)(2,1)S(1)} %collective-permute-done.refs_1_, bf16[128,3072]{1,0:T(8,128)(2,1)} %collective-permute-done.1.refs_2_, ...), custom_call_target="tpu_custom_call" | custom-call | flops 50734301184 | tf_op jit(solution)/shard_map/group_0/group/pallas_call | solution.py:166
  86.8 1.6 collective-permute-start.14
  90.4 23.6 %group.5 = (bf16[2,256,3840]{2,1,0:T(8,128)(2,1)}, bf16[2,256,768]{2,1,0:T(8,128)(2,1)S(1)}, bf16[128,3072]{1,0:T(8,128)(2,1)S(1)}, f32[128,3072]{1,0:T(8,128)}) custom-call(s32[3]{0:T(128)S(1)} %pad_add_fusion.spots, bf16[128,3072]{1,0:T(8,128)(2,1)S(1)} %collective-permute-done.5.refs_0_, bf16[128,3072]{1,0:T(8,128)(2,1)S(1)} %collective-permute-done.6.refs_1_, ...), custom_call_target="tpu_custom_call" | custom-call | flops 130459631616 | tf_op jit(solution)/shard_map/group_1/group/pallas_call | solution.py:166
  114.7 12.0 %weights.2 = (bf16[768,3072]{1,0:T(8,128)(2,1)S(1)}, bf16[3072,768]{1,0:T(8,128)(2,1)}) custom-call(bf16[2,384,3840]{2,1,0:T(8,128)(2,1)} %get-tuple-element.30.refs_6_.refs_0_, bf16[2,384,3840]{2,1,0:T(8,128)(2,1)} %collective-permute-done.10.refs_1_.refs_3_, bf16[2,384,768]{2,1,0:T(8,128)(2,1)S(1)} %copy-done.1, ...), custom_call_target="tpu_custom_call" | custom-call | tf_op jit(solution)/shard_map/weights/pallas_call | solution.py:237
  126.7 2.1 %copy-done = bf16[768,3072]{1,0:T(8,128)(2,1)} copy-done((bf16[768,3072]{1,0:T(8,128)(2,1)}, bf16[768,3072]{1,0:T(8,128)(2,1)S(1)}, u32[]{:S(2)}) %copy-start) | copy-done | bytes 4718616
  128.9 1.5 collective-permute-start.17
  130.4 2.0 %collective-permute-start.20 = (bf16[128,3072]{1,0:T(8,128)(2,1)S(1)}, bf16[128,3072]{1,0:T(8,128)(2,1)S(1)}, u32[]{:S(2)}, u32[]{:S(2)}) collective-permute-start(bf16[128,3072]{1,0:T(8,128)(2,1)S(1)} %get-tuple-element.51), channel_id=1, source_target_pairs={{0,1},{1,2},{2,3},{3,0},{4,5},{5,6},{6,7},{7,4},{8,9},{9,10},{10,1... | collective-permute-start | bytes 2359304 | tf_op jit(solution)/shard_map/sum_up_2/ppermute | solution.py:276
  132.4 22.9 %group.6 = (bf16[2,256,3840]{2,1,0:T(8,128)(2,1)}, bf16[2,256,768]{2,1,0:T(8,128)(2,1)S(1)}, bf16[128,3072]{1,0:T(8,128)(2,1)S(1)}) custom-call(s32[3]{0:T(128)S(1)} %pad_add_fusion.spots, bf16[128,3072]{1,0:T(8,128)(2,1)S(1)} %collective-permute-done.11.refs_0_, bf16[128,3072]{1,0:T(8,128)(2,1)S(1)} %collective-permute-done.12.refs_1_, ...), custom_call_target="tpu_custom_call" | custom-call | flops 36238786560 | tf_op jit(solution)/shard_map/group_2/group/pallas_call | solution.py:166
  155.3 1.8 collective-permute-start.18
  157.1 16.0 %group.7 = (bf16[2,128,3840]{2,1,0:T(8,128)(2,1)S(1)}, bf16[2,128,768]{2,1,0:T(8,128)(2,1)S(1)}) custom-call(s32[3]{0:T(128)S(1)} %pad_add_fusion.spots, bf16[128,3072]{1,0:T(8,128)(2,1)S(1)} %collective-permute-done.16.refs_0_, bf16[128,3072]{1,0:T(8,128)(2,1)S(1)} %collective-permute-done.17.refs_1_, s32[512,1]{1,0:T(8,128)S(1)} %copy.15.refs_6_.refs_4_.refs_2_, ...), custom_call_target="tpu_custom_call" | custom-call | flops 43486543872 | tf_op jit(solution)/shard_map/group_3/group/pallas_call | solution.py:166
  173.1 1.4 collective-permute-done.18
  174.7 1.8 collective-permute-start.21
  176.5 2.0 %collective-permute-done.19.refs_5_.refs_11_ = bf16[2,128,3840]{2,1,0:T(8,128)(2,1)S(1)} collective-permute-done((bf16[2,128,3840]{2,1,0:T(8,128)(2,1)S(1)}, bf16[2,128,3840]{2,1,0:T(8,128)(2,1)S(1)}, u32[]{:S(2)}, u32[]{:S(2)}) %collective-permute-start.19) | collective-permute-done | bytes 1966112 | tf_op jit(solution)/shard_map/swap_3/ppermute | solution.py:276
  178.6 17.9 %weights.3 = (bf16[768,3072]{1,0:T(8,128)(2,1)}, bf16[3072,768]{1,0:T(8,128)(2,1)}) custom-call(bf16[2,256,3840]{2,1,0:T(8,128)(2,1)} %get-tuple-element.31.refs_0_, bf16[2,256,3840]{2,1,0:T(8,128)(2,1)} %collective-permute-done.9.refs_1_.refs_7_, bf16[2,256,3840]{2,1,0:T(8,128)(2,1)} %get-tuple-element.35.refs_2_, ...), custom_call_target="tpu_custom_call" | custom-call | tf_op jit(solution)/shard_map/weights/pallas_call | solution.py:237
  197.3 1.6 fusion.10
  (79 shorter events, 12.4 us)
Async XLA Ops:
  5.8 10.1 %collective-permute-start.3 = (s32[512,1]{1,0:T(8,128)S(1)}, s32[512,1]{1,0:T(8,128)S(1)}, u32[]{:S(2)}, u32[]{:S(2)}) collective-permute-start(s32[512,1]{1,0:T(8,128)S(1)} %copy.15.refs_6_.refs_4_.refs_2_), channel_id=1, source_target_pairs={{8,0},{12,4},{0,8},{4,12},{9,1},{13,5},{1,9},{5,13},{10,2},{14,6},... | collective-permute-start | bytes 6152 | tf_op jit(solution)/shard_map/chip_limits/ppermute | solution.py:276
  11.1 40.5 %collective-permute-start.1 = (bf16[128,3072]{1,0:T(8,128)(2,1)S(1)}, bf16[128,3072]{1,0:T(8,128)(2,1)}, u32[]{:S(2)}, u32[]{:S(2)}) collective-permute-start(bf16[128,3072]{1,0:T(8,128)(2,1)S(1)} %fusion.5.refs_0_), channel_id=1, source_target_pairs={{8,0},{12,4},{0,8},{4,12},{9,1},{13,5},{1,9},{5,13},{10,2},{14,6},... | collective-permute-start | bytes 2359304 | tf_op jit(solution)/shard_map/chip_0_normed/ppermute | solution.py:276
  11.1 22.1 %collective-permute-start = (bf16[128,3072]{1,0:T(8,128)(2,1)S(1)}, bf16[128,3072]{1,0:T(8,128)(2,1)S(1)}, u32[]{:S(2)}, u32[]{:S(2)}) collective-permute-start(bf16[128,3072]{1,0:T(8,128)(2,1)S(1)} %fusion.5.refs_0_), channel_id=1, source_target_pairs={{1,0},{2,1},{3,2},{0,3},{5,4},{6,5},{7,6},{4,7},{9,8},{10,9},{11,1... | collective-permute-start | bytes 2359304 | tf_op jit(solution)/shard_map/ring_1_normed/ppermute | solution.py:276
  15.2 34.9 %collective-permute-start.2 = (bf16[128,3072]{1,0:T(8,128)(2,1)S(1)}, bf16[128,3072]{1,0:T(8,128)(2,1)S(1)}, u32[]{:S(2)}, u32[]{:S(2)}) collective-permute-start(bf16[128,3072]{1,0:T(8,128)(2,1)S(1)} %copy-done.2), channel_id=1, source_target_pairs={{1,0},{2,1},{3,2},{0,3},{5,4},{6,5},{7,6},{4,7},{9,8},{10,9},{11,1... | collective-permute-start | bytes 2359304 | tf_op jit(solution)/shard_map/ring_1_grad/ppermute | solution.py:276
  16.7 39.2 %collective-permute-start.4 = (bf16[128,3072]{1,0:T(8,128)(2,1)S(1)}, bf16[128,3072]{1,0:T(8,128)(2,1)}, u32[]{:S(2)}, u32[]{:S(2)}) collective-permute-start(bf16[128,3072]{1,0:T(8,128)(2,1)S(1)} %copy-done.2), channel_id=1, source_target_pairs={{8,0},{12,4},{0,8},{4,12},{9,1},{13,5},{1,9},{5,13},{10,2},{14,6},... | collective-permute-start | bytes 2359304 | tf_op jit(solution)/shard_map/chip_0_grad/ppermute | solution.py:276
  33.2 53.6 %collective-permute-start.6 = (bf16[128,3072]{1,0:T(8,128)(2,1)S(1)}, bf16[128,3072]{1,0:T(8,128)(2,1)S(1)}, u32[]{:S(2)}, u32[]{:S(2)}) collective-permute-start(bf16[128,3072]{1,0:T(8,128)(2,1)S(1)} %collective-permute-done.refs_1_), channel_id=1, source_target_pairs={{8,0},{12,4},{0,8},{4,12},{9,1},{13,5},{1,9},{5,13},{10,2},{14,6},... | collective-permute-start | bytes 2359304 | tf_op jit(solution)/shard_map/chip_1_normed/ppermute | solution.py:276
  34.7 51.5 %collective-permute-start.5 = (bf16[128,3072]{1,0:T(8,128)(2,1)S(1)}, bf16[128,3072]{1,0:T(8,128)(2,1)S(1)}, u32[]{:S(2)}, u32[]{:S(2)}) collective-permute-start(bf16[128,3072]{1,0:T(8,128)(2,1)S(1)} %collective-permute-done.refs_1_), channel_id=1, source_target_pairs={{1,0},{2,1},{3,2},{0,3},{5,4},{6,5},{7,6},{4,7},{9,8},{10,9},{11,1... | collective-permute-start | bytes 2359304 | tf_op jit(solution)/shard_map/ring_2_normed/ppermute | solution.py:276
  50.1 38.3 %collective-permute-start.8 = (bf16[128,3072]{1,0:T(8,128)(2,1)S(1)}, bf16[128,3072]{1,0:T(8,128)(2,1)S(1)}, u32[]{:S(2)}, u32[]{:S(2)}) collective-permute-start(bf16[128,3072]{1,0:T(8,128)(2,1)S(1)} %collective-permute-done.2.refs_4_), channel_id=1, source_target_pairs={{8,0},{12,4},{0,8},{4,12},{9,1},{13,5},{1,9},{5,13},{10,2},{14,6},... | collective-permute-start | bytes 2359304 | tf_op jit(solution)/shard_map/chip_1_grad/ppermute | solution.py:276
  51.6 35.3 %collective-permute-start.7 = (bf16[128,3072]{1,0:T(8,128)(2,1)S(1)}, bf16[128,3072]{1,0:T(8,128)(2,1)S(1)}, u32[]{:S(2)}, u32[]{:S(2)}) collective-permute-start(bf16[128,3072]{1,0:T(8,128)(2,1)S(1)} %collective-permute-done.2.refs_4_), channel_id=1, source_target_pairs={{1,0},{2,1},{3,2},{0,3},{5,4},{6,5},{7,6},{4,7},{9,8},{10,9},{11,1... | collective-permute-start | bytes 2359304 | tf_op jit(solution)/shard_map/ring_2_grad/ppermute | solution.py:276
  56.8 32.5 %copy-start.7 = (s32[512,1]{1,0:T(8,128)S(1)}, s32[512,1]{1,0:T(8,128)}, u32[]{:S(2)}) copy-start(s32[512,1]{1,0:T(8,128)} %copy-done.5) | copy-start | bytes 6148
  86.1 28.6 %copy-start.1 = (bf16[2,384,768]{2,1,0:T(8,128)(2,1)S(1)}, bf16[2,384,768]{2,1,0:T(8,128)(2,1)}, u32[]{:S(2)}) copy-start(bf16[2,384,768]{2,1,0:T(8,128)(2,1)} %get-tuple-element.32.refs_2_) | copy-start | bytes 3538948
  86.1 28.0 %collective-permute-start.10 = (bf16[2,384,3840]{2,1,0:T(8,128)(2,1)}, bf16[2,384,3840]{2,1,0:T(8,128)(2,1)}, u32[]{:S(2)}, u32[]{:S(2)}) collective-permute-start(bf16[2,384,3840]{2,1,0:T(8,128)(2,1)} %get-tuple-element.30.refs_6_.refs_0_), channel_id=1, source_target_pairs={{0,4},{4,0},{8,12},{12,8},{1,5},{5,1},{9,13},{13,9},{2,6},{6,2},{1... | collective-permute-start | bytes 17694728 | tf_op jit(solution)/shard_map/swap_0/ppermute | solution.py:276
  86.2 44.2 %collective-permute-start.12 = (bf16[128,3072]{1,0:T(8,128)(2,1)S(1)}, bf16[128,3072]{1,0:T(8,128)(2,1)S(1)}, u32[]{:S(2)}, u32[]{:S(2)}) collective-permute-start(bf16[128,3072]{1,0:T(8,128)(2,1)S(1)} %collective-permute-done.5.refs_0_), channel_id=1, source_target_pairs={{8,0},{12,4},{0,8},{4,12},{9,1},{13,5},{1,9},{5,13},{10,2},{14,6},... | collective-permute-start | bytes 2359304 | tf_op jit(solution)/shard_map/chip_2_normed/ppermute | solution.py:276
  86.8 27.2 %collective-permute-start.11 = (bf16[128,3072]{1,0:T(8,128)(2,1)S(1)}, bf16[128,3072]{1,0:T(8,128)(2,1)S(1)}, u32[]{:S(2)}, u32[]{:S(2)}) collective-permute-start(bf16[128,3072]{1,0:T(8,128)(2,1)S(1)} %collective-permute-done.5.refs_0_), channel_id=1, source_target_pairs={{1,0},{2,1},{3,2},{0,3},{5,4},{6,5},{7,6},{4,7},{9,8},{10,9},{11,1... | collective-permute-start | bytes 2359304 | tf_op jit(solution)/shard_map/ring_3_normed/ppermute | solution.py:276
  86.8 45.6 %collective-permute-start.14 = (bf16[128,3072]{1,0:T(8,128)(2,1)S(1)}, bf16[128,3072]{1,0:T(8,128)(2,1)S(1)}, u32[]{:S(2)}, u32[]{:S(2)}) collective-permute-start(bf16[128,3072]{1,0:T(8,128)(2,1)S(1)} %collective-permute-done.7.refs_2_), channel_id=1, source_target_pairs={{8,0},{12,4},{0,8},{4,12},{9,1},{13,5},{1,9},{5,13},{10,2},{14,6},... | collective-permute-start | bytes 2359304 | tf_op jit(solution)/shard_map/chip_2_grad/ppermute | solution.py:276
  89.3 39.6 %collective-permute-start.13 = (bf16[128,3072]{1,0:T(8,128)(2,1)S(1)}, bf16[128,3072]{1,0:T(8,128)(2,1)S(1)}, u32[]{:S(2)}, u32[]{:S(2)}) collective-permute-start(bf16[128,3072]{1,0:T(8,128)(2,1)S(1)} %collective-permute-done.7.refs_2_), channel_id=1, source_target_pairs={{1,0},{2,1},{3,2},{0,3},{5,4},{6,5},{7,6},{4,7},{9,8},{10,9},{11,1... | collective-permute-start | bytes 2359304 | tf_op jit(solution)/shard_map/ring_3_grad/ppermute | solution.py:276
  114.0 62.5 %collective-permute-start.9 = (bf16[2,256,3840]{2,1,0:T(8,128)(2,1)}, bf16[2,256,3840]{2,1,0:T(8,128)(2,1)}, u32[]{:S(2)}, u32[]{:S(2)}) collective-permute-start(bf16[2,256,3840]{2,1,0:T(8,128)(2,1)} %get-tuple-element.31.refs_0_), channel_id=1, source_target_pairs={{0,4},{4,0},{8,12},{12,8},{1,5},{5,1},{9,13},{13,9},{2,6},{6,2},{1... | collective-permute-start | bytes 11796488 | tf_op jit(solution)/shard_map/swap_1/ppermute | solution.py:276
  114.1 43.0 %collective-permute-start.16 = (bf16[128,3072]{1,0:T(8,128)(2,1)S(1)}, bf16[128,3072]{1,0:T(8,128)(2,1)S(1)}, u32[]{:S(2)}, u32[]{:S(2)}) collective-permute-start(bf16[128,3072]{1,0:T(8,128)(2,1)S(1)} %collective-permute-done.11.refs_0_), channel_id=1, source_target_pairs={{8,0},{12,4},{0,8},{4,12},{9,1},{13,5},{1,9},{5,13},{10,2},{14,6},... | collective-permute-start | bytes 2359304 | tf_op jit(solution)/shard_map/chip_3_normed/ppermute | solution.py:276
  128.9 28.2 %collective-permute-start.17 = (bf16[128,3072]{1,0:T(8,128)(2,1)S(1)}, bf16[128,3072]{1,0:T(8,128)(2,1)S(1)}, u32[]{:S(2)}, u32[]{:S(2)}) collective-permute-start(bf16[128,3072]{1,0:T(8,128)(2,1)S(1)} %collective-permute-done.13.refs_2_), channel_id=1, source_target_pairs={{8,0},{12,4},{0,8},{4,12},{9,1},{13,5},{1,9},{5,13},{10,2},{14,6},... | collective-permute-start | bytes 2359304 | tf_op jit(solution)/shard_map/chip_3_grad/ppermute | solution.py:276
  130.4 44.2 %collective-permute-start.20 = (bf16[128,3072]{1,0:T(8,128)(2,1)S(1)}, bf16[128,3072]{1,0:T(8,128)(2,1)S(1)}, u32[]{:S(2)}, u32[]{:S(2)}) collective-permute-start(bf16[128,3072]{1,0:T(8,128)(2,1)S(1)} %get-tuple-element.51), channel_id=1, source_target_pairs={{0,1},{1,2},{2,3},{3,0},{4,5},{5,6},{6,7},{7,4},{8,9},{9,10},{10,1... | collective-permute-start | bytes 2359304 | tf_op jit(solution)/shard_map/sum_up_2/ppermute | solution.py:276
  155.3 19.3 %collective-permute-start.18 = (bf16[128,3072]{1,0:T(8,128)(2,1)S(1)}, bf16[128,3072]{1,0:T(8,128)(2,1)S(1)}, u32[]{:S(2)}, u32[]{:S(2)}) collective-permute-start(bf16[128,3072]{1,0:T(8,128)(2,1)S(1)} %get-tuple-element.41), channel_id=1, source_target_pairs={{1,0},{2,1},{3,2},{0,3},{5,4},{6,5},{7,6},{4,7},{9,8},{10,9},{11,1... | collective-permute-start | bytes 2359304 | tf_op jit(solution)/shard_map/sum_down_3/ppermute | solution.py:276
  157.1 21.4 %collective-permute-start.15 = (bf16[2,256,3840]{2,1,0:T(8,128)(2,1)}, bf16[2,256,3840]{2,1,0:T(8,128)(2,1)}, u32[]{:S(2)}, u32[]{:S(2)}) collective-permute-start(bf16[2,256,3840]{2,1,0:T(8,128)(2,1)} %get-tuple-element.35.refs_2_), channel_id=1, source_target_pairs={{0,4},{4,0},{8,12},{12,8},{1,5},{5,1},{9,13},{13,9},{2,6},{6,2},{1... | collective-permute-start | bytes 11796488 | tf_op jit(solution)/shard_map/swap_2/ppermute | solution.py:276
  174.5 4.0 %collective-permute-start.19 = (bf16[2,128,3840]{2,1,0:T(8,128)(2,1)S(1)}, bf16[2,128,3840]{2,1,0:T(8,128)(2,1)S(1)}, u32[]{:S(2)}, u32[]{:S(2)}) collective-permute-start(bf16[2,128,3840]{2,1,0:T(8,128)(2,1)S(1)} %get-tuple-element.42.refs_4_), channel_id=1, source_target_pairs={{0,4},{4,0},{8,12},{12,8},{1,5},{5,1},{9,13},{13,9},{2,6},{6,2},{1... | collective-permute-start | bytes 5898248 | tf_op jit(solution)/shard_map/swap_3/ppermute | solution.py:276
  174.7 21.8 %collective-permute-start.21 = (bf16[128,3072]{1,0:T(8,128)(2,1)S(1)}, bf16[128,3072]{1,0:T(8,128)(2,1)S(1)}, u32[]{:S(2)}, u32[]{:S(2)}) collective-permute-start(bf16[128,3072]{1,0:T(8,128)(2,1)S(1)} %add_convert_fusion), channel_id=1, source_target_pairs={{0,1},{1,2},{2,3},{3,0},{4,5},{5,6},{6,7},{7,4},{8,9},{9,10},{10,1... | collective-permute-start | bytes 2359304 | tf_op jit(solution)/shard_map/sum_up_1/ppermute | solution.py:276
  (17 other events, 171.6 us)

commit v12 on v8

--- a/solution.py
+++ b/solution.py
@@ -287,12 +287,12 @@
         near[step] = move(near[step - 1], "tensor", from_next, f"ring_{step}")
     sets = [[near[step] for step in range(ring)]]
     for chip in range(1, chips):
-        sets.append(
-            [
-                None if step == ring - 1 else move(piece, "dp", from_chip, f"chip_{step}")
-                for step, piece in enumerate(sets[-1])
-            ]
-        )
+        far = []
+        for step, piece in enumerate(sets[-1]):
+            if step == 0:
+                piece = (after(piece[0], *level_sets[1:]), piece[1])
+            far.append(None if step == ring - 1 else move(piece, "dp", from_chip, f"chip_{step}"))
+        sets.append(far)
 
     def last_over_chips(early, gates):
         for chip in range(1, chips):

time: 199 us -> 196 us (0.985)
  waiting for transfers between devices: 28.2 us -> 24.3 us
    ppermute x22, waiting for transfers between devices: 28.2 us -> 24.3 us  [send(): return lax.ppermute(one, axis, pairs)]
    unnamed x34 -> x36, local copies, waits for them, and re-layouts: 5.01 us -> 5 us
  transfers between devices with their start and end apart: 22 -> 22, of which waited for: 4 -> 4; matrix products, arithmetic and copies ran while one was open for 3% -> 4% of each run, Pallas kernels for 62% -> 63%
where the time goes in v12:
time: 196 us; the launch traced here: 195 us
  Pallas kernels  122 us (62%)
  starting transfers between devices  28 us (14%)
  waiting for transfers between devices  24.3 us (12%)
  other arithmetic  9.47 us (5%)
  local copies, waits for them, and re-layouts  6.54 us (3%)
  between operations  4.77 us (2%)
    pallas_call x4, Pallas kernels, group_call(): pl.pallas_call(functools.partial(group_kernel, limit_at=limit_at, owned=o...  92.5 us
    pallas_call x2, Pallas kernels, weights_call(): pl.pallas_call(functools.partial(weights_kernel, groups=len(acts), scale=...  29.9 us
    ppermute x22, starting transfers between devices, send(): return lax.ppermute(one, axis, pairs)  28 us
    ppermute x22, waiting for transfers between devices, send(): return lax.ppermute(one, axis, pairs)  24.3 us
    unnamed x36, local copies, waits for them, and re-layouts  5 us
  transfers between devices with their start and end apart: 22, of which 4 were waited for; matrix products, arithmetic and copies ran while one was open for 4% of the time, Pallas kernels for 63%

profile of v12, /device:TPU:0, one launch (start us, length us, event | category | flops | bytes accessed | tf_op | source)
XLA Modules:
  0.0 195.4 jit_solution(13373469274532420598)
XLA Ops:
  1.5 3.0 %collective-permute-start.1 = (s32[516]{0:T(1024)S(1)}, s32[516]{0:T(1024)S(1)}, u32[]{:S(2)}, u32[]{:S(2)}) collective-permute-start(s32[516]{0:T(1024)S(1)} %pad_add_fusion), channel_id=1, source_target_pairs={{8,0},{12,4},{0,8},{4,12},{9,1},{13,5},{1,9},{5,13},{10,2},{14,6},... | collective-permute-start | bytes 6200 | tf_op jit(solution)/shard_map/chip_levels/ppermute | solution.py:262
  4.5 1.3 convert_reduce_fusion
  5.8 1.5 fusion.11
  7.6 3.7 %collective-permute-start = (bf16[128,3072]{1,0:T(8,128)(2,1)S(1)}, bf16[128,3072]{1,0:T(8,128)(2,1)}, u32[]{:S(2)}, u32[]{:S(2)}) collective-permute-start(bf16[128,3072]{1,0:T(8,128)(2,1)S(1)} %fusion.5.refs_0_), channel_id=1, source_target_pairs={{1,0},{2,1},{3,2},{0,3},{5,4},{6,5},{7,6},{4,7},{9,8},{10,9},{11,1... | collective-permute-start | bytes 2359304 | tf_op jit(solution)/shard_map/ring_1_normed/ppermute | solution.py:262
  12.3 1.5 collective-permute-start.2
  21.2 8.0 %collective-permute-done.refs_1_ = bf16[128,3072]{1,0:T(8,128)(2,1)} collective-permute-done((bf16[128,3072]{1,0:T(8,128)(2,1)S(1)}, bf16[128,3072]{1,0:T(8,128)(2,1)}, u32[]{:S(2)}, u32[]{:S(2)}) %collective-permute-start) | collective-permute-done | bytes 786464 | tf_op jit(solution)/shard_map/ring_1_normed/ppermute | solution.py:262
  29.8 4.4 %collective-permute-start.5 = (bf16[128,3072]{1,0:T(8,128)(2,1)}, bf16[128,3072]{1,0:T(8,128)(2,1)S(1)}, u32[]{:S(2)}, u32[]{:S(2)}) collective-permute-start(bf16[128,3072]{1,0:T(8,128)(2,1)} %collective-permute-done.refs_1_), channel_id=1, source_target_pairs={{1,0},{2,1},{3,2},{0,3},{5,4},{6,5},{7,6},{4,7},{9,8},{10,9},{11,1... | collective-permute-start | bytes 2359304 | tf_op jit(solution)/shard_map/ring_2_normed/ppermute | solution.py:262
  34.2 11.9 %collective-permute-done.3.refs_4_ = bf16[128,3072]{1,0:T(8,128)(2,1)S(1)} collective-permute-done((bf16[128,3072]{1,0:T(8,128)(2,1)S(1)}, bf16[128,3072]{1,0:T(8,128)(2,1)S(1)}, u32[]{:S(2)}, u32[]{:S(2)}) %collective-permute-start.3) | collective-permute-done | bytes 786464 | tf_op jit(solution)/shard_map/ring_1_grad/ppermute | solution.py:262
  46.7 4.3 %collective-permute-start.7 = (bf16[128,3072]{1,0:T(8,128)(2,1)S(1)}, bf16[128,3072]{1,0:T(8,128)(2,1)S(1)}, u32[]{:S(2)}, u32[]{:S(2)}) collective-permute-start(bf16[128,3072]{1,0:T(8,128)(2,1)S(1)} %collective-permute-done.3.refs_4_), channel_id=1, source_target_pairs={{1,0},{2,1},{3,2},{0,3},{5,4},{6,5},{7,6},{4,7},{9,8},{10,9},{11,1... | collective-permute-start | bytes 2359304 | tf_op jit(solution)/shard_map/ring_2_grad/ppermute | solution.py:262
  51.0 30.8 %group.4 = (bf16[2,384,3840]{2,1,0:T(8,128)(2,1)}, bf16[2,384,768]{2,1,0:T(8,128)(2,1)}, f32[128,3072]{1,0:T(8,128)}, f32[128,3072]{1,0:T(8,128)}) custom-call(s32[3]{0:T(128)S(1)} %pad_add_fusion.1.spots, bf16[128,3072]{1,0:T(8,128)(2,1)S(1)} %fusion.5.refs_0_, bf16[128,3072]{1,0:T(8,128)(2,1)} %collective-permute-done.refs_1_, ...), custom_call_target="tpu_custom_call" | custom-call | flops 57982058496 | tf_op jit(solution)/shard_map/group_0/group/pallas_call | solution.py:162
  81.9 1.6 collective-permute-start.12
  84.1 22.8 %group.5 = (bf16[2,256,3840]{2,1,0:T(8,128)(2,1)}, bf16[2,256,768]{2,1,0:T(8,128)(2,1)S(1)}, bf16[128,3072]{1,0:T(8,128)(2,1)S(1)}) custom-call(s32[3]{0:T(128)S(1)} %pad_add_fusion.1.spots, bf16[128,3072]{1,0:T(8,128)(2,1)S(1)} %collective-permute-done.5.refs_0_, bf16[128,3072]{1,0:T(8,128)(2,1)S(1)} %collective-permute-done.6.refs_1_, ...), custom_call_target="tpu_custom_call" | custom-call | flops 108716359680 | tf_op jit(solution)/shard_map/group_1/group/pallas_call | solution.py:162
  106.9 1.6 collective-permute-start.16
  108.5 12.0 %weights.2 = (bf16[768,3072]{1,0:T(8,128)(2,1)S(1)}, bf16[3072,768]{1,0:T(8,128)(2,1)}) custom-call(bf16[2,384,3840]{2,1,0:T(8,128)(2,1)} %get-tuple-element.31.refs_0_, bf16[2,384,3840]{2,1,0:T(8,128)(2,1)} %collective-permute-done.10.refs_1_.refs_3_, bf16[2,384,768]{2,1,0:T(8,128)(2,1)S(1)} %copy-done.1, ...), custom_call_target="tpu_custom_call" | custom-call | tf_op jit(solution)/shard_map/weights/pallas_call | solution.py:223
  120.5 2.1 %copy-done = bf16[768,3072]{1,0:T(8,128)(2,1)} copy-done((bf16[768,3072]{1,0:T(8,128)(2,1)}, bf16[768,3072]{1,0:T(8,128)(2,1)S(1)}, u32[]{:S(2)}) %copy-start) | copy-done | bytes 4718616
  123.2 2.0 %collective-permute-start.20 = (bf16[128,3072]{1,0:T(8,128)(2,1)S(1)}, bf16[128,3072]{1,0:T(8,128)(2,1)}, u32[]{:S(2)}, u32[]{:S(2)}) collective-permute-start(bf16[128,3072]{1,0:T(8,128)(2,1)S(1)} %get-tuple-element.51), channel_id=1, source_target_pairs={{0,1},{1,2},{2,3},{3,0},{4,5},{5,6},{6,7},{7,4},{8,9},{9,10},{10,1... | collective-permute-start | bytes 2359304 | tf_op jit(solution)/shard_map/sum_up_2/ppermute | solution.py:262
  125.2 22.8 %group.6 = (bf16[2,256,3840]{2,1,0:T(8,128)(2,1)}, bf16[2,256,768]{2,1,0:T(8,128)(2,1)S(1)}, bf16[128,3072]{1,0:T(8,128)(2,1)S(1)}) custom-call(s32[3]{0:T(128)S(1)} %pad_add_fusion.1.spots, bf16[128,3072]{1,0:T(8,128)(2,1)S(1)} %collective-permute-done.11.refs_0_, bf16[128,3072]{1,0:T(8,128)(2,1)S(1)} %collective-permute-done.12.refs_1_, ...), custom_call_target="tpu_custom_call" | custom-call | flops 36238786560 | tf_op jit(solution)/shard_map/group_2/group/pallas_call | solution.py:162
  148.0 1.8 collective-permute-start.18
  149.8 2.5 %collective-permute-done.17.refs_1_ = bf16[128,3072]{1,0:T(8,128)(2,1)S(1)} collective-permute-done((bf16[128,3072]{1,0:T(8,128)(2,1)S(1)}, bf16[128,3072]{1,0:T(8,128)(2,1)S(1)}, u32[]{:S(2)}, u32[]{:S(2)}) %collective-permute-start.17) | collective-permute-done | bytes 786464 | tf_op jit(solution)/shard_map/chip_3_grad/ppermute | solution.py:262
  152.4 16.0 %group.7 = (bf16[2,128,3840]{2,1,0:T(8,128)(2,1)S(1)}, bf16[2,128,768]{2,1,0:T(8,128)(2,1)S(1)}) custom-call(s32[3]{0:T(128)S(1)} %pad_add_fusion.1.spots, bf16[128,3072]{1,0:T(8,128)(2,1)S(1)} %collective-permute-done.16.refs_0_, bf16[128,3072]{1,0:T(8,128)(2,1)S(1)} %collective-permute-done.17.refs_1_, s32[512,1]{1,0:T(8,128)S(1)} %copy.18.refs_6_.refs_4_.refs_2_, ...), custom_call_target="tpu_custom_call" | custom-call | flops 43486543872 | tf_op jit(solution)/shard_map/group_3/group/pallas_call | solution.py:162
  171.5 1.8 collective-permute-done.19.refs_5_.refs_11_
  173.2 1.9 copy-done.5
  175.2 17.8 %weights.3 = (bf16[768,3072]{1,0:T(8,128)(2,1)}, bf16[3072,768]{1,0:T(8,128)(2,1)}) custom-call(bf16[2,256,3840]{2,1,0:T(8,128)(2,1)} %get-tuple-element.30.refs_0_, bf16[2,256,3840]{2,1,0:T(8,128)(2,1)} %collective-permute-done.9.refs_1_.refs_7_, bf16[2,256,3840]{2,1,0:T(8,128)(2,1)} %get-tuple-element.35.refs_2_, bf16[2,256,3840]{2,1,0:T(8,128)(2,1)} %copy-done.5, ...), custom_call_target="tpu_custom_call" | custom-call | tf_op jit(solution)/shard_map/weights/pallas_call | solution.py:223
  193.8 1.6 fusion.10
  (82 shorter events, 11.8 us)
Async XLA Ops:
  1.5 10.8 %collective-permute-start.1 = (s32[516]{0:T(1024)S(1)}, s32[516]{0:T(1024)S(1)}, u32[]{:S(2)}, u32[]{:S(2)}) collective-permute-start(s32[516]{0:T(1024)S(1)} %pad_add_fusion), channel_id=1, source_target_pairs={{8,0},{12,4},{0,8},{4,12},{9,1},{13,5},{1,9},{5,13},{10,2},{14,6},... | collective-permute-start | bytes 6200 | tf_op jit(solution)/shard_map/chip_levels/ppermute | solution.py:262
  7.6 21.6 %collective-permute-start = (bf16[128,3072]{1,0:T(8,128)(2,1)S(1)}, bf16[128,3072]{1,0:T(8,128)(2,1)}, u32[]{:S(2)}, u32[]{:S(2)}) collective-permute-start(bf16[128,3072]{1,0:T(8,128)(2,1)S(1)} %fusion.5.refs_0_), channel_id=1, source_target_pairs={{1,0},{2,1},{3,2},{0,3},{5,4},{6,5},{7,6},{4,7},{9,8},{10,9},{11,1... | collective-permute-start | bytes 2359304 | tf_op jit(solution)/shard_map/ring_1_normed/ppermute | solution.py:262
  11.3 34.8 %collective-permute-start.3 = (bf16[128,3072]{1,0:T(8,128)(2,1)S(1)}, bf16[128,3072]{1,0:T(8,128)(2,1)S(1)}, u32[]{:S(2)}, u32[]{:S(2)}) collective-permute-start(bf16[128,3072]{1,0:T(8,128)(2,1)S(1)} %copy-done.2), channel_id=1, source_target_pairs={{1,0},{2,1},{3,2},{0,3},{5,4},{6,5},{7,6},{4,7},{9,8},{10,9},{11,1... | collective-permute-start | bytes 2359304 | tf_op jit(solution)/shard_map/ring_1_grad/ppermute | solution.py:262
  11.8 34.9 %collective-permute-start.4 = (bf16[128,3072]{1,0:T(8,128)(2,1)S(1)}, bf16[128,3072]{1,0:T(8,128)(2,1)}, u32[]{:S(2)}, u32[]{:S(2)}) collective-permute-start(bf16[128,3072]{1,0:T(8,128)(2,1)S(1)} %copy-done.2), channel_id=1, source_target_pairs={{8,0},{12,4},{0,8},{4,12},{9,1},{13,5},{1,9},{5,13},{10,2},{14,6},... | collective-permute-start | bytes 2359304 | tf_op jit(solution)/shard_map/chip_0_grad/ppermute | solution.py:262
  12.3 38.7 %collective-permute-start.2 = (bf16[128,3072]{1,0:T(8,128)(2,1)S(1)}, bf16[128,3072]{1,0:T(8,128)(2,1)}, u32[]{:S(2)}, u32[]{:S(2)}) collective-permute-start(bf16[128,3072]{1,0:T(8,128)(2,1)S(1)} %fusion.5.refs_0_), channel_id=1, source_target_pairs={{8,0},{12,4},{0,8},{4,12},{9,1},{13,5},{1,9},{5,13},{10,2},{14,6},... | collective-permute-start | bytes 2359304 | tf_op jit(solution)/shard_map/chip_0_normed/ppermute | solution.py:262
  29.3 54.1 %collective-permute-start.6 = (bf16[128,3072]{1,0:T(8,128)(2,1)}, bf16[128,3072]{1,0:T(8,128)(2,1)S(1)}, u32[]{:S(2)}, u32[]{:S(2)}) collective-permute-start(bf16[128,3072]{1,0:T(8,128)(2,1)} %collective-permute-done.refs_1_), channel_id=1, source_target_pairs={{8,0},{12,4},{0,8},{4,12},{9,1},{13,5},{1,9},{5,13},{10,2},{14,6},... | collective-permute-start | bytes 2359304 | tf_op jit(solution)/shard_map/chip_1_normed/ppermute | solution.py:262
  29.8 52.0 %collective-permute-start.5 = (bf16[128,3072]{1,0:T(8,128)(2,1)}, bf16[128,3072]{1,0:T(8,128)(2,1)S(1)}, u32[]{:S(2)}, u32[]{:S(2)}) collective-permute-start(bf16[128,3072]{1,0:T(8,128)(2,1)} %collective-permute-done.refs_1_), channel_id=1, source_target_pairs={{1,0},{2,1},{3,2},{0,3},{5,4},{6,5},{7,6},{4,7},{9,8},{10,9},{11,1... | collective-permute-start | bytes 2359304 | tf_op jit(solution)/shard_map/ring_2_normed/ppermute | solution.py:262
  46.1 37.9 %collective-permute-start.8 = (bf16[128,3072]{1,0:T(8,128)(2,1)S(1)}, bf16[128,3072]{1,0:T(8,128)(2,1)S(1)}, u32[]{:S(2)}, u32[]{:S(2)}) collective-permute-start(bf16[128,3072]{1,0:T(8,128)(2,1)S(1)} %collective-permute-done.3.refs_4_), channel_id=1, source_target_pairs={{8,0},{12,4},{0,8},{4,12},{9,1},{13,5},{1,9},{5,13},{10,2},{14,6},... | collective-permute-start | bytes 2359304 | tf_op jit(solution)/shard_map/chip_1_grad/ppermute | solution.py:262
  46.7 36.8 %collective-permute-start.7 = (bf16[128,3072]{1,0:T(8,128)(2,1)S(1)}, bf16[128,3072]{1,0:T(8,128)(2,1)S(1)}, u32[]{:S(2)}, u32[]{:S(2)}) collective-permute-start(bf16[128,3072]{1,0:T(8,128)(2,1)S(1)} %collective-permute-done.3.refs_4_), channel_id=1, source_target_pairs={{1,0},{2,1},{3,2},{0,3},{5,4},{6,5},{7,6},{4,7},{9,8},{10,9},{11,1... | collective-permute-start | bytes 2359304 | tf_op jit(solution)/shard_map/ring_2_grad/ppermute | solution.py:262
  81.8 26.7 %copy-start.1 = (bf16[2,384,768]{2,1,0:T(8,128)(2,1)S(1)}, bf16[2,384,768]{2,1,0:T(8,128)(2,1)}, u32[]{:S(2)}) copy-start(bf16[2,384,768]{2,1,0:T(8,128)(2,1)} %get-tuple-element.32.refs_2_) | copy-start | bytes 3538948
  81.8 25.1 %collective-permute-start.10 = (bf16[2,384,3840]{2,1,0:T(8,128)(2,1)}, bf16[2,384,3840]{2,1,0:T(8,128)(2,1)}, u32[]{:S(2)}, u32[]{:S(2)}) collective-permute-start(bf16[2,384,3840]{2,1,0:T(8,128)(2,1)} %get-tuple-element.31.refs_0_), channel_id=1, source_target_pairs={{0,4},{4,0},{8,12},{12,8},{1,5},{5,1},{9,13},{13,9},{2,6},{6,2},{1... | collective-permute-start | bytes 17694728 | tf_op jit(solution)/shard_map/swap_0/ppermute | solution.py:262
  81.9 41.3 %collective-permute-start.12 = (bf16[128,3072]{1,0:T(8,128)(2,1)S(1)}, bf16[128,3072]{1,0:T(8,128)(2,1)S(1)}, u32[]{:S(2)}, u32[]{:S(2)}) collective-permute-start(bf16[128,3072]{1,0:T(8,128)(2,1)S(1)} %collective-permute-done.5.refs_0_), channel_id=1, source_target_pairs={{8,0},{12,4},{0,8},{4,12},{9,1},{13,5},{1,9},{5,13},{10,2},{14,6},... | collective-permute-start | bytes 2359304 | tf_op jit(solution)/shard_map/chip_2_normed/ppermute | solution.py:262
  83.4 23.5 %collective-permute-start.11 = (bf16[128,3072]{1,0:T(8,128)(2,1)S(1)}, bf16[128,3072]{1,0:T(8,128)(2,1)S(1)}, u32[]{:S(2)}, u32[]{:S(2)}) collective-permute-start(bf16[128,3072]{1,0:T(8,128)(2,1)S(1)} %collective-permute-done.5.refs_0_), channel_id=1, source_target_pairs={{1,0},{2,1},{3,2},{0,3},{5,4},{6,5},{7,6},{4,7},{9,8},{10,9},{11,1... | collective-permute-start | bytes 2359304 | tf_op jit(solution)/shard_map/ring_3_normed/ppermute | solution.py:262
  83.4 41.7 %collective-permute-start.14 = (bf16[128,3072]{1,0:T(8,128)(2,1)S(1)}, bf16[128,3072]{1,0:T(8,128)(2,1)S(1)}, u32[]{:S(2)}, u32[]{:S(2)}) collective-permute-start(bf16[128,3072]{1,0:T(8,128)(2,1)S(1)} %collective-permute-done.7.refs_2_), channel_id=1, source_target_pairs={{8,0},{12,4},{0,8},{4,12},{9,1},{13,5},{1,9},{5,13},{10,2},{14,6},... | collective-permute-start | bytes 2359304 | tf_op jit(solution)/shard_map/chip_2_grad/ppermute | solution.py:262
  84.0 38.6 %collective-permute-start.13 = (bf16[128,3072]{1,0:T(8,128)(2,1)S(1)}, bf16[128,3072]{1,0:T(8,128)(2,1)S(1)}, u32[]{:S(2)}, u32[]{:S(2)}) collective-permute-start(bf16[128,3072]{1,0:T(8,128)(2,1)S(1)} %collective-permute-done.7.refs_2_), channel_id=1, source_target_pairs={{1,0},{2,1},{3,2},{0,3},{5,4},{6,5},{7,6},{4,7},{9,8},{10,9},{11,1... | collective-permute-start | bytes 2359304 | tf_op jit(solution)/shard_map/ring_3_grad/ppermute | solution.py:262
  106.9 64.6 %collective-permute-start.9 = (bf16[2,256,3840]{2,1,0:T(8,128)(2,1)}, bf16[2,256,3840]{2,1,0:T(8,128)(2,1)}, u32[]{:S(2)}, u32[]{:S(2)}) collective-permute-start(bf16[2,256,3840]{2,1,0:T(8,128)(2,1)} %get-tuple-element.30.refs_0_), channel_id=1, source_target_pairs={{0,4},{4,0},{8,12},{12,8},{1,5},{5,1},{9,13},{13,9},{2,6},{6,2},{1... | collective-permute-start | bytes 11796488 | tf_op jit(solution)/shard_map/swap_1/ppermute | solution.py:262
  106.9 42.9 %collective-permute-start.16 = (bf16[128,3072]{1,0:T(8,128)(2,1)S(1)}, bf16[128,3072]{1,0:T(8,128)(2,1)S(1)}, u32[]{:S(2)}, u32[]{:S(2)}) collective-permute-start(bf16[128,3072]{1,0:T(8,128)(2,1)S(1)} %collective-permute-done.11.refs_0_), channel_id=1, source_target_pairs={{8,0},{12,4},{0,8},{4,12},{9,1},{13,5},{1,9},{5,13},{10,2},{14,6},... | collective-permute-start | bytes 2359304 | tf_op jit(solution)/shard_map/chip_3_normed/ppermute | solution.py:262
  122.6 29.7 %collective-permute-start.17 = (bf16[128,3072]{1,0:T(8,128)(2,1)S(1)}, bf16[128,3072]{1,0:T(8,128)(2,1)S(1)}, u32[]{:S(2)}, u32[]{:S(2)}) collective-permute-start(bf16[128,3072]{1,0:T(8,128)(2,1)S(1)} %collective-permute-done.13.refs_2_), channel_id=1, source_target_pairs={{8,0},{12,4},{0,8},{4,12},{9,1},{13,5},{1,9},{5,13},{10,2},{14,6},... | collective-permute-start | bytes 2359304 | tf_op jit(solution)/shard_map/chip_3_grad/ppermute | solution.py:262
  123.2 46.1 %collective-permute-start.20 = (bf16[128,3072]{1,0:T(8,128)(2,1)S(1)}, bf16[128,3072]{1,0:T(8,128)(2,1)}, u32[]{:S(2)}, u32[]{:S(2)}) collective-permute-start(bf16[128,3072]{1,0:T(8,128)(2,1)S(1)} %get-tuple-element.51), channel_id=1, source_target_pairs={{0,1},{1,2},{2,3},{3,0},{4,5},{5,6},{6,7},{7,4},{8,9},{9,10},{10,1... | collective-permute-start | bytes 2359304 | tf_op jit(solution)/shard_map/sum_up_2/ppermute | solution.py:262
  148.0 20.4 %collective-permute-start.18 = (bf16[128,3072]{1,0:T(8,128)(2,1)S(1)}, bf16[128,3072]{1,0:T(8,128)(2,1)S(1)}, u32[]{:S(2)}, u32[]{:S(2)}) collective-permute-start(bf16[128,3072]{1,0:T(8,128)(2,1)S(1)} %get-tuple-element.41), channel_id=1, source_target_pairs={{1,0},{2,1},{3,2},{0,3},{5,4},{6,5},{7,6},{4,7},{9,8},{10,9},{11,1... | collective-permute-start | bytes 2359304 | tf_op jit(solution)/shard_map/sum_down_3/ppermute | solution.py:262
  149.8 19.5 %copy-start.6 = (f32[128,3072]{1,0:T(8,128)S(1)}, f32[128,3072]{1,0:T(8,128)}, u32[]{:S(2)}) copy-start(f32[128,3072]{1,0:T(8,128)} %get-tuple-element.49) | copy-start | bytes 4718596
  149.8 23.4 %collective-permute-start.15 = (bf16[2,256,3840]{2,1,0:T(8,128)(2,1)}, bf16[2,256,3840]{2,1,0:T(8,128)(2,1)S(1)}, u32[]{:S(2)}, u32[]{:S(2)}) collective-permute-start(bf16[2,256,3840]{2,1,0:T(8,128)(2,1)} %get-tuple-element.35.refs_2_), channel_id=1, source_target_pairs={{0,4},{4,0},{8,12},{12,8},{1,5},{5,1},{9,13},{13,9},{2,6},{6,2},{1... | collective-permute-start | bytes 11796488 | tf_op jit(solution)/shard_map/swap_2/ppermute | solution.py:262
  169.3 4.0 %collective-permute-start.19 = (bf16[2,128,3840]{2,1,0:T(8,128)(2,1)S(1)}, bf16[2,128,3840]{2,1,0:T(8,128)(2,1)S(1)}, u32[]{:S(2)}, u32[]{:S(2)}) collective-permute-start(bf16[2,128,3840]{2,1,0:T(8,128)(2,1)S(1)} %get-tuple-element.42.refs_4_), channel_id=1, source_target_pairs={{0,4},{4,0},{8,12},{12,8},{1,5},{5,1},{9,13},{13,9},{2,6},{6,2},{1... | collective-permute-start | bytes 5898248 | tf_op jit(solution)/shard_map/swap_3/ppermute | solution.py:262
  170.6 22.5 %collective-permute-start.21 = (bf16[128,3072]{1,0:T(8,128)(2,1)S(1)}, bf16[128,3072]{1,0:T(8,128)(2,1)S(1)}, u32[]{:S(2)}, u32[]{:S(2)}) collective-permute-start(bf16[128,3072]{1,0:T(8,128)(2,1)S(1)} %add_convert_fusion), channel_id=1, source_target_pairs={{0,1},{1,2},{2,3},{3,0},{4,5},{5,6},{6,7},{7,4},{8,9},{9,10},{10,1... | collective-permute-start | bytes 2359304 | tf_op jit(solution)/shard_map/sum_up_1/ppermute | solution.py:262
  (16 other events, 187.1 us)
